TPU v7x, 32 devices: a whole 2x2x4 slice. The times are simulated.
32 devices in a mesh: replica: 2 (over x), fsdp: 16 (over z, y, core).
Axes of the slice: x: 2, y: 2, z: 4, core: 2. Of those that a mesh axis runs over, the one named last changes fastest.
Arguments:
- counts: int32 [2], P('replica'), may hold values from 100 to 1000
- inner: bfloat16 [2, 3, 2, 8192, 1024], P('replica', None, None, 'fsdp'), may hold values from -6 to 6
- anchor: bfloat16 [3, 2, 8192, 1024], P(None, None, 'fsdp'), may hold values from -6 to 6
- momentum: float32 [3, 2, 8192, 1024], P(None, None, ('fsdp', 'replica')), may hold values from -6 to 6
Outputs:
- new_weights: bfloat16 [3, 2, 8192, 1024], P(None, None, 'fsdp')
- new_momentum: float32 [3, 2, 8192, 1024], P(None, None, ('fsdp', 'replica'))
Inputs may be any that keep to these rules, and one draw needn't show every extreme that they name: `counts`: inner steps of a group.
All inputs are finite; a program needn't handle non-finite values.
Results may differ from a plain program's by a relative error of at most 0.001.
Values may be sent and summed in bfloat16 or wider, within the bound.
No kernel may reach another device: no remote copies, remote signals or barrier semaphores. Data moves between devices by JAX's collectives and lax.ppermute only.
A program may use at most 128 MiB of HBM per device.

v0:
```python
import jax
import jax.numpy as jnp
from jax import lax
from jax.sharding import PartitionSpec as P

LAYERS = 3


outer_rate = 0.7
momentum_rate = 0.9


def on_device(counts, inner, anchor, momentum):
    total = lax.psum(counts[0], "replica").astype(jnp.float32)
    share = counts[0].astype(jnp.float32) / total
    owned_rows = momentum.shape[2]
    start = lax.axis_index("replica") * owned_rows
    weight_list = []
    moment_list = []
    for layer in range(LAYERS):
        base = anchor[layer].astype(jnp.float32)
        term = share * (base - inner[0, layer].astype(jnp.float32))
        pseudo = lax.psum(term, "replica")
        moment_full = lax.all_gather(momentum[layer], "replica", axis=1, tiled=True)
        moment_next = momentum_rate * moment_full + pseudo
        weights_next = (base - outer_rate * (pseudo + momentum_rate * moment_next)).astype(
            jnp.bfloat16
        )
        moment_list.append(lax.dynamic_slice_in_dim(moment_next, start, owned_rows, 1))
        weight_list.append(weights_next)
    return (jnp.stack(weight_list), jnp.stack(moment_list))


def solution(mesh):
    placed = (
        P("replica"),
        P("replica", None, None, "fsdp", None),
        P(None, None, "fsdp", None),
        P(None, None, ("fsdp", "replica"), None),
    )
    return jax.shard_map(
        on_device,
        mesh=mesh,
        in_specs=placed,
        out_specs=(P(None, None, "fsdp", None), P(None, None, ("fsdp", "replica"), None)),
        check_vma=False,
    )
```

profile of v0, /device:TPU:0, one launch (start us, length us, event | category | flops | bytes accessed | tf_op | source)
XLA Modules:
  0.0 502.4 jit_solution(7992731957040013166)
XLA Ops:
  7.2 0.0 all-gather.11.cloned.1.call-start
  7.2 5.8 %fusion.9 = (f32[1,2,256,1024]{3,2,1,0:T(8,128)}, f32[1,2,256,1024]{3,2,1,0:T(8,128)}, f32[1,2,256,1024]{3,2,1,0:T(8,128)}) fusion(f32[3,2,256,1024]{3,2,1,0:T(8,128)} %param.7), kind=kLoop, calls=%fused_computation.23 | loop fusion | bytes 12582912 | tf_op jit(solution)/shard_map/slice | solution.py:24
  13.0 0.0 all-gather.11.cloned.1.call-update
  13.0 0.0 all-reduce.3.cloned.1.call-start
  13.0 5.9 %psum.28 = s32[]{:T(128)} all-reduce(s32[]{:T(128)} %bitcast.1), channel_id=1, replica_groups=mesh['replica'=2,'fsdp'=16] {'replica'}, use_global_device_ids=true, to_apply=%region_0.0 | all-reduce | flops 1 | bytes 8 | tf_op jit(solution)/shard_map/psum | solution.py:14
  20.2 11.4 %fusion = (f32[2,512,1024]{2,1,0:T(8,128)}, f32[2,512,1024]{2,1,0:T(8,128)}, f32[2,512,1024]{2,1,0:T(8,128)}) fusion(bf16[1,3,2,512,1024]{4,3,2,1,0:T(8,128)(2,1)} %param.5, f32[]{:T(128)S(6)} %div.3, bf16[3,2,512,1024]{3,2,1,0:T(8,128)(2,1)} %param.6), kind=kLoop, calls=%fused_computation.8 | loop fusion | flops 12582912 | bytes 25165828 | tf_op jit(solution)/shard_map/mul | solution.py:22
  31.6 0.0 all-reduce.3.cloned.1.call-update
  31.7 0.0 all-gather.9.cloned.1.call-start
  31.7 0.7 all-gather.9.cloned.1.call-update
  32.4 0.0 all-gather.7.cloned.1.call-start
  32.4 0.5 all-gather.7.cloned.1.call-update
  33.0 39.6 %all-gather.11.cloned.1.call-done = f32[1,2,512,1024]{3,2,1,0:T(8,128)} async-done(((f32[1,2,256,1024]{3,2,1,0:T(8,128)}), f32[1,2,512,1024]{3,2,1,0:T(8,128)}) %all-gather.11.cloned.1.call-update) | async-done | bytes 4194320 | tf_op jit(solution)/shard_map/all_gather | solution.py:24
  72.6 292.7 %all-reduce.3.cloned.1.call-done = (f32[2,512,1024]{2,1,0:T(8,128)}, f32[2,512,1024]{2,1,0:T(8,128)}, f32[2,512,1024]{2,1,0:T(8,128)}) async-done(((f32[2,512,1024]{2,1,0:T(8,128)}, f32[2,512,1024]{2,1,0:T(8,128)}, f32[2,512,1024]{2,1,0:T(8,128)}), (f32[2,512,1024]{2,1,0:T(8,128)}, f32[2,512,1024]{2,1,0:T(8,128)}, f32[2,512,1024]{2,1,0:T(8,128)})) %all-reduce.3.cloned.1.call-update) | async-done | bytes 12582928 | tf_op jit(solution)/shard_map/psum | solution.py:23
  365.3 6.7 %bitcast_add_fusion = (f32[2,512,1024]{2,1,0:T(8,128)S(1)}, bf16[1,2,512,1024]{3,2,1,0:T(8,128)(2,1)}) fusion(f32[2,512,1024]{2,1,0:T(8,128)} %get-tuple-element.2, f32[1,2,512,1024]{3,2,1,0:T(8,128)} %all-gather.11.cloned.1.call-done, bf16[3,2,512,1024]{3,2,1,0:T(8,128)(2,1)} %param.6), kind=kLoop, calls=%fused_computation.14 | loop fusion | flops 8388608 | bytes 16777216 | tf_op jit(solution)/shard_map/add | solution.py:25
  372.0 0.2 dynamic-slice_bitcast_fusion
  372.3 51.4 %all-gather.9.cloned.1.call-done = f32[1,2,512,1024]{3,2,1,0:T(8,128)} async-done(((f32[1,2,256,1024]{3,2,1,0:T(8,128)}), f32[1,2,512,1024]{3,2,1,0:T(8,128)}) %all-gather.9.cloned.1.call-update) | async-done | bytes 4194320 | tf_op jit(solution)/shard_map/all_gather | solution.py:24
  423.7 6.7 %bitcast_add_fusion.1 = (f32[2,512,1024]{2,1,0:T(8,128)S(1)}, bf16[1,2,512,1024]{3,2,1,0:T(8,128)(2,1)}) fusion(f32[2,512,1024]{2,1,0:T(8,128)} %get-tuple-element.3, f32[1,2,512,1024]{3,2,1,0:T(8,128)} %all-gather.9.cloned.1.call-done, bf16[3,2,512,1024]{3,2,1,0:T(8,128)(2,1)} %param.6), kind=kLoop, calls=%fused_computation.15 | loop fusion | flops 8388608 | bytes 16777216 | tf_op jit(solution)/shard_map/add | solution.py:25
  430.4 1.5 dynamic-slice_bitcast_fusion.1
  431.8 50.0 %all-gather.7.cloned.1.call-done = f32[1,2,512,1024]{3,2,1,0:T(8,128)} async-done(((f32[1,2,256,1024]{3,2,1,0:T(8,128)}), f32[1,2,512,1024]{3,2,1,0:T(8,128)}) %all-gather.7.cloned.1.call-update) | async-done | bytes 4194320 | tf_op jit(solution)/shard_map/all_gather | solution.py:24
  481.9 5.4 %bitcast_add_fusion.2 = (f32[2,512,1024]{2,1,0:T(8,128)S(1)}, bf16[1,2,512,1024]{3,2,1,0:T(8,128)(2,1)S(1)}) fusion(f32[2,512,1024]{2,1,0:T(8,128)} %get-tuple-element.4, f32[1,2,512,1024]{3,2,1,0:T(8,128)} %all-gather.7.cloned.1.call-done, bf16[3,2,512,1024]{3,2,1,0:T(8,128)(2,1)} %param.6), kind=kLoop, calls=%fused_computation.16 | loop fusion | flops 8388608 | bytes 16777216 | tf_op jit(solution)/shard_map/add | solution.py:25
  487.2 0.0 copy-start
  487.2 0.1 dynamic-slice_bitcast_fusion.2
  487.4 1.4 copy-done
  488.8 0.0 copy-start.1
  488.8 0.0 copy-start.2
  488.8 3.5 pad_maximum_fusion.1
  492.3 0.0 copy-done.1
  492.3 0.4 copy-done.2
  492.7 3.1 pad_maximum_fusion
Async XLA Ops:
  7.2 65.4 %all-gather.11.cloned.1.call-start = ((), (), s32[]{:S(2)}) async-start(), calls=%async_computation.2 | async-start | bytes 6291456 | tf_op jit(solution)/shard_map/all_gather | solution.py:24
  13.0 352.3 %all-reduce.3.cloned.1.call-start = ((), (), s32[]{:S(2)}) async-start(), calls=%async_computation.3 | async-start | bytes 25165824 | tf_op jit(solution)/shard_map/psum | solution.py:23
  31.7 392.0 %all-gather.9.cloned.1.call-start = ((), (), s32[]{:S(2)}) async-start(), calls=%async_computation.1 | async-start | bytes 6291456 | tf_op jit(solution)/shard_map/all_gather | solution.py:24
  32.4 449.5 %all-gather.7.cloned.1.call-start = ((), (), s32[]{:S(2)}) async-start(), calls=%async_computation | async-start | bytes 6291456 | tf_op jit(solution)/shard_map/all_gather | solution.py:24
  487.2 1.6 copy-start
  488.8 3.5 copy-start.1
  488.8 3.9 copy-start.2
Sparse Core Ops, SparseCore 0:
  13.1 59.4 all-gather.10
  75.9 289.4 all-reduce.2
  366.9 56.7 all-gather.8
  425.1 56.7 all-gather.6
where the time goes:
time: 503 us; the launch traced here: 502 us
  waiting for transfers between devices  435 us (86%)
  other arithmetic  36.8 us (7%)
  between operations  15.1 us (3%)
  local copies, waits for them, and re-layouts  9.43 us (2%)
  blocking collectives  5.85 us (1%)
    psum x1, waiting for transfers between devices, on_device(): pseudo = lax.psum(term, 'replica')  293 us
    all_gather x3, waiting for transfers between devices, on_device(): moment_full = lax.all_gather(momentum[layer], 'replica', axis=1, tiled=True)  141 us
    add x3, other arithmetic, on_device(): moment_next = momentum_rate * moment_full + pseudo  18.8 us
    mul x1, other arithmetic, on_device(): term = share * (base - inner[0, layer].astype(jnp.float32))  11.4 us
  transfers between devices with their start and end apart: 4, of which 4 were waited for; matrix products, arithmetic and copies ran while one was open for 5% of the time, Pallas kernels for 0%

commit v1 on v0

v1 whole, which is shorter than its diff:
```python
import jax
import jax.numpy as jnp
from jax import lax
from jax.sharding import PartitionSpec as P

outer_rate = 0.7
momentum_rate = 0.9


def solution(mesh):
    groups = mesh.shape["replica"]

    def shifted(value, shift):
        pairs = [(i, (i + shift) % groups) for i in range(groups)]
        return lax.ppermute(value, "replica", pairs)

    def on_device(counts, inner, anchor, momentum):
        layers, kinds, owned = momentum.shape[:3]
        me = lax.axis_index("replica")
        start = me * owned
        parts = [(i, j) for i in range(layers) for j in range(kinds)]
        mine = counts[0].astype(jnp.float32)
        others = [shifted(counts, s)[0].astype(jnp.float32) for s in range(1, groups)]
        total = mine + sum(others)

        def rows(array, part, at):
            return lax.dynamic_slice_in_dim(array[part], at * owned, owned, 0)

        arrived = {}
        for part in parts:
            arrived[part] = [
                shifted(rows(inner[0], part, (me + s) % groups), s) for s in range(1, groups)
            ]
        weights = jnp.zeros(anchor.shape, jnp.bfloat16)
        moments = jnp.zeros(momentum.shape, jnp.float32)
        for part in parts:
            base = rows(anchor, part, me).astype(jnp.float32)
            acc = mine * (base - rows(inner[0], part, me).astype(jnp.float32))
            for count, block in zip(others, arrived[part]):
                acc = acc + count * (base - block.astype(jnp.float32))
            pseudo = acc / total
            moment = momentum_rate * momentum[part] + pseudo
            new = (base - outer_rate * (pseudo + momentum_rate * moment)).astype(jnp.bfloat16)
            moments = moments.at[part].set(moment)
            weights = lax.dynamic_update_slice(weights, new[None, None], (*part, start, 0))
            for s in range(1, groups):
                block = shifted(new, s)
                source = (me - s) % groups
                weights = lax.dynamic_update_slice(
                    weights, block[None, None], (*part, source * owned, 0)
                )
        return weights, moments

    placed = (
        P("replica"),
        P("replica", None, None, "fsdp", None),
        P(None, None, "fsdp", None),
        P(None, None, ("fsdp", "replica"), None),
    )
    return jax.shard_map(
        on_device,
        mesh=mesh,
        in_specs=placed,
        out_specs=(P(None, None, "fsdp", None), P(None, None, ("fsdp", "replica"), None)),
        check_vma=False,
    )
```

time: 503 us -> 163 us (0.32)
  waiting for transfers between devices: 435 us -> 103 us
  other arithmetic: 36.8 us -> 18.4 us
  starting transfers between devices: 0.16 us -> 15.2 us
  local copies, waits for them, and re-layouts: 9.43 us -> 23.8 us
  between operations: 15.1 us -> 2.18 us
  blocking collectives: 5.85 us -> 0 us
    psum x1 -> x0, waiting for transfers between devices: 293 us -> none  [on_device(): pseudo = lax.psum(term, 'replica')]
    all_gather x3 -> x0, waiting for transfers between devices: 141 us -> none  [on_device(): moment_full = lax.all_gather(momentum[layer], 'replica', axis=1, tiled=True)]
    ppermute x0 -> x13, waiting for transfers between devices: none -> 103 us  [shifted(): return lax.ppermute(value, 'replica', pairs)]
    add x3 -> x0, other arithmetic: 18.8 us -> none  [on_device(): moment_next = momentum_rate * moment_full + pseudo]
    ppermute x0 -> x13, starting transfers between devices: none -> 15.2 us  [shifted(): return lax.ppermute(value, 'replica', pairs)]
    dynamic_update_slice x0 -> x6, other arithmetic: none -> 12.6 us  [on_device(): lax.dynamic_update_slice(weights, new[None, None], (*part, start, 0))]
    mul x1 -> x0, other arithmetic: 11.4 us -> none  [on_device(): term = share * (base - inner[0, layer].astype(jnp.float32))]
    dynamic_update_slice x0 -> x6, local copies, waits for them, and re-layouts: none -> 6 us  [on_device(): lax.dynamic_update_slice(weights, block[None, None], (*part, source * own...]
  transfers between devices with their start and end apart: 4 -> 13, of which waited for: 4 -> 10; matrix products, arithmetic and copies ran while one was open for 5% -> 14% of each run, Pallas kernels for 0% -> 0%
where the time goes in v1:
time: 163 us
  waiting for transfers between devices  103 us (63%)
  local copies, waits for them, and re-layouts  23.8 us (15%)
  other arithmetic  18.4 us (11%)
  starting transfers between devices  15.2 us (9%)
  between operations  2.18 us (1%)
    ppermute x13, waiting for transfers between devices, shifted(): return lax.ppermute(value, 'replica', pairs)  103 us
    ppermute x13, starting transfers between devices, shifted(): return lax.ppermute(value, 'replica', pairs)  15.2 us
    dynamic_update_slice x6, other arithmetic, on_device(): lax.dynamic_update_slice(weights, new[None, None], (*part, start, 0))  12.6 us
    slice x2, local copies, waits for them, and re-layouts, rows(): return lax.dynamic_slice_in_dim(array[part], at * owned, owned, 0)  10.7 us
    dynamic_update_slice x6, local copies, waits for them, and re-layouts, on_device(): lax.dynamic_update_slice(weights, block[None, None], (*part, source * own...  6 us
    scatter x5, other arithmetic, on_device(): moments = moments.at[part].set(moment)  4.29 us
    dynamic_slice x6, local copies, waits for them, and re-layouts, rows(): return lax.dynamic_slice_in_dim(array[part], at * owned, owned, 0)  4.17 us
  transfers between devices with their start and end apart: 13, of which 10 were waited for; matrix products, arithmetic and copies ran while one was open for 14% of the time, Pallas kernels for 0%

profile of v1, /device:TPU:0, one launch (start us, length us, event | category | flops | bytes accessed | tf_op | source)
XLA Modules:
  0.0 162.9 jit_solution(11287657527683224095)
XLA Ops:
  0.6 5.2 %fusion.38 = (bf16[1,1,512,1024]{3,2,1,0:T(8,128)(2,1)S(1)}, bf16[1,1,512,1024]{3,2,1,0:T(8,128)(2,1)S(1)}, bf16[1,1,512,1024]{3,2,1,0:T(8,128)(2,1)S(1)}, bf16[...) fusion(bf16[3,2,512,1024]{3,2,1,0:T(8,128)(2,1)} %bitcast.199), kind=kLoop, calls=%fused_computation.79 | loop fusion | bytes 12582912 | tf_op jit(solution)/shard_map/slice | solution.py:27
  5.8 1.9 %dynamic-slice_bitcast_fusion.5 = bf16[256,1024]{1,0:T(8,128)(2,1)} fusion(bf16[1,1,512,1024]{3,2,1,0:T(8,128)(2,1)} %get-tuple-element.97, s32[]{:T(128)S(6)} %select_n.69), kind=kLoop, calls=%fused_computation.77 | loop fusion | bytes 1048580 | tf_op jit(solution)/shard_map/dynamic_slice | solution.py:27
  7.7 2.9 %collective-permute-start.1 = (bf16[256,1024]{1,0:T(8,128)(2,1)}, bf16[256,1024]{1,0:T(8,128)(2,1)}, u32[]{:S(2)}, u32[]{:S(2)}) collective-permute-start(bf16[256,1024]{1,0:T(8,128)(2,1)} %dynamic-slice_bitcast_fusion.5), channel_id=1, source_target_pairs={{0,16},{16,0},{1,17},{17,1},{2,18},{18,2},{3,19},{19,3},{4,20},{20... | collective-permute-start | bytes 1572872 | tf_op jit(solution)/shard_map/ppermute | solution.py:15
  11.3 5.5 %fusion.37 = (bf16[1,1,512,1024]{3,2,1,0:T(8,128)(2,1)}, bf16[1,1,512,1024]{3,2,1,0:T(8,128)(2,1)}, bf16[1,1,512,1024]{3,2,1,0:T(8,128)(2,1)}, bf16[1,1,512,1024...) fusion(bf16[3,2,512,1024]{3,2,1,0:T(8,128)(2,1)} %param.18), kind=kLoop, calls=%fused_computation.78 | loop fusion | bytes 12582912 | tf_op jit(solution)/shard_map/slice | solution.py:27
  16.9 6.0 %collective-permute-done = s32[1]{0:T(128)} collective-permute-done((s32[1]{0:T(128)}, s32[1]{0:T(128)}, u32[]{:S(2)}, u32[]{:S(2)}) %collective-permute-start) | collective-permute-done | bytes 36 | tf_op jit(solution)/shard_map/ppermute | solution.py:15
  25.1 2.7 %bitcast_dynamic-update-slice_fusion.16 = (bf16[3,2,512,1024]{3,2,1,0:T(8,128)(2,1)S(1)}, bf16[256,1024]{1,0:T(8,128)(2,1)}) fusion(bf16[3,2,512,1024]{3,2,1,0:T(8,128)(2,1)S(1)} %broadcast_in_dim.40, s32[]{:T(128)S(6)} %select_n.67, f32[3,2,256,1024]{3,2,1,0:T(8,128)} %param.19, f32[]{:T(128)S(6)} %add.138, bf16[256,1024]{1,0:T(8,128)(2,1)} %collective-permute-done.1, ...), kind=kLoop, calls=%fused_computation.71 | loop fusion | flops 4194304 | bytes 3670032 | tf_op jit(solution)/shard_map/dynamic_update_slice | solution.py:45
  27.8 1.7 %collective-permute-start.2 = (bf16[256,1024]{1,0:T(8,128)(2,1)}, bf16[256,1024]{1,0:T(8,128)(2,1)}, u32[]{:S(2)}, u32[]{:S(2)}) collective-permute-start(bf16[256,1024]{1,0:T(8,128)(2,1)} %get-tuple-element.85), channel_id=1, source_target_pairs={{0,16},{16,0},{1,17},{17,1},{2,18},{18,2},{3,19},{19,3},{4,20},{20... | collective-permute-start | bytes 1572872 | tf_op jit(solution)/shard_map/ppermute | solution.py:15
  29.5 1.1 dynamic-slice_bitcast_fusion.4
  30.7 1.7 %collective-permute-start.3 = (bf16[256,1024]{1,0:T(8,128)(2,1)}, bf16[256,1024]{1,0:T(8,128)(2,1)}, u32[]{:S(2)}, u32[]{:S(2)}) collective-permute-start(bf16[256,1024]{1,0:T(8,128)(2,1)} %dynamic-slice_bitcast_fusion.4), channel_id=1, source_target_pairs={{0,16},{16,0},{1,17},{17,1},{2,18},{18,2},{3,19},{19,3},{4,20},{20... | collective-permute-start | bytes 1572872 | tf_op jit(solution)/shard_map/ppermute | solution.py:15
  32.4 10.6 %collective-permute-done.2 = bf16[256,1024]{1,0:T(8,128)(2,1)} collective-permute-done((bf16[256,1024]{1,0:T(8,128)(2,1)}, bf16[256,1024]{1,0:T(8,128)(2,1)}, u32[]{:S(2)}, u32[]{:S(2)}) %collective-permute-start.2) | collective-permute-done | bytes 524320 | tf_op jit(solution)/shard_map/ppermute | solution.py:15
  43.0 1.9 %bitcast_dynamic-update-slice_fusion.15 = bf16[3,2,512,1024]{3,2,1,0:T(8,128)(2,1)} fusion(bf16[3,2,512,1024]{3,2,1,0:T(8,128)(2,1)} %copy-done.5, s32[]{:T(128)S(6)} %select_n.71, bf16[256,1024]{1,0:T(8,128)(2,1)} %collective-permute-done.2), kind=kLoop, calls=%fused_computation.70 | loop fusion | bytes 1048580 | tf_op jit(solution)/shard_map/dynamic_update_slice | solution.py:49
  44.8 7.6 %collective-permute-done.3 = bf16[256,1024]{1,0:T(8,128)(2,1)} collective-permute-done((bf16[256,1024]{1,0:T(8,128)(2,1)}, bf16[256,1024]{1,0:T(8,128)(2,1)}, u32[]{:S(2)}, u32[]{:S(2)}) %collective-permute-start.3) | collective-permute-done | bytes 524320 | tf_op jit(solution)/shard_map/ppermute | solution.py:15
  52.5 3.2 %bitcast_dynamic-update-slice_fusion.14 = (bf16[3,2,512,1024]{3,2,1,0:T(8,128)(2,1)}, bf16[256,1024]{1,0:T(8,128)(2,1)S(1)}) fusion(bf16[3,2,512,1024]{3,2,1,0:T(8,128)(2,1)} %bitcast_dynamic-update-slice_fusion.15, s32[]{:T(128)S(6)} %select_n.67, f32[3,2,256,1024]{3,2,1,0:T(8,128)} %param.19, f32[]{:T(128)S(6)} %add.138, ...), kind=kLoop, calls=%fused_computation.69 | loop fusion | flops 4194304 | bytes 3671048 | tf_op jit(solution)/shard_map/dynamic_update_slice | solution.py:45
  55.6 1.4 collective-permute-start.4
  57.0 1.1 dynamic-slice_bitcast_fusion.3
  58.8 11.7 %collective-permute-done.4 = bf16[256,1024]{1,0:T(8,128)(2,1)S(1)} collective-permute-done((bf16[256,1024]{1,0:T(8,128)(2,1)S(1)}, bf16[256,1024]{1,0:T(8,128)(2,1)S(1)}, u32[]{:S(2)}, u32[]{:S(2)}) %collective-permute-start.4) | collective-permute-done | bytes 524320 | tf_op jit(solution)/shard_map/ppermute | solution.py:15
  71.3 7.7 %collective-permute-done.5 = bf16[256,1024]{1,0:T(8,128)(2,1)S(1)} collective-permute-done((bf16[256,1024]{1,0:T(8,128)(2,1)S(1)}, bf16[256,1024]{1,0:T(8,128)(2,1)S(1)}, u32[]{:S(2)}, u32[]{:S(2)}) %collective-permute-start.5) | collective-permute-done | bytes 524320 | tf_op jit(solution)/shard_map/ppermute | solution.py:15
  79.0 2.7 %bitcast_dynamic-update-slice_fusion.12 = (bf16[3,2,512,1024]{3,2,1,0:T(8,128)(2,1)}, bf16[256,1024]{1,0:T(8,128)(2,1)S(1)}) fusion(bf16[3,2,512,1024]{3,2,1,0:T(8,128)(2,1)} %bitcast_dynamic-update-slice_fusion.13, s32[]{:T(128)S(6)} %select_n.67, f32[3,2,256,1024]{3,2,1,0:T(8,128)} %param.19, f32[]{:T(128)S(6)} %add.138, ...), kind=kLoop, calls=%fused_computation.67 | loop fusion | flops 4194304 | bytes 3671048 | tf_op jit(solution)/shard_map/dynamic_update_slice | solution.py:45
  81.8 1.1 collective-permute-start.6
  82.9 1.0 collective-permute-start.7
  83.9 1.2 collective-permute-start.9
  86.7 9.9 %collective-permute-done.6 = bf16[256,1024]{1,0:T(8,128)(2,1)S(1)} collective-permute-done((bf16[256,1024]{1,0:T(8,128)(2,1)S(1)}, bf16[256,1024]{1,0:T(8,128)(2,1)S(1)}, u32[]{:S(2)}, u32[]{:S(2)}) %collective-permute-start.6) | collective-permute-done | bytes 524320 | tf_op jit(solution)/shard_map/ppermute | solution.py:15
  97.5 10.4 %collective-permute-done.7 = bf16[256,1024]{1,0:T(8,128)(2,1)S(1)} collective-permute-done((bf16[256,1024]{1,0:T(8,128)(2,1)S(1)}, bf16[256,1024]{1,0:T(8,128)(2,1)S(1)}, u32[]{:S(2)}, u32[]{:S(2)}) %collective-permute-start.7) | collective-permute-done | bytes 524320 | tf_op jit(solution)/shard_map/ppermute | solution.py:15
  107.9 1.3 bitcast_dynamic-update-slice_fusion.10
  109.2 1.1 collective-permute-start.8
  110.3 1.5 fusion.30
  112.6 2.7 %bitcast_dynamic-update-slice_fusion.4 = f32[3,2,256,1024]{3,2,1,0:T(8,128)S(1)} fusion(f32[3,2,256,1024]{3,2,1,0:T(8,128)S(1)} %scatter.20, s32[]{:T(128)} %bitcast.47, s32[]{:T(128)} %bitcast.48, f32[3,2,256,1024]{3,2,1,0:T(8,128)S(1)} %bitcast.198, f32[]{:T(128)S(6)} %add.138, bf16[256,1024]{1,0:T(8,128)(2,1)} %collective-permute-done.3, f32[]{:T(128)} %bitcast.5, ...), kind=kLoop, calls=%fused_computation.52 | loop fusion | flops 2883584 | bytes 3670040 | tf_op jit(solution)/shard_map/scatter | solution.py:44
  115.3 22.7 %collective-permute-done.8 = bf16[256,1024]{1,0:T(8,128)(2,1)S(1)} collective-permute-done((bf16[256,1024]{1,0:T(8,128)(2,1)S(1)}, bf16[256,1024]{1,0:T(8,128)(2,1)S(1)}, u32[]{:S(2)}, u32[]{:S(2)}) %collective-permute-start.8) | collective-permute-done | bytes 524320 | tf_op jit(solution)/shard_map/ppermute | solution.py:15
  138.8 1.3 bitcast_dynamic-update-slice_fusion.8
  141.8 8.7 %collective-permute-done.10 = bf16[256,1024]{1,0:T(8,128)(2,1)S(1)} collective-permute-done((bf16[256,1024]{1,0:T(8,128)(2,1)S(1)}, bf16[256,1024]{1,0:T(8,128)(2,1)S(1)}, u32[]{:S(2)}, u32[]{:S(2)}) %collective-permute-start.10) | collective-permute-done | bytes 524320 | tf_op jit(solution)/shard_map/ppermute | solution.py:15
  151.3 1.3 bitcast_dynamic-update-slice_fusion.6
  154.0 8.1 %collective-permute-done.12 = bf16[256,1024]{1,0:T(8,128)(2,1)S(1)} collective-permute-done((bf16[256,1024]{1,0:T(8,128)(2,1)S(1)}, bf16[256,1024]{1,0:T(8,128)(2,1)S(1)}, u32[]{:S(2)}, u32[]{:S(2)}) %collective-permute-start.12) | collective-permute-done | bytes 524320 | tf_op jit(solution)/shard_map/ppermute | solution.py:15
  (57 shorter events, 11.7 us)
Async XLA Ops:
  7.7 15.9 %collective-permute-start.1 = (bf16[256,1024]{1,0:T(8,128)(2,1)}, bf16[256,1024]{1,0:T(8,128)(2,1)}, u32[]{:S(2)}, u32[]{:S(2)}) collective-permute-start(bf16[256,1024]{1,0:T(8,128)(2,1)} %dynamic-slice_bitcast_fusion.5), channel_id=1, source_target_pairs={{0,16},{16,0},{1,17},{17,1},{2,18},{18,2},{3,19},{19,3},{4,20},{20... | collective-permute-start | bytes 1572872 | tf_op jit(solution)/shard_map/ppermute | solution.py:15
  10.6 12.2 %collective-permute-start = (s32[1]{0:T(128)}, s32[1]{0:T(128)}, u32[]{:S(2)}, u32[]{:S(2)}) collective-permute-start(s32[1]{0:T(128)} %param.16), channel_id=1, source_target_pairs={{0,16},{16,0},{1,17},{17,1},{2,18},{18,2},{3,19},{19,3},{4,20},{20... | collective-permute-start | bytes 20 | tf_op jit(solution)/shard_map/ppermute | solution.py:15
  23.6 1.2 copy-start.1
  23.6 1.5 copy-start.11
  23.6 6.0 %copy-start.3 = (bf16[1,1,512,1024]{3,2,1,0:T(8,128)(2,1)S(1)}, bf16[1,1,512,1024]{3,2,1,0:T(8,128)(2,1)}, u32[]{:S(2)}) copy-start(bf16[1,1,512,1024]{3,2,1,0:T(8,128)(2,1)} %get-tuple-element.96) | copy-start | bytes 3145732
  27.8 2.9 %copy-start.5 = (bf16[3,2,512,1024]{3,2,1,0:T(8,128)(2,1)}, bf16[3,2,512,1024]{3,2,1,0:T(8,128)(2,1)S(1)}, u32[]{:S(2)}) copy-start(bf16[3,2,512,1024]{3,2,1,0:T(8,128)(2,1)S(1)} %get-tuple-element.84) | copy-start | bytes 18874372
  27.8 15.2 %collective-permute-start.2 = (bf16[256,1024]{1,0:T(8,128)(2,1)}, bf16[256,1024]{1,0:T(8,128)(2,1)}, u32[]{:S(2)}, u32[]{:S(2)}) collective-permute-start(bf16[256,1024]{1,0:T(8,128)(2,1)} %get-tuple-element.85), channel_id=1, source_target_pairs={{0,16},{16,0},{1,17},{17,1},{2,18},{18,2},{3,19},{19,3},{4,20},{20... | collective-permute-start | bytes 1572872 | tf_op jit(solution)/shard_map/ppermute | solution.py:15
  30.7 21.8 %collective-permute-start.3 = (bf16[256,1024]{1,0:T(8,128)(2,1)}, bf16[256,1024]{1,0:T(8,128)(2,1)}, u32[]{:S(2)}, u32[]{:S(2)}) collective-permute-start(bf16[256,1024]{1,0:T(8,128)(2,1)} %dynamic-slice_bitcast_fusion.4), channel_id=1, source_target_pairs={{0,16},{16,0},{1,17},{17,1},{2,18},{18,2},{3,19},{19,3},{4,20},{20... | collective-permute-start | bytes 1572872 | tf_op jit(solution)/shard_map/ppermute | solution.py:15
  32.4 46.6 %copy-start = (bf16[1,1,512,1024]{3,2,1,0:T(8,128)(2,1)S(1)}, bf16[1,1,512,1024]{3,2,1,0:T(8,128)(2,1)}, u32[]{:S(2)}) copy-start(bf16[1,1,512,1024]{3,2,1,0:T(8,128)(2,1)} %get-tuple-element.95) | copy-start | bytes 3145732
  32.4 46.6 %copy-start.10 = (bf16[1,1,512,1024]{3,2,1,0:T(8,128)(2,1)S(1)}, bf16[1,1,512,1024]{3,2,1,0:T(8,128)(2,1)}, u32[]{:S(2)}) copy-start(bf16[1,1,512,1024]{3,2,1,0:T(8,128)(2,1)} %get-tuple-element.88) | copy-start | bytes 3145732
  52.5 55.4 %slice-start = ((s8[6291456]{0:T(1024)(128)(4,1)}), s8[4194304]{0:T(1024)(128)(4,1)S(1)}, s32[]{:S(2)}) async-start(s8[6291456]{0:T(1024)(128)(4,1)} %bitcast.197), calls=%async_computation | async-start | bytes 8388608
  52.5 55.4 %copy-start.9 = (bf16[1,1,512,1024]{3,2,1,0:T(8,128)(2,1)S(1)}, bf16[1,1,512,1024]{3,2,1,0:T(8,128)(2,1)}, u32[]{:S(2)}) copy-start(bf16[1,1,512,1024]{3,2,1,0:T(8,128)(2,1)} %get-tuple-element.87) | copy-start | bytes 3145732
  55.6 14.9 %collective-permute-start.4 = (bf16[256,1024]{1,0:T(8,128)(2,1)S(1)}, bf16[256,1024]{1,0:T(8,128)(2,1)S(1)}, u32[]{:S(2)}, u32[]{:S(2)}) collective-permute-start(bf16[256,1024]{1,0:T(8,128)(2,1)S(1)} %get-tuple-element.83), channel_id=1, source_target_pairs={{0,16},{16,0},{1,17},{17,1},{2,18},{18,2},{3,19},{19,3},{4,20},{20... | collective-permute-start | bytes 1572872 | tf_op jit(solution)/shard_map/ppermute | solution.py:15
  58.1 20.9 %collective-permute-start.5 = (bf16[256,1024]{1,0:T(8,128)(2,1)S(1)}, bf16[256,1024]{1,0:T(8,128)(2,1)S(1)}, u32[]{:S(2)}, u32[]{:S(2)}) collective-permute-start(bf16[256,1024]{1,0:T(8,128)(2,1)S(1)} %dynamic-slice_bitcast_fusion.3), channel_id=1, source_target_pairs={{0,16},{16,0},{1,17},{17,1},{2,18},{18,2},{3,19},{19,3},{4,20},{20... | collective-permute-start | bytes 1572872 | tf_op jit(solution)/shard_map/ppermute | solution.py:15
  70.5 39.9 %copy-start.2 = (bf16[1,1,512,1024]{3,2,1,0:T(8,128)(2,1)S(1)}, bf16[1,1,512,1024]{3,2,1,0:T(8,128)(2,1)}, u32[]{:S(2)}) copy-start(bf16[1,1,512,1024]{3,2,1,0:T(8,128)(2,1)} %get-tuple-element.97) | copy-start | bytes 3145732
  70.5 39.9 %copy-start.12 = (bf16[1,1,512,1024]{3,2,1,0:T(8,128)(2,1)S(1)}, bf16[1,1,512,1024]{3,2,1,0:T(8,128)(2,1)}, u32[]{:S(2)}) copy-start(bf16[1,1,512,1024]{3,2,1,0:T(8,128)(2,1)} %get-tuple-element.90) | copy-start | bytes 3145732
  79.0 28.8 %slice-start.1 = ((s8[6291456]{0:T(1024)(128)(4,1)}), s8[2097152]{0:T(1024)(128)(4,1)S(1)}, s32[]{:S(2)}) async-start(s8[6291456]{0:T(1024)(128)(4,1)} %bitcast.197), calls=%async_computation.1 | async-start | bytes 4194304
  81.8 14.9 %collective-permute-start.6 = (bf16[256,1024]{1,0:T(8,128)(2,1)S(1)}, bf16[256,1024]{1,0:T(8,128)(2,1)S(1)}, u32[]{:S(2)}, u32[]{:S(2)}) collective-permute-start(bf16[256,1024]{1,0:T(8,128)(2,1)S(1)} %get-tuple-element.81), channel_id=1, source_target_pairs={{0,16},{16,0},{1,17},{17,1},{2,18},{18,2},{3,19},{19,3},{4,20},{20... | collective-permute-start | bytes 1572872 | tf_op jit(solution)/shard_map/ppermute | solution.py:15
  82.9 25.0 %collective-permute-start.7 = (bf16[256,1024]{1,0:T(8,128)(2,1)S(1)}, bf16[256,1024]{1,0:T(8,128)(2,1)S(1)}, u32[]{:S(2)}, u32[]{:S(2)}) collective-permute-start(bf16[256,1024]{1,0:T(8,128)(2,1)S(1)} %dynamic-slice_bitcast_fusion.2), channel_id=1, source_target_pairs={{0,16},{16,0},{1,17},{17,1},{2,18},{18,2},{3,19},{19,3},{4,20},{20... | collective-permute-start | bytes 1572872 | tf_op jit(solution)/shard_map/ppermute | solution.py:15
  83.9 54.9 %collective-permute-start.9 = (bf16[256,1024]{1,0:T(8,128)(2,1)S(1)}, bf16[256,1024]{1,0:T(8,128)(2,1)S(1)}, u32[]{:S(2)}, u32[]{:S(2)}) collective-permute-start(bf16[256,1024]{1,0:T(8,128)(2,1)S(1)} %dynamic-slice_bitcast_fusion.1), channel_id=1, source_target_pairs={{0,16},{16,0},{1,17},{17,1},{2,18},{18,2},{3,19},{19,3},{4,20},{20... | collective-permute-start | bytes 1572872 | tf_op jit(solution)/shard_map/ppermute | solution.py:15
  85.1 66.2 %collective-permute-start.11 = (bf16[256,1024]{1,0:T(8,128)(2,1)S(1)}, bf16[256,1024]{1,0:T(8,128)(2,1)S(1)}, u32[]{:S(2)}, u32[]{:S(2)}) collective-permute-start(bf16[256,1024]{1,0:T(8,128)(2,1)S(1)} %dynamic-slice_bitcast_fusion), channel_id=1, source_target_pairs={{0,16},{16,0},{1,17},{17,1},{2,18},{18,2},{3,19},{19,3},{4,20},{20... | collective-permute-start | bytes 1572872 | tf_op jit(solution)/shard_map/ppermute | solution.py:15
  109.2 3.4 %copy-start.4 = (bf16[1,1,512,1024]{3,2,1,0:T(8,128)(2,1)S(1)}, bf16[1,1,512,1024]{3,2,1,0:T(8,128)(2,1)}, u32[]{:S(2)}) copy-start(bf16[1,1,512,1024]{3,2,1,0:T(8,128)(2,1)} %get-tuple-element.96) | copy-start | bytes 3145732
  109.2 3.4 %copy-start.13 = (bf16[1,1,512,1024]{3,2,1,0:T(8,128)(2,1)S(1)}, bf16[1,1,512,1024]{3,2,1,0:T(8,128)(2,1)}, u32[]{:S(2)}) copy-start(bf16[1,1,512,1024]{3,2,1,0:T(8,128)(2,1)} %get-tuple-element.89) | copy-start | bytes 3145732
  109.2 28.7 %collective-permute-start.8 = (bf16[256,1024]{1,0:T(8,128)(2,1)S(1)}, bf16[256,1024]{1,0:T(8,128)(2,1)S(1)}, u32[]{:S(2)}, u32[]{:S(2)}) collective-permute-start(bf16[256,1024]{1,0:T(8,128)(2,1)S(1)} %get-tuple-element.79), channel_id=1, source_target_pairs={{0,16},{16,0},{1,17},{17,1},{2,18},{18,2},{3,19},{19,3},{4,20},{20... | collective-permute-start | bytes 1572872 | tf_op jit(solution)/shard_map/ppermute | solution.py:15
  111.8 27.0 %copy-start.8 = (bf16[1,1,512,1024]{3,2,1,0:T(8,128)(2,1)S(1)}, bf16[1,1,512,1024]{3,2,1,0:T(8,128)(2,1)}, u32[]{:S(2)}) copy-start(bf16[1,1,512,1024]{3,2,1,0:T(8,128)(2,1)} %get-tuple-element.91) | copy-start | bytes 3145732
  138.8 12.5 %copy-start.7 = (bf16[1,1,512,1024]{3,2,1,0:T(8,128)(2,1)S(1)}, bf16[1,1,512,1024]{3,2,1,0:T(8,128)(2,1)}, u32[]{:S(2)}) copy-start(bf16[1,1,512,1024]{3,2,1,0:T(8,128)(2,1)} %get-tuple-element.86) | copy-start | bytes 3145732
  140.2 10.3 %collective-permute-start.10 = (bf16[256,1024]{1,0:T(8,128)(2,1)S(1)}, bf16[256,1024]{1,0:T(8,128)(2,1)S(1)}, u32[]{:S(2)}, u32[]{:S(2)}) collective-permute-start(bf16[256,1024]{1,0:T(8,128)(2,1)S(1)} %get-tuple-element.77), channel_id=1, source_target_pairs={{0,16},{16,0},{1,17},{17,1},{2,18},{18,2},{3,19},{19,3},{4,20},{20... | collective-permute-start | bytes 1572872 | tf_op jit(solution)/shard_map/ppermute | solution.py:15
  152.7 9.4 %collective-permute-start.12 = (bf16[256,1024]{1,0:T(8,128)(2,1)S(1)}, bf16[256,1024]{1,0:T(8,128)(2,1)S(1)}, u32[]{:S(2)}, u32[]{:S(2)}) collective-permute-start(bf16[256,1024]{1,0:T(8,128)(2,1)S(1)} %get-tuple-element.75), channel_id=1, source_target_pairs={{0,16},{16,0},{1,17},{17,1},{2,18},{18,2},{3,19},{19,3},{4,20},{20... | collective-permute-start | bytes 1572872 | tf_op jit(solution)/shard_map/ppermute | solution.py:15
  154.0 9.0 %copy-start.6 = (f32[3,2,256,1024]{3,2,1,0:T(8,128)}, f32[3,2,256,1024]{3,2,1,0:T(8,128)S(1)}, u32[]{:S(2)}) copy-start(f32[3,2,256,1024]{3,2,1,0:T(8,128)S(1)} %bitcast_dynamic-update-slice_fusion) | copy-start | bytes 18874372

commit v2 on v1

--- a/solution.py
+++ b/solution.py
@@ -24,18 +24,21 @@
         total = mine + sum(others)
 
         def rows(array, part, at):
-            return lax.dynamic_slice_in_dim(array[part], at * owned, owned, 0)
+            lead = (0,) * (array.ndim - 4)
+            sizes = (1,) * (array.ndim - 2) + (owned, array.shape[-1])
+            block = lax.dynamic_slice(array, (*lead, *part, at * owned, 0), sizes)
+            return block.reshape(sizes[-2:])
 
-        arrived = {}
-        for part in parts:
-            arrived[part] = [
-                shifted(rows(inner[0], part, (me + s) % groups), s) for s in range(1, groups)
-            ]
+        arrived = {
+            part: [shifted(rows(inner, part, (me + s) % groups), s) for s in range(1, groups)]
+            for part in parts
+        }
         weights = jnp.zeros(anchor.shape, jnp.bfloat16)
         moments = jnp.zeros(momentum.shape, jnp.float32)
+        travelled = {}
         for part in parts:
             base = rows(anchor, part, me).astype(jnp.float32)
-            acc = mine * (base - rows(inner[0], part, me).astype(jnp.float32))
+            acc = mine * (base - rows(inner, part, me).astype(jnp.float32))
             for count, block in zip(others, arrived[part]):
                 acc = acc + count * (base - block.astype(jnp.float32))
             pseudo = acc / total
@@ -43,8 +46,9 @@
             new = (base - outer_rate * (pseudo + momentum_rate * moment)).astype(jnp.bfloat16)
             moments = moments.at[part].set(moment)
             weights = lax.dynamic_update_slice(weights, new[None, None], (*part, start, 0))
-            for s in range(1, groups):
-                block = shifted(new, s)
+            travelled[part] = [shifted(new, s) for s in range(1, groups)]
+        for part in parts:
+            for s, block in enumerate(travelled[part], 1):
                 source = (me - s) % groups
                 weights = lax.dynamic_update_slice(
                     weights, block[None, None], (*part, source * owned, 0)

time: 163 us -> 146 us (0.90)
  local copies, waits for them, and re-layouts: 23.8 us -> 14.2 us
  waiting for transfers between devices: 103 us -> 93.7 us
  starting transfers between devices: 15.2 us -> 21.5 us
  other arithmetic: 18.4 us -> 14.1 us
    slice x2 -> x0, local copies, waits for them, and re-layouts: 10.7 us -> none  [rows(): return lax.dynamic_slice_in_dim(array[part], at * owned, owned, 0)]
    ppermute x13, waiting for transfers between devices: 103 us -> 93.7 us  [shifted(): return lax.ppermute(value, 'replica', pairs)]
    ppermute x13, starting transfers between devices: 15.2 us -> 21.5 us  [shifted(): return lax.ppermute(value, 'replica', pairs)]
    dynamic_update_slice x6, other arithmetic: 12.6 us -> 6.56 us  [on_device(): lax.dynamic_update_slice(weights, new[None, None], (*part, start, 0))]
    dynamic_update_slice x6, local copies, waits for them, and re-layouts: 6 us -> 0.25 us  [on_device(): lax.dynamic_update_slice(weights, block[None, None], (*part, source * own...]
    unnamed x32 -> x16, local copies, waits for them, and re-layouts: 0.76 us -> 4.93 us
    dynamic_slice x6 -> x0, local copies, waits for them, and re-layouts: 4.17 us -> none  [rows(): return lax.dynamic_slice_in_dim(array[part], at * owned, owned, 0)]
    reshape x0 -> x1, local copies, waits for them, and re-layouts: none -> 3.67 us  [rows(): return block.reshape(sizes[-2:])]
  transfers between devices with their start and end apart: 13 -> 13, of which waited for: 10 -> 11; matrix products, arithmetic and copies ran while one was open for 14% -> 13% of each run, Pallas kernels for 0% -> 0%
where the time goes in v2:
time: 146 us
  waiting for transfers between devices  93.7 us (64%)
  starting transfers between devices  21.5 us (15%)
  local copies, waits for them, and re-layouts  14.2 us (10%)
  other arithmetic  14.1 us (10%)
  between operations  2.24 us (2%)
    ppermute x13, waiting for transfers between devices, shifted(): return lax.ppermute(value, 'replica', pairs)  93.7 us
    ppermute x13, starting transfers between devices, shifted(): return lax.ppermute(value, 'replica', pairs)  21.5 us
    dynamic_update_slice x6, other arithmetic, on_device(): lax.dynamic_update_slice(weights, new[None, None], (*part, start, 0))  6.56 us
    scatter x5, other arithmetic, on_device(): moments = moments.at[part].set(moment)  5.31 us
    unnamed x16, local copies, waits for them, and re-layouts  4.93 us
    scatter x1, local copies, waits for them, and re-layouts, on_device(): moments = moments.at[part].set(moment)  3.98 us
    reshape x1, local copies, waits for them, and re-layouts, rows(): return block.reshape(sizes[-2:])  3.67 us
  transfers between devices with their start and end apart: 13, of which 11 were waited for; matrix products, arithmetic and copies ran while one was open for 13% of the time, Pallas kernels for 0%

profile of v2, /device:TPU:0, one launch (start us, length us, event | category | flops | bytes accessed | tf_op | source)
XLA Modules:
  0.0 145.8 jit_solution(13253424153244737610)
XLA Ops:
  0.7 3.7 %dynamic-slice_bitcast_fusion = (bf16[256,1024]{1,0:T(8,128)(2,1)}, bf16[256,1024]{1,0:T(8,128)(2,1)}, bf16[256,1024]{1,0:T(8,128)(2,1)}, bf16[256,1024]{1,0:T(8...) fusion(bf16[1,3,2,512,1024]{4,3,2,1,0:T(8,128)(2,1)} %param.17, s32[]{:T(128)S(6)} %select_n.69), kind=kLoop, calls=%fused_computation.72 | loop fusion | bytes 6291460 | tf_op jit(solution)/shard_map/reshape | solution.py:30
  4.3 2.9 %collective-permute-start.1 = (bf16[256,1024]{1,0:T(8,128)(2,1)}, bf16[256,1024]{1,0:T(8,128)(2,1)}, u32[]{:S(2)}, u32[]{:S(2)}) collective-permute-start(bf16[256,1024]{1,0:T(8,128)(2,1)} %get-tuple-element.91), channel_id=1, source_target_pairs={{0,16},{16,0},{1,17},{17,1},{2,18},{18,2},{3,19},{19,3},{4,20},{20... | collective-permute-start | bytes 1572872 | tf_op jit(solution)/shard_map/ppermute | solution.py:15
  7.3 2.0 %collective-permute-start.2 = (bf16[256,1024]{1,0:T(8,128)(2,1)}, bf16[256,1024]{1,0:T(8,128)(2,1)}, u32[]{:S(2)}, u32[]{:S(2)}) collective-permute-start(bf16[256,1024]{1,0:T(8,128)(2,1)} %get-tuple-element.90), channel_id=1, source_target_pairs={{0,16},{16,0},{1,17},{17,1},{2,18},{18,2},{3,19},{19,3},{4,20},{20... | collective-permute-start | bytes 1572872 | tf_op jit(solution)/shard_map/ppermute | solution.py:15
  9.3 2.0 %collective-permute-start.4 = (bf16[256,1024]{1,0:T(8,128)(2,1)}, bf16[256,1024]{1,0:T(8,128)(2,1)S(1)}, u32[]{:S(2)}, u32[]{:S(2)}) collective-permute-start(bf16[256,1024]{1,0:T(8,128)(2,1)} %get-tuple-element.88), channel_id=1, source_target_pairs={{0,16},{16,0},{1,17},{17,1},{2,18},{18,2},{3,19},{19,3},{4,20},{20... | collective-permute-start | bytes 1572872 | tf_op jit(solution)/shard_map/ppermute | solution.py:15
  12.6 7.7 %collective-permute-done = s32[1]{0:T(128)} collective-permute-done((s32[1]{0:T(128)}, s32[1]{0:T(128)}, u32[]{:S(2)}, u32[]{:S(2)}) %collective-permute-start) | collective-permute-done | bytes 36 | tf_op jit(solution)/shard_map/ppermute | solution.py:15
  20.3 2.1 %collective-permute-start.5 = (bf16[256,1024]{1,0:T(8,128)(2,1)}, bf16[256,1024]{1,0:T(8,128)(2,1)}, u32[]{:S(2)}, u32[]{:S(2)}) collective-permute-start(bf16[256,1024]{1,0:T(8,128)(2,1)} %get-tuple-element.87), channel_id=1, source_target_pairs={{0,16},{16,0},{1,17},{17,1},{2,18},{18,2},{3,19},{19,3},{4,20},{20... | collective-permute-start | bytes 1572872 | tf_op jit(solution)/shard_map/ppermute | solution.py:15
  23.2 2.2 %fusion.30 = f32[1,1,256,1024]{3,2,1,0:T(8,128)S(1)} fusion(f32[3,2,256,1024]{3,2,1,0:T(8,128)} %param.19, f32[]{:T(128)S(6)} %add.138, bf16[256,1024]{1,0:T(8,128)(2,1)} %collective-permute-done.1, f32[]{:T(128)} %bitcast.4, bf16[1,3,2,512,1024]{4,3,2,1,0:T(8,128)(2,1)} %param.17, s32[]{:T(128)S(6)} %select_n.67, bf16[3,2,512,1024]{3,2,1,0:T(8,128)(2,1)} %param.18, ...), kind=kLoop, calls=%fused_computation.59 | loop fusion | flops 2883584 | bytes 3670032 | tf_op jit(solution)/shard_map/reshape.233
  25.5 4.0 %scatter.20 = f32[3,2,256,1024]{3,2,1,0:T(8,128)} pad(f32[1,1,256,1024]{3,2,1,0:T(8,128)S(1)} %fusion.30, f32[]{:T(128)} %constant.235.clone.1), padding=0_2x0_1x0_0x0_0 | pad | bytes 7340036 | tf_op jit(solution)/shard_map/scatter | solution.py:47
  29.4 0.8 broadcast_in_dim.40
  30.7 1.8 %copy-done = bf16[3,2,512,1024]{3,2,1,0:T(8,128)(2,1)S(1)} copy-done((bf16[3,2,512,1024]{3,2,1,0:T(8,128)(2,1)S(1)}, bf16[3,2,512,1024]{3,2,1,0:T(8,128)(2,1)}, u32[]{:S(2)}) %copy-start) | copy-done | bytes 6291480
  32.5 1.6 %bitcast_dynamic-update-slice_fusion.16 = (bf16[3,2,512,1024]{3,2,1,0:T(8,128)(2,1)S(1)}, bf16[256,1024]{1,0:T(8,128)(2,1)S(1)}) fusion(bf16[3,2,512,1024]{3,2,1,0:T(8,128)(2,1)S(1)} %broadcast_in_dim.40, s32[]{:T(128)S(6)} %select_n.67, f32[3,2,256,1024]{3,2,1,0:T(8,128)S(1)} %bitcast.197, f32[]{:T(128)S(6)} %add.138, ...), kind=kLoop, calls=%fused_computation.71 | loop fusion | flops 4194304 | bytes 3670032 | tf_op jit(solution)/shard_map/dynamic_update_slice | solution.py:48
  34.1 2.1 %collective-permute-start.7 = (bf16[256,1024]{1,0:T(8,128)(2,1)S(1)}, bf16[256,1024]{1,0:T(8,128)(2,1)S(1)}, u32[]{:S(2)}, u32[]{:S(2)}) collective-permute-start(bf16[256,1024]{1,0:T(8,128)(2,1)S(1)} %get-tuple-element.85), channel_id=1, source_target_pairs={{0,16},{16,0},{1,17},{17,1},{2,18},{18,2},{3,19},{19,3},{4,20},{20... | collective-permute-start | bytes 1572872 | tf_op jit(solution)/shard_map/ppermute | solution.py:15
  36.2 1.6 %bitcast_dynamic-update-slice_fusion.15 = (bf16[3,2,512,1024]{3,2,1,0:T(8,128)(2,1)S(1)}, bf16[256,1024]{1,0:T(8,128)(2,1)S(1)}) fusion(bf16[3,2,512,1024]{3,2,1,0:T(8,128)(2,1)S(1)} %get-tuple-element.84, s32[]{:T(128)S(6)} %select_n.67, f32[3,2,256,1024]{3,2,1,0:T(8,128)S(1)} %bitcast.197, f32[]{:T(128)S(6)} %add.138, ...), kind=kLoop, calls=%fused_computation.70 | loop fusion | flops 4194304 | bytes 3670032 | tf_op jit(solution)/shard_map/dynamic_update_slice | solution.py:48
  37.8 4.9 %collective-permute-done.3 = bf16[256,1024]{1,0:T(8,128)(2,1)S(1)} collective-permute-done((bf16[256,1024]{1,0:T(8,128)(2,1)}, bf16[256,1024]{1,0:T(8,128)(2,1)S(1)}, u32[]{:S(2)}, u32[]{:S(2)}) %collective-permute-start.3) | collective-permute-done | bytes 524320 | tf_op jit(solution)/shard_map/ppermute | solution.py:15
  42.7 2.1 %collective-permute-start.8 = (bf16[256,1024]{1,0:T(8,128)(2,1)S(1)}, bf16[256,1024]{1,0:T(8,128)(2,1)S(1)}, u32[]{:S(2)}, u32[]{:S(2)}) collective-permute-start(bf16[256,1024]{1,0:T(8,128)(2,1)S(1)} %get-tuple-element.83), channel_id=1, source_target_pairs={{0,16},{16,0},{1,17},{17,1},{2,18},{18,2},{3,19},{19,3},{4,20},{20... | collective-permute-start | bytes 1572872 | tf_op jit(solution)/shard_map/ppermute | solution.py:15
  45.4 8.6 %collective-permute-done.4 = bf16[256,1024]{1,0:T(8,128)(2,1)S(1)} collective-permute-done((bf16[256,1024]{1,0:T(8,128)(2,1)}, bf16[256,1024]{1,0:T(8,128)(2,1)S(1)}, u32[]{:S(2)}, u32[]{:S(2)}) %collective-permute-start.4) | collective-permute-done | bytes 524320 | tf_op jit(solution)/shard_map/ppermute | solution.py:15
  53.9 2.1 %collective-permute-start.9 = (bf16[256,1024]{1,0:T(8,128)(2,1)S(1)}, bf16[256,1024]{1,0:T(8,128)(2,1)S(1)}, u32[]{:S(2)}, u32[]{:S(2)}) collective-permute-start(bf16[256,1024]{1,0:T(8,128)(2,1)S(1)} %get-tuple-element.81), channel_id=1, source_target_pairs={{0,16},{16,0},{1,17},{17,1},{2,18},{18,2},{3,19},{19,3},{4,20},{20... | collective-permute-start | bytes 1572872 | tf_op jit(solution)/shard_map/ppermute | solution.py:15
  56.6 2.6 %bitcast_dynamic-update-slice_fusion.4 = f32[3,2,256,1024]{3,2,1,0:T(8,128)S(1)} fusion(f32[3,2,256,1024]{3,2,1,0:T(8,128)S(1)} %copy-done.2, s32[]{:T(128)} %bitcast.46, s32[]{:T(128)} %bitcast.47, f32[3,2,256,1024]{3,2,1,0:T(8,128)S(1)} %bitcast.197, f32[]{:T(128)S(6)} %add.138, bf16[256,1024]{1,0:T(8,128)(2,1)} %collective-permute-done.2, f32[]{:T(128)} %bitcast.4, ...), kind=kLoop, calls=%fused_computation.52 | loop fusion | flops 2883584 | bytes 3670040 | tf_op jit(solution)/shard_map/scatter | solution.py:47
  60.0 5.2 %collective-permute-done.5 = bf16[256,1024]{1,0:T(8,128)(2,1)} collective-permute-done((bf16[256,1024]{1,0:T(8,128)(2,1)}, bf16[256,1024]{1,0:T(8,128)(2,1)}, u32[]{:S(2)}, u32[]{:S(2)}) %collective-permute-start.5) | collective-permute-done | bytes 524320 | tf_op jit(solution)/shard_map/ppermute | solution.py:15
  65.3 2.1 %collective-permute-start.10 = (bf16[256,1024]{1,0:T(8,128)(2,1)S(1)}, bf16[256,1024]{1,0:T(8,128)(2,1)S(1)}, u32[]{:S(2)}, u32[]{:S(2)}) collective-permute-start(bf16[256,1024]{1,0:T(8,128)(2,1)S(1)} %get-tuple-element.79), channel_id=1, source_target_pairs={{0,16},{16,0},{1,17},{17,1},{2,18},{18,2},{3,19},{19,3},{4,20},{20... | collective-permute-start | bytes 1572872 | tf_op jit(solution)/shard_map/ppermute | solution.py:15
  67.4 1.6 %bitcast_dynamic-update-slice_fusion.12 = (bf16[3,2,512,1024]{3,2,1,0:T(8,128)(2,1)S(1)}, bf16[256,1024]{1,0:T(8,128)(2,1)S(1)}) fusion(bf16[3,2,512,1024]{3,2,1,0:T(8,128)(2,1)S(1)} %get-tuple-element.78, s32[]{:T(128)S(6)} %select_n.67, f32[3,2,256,1024]{3,2,1,0:T(8,128)S(1)} %bitcast.197, f32[]{:T(128)S(6)} %add.138, ...), kind=kLoop, calls=%fused_computation.67 | loop fusion | flops 4194304 | bytes 3670032 | tf_op jit(solution)/shard_map/dynamic_update_slice | solution.py:48
  69.0 7.5 %collective-permute-done.6 = bf16[256,1024]{1,0:T(8,128)(2,1)S(1)} collective-permute-done((bf16[256,1024]{1,0:T(8,128)(2,1)}, bf16[256,1024]{1,0:T(8,128)(2,1)S(1)}, u32[]{:S(2)}, u32[]{:S(2)}) %collective-permute-start.6) | collective-permute-done | bytes 524320 | tf_op jit(solution)/shard_map/ppermute | solution.py:15
  76.4 2.1 %collective-permute-start.11 = (bf16[256,1024]{1,0:T(8,128)(2,1)S(1)}, bf16[256,1024]{1,0:T(8,128)(2,1)S(1)}, u32[]{:S(2)}, u32[]{:S(2)}) collective-permute-start(bf16[256,1024]{1,0:T(8,128)(2,1)S(1)} %get-tuple-element.77), channel_id=1, source_target_pairs={{0,16},{16,0},{1,17},{17,1},{2,18},{18,2},{3,19},{19,3},{4,20},{20... | collective-permute-start | bytes 1572872 | tf_op jit(solution)/shard_map/ppermute | solution.py:15
  79.1 1.5 %bitcast_dynamic-update-slice_fusion.1 = f32[3,2,256,1024]{3,2,1,0:T(8,128)S(1)} fusion(f32[3,2,256,1024]{3,2,1,0:T(8,128)S(1)} %bitcast_dynamic-update-slice_fusion.2, f32[3,2,256,1024]{3,2,1,0:T(8,128)S(1)} %bitcast.197, f32[]{:T(128)S(6)} %add.138, bf16[256,1024]{1,0:T(8,128)(2,1)} %collective-permute-done.5, f32[]{:T(128)} %bitcast.4, ...), kind=kLoop, calls=%fused_computation.49 | loop fusion | flops 2883584 | bytes 3670032 | tf_op jit(solution)/shard_map/scatter | solution.py:47
  80.9 6.7 %collective-permute-done.7 = bf16[256,1024]{1,0:T(8,128)(2,1)S(1)} collective-permute-done((bf16[256,1024]{1,0:T(8,128)(2,1)S(1)}, bf16[256,1024]{1,0:T(8,128)(2,1)S(1)}, u32[]{:S(2)}, u32[]{:S(2)}) %collective-permute-start.7) | collective-permute-done | bytes 524320 | tf_op jit(solution)/shard_map/ppermute | solution.py:15
  87.7 2.1 %collective-permute-start.12 = (bf16[256,1024]{1,0:T(8,128)(2,1)S(1)}, bf16[256,1024]{1,0:T(8,128)(2,1)S(1)}, u32[]{:S(2)}, u32[]{:S(2)}) collective-permute-start(bf16[256,1024]{1,0:T(8,128)(2,1)S(1)} %get-tuple-element.75), channel_id=1, source_target_pairs={{0,16},{16,0},{1,17},{17,1},{2,18},{18,2},{3,19},{19,3},{4,20},{20... | collective-permute-start | bytes 1572872 | tf_op jit(solution)/shard_map/ppermute | solution.py:15
  89.8 9.1 %collective-permute-done.8 = bf16[256,1024]{1,0:T(8,128)(2,1)S(1)} collective-permute-done((bf16[256,1024]{1,0:T(8,128)(2,1)S(1)}, bf16[256,1024]{1,0:T(8,128)(2,1)S(1)}, u32[]{:S(2)}, u32[]{:S(2)}) %collective-permute-start.8) | collective-permute-done | bytes 524320 | tf_op jit(solution)/shard_map/ppermute | solution.py:15
  98.9 11.2 %collective-permute-done.9 = bf16[256,1024]{1,0:T(8,128)(2,1)S(1)} collective-permute-done((bf16[256,1024]{1,0:T(8,128)(2,1)S(1)}, bf16[256,1024]{1,0:T(8,128)(2,1)S(1)}, u32[]{:S(2)}, u32[]{:S(2)}) %collective-permute-start.9) | collective-permute-done | bytes 524320 | tf_op jit(solution)/shard_map/ppermute | solution.py:15
  110.2 11.2 %collective-permute-done.10 = bf16[256,1024]{1,0:T(8,128)(2,1)S(1)} collective-permute-done((bf16[256,1024]{1,0:T(8,128)(2,1)S(1)}, bf16[256,1024]{1,0:T(8,128)(2,1)S(1)}, u32[]{:S(2)}, u32[]{:S(2)}) %collective-permute-start.10) | collective-permute-done | bytes 524320 | tf_op jit(solution)/shard_map/ppermute | solution.py:15
  121.4 11.2 %collective-permute-done.11 = bf16[256,1024]{1,0:T(8,128)(2,1)S(1)} collective-permute-done((bf16[256,1024]{1,0:T(8,128)(2,1)S(1)}, bf16[256,1024]{1,0:T(8,128)(2,1)S(1)}, u32[]{:S(2)}, u32[]{:S(2)}) %collective-permute-start.11) | collective-permute-done | bytes 524320 | tf_op jit(solution)/shard_map/ppermute | solution.py:15
  132.6 10.4 %collective-permute-done.12 = bf16[256,1024]{1,0:T(8,128)(2,1)S(1)} collective-permute-done((bf16[256,1024]{1,0:T(8,128)(2,1)S(1)}, bf16[256,1024]{1,0:T(8,128)(2,1)S(1)}, u32[]{:S(2)}, u32[]{:S(2)}) %collective-permute-start.12) | collective-permute-done | bytes 524320 | tf_op jit(solution)/shard_map/ppermute | solution.py:15
  143.1 2.7 %copy-done.1 = bf16[3,2,512,1024]{3,2,1,0:T(8,128)(2,1)} copy-done((bf16[3,2,512,1024]{3,2,1,0:T(8,128)(2,1)}, bf16[3,2,512,1024]{3,2,1,0:T(8,128)(2,1)S(1)}, u32[]{:S(2)}) %copy-start.1) | copy-done | bytes 6291480
  (35 shorter events, 4.4 us)
Async XLA Ops:
  0.6 29.6 %slice-start.2 = ((s8[6291456]{0:T(1024)(128)(4,1)}), s8[2097152]{0:T(1024)(128)(4,1)S(1)}, s32[]{:S(2)}) async-start(s8[6291456]{0:T(1024)(128)(4,1)} %bitcast.198), calls=%async_computation.2 | async-start | bytes 4194304
  4.3 18.8 %collective-permute-start.1 = (bf16[256,1024]{1,0:T(8,128)(2,1)}, bf16[256,1024]{1,0:T(8,128)(2,1)}, u32[]{:S(2)}, u32[]{:S(2)}) collective-permute-start(bf16[256,1024]{1,0:T(8,128)(2,1)} %get-tuple-element.91), channel_id=1, source_target_pairs={{0,16},{16,0},{1,17},{17,1},{2,18},{18,2},{3,19},{19,3},{4,20},{20... | collective-permute-start | bytes 1572872 | tf_op jit(solution)/shard_map/ppermute | solution.py:15
  7.3 13.1 %collective-permute-start = (s32[1]{0:T(128)}, s32[1]{0:T(128)}, u32[]{:S(2)}, u32[]{:S(2)}) collective-permute-start(s32[1]{0:T(128)} %param.16), channel_id=1, source_target_pairs={{0,16},{16,0},{1,17},{17,1},{2,18},{18,2},{3,19},{19,3},{4,20},{20... | collective-permute-start | bytes 20 | tf_op jit(solution)/shard_map/ppermute | solution.py:15
  7.3 26.8 %collective-permute-start.2 = (bf16[256,1024]{1,0:T(8,128)(2,1)}, bf16[256,1024]{1,0:T(8,128)(2,1)}, u32[]{:S(2)}, u32[]{:S(2)}) collective-permute-start(bf16[256,1024]{1,0:T(8,128)(2,1)} %get-tuple-element.90), channel_id=1, source_target_pairs={{0,16},{16,0},{1,17},{17,1},{2,18},{18,2},{3,19},{19,3},{4,20},{20... | collective-permute-start | bytes 1572872 | tf_op jit(solution)/shard_map/ppermute | solution.py:15
  9.3 33.4 %collective-permute-start.3 = (bf16[256,1024]{1,0:T(8,128)(2,1)}, bf16[256,1024]{1,0:T(8,128)(2,1)S(1)}, u32[]{:S(2)}, u32[]{:S(2)}) collective-permute-start(bf16[256,1024]{1,0:T(8,128)(2,1)} %get-tuple-element.89), channel_id=1, source_target_pairs={{0,16},{16,0},{1,17},{17,1},{2,18},{18,2},{3,19},{19,3},{4,20},{20... | collective-permute-start | bytes 1572872 | tf_op jit(solution)/shard_map/ppermute | solution.py:15
  9.3 44.6 %collective-permute-start.4 = (bf16[256,1024]{1,0:T(8,128)(2,1)}, bf16[256,1024]{1,0:T(8,128)(2,1)S(1)}, u32[]{:S(2)}, u32[]{:S(2)}) collective-permute-start(bf16[256,1024]{1,0:T(8,128)(2,1)} %get-tuple-element.88), channel_id=1, source_target_pairs={{0,16},{16,0},{1,17},{17,1},{2,18},{18,2},{3,19},{19,3},{4,20},{20... | collective-permute-start | bytes 1572872 | tf_op jit(solution)/shard_map/ppermute | solution.py:15
  20.3 45.0 %collective-permute-start.5 = (bf16[256,1024]{1,0:T(8,128)(2,1)}, bf16[256,1024]{1,0:T(8,128)(2,1)}, u32[]{:S(2)}, u32[]{:S(2)}) collective-permute-start(bf16[256,1024]{1,0:T(8,128)(2,1)} %get-tuple-element.87), channel_id=1, source_target_pairs={{0,16},{16,0},{1,17},{17,1},{2,18},{18,2},{3,19},{19,3},{4,20},{20... | collective-permute-start | bytes 1572872 | tf_op jit(solution)/shard_map/ppermute | solution.py:15
  23.1 53.3 %collective-permute-start.6 = (bf16[256,1024]{1,0:T(8,128)(2,1)}, bf16[256,1024]{1,0:T(8,128)(2,1)S(1)}, u32[]{:S(2)}, u32[]{:S(2)}) collective-permute-start(bf16[256,1024]{1,0:T(8,128)(2,1)} %get-tuple-element.86), channel_id=1, source_target_pairs={{0,16},{16,0},{1,17},{17,1},{2,18},{18,2},{3,19},{19,3},{4,20},{20... | collective-permute-start | bytes 1572872 | tf_op jit(solution)/shard_map/ppermute | solution.py:15
  23.2 7.1 %slice-start = ((s8[6291456]{0:T(1024)(128)(4,1)}), s8[4194304]{0:T(1024)(128)(4,1)S(1)}, s32[]{:S(2)}) async-start(s8[6291456]{0:T(1024)(128)(4,1)} %bitcast.196), calls=%async_computation | async-start | bytes 8388608
  25.4 4.8 %slice-start.1 = ((s8[6291456]{0:T(1024)(128)(4,1)}), s8[2097152]{0:T(1024)(128)(4,1)S(1)}, s32[]{:S(2)}) async-start(s8[6291456]{0:T(1024)(128)(4,1)} %bitcast.196), calls=%async_computation.1 | async-start | bytes 4194304
  25.4 5.2 %slice-start.3 = ((s8[6291456]{0:T(1024)(128)(4,1)}), s8[4194304]{0:T(1024)(128)(4,1)S(1)}, s32[]{:S(2)}) async-start(s8[6291456]{0:T(1024)(128)(4,1)} %bitcast.198), calls=%async_computation.3 | async-start | bytes 8388608
  25.4 7.0 %copy-start = (bf16[3,2,512,1024]{3,2,1,0:T(8,128)(2,1)S(1)}, bf16[3,2,512,1024]{3,2,1,0:T(8,128)(2,1)}, u32[]{:S(2)}) copy-start(bf16[3,2,512,1024]{3,2,1,0:T(8,128)(2,1)} %param.18) | copy-start | bytes 18874372
  34.1 22.5 %copy-start.2 = (f32[3,2,256,1024]{3,2,1,0:T(8,128)S(1)}, f32[3,2,256,1024]{3,2,1,0:T(8,128)}, u32[]{:S(2)}) copy-start(f32[3,2,256,1024]{3,2,1,0:T(8,128)} %scatter.20) | copy-start | bytes 18874372
  34.1 53.6 %collective-permute-start.7 = (bf16[256,1024]{1,0:T(8,128)(2,1)S(1)}, bf16[256,1024]{1,0:T(8,128)(2,1)S(1)}, u32[]{:S(2)}, u32[]{:S(2)}) collective-permute-start(bf16[256,1024]{1,0:T(8,128)(2,1)S(1)} %get-tuple-element.85), channel_id=1, source_target_pairs={{0,16},{16,0},{1,17},{17,1},{2,18},{18,2},{3,19},{19,3},{4,20},{20... | collective-permute-start | bytes 1572872 | tf_op jit(solution)/shard_map/ppermute | solution.py:15
  42.7 56.2 %collective-permute-start.8 = (bf16[256,1024]{1,0:T(8,128)(2,1)S(1)}, bf16[256,1024]{1,0:T(8,128)(2,1)S(1)}, u32[]{:S(2)}, u32[]{:S(2)}) collective-permute-start(bf16[256,1024]{1,0:T(8,128)(2,1)S(1)} %get-tuple-element.83), channel_id=1, source_target_pairs={{0,16},{16,0},{1,17},{17,1},{2,18},{18,2},{3,19},{19,3},{4,20},{20... | collective-permute-start | bytes 1572872 | tf_op jit(solution)/shard_map/ppermute | solution.py:15
  53.9 56.2 %collective-permute-start.9 = (bf16[256,1024]{1,0:T(8,128)(2,1)S(1)}, bf16[256,1024]{1,0:T(8,128)(2,1)S(1)}, u32[]{:S(2)}, u32[]{:S(2)}) collective-permute-start(bf16[256,1024]{1,0:T(8,128)(2,1)S(1)} %get-tuple-element.81), channel_id=1, source_target_pairs={{0,16},{16,0},{1,17},{17,1},{2,18},{18,2},{3,19},{19,3},{4,20},{20... | collective-permute-start | bytes 1572872 | tf_op jit(solution)/shard_map/ppermute | solution.py:15
  65.3 56.1 %collective-permute-start.10 = (bf16[256,1024]{1,0:T(8,128)(2,1)S(1)}, bf16[256,1024]{1,0:T(8,128)(2,1)S(1)}, u32[]{:S(2)}, u32[]{:S(2)}) collective-permute-start(bf16[256,1024]{1,0:T(8,128)(2,1)S(1)} %get-tuple-element.79), channel_id=1, source_target_pairs={{0,16},{16,0},{1,17},{17,1},{2,18},{18,2},{3,19},{19,3},{4,20},{20... | collective-permute-start | bytes 1572872 | tf_op jit(solution)/shard_map/ppermute | solution.py:15
  76.4 56.2 %collective-permute-start.11 = (bf16[256,1024]{1,0:T(8,128)(2,1)S(1)}, bf16[256,1024]{1,0:T(8,128)(2,1)S(1)}, u32[]{:S(2)}, u32[]{:S(2)}) collective-permute-start(bf16[256,1024]{1,0:T(8,128)(2,1)S(1)} %get-tuple-element.77), channel_id=1, source_target_pairs={{0,16},{16,0},{1,17},{17,1},{2,18},{18,2},{3,19},{19,3},{4,20},{20... | collective-permute-start | bytes 1572872 | tf_op jit(solution)/shard_map/ppermute | solution.py:15
  80.9 62.1 %copy-start.3 = (f32[3,2,256,1024]{3,2,1,0:T(8,128)}, f32[3,2,256,1024]{3,2,1,0:T(8,128)S(1)}, u32[]{:S(2)}) copy-start(f32[3,2,256,1024]{3,2,1,0:T(8,128)S(1)} %bitcast_dynamic-update-slice_fusion) | copy-start | bytes 18874372
  87.7 55.3 %collective-permute-start.12 = (bf16[256,1024]{1,0:T(8,128)(2,1)S(1)}, bf16[256,1024]{1,0:T(8,128)(2,1)S(1)}, u32[]{:S(2)}, u32[]{:S(2)}) collective-permute-start(bf16[256,1024]{1,0:T(8,128)(2,1)S(1)} %get-tuple-element.75), channel_id=1, source_target_pairs={{0,16},{16,0},{1,17},{17,1},{2,18},{18,2},{3,19},{19,3},{4,20},{20... | collective-permute-start | bytes 1572872 | tf_op jit(solution)/shard_map/ppermute | solution.py:15
  143.1 2.7 %copy-start.1 = (bf16[3,2,512,1024]{3,2,1,0:T(8,128)(2,1)}, bf16[3,2,512,1024]{3,2,1,0:T(8,128)(2,1)S(1)}, u32[]{:S(2)}) copy-start(bf16[3,2,512,1024]{3,2,1,0:T(8,128)(2,1)S(1)} %bitcast_dynamic-update-slice_fusion.5) | copy-start | bytes 18874372

commit v3 on v0

v3 whole, which is shorter than its diff:
```python
import functools

import jax
import jax.numpy as jnp
from jax import lax
from jax.experimental import pallas as pl
from jax.experimental.pallas import tpu as pltpu
from jax.sharding import PartitionSpec as P

outer_rate = 0.7
momentum_rate = 0.9
vmem_bytes = 48 * 1024 * 1024


def update_kernel(groups, me_ref, mine_ref, *refs):
    others, refs = refs[: groups - 1], refs[groups - 1 :]
    anchor_ref, inner_ref, refs = refs[0], refs[1], refs[2:]
    arrived, refs = refs[: groups - 1], refs[groups - 1 :]
    momentum_ref, refs = refs[0], refs[1:]
    new_ref, weights_ref, moments_ref = refs[-3:]
    base = anchor_ref[...].astype(jnp.float32)
    mine = mine_ref[0].astype(jnp.float32)
    total = mine
    acc = mine * (base - inner_ref[...].astype(jnp.float32))
    for count_ref, block_ref in zip(others, arrived):
        count = count_ref[0].astype(jnp.float32)
        total = total + count
        acc = acc + count * (base - block_ref[...].astype(jnp.float32))
    pseudo = acc / total
    moment = momentum_rate * momentum_ref[...] + pseudo
    new = (base - outer_rate * (pseudo + momentum_rate * moment)).astype(jnp.bfloat16)
    moments_ref[...] = moment
    weights_ref[...] = new
    new_ref[...] = new


def update(groups, chunk, me, counts, anchor, inner, arrived, momentum, held):
    lo, hi = chunk
    parts, owned, width = momentum.shape
    rows = min(owned, 128)
    steps = owned // rows
    block = (1, rows, width)
    scalar = pl.BlockSpec(memory_space=pltpu.SMEM)
    spread = pl.BlockSpec(block, lambda p, r, me_ref: (lo + p, me_ref[0] * steps + r, 0))
    packed = pl.BlockSpec(block, lambda p, r, me_ref: (p, r, 0))
    kept = pl.BlockSpec(block, lambda p, r, me_ref: (lo + p, r, 0))
    aliases = {}
    if held:
        first = 1 + groups + 2 + (groups - 1) + 1
        aliases = {first: 1, first + 1: 2}
    size = (hi - lo) * owned * width
    return pl.pallas_call(
        functools.partial(update_kernel, groups),
        grid_spec=pltpu.PrefetchScalarGridSpec(
            num_scalar_prefetch=1,
            grid=(hi - lo, steps),
            in_specs=[scalar] * groups
            + [spread, spread]
            + [packed] * (groups - 1)
            + [kept]
            + [pl.BlockSpec(memory_space=pl.ANY)] * len(held),
            out_specs=[packed, spread, kept],
        ),
        out_shape=[
            jax.ShapeDtypeStruct((hi - lo, owned, width), jnp.bfloat16),
            jax.ShapeDtypeStruct(anchor.shape, jnp.bfloat16),
            jax.ShapeDtypeStruct(momentum.shape, jnp.float32),
        ],
        input_output_aliases=aliases,
        compiler_params=pltpu.CompilerParams(vmem_limit_bytes=vmem_bytes),
        cost_estimate=pl.CostEstimate(
            flops=12 * size, bytes_accessed=(14 + 2 * groups) * size, transcendentals=0
        ),
        name="update",
    )(me, *counts, anchor, inner, *arrived, momentum, *held)


def place_kernel(lo, at_ref, block_ref, _, weights_ref, sem):
    parts, owned, _ = block_ref.shape
    start = pl.multiple_of(at_ref[0] * owned, owned)
    copy = pltpu.make_async_copy(
        block_ref, weights_ref.at[pl.ds(lo, parts), pl.ds(start, owned), :], sem
    )
    copy.start()
    copy.wait()


def place(chunk, at, block, weights):
    anywhere = pl.BlockSpec(memory_space=pl.ANY)
    return pl.pallas_call(
        functools.partial(place_kernel, chunk[0]),
        in_specs=[pl.BlockSpec(memory_space=pltpu.SMEM), anywhere, anywhere],
        out_specs=anywhere,
        out_shape=jax.ShapeDtypeStruct(weights.shape, weights.dtype),
        scratch_shapes=[pltpu.SemaphoreType.DMA],
        input_output_aliases={2: 0},
        compiler_params=pltpu.CompilerParams(vmem_limit_bytes=vmem_bytes),
        cost_estimate=pl.CostEstimate(flops=0, bytes_accessed=4 * block.size, transcendentals=0),
        name="place",
    )(at, block, weights)


def solution(mesh):
    groups = mesh.shape["replica"]

    def shifted(value, shift):
        pairs = [(i, (i + shift) % groups) for i in range(groups)]
        return lax.ppermute(value, "replica", pairs)

    def on_device(counts, inner, anchor, momentum):
        shape = anchor.shape
        owned, width = momentum.shape[-2:]
        parts = shape[0] * shape[1]
        inner = inner.reshape(parts, *shape[-2:])
        anchor = anchor.reshape(parts, *shape[-2:])
        momentum = momentum.reshape(parts, owned, width)
        me = lax.axis_index("replica")
        chunks = [(p, p + 1) for p in range(parts)]
        shifts = range(1, groups)

        def rows_for(array, chunk, target):
            sizes = (chunk[1] - chunk[0], owned, width)
            return lax.dynamic_slice(array, (chunk[0], target * owned, 0), sizes)

        targets = [(me + s) % groups for s in shifts]
        first = [rows_for(inner, chunks[0], t) for t in targets]
        first, rest = lax.optimization_barrier((first, inner))
        sent = [first] + [[rows_for(rest, c, t) for t in targets] for c in chunks[1:]]
        arrived = [[shifted(v, s) for v, s in zip(values, shifts)] for values in sent]
        all_counts = [counts] + [shifted(counts, s) for s in shifts]

        where = me.reshape(1).astype(jnp.int32)
        held = []
        travelled = []
        for chunk, blocks in zip(chunks, arrived):
            new, *held = update(
                groups, chunk, where, all_counts, anchor, inner, blocks, momentum, held
            )
            travelled.append([shifted(new, s) for s in shifts])
        weights, moments = held
        for chunk, blocks in zip(chunks, travelled):
            for s, block in zip(shifts, blocks):
                source = ((me - s) % groups).reshape(1).astype(jnp.int32)
                weights = place(chunk, source, block, weights)
        return weights.reshape(shape), moments.reshape(*shape[:2], owned, width)

    placed = (
        P("replica"),
        P("replica", None, None, "fsdp", None),
        P(None, None, "fsdp", None),
        P(None, None, ("fsdp", "replica"), None),
    )
    return jax.shard_map(
        on_device,
        mesh=mesh,
        in_specs=placed,
        out_specs=(P(None, None, "fsdp", None), P(None, None, ("fsdp", "replica"), None)),
        check_vma=False,
    )
```

time: 503 us -> 143 us (0.28)
  waiting for transfers between devices: 435 us -> 96.1 us
  other arithmetic: 36.8 us -> 0 us
  Pallas kernels: 0 us -> 25.6 us
  starting transfers between devices: 0.16 us -> 16.8 us
  between operations: 15.1 us -> 1.37 us
  local copies, waits for them, and re-layouts: 9.43 us -> 2.99 us
  blocking collectives: 5.85 us -> 0 us
    psum x1 -> x0, waiting for transfers between devices: 293 us -> none  [on_device(): pseudo = lax.psum(term, 'replica')]
    all_gather x3 -> x0, waiting for transfers between devices: 141 us -> none  [on_device(): moment_full = lax.all_gather(momentum[layer], 'replica', axis=1, tiled=True)]
    ppermute x0 -> x13, waiting for transfers between devices: none -> 96.1 us  [shifted(): return lax.ppermute(value, 'replica', pairs)]
    pallas_call x0 -> x12, Pallas kernels: none -> 25.6 us  [the longest x6 20.8 us: update(): pl.pallas_call(functools.partial(update_kernel, groups), grid_spec=pltpu....]
    add x3 -> x0, other arithmetic: 18.8 us -> none  [on_device(): moment_next = momentum_rate * moment_full + pseudo]
    ppermute x0 -> x13, starting transfers between devices: none -> 16.8 us  [shifted(): return lax.ppermute(value, 'replica', pairs)]
    mul x1 -> x0, other arithmetic: 11.4 us -> none  [on_device(): term = share * (base - inner[0, layer].astype(jnp.float32))]
    another operation x2 -> x0, other arithmetic: 6.6 us -> none  [on_device(): return (jnp.stack(weight_list), jnp.stack(moment_list))]
  transfers between devices with their start and end apart: 4 -> 13, of which waited for: 4 -> 8; matrix products, arithmetic and copies ran while one was open for 5% -> 1% of each run, Pallas kernels for 0% -> 17%
where the time goes in v3:
time: 143 us
  waiting for transfers between devices  96.1 us (67%)
  Pallas kernels  25.6 us (18%)
  starting transfers between devices  16.8 us (12%)
  local copies, waits for them, and re-layouts  2.99 us (2%)
    ppermute x13, waiting for transfers between devices, shifted(): return lax.ppermute(value, 'replica', pairs)  96.1 us
    pallas_call x6, Pallas kernels, update(): pl.pallas_call(functools.partial(update_kernel, groups), grid_spec=pltpu....  20.8 us
    ppermute x13, starting transfers between devices, shifted(): return lax.ppermute(value, 'replica', pairs)  16.8 us
    pallas_call x6, Pallas kernels, place(): pl.pallas_call(functools.partial(place_kernel, chunk[0]), in_specs=[pl.Bl...  4.8 us
    dynamic_slice x2, local copies, waits for them, and re-layouts, rows_for(): return lax.dynamic_slice(array, (chunk[0], target * owned, 0), sizes)  2.99 us
  transfers between devices with their start and end apart: 13, of which 8 were waited for; matrix products, arithmetic and copies ran while one was open for 1% of the time, Pallas kernels for 17%

profile of v3, /device:TPU:0, one launch (start us, length us, event | category | flops | bytes accessed | tf_op | source)
XLA Modules:
  0.0 142.9 jit_solution(15608901586742765485)
XLA Ops:
  0.6 1.1 constant_dynamic-slice_fusion.5
  1.7 3.0 %collective-permute-start.6 = (bf16[1,256,1024]{2,1,0:T(8,128)(2,1)S(1)}, bf16[1,256,1024]{2,1,0:T(8,128)(2,1)S(1)}, u32[]{:S(2)}, u32[]{:S(2)}) collective-permute-start(bf16[1,256,1024]{2,1,0:T(8,128)(2,1)S(1)} %constant_dynamic-slice_fusion.5), channel_id=1, source_target_pairs={{0,16},{16,0},{1,17},{17,1},{2,18},{18,2},{3,19},{19,3},{4,20},{20... | collective-permute-start | bytes 1572872 | tf_op jit(solution)/shard_map/ppermute | solution.py:108
  4.7 1.9 %constant_dynamic-slice_fusion = (bf16[1,256,1024]{2,1,0:T(8,128)(2,1)S(1)}, bf16[1,256,1024]{2,1,0:T(8,128)(2,1)S(1)}, bf16[1,256,1024]{2,1,0:T(8,128)(2,1)S(1)...) fusion(bf16[6,512,1024]{2,1,0:T(8,128)(2,1)} %bitcast.9, s32[]{:T(128)S(6)} %select_n.31), kind=kLoop, calls=%fused_computation | loop fusion | bytes 5242884 | tf_op jit(solution)/shard_map/dynamic_slice | solution.py:123
  6.7 2.0 %collective-permute-start.4 = (bf16[1,256,1024]{2,1,0:T(8,128)(2,1)S(1)}, bf16[1,256,1024]{2,1,0:T(8,128)(2,1)S(1)}, u32[]{:S(2)}, u32[]{:S(2)}) collective-permute-start(bf16[1,256,1024]{2,1,0:T(8,128)(2,1)S(1)} %get-tuple-element.43), channel_id=1, source_target_pairs={{0,16},{16,0},{1,17},{17,1},{2,18},{18,2},{3,19},{19,3},{4,20},{20... | collective-permute-start | bytes 1572872 | tf_op jit(solution)/shard_map/ppermute | solution.py:108
  8.8 1.9 %collective-permute-start = (s32[1]{0:T(128)}, s32[1]{0:T(128)}, u32[]{:S(2)}, u32[]{:S(2)}) collective-permute-start(s32[1]{0:T(128)} %param.4), channel_id=1, source_target_pairs={{0,16},{16,0},{1,17},{17,1},{2,18},{18,2},{3,19},{19,3},{4,20},{20... | collective-permute-start | bytes 20 | tf_op jit(solution)/shard_map/ppermute | solution.py:108
  10.8 39.8 %collective-permute-done.refs_0_ = s32[1]{0:T(128)} collective-permute-done((s32[1]{0:T(128)}, s32[1]{0:T(128)}, u32[]{:S(2)}, u32[]{:S(2)}) %collective-permute-start) | collective-permute-done | bytes 36 | tf_op jit(solution)/shard_map/ppermute | solution.py:108
  50.5 1.7 %collective-permute-start.2 = (bf16[1,256,1024]{2,1,0:T(8,128)(2,1)S(1)}, bf16[1,256,1024]{2,1,0:T(8,128)(2,1)S(1)}, u32[]{:S(2)}, u32[]{:S(2)}) collective-permute-start(bf16[1,256,1024]{2,1,0:T(8,128)(2,1)S(1)} %get-tuple-element.45), channel_id=1, source_target_pairs={{0,16},{16,0},{1,17},{17,1},{2,18},{18,2},{3,19},{19,3},{4,20},{20... | collective-permute-start | bytes 1572872 | tf_op jit(solution)/shard_map/ppermute | solution.py:108
  52.9 0.4 collective-permute-start.1
  53.3 3.3 %update.6 = (bf16[1,256,1024]{2,1,0:T(8,128)(2,1)S(1)}, bf16[6,512,1024]{2,1,0:T(8,128)(2,1)}, f32[6,256,1024]{2,1,0:T(8,128)}) custom-call(s32[1]{0:T(128)} %bitcast.1.me_ref, s32[1]{0:T(128)S(6)} %copy.38.mine_ref, s32[1]{0:T(128)} %collective-permute-done.refs_0_, bf16[6,512,1024]{2,1,0:T(8,128)(2,1)} %bitcast.16, bf16[6,512,1024]{2,1,0:T(8,128)(2,1)} %bitcast.10, ...), custom_call_target="tpu_custom_call" | custom-call | flops 3145728 | bytes 4718592 | tf_op jit(solution)/shard_map/update/pallas_call | solution.py:52
  56.6 1.8 %collective-permute-start.12 = (bf16[1,256,1024]{2,1,0:T(8,128)(2,1)S(1)}, bf16[1,256,1024]{2,1,0:T(8,128)(2,1)S(1)}, u32[]{:S(2)}, u32[]{:S(2)}) collective-permute-start(bf16[1,256,1024]{2,1,0:T(8,128)(2,1)S(1)} %get-tuple-element.39), channel_id=1, source_target_pairs={{0,16},{16,0},{1,17},{17,1},{2,18},{18,2},{3,19},{19,3},{4,20},{20... | collective-permute-start | bytes 1572872 | tf_op jit(solution)/shard_map/ppermute | solution.py:108
  58.4 3.5 %update.7 = (bf16[1,256,1024]{2,1,0:T(8,128)(2,1)}, bf16[6,512,1024]{2,1,0:T(8,128)(2,1)}, f32[6,256,1024]{2,1,0:T(8,128)}) custom-call(s32[1]{0:T(128)} %bitcast.1.me_ref, s32[1]{0:T(128)S(6)} %copy.38.mine_ref, s32[1]{0:T(128)} %collective-permute-done.refs_0_, bf16[6,512,1024]{2,1,0:T(8,128)(2,1)} %bitcast.17, ...), custom_call_target="tpu_custom_call", output_to_operand_aliasing={{1}: (7, {}), {2}: (8, {})} | custom-call | flops 3145728 | bytes 4718592 | tf_op jit(solution)/shard_map/update/pallas_call | solution.py:52
  61.9 0.3 collective-permute-start.11
  62.2 3.5 %update.8 = (bf16[1,256,1024]{2,1,0:T(8,128)(2,1)}, bf16[6,512,1024]{2,1,0:T(8,128)(2,1)}, f32[6,256,1024]{2,1,0:T(8,128)}) custom-call(s32[1]{0:T(128)} %bitcast.1.me_ref, s32[1]{0:T(128)S(6)} %copy.38.mine_ref, s32[1]{0:T(128)} %collective-permute-done.refs_0_, bf16[6,512,1024]{2,1,0:T(8,128)(2,1)} %bitcast.18, ...), custom_call_target="tpu_custom_call", output_to_operand_aliasing={{1}: (7, {}), {2}: (8, {})} | custom-call | flops 3145728 | bytes 4718592 | tf_op jit(solution)/shard_map/update/pallas_call | solution.py:52
  65.7 1.7 %collective-permute-start.10 = (bf16[1,256,1024]{2,1,0:T(8,128)(2,1)}, bf16[1,256,1024]{2,1,0:T(8,128)(2,1)S(1)}, u32[]{:S(2)}, u32[]{:S(2)}) collective-permute-start(bf16[1,256,1024]{2,1,0:T(8,128)(2,1)} %get-tuple-element.37), channel_id=1, source_target_pairs={{0,16},{16,0},{1,17},{17,1},{2,18},{18,2},{3,19},{19,3},{4,20},{20... | collective-permute-start | bytes 1572872 | tf_op jit(solution)/shard_map/ppermute | solution.py:108
  67.4 3.5 %update.9 = (bf16[1,256,1024]{2,1,0:T(8,128)(2,1)}, bf16[6,512,1024]{2,1,0:T(8,128)(2,1)}, f32[6,256,1024]{2,1,0:T(8,128)}) custom-call(s32[1]{0:T(128)} %bitcast.1.me_ref, s32[1]{0:T(128)S(6)} %copy.38.mine_ref, s32[1]{0:T(128)} %collective-permute-done.refs_0_, bf16[6,512,1024]{2,1,0:T(8,128)(2,1)} %bitcast.19, ...), custom_call_target="tpu_custom_call", output_to_operand_aliasing={{1}: (7, {}), {2}: (8, {})} | custom-call | flops 3145728 | bytes 4718592 | tf_op jit(solution)/shard_map/update/pallas_call | solution.py:52
  71.2 3.5 %update.10 = (bf16[1,256,1024]{2,1,0:T(8,128)(2,1)}, bf16[6,512,1024]{2,1,0:T(8,128)(2,1)}, f32[6,256,1024]{2,1,0:T(8,128)}) custom-call(s32[1]{0:T(128)} %bitcast.1.me_ref, s32[1]{0:T(128)S(6)} %copy.38.mine_ref, s32[1]{0:T(128)} %collective-permute-done.refs_0_, bf16[6,512,1024]{2,1,0:T(8,128)(2,1)} %bitcast.20, ...), custom_call_target="tpu_custom_call", output_to_operand_aliasing={{1}: (7, {}), {2}: (8, {})} | custom-call | flops 3145728 | bytes 4718592 | tf_op jit(solution)/shard_map/update/pallas_call | solution.py:52
  74.7 1.9 %collective-permute-done.1.refs_3_ = bf16[1,256,1024]{2,1,0:T(8,128)(2,1)S(1)} collective-permute-done((bf16[1,256,1024]{2,1,0:T(8,128)(2,1)S(1)}, bf16[1,256,1024]{2,1,0:T(8,128)(2,1)S(1)}, u32[]{:S(2)}, u32[]{:S(2)}) %collective-permute-start.1) | collective-permute-done | bytes 524320 | tf_op jit(solution)/shard_map/ppermute | solution.py:108
  76.6 1.7 %collective-permute-start.8 = (bf16[1,256,1024]{2,1,0:T(8,128)(2,1)}, bf16[1,256,1024]{2,1,0:T(8,128)(2,1)S(1)}, u32[]{:S(2)}, u32[]{:S(2)}) collective-permute-start(bf16[1,256,1024]{2,1,0:T(8,128)(2,1)} %get-tuple-element.35), channel_id=1, source_target_pairs={{0,16},{16,0},{1,17},{17,1},{2,18},{18,2},{3,19},{19,3},{4,20},{20... | collective-permute-start | bytes 1572872 | tf_op jit(solution)/shard_map/ppermute | solution.py:108
  78.4 3.5 %update.11 = (bf16[1,256,1024]{2,1,0:T(8,128)(2,1)}, bf16[6,512,1024]{2,1,0:T(8,128)(2,1)}, f32[6,256,1024]{2,1,0:T(8,128)}) custom-call(s32[1]{0:T(128)} %bitcast.1.me_ref, s32[1]{0:T(128)S(6)} %copy.38.mine_ref, s32[1]{0:T(128)} %collective-permute-done.refs_0_, bf16[6,512,1024]{2,1,0:T(8,128)(2,1)} %bitcast.21, ...), custom_call_target="tpu_custom_call", output_to_operand_aliasing={{1}: (7, {}), {2}: (8, {})} | custom-call | flops 3145728 | bytes 4718592 | tf_op jit(solution)/shard_map/update/pallas_call | solution.py:52
  81.9 6.0 %collective-permute-done.12.block_ref = bf16[1,256,1024]{2,1,0:T(8,128)(2,1)S(1)} collective-permute-done((bf16[1,256,1024]{2,1,0:T(8,128)(2,1)S(1)}, bf16[1,256,1024]{2,1,0:T(8,128)(2,1)S(1)}, u32[]{:S(2)}, u32[]{:S(2)}) %collective-permute-start.12) | collective-permute-done | bytes 524320 | tf_op jit(solution)/shard_map/ppermute | solution.py:108
  87.9 1.7 %collective-permute-start.7 = (bf16[1,256,1024]{2,1,0:T(8,128)(2,1)}, bf16[1,256,1024]{2,1,0:T(8,128)(2,1)S(1)}, u32[]{:S(2)}, u32[]{:S(2)}) collective-permute-start(bf16[1,256,1024]{2,1,0:T(8,128)(2,1)} %get-tuple-element.34), channel_id=1, source_target_pairs={{0,16},{16,0},{1,17},{17,1},{2,18},{18,2},{3,19},{19,3},{4,20},{20... | collective-permute-start | bytes 1572872 | tf_op jit(solution)/shard_map/ppermute | solution.py:108
  89.6 0.8 place.6._
  90.4 8.7 %collective-permute-done.11.block_ref = bf16[1,256,1024]{2,1,0:T(8,128)(2,1)S(1)} collective-permute-done((bf16[1,256,1024]{2,1,0:T(8,128)(2,1)}, bf16[1,256,1024]{2,1,0:T(8,128)(2,1)S(1)}, u32[]{:S(2)}, u32[]{:S(2)}) %collective-permute-start.11) | collective-permute-done | bytes 524320 | tf_op jit(solution)/shard_map/ppermute | solution.py:108
  99.1 0.8 place.7._
  99.9 10.4 %collective-permute-done.10.block_ref = bf16[1,256,1024]{2,1,0:T(8,128)(2,1)S(1)} collective-permute-done((bf16[1,256,1024]{2,1,0:T(8,128)(2,1)}, bf16[1,256,1024]{2,1,0:T(8,128)(2,1)S(1)}, u32[]{:S(2)}, u32[]{:S(2)}) %collective-permute-start.10) | collective-permute-done | bytes 524320 | tf_op jit(solution)/shard_map/ppermute | solution.py:108
  110.3 0.8 place.8._
  111.1 10.4 %collective-permute-done.9.block_ref = bf16[1,256,1024]{2,1,0:T(8,128)(2,1)S(1)} collective-permute-done((bf16[1,256,1024]{2,1,0:T(8,128)(2,1)}, bf16[1,256,1024]{2,1,0:T(8,128)(2,1)S(1)}, u32[]{:S(2)}, u32[]{:S(2)}) %collective-permute-start.9) | collective-permute-done | bytes 524320 | tf_op jit(solution)/shard_map/ppermute | solution.py:108
  121.6 0.8 place.9._
  122.4 10.4 %collective-permute-done.8.block_ref = bf16[1,256,1024]{2,1,0:T(8,128)(2,1)S(1)} collective-permute-done((bf16[1,256,1024]{2,1,0:T(8,128)(2,1)}, bf16[1,256,1024]{2,1,0:T(8,128)(2,1)S(1)}, u32[]{:S(2)}, u32[]{:S(2)}) %collective-permute-start.8) | collective-permute-done | bytes 524320 | tf_op jit(solution)/shard_map/ppermute | solution.py:108
  132.8 0.8 place.10._
  133.6 8.5 %collective-permute-done.7.block_ref = bf16[1,256,1024]{2,1,0:T(8,128)(2,1)S(1)} collective-permute-done((bf16[1,256,1024]{2,1,0:T(8,128)(2,1)}, bf16[1,256,1024]{2,1,0:T(8,128)(2,1)S(1)}, u32[]{:S(2)}, u32[]{:S(2)}) %collective-permute-start.7) | collective-permute-done | bytes 524320 | tf_op jit(solution)/shard_map/ppermute | solution.py:108
  142.1 0.8 place.11
  (8 shorter events, 0.5 us)
Async XLA Ops:
  1.7 51.2 %collective-permute-start.6 = (bf16[1,256,1024]{2,1,0:T(8,128)(2,1)S(1)}, bf16[1,256,1024]{2,1,0:T(8,128)(2,1)S(1)}, u32[]{:S(2)}, u32[]{:S(2)}) collective-permute-start(bf16[1,256,1024]{2,1,0:T(8,128)(2,1)S(1)} %constant_dynamic-slice_fusion.5), channel_id=1, source_target_pairs={{0,16},{16,0},{1,17},{17,1},{2,18},{18,2},{3,19},{19,3},{4,20},{20... | collective-permute-start | bytes 1572872 | tf_op jit(solution)/shard_map/ppermute | solution.py:108
  6.7 49.9 %collective-permute-start.5 = (bf16[1,256,1024]{2,1,0:T(8,128)(2,1)S(1)}, bf16[1,256,1024]{2,1,0:T(8,128)(2,1)S(1)}, u32[]{:S(2)}, u32[]{:S(2)}) collective-permute-start(bf16[1,256,1024]{2,1,0:T(8,128)(2,1)S(1)} %get-tuple-element.42), channel_id=1, source_target_pairs={{0,16},{16,0},{1,17},{17,1},{2,18},{18,2},{3,19},{19,3},{4,20},{20... | collective-permute-start | bytes 1572872 | tf_op jit(solution)/shard_map/ppermute | solution.py:108
  6.7 55.2 %collective-permute-start.4 = (bf16[1,256,1024]{2,1,0:T(8,128)(2,1)S(1)}, bf16[1,256,1024]{2,1,0:T(8,128)(2,1)S(1)}, u32[]{:S(2)}, u32[]{:S(2)}) collective-permute-start(bf16[1,256,1024]{2,1,0:T(8,128)(2,1)S(1)} %get-tuple-element.43), channel_id=1, source_target_pairs={{0,16},{16,0},{1,17},{17,1},{2,18},{18,2},{3,19},{19,3},{4,20},{20... | collective-permute-start | bytes 1572872 | tf_op jit(solution)/shard_map/ppermute | solution.py:108
  8.7 57.0 %collective-permute-start.3 = (bf16[1,256,1024]{2,1,0:T(8,128)(2,1)S(1)}, bf16[1,256,1024]{2,1,0:T(8,128)(2,1)S(1)}, u32[]{:S(2)}, u32[]{:S(2)}) collective-permute-start(bf16[1,256,1024]{2,1,0:T(8,128)(2,1)S(1)} %get-tuple-element.44), channel_id=1, source_target_pairs={{0,16},{16,0},{1,17},{17,1},{2,18},{18,2},{3,19},{19,3},{4,20},{20... | collective-permute-start | bytes 1572872 | tf_op jit(solution)/shard_map/ppermute | solution.py:108
  8.8 41.7 %collective-permute-start = (s32[1]{0:T(128)}, s32[1]{0:T(128)}, u32[]{:S(2)}, u32[]{:S(2)}) collective-permute-start(s32[1]{0:T(128)} %param.4), channel_id=1, source_target_pairs={{0,16},{16,0},{1,17},{17,1},{2,18},{18,2},{3,19},{19,3},{4,20},{20... | collective-permute-start | bytes 20 | tf_op jit(solution)/shard_map/ppermute | solution.py:108
  50.5 20.4 %collective-permute-start.2 = (bf16[1,256,1024]{2,1,0:T(8,128)(2,1)S(1)}, bf16[1,256,1024]{2,1,0:T(8,128)(2,1)S(1)}, u32[]{:S(2)}, u32[]{:S(2)}) collective-permute-start(bf16[1,256,1024]{2,1,0:T(8,128)(2,1)S(1)} %get-tuple-element.45), channel_id=1, source_target_pairs={{0,16},{16,0},{1,17},{17,1},{2,18},{18,2},{3,19},{19,3},{4,20},{20... | collective-permute-start | bytes 1572872 | tf_op jit(solution)/shard_map/ppermute | solution.py:108
  52.9 23.7 %collective-permute-start.1 = (bf16[1,256,1024]{2,1,0:T(8,128)(2,1)S(1)}, bf16[1,256,1024]{2,1,0:T(8,128)(2,1)S(1)}, u32[]{:S(2)}, u32[]{:S(2)}) collective-permute-start(bf16[1,256,1024]{2,1,0:T(8,128)(2,1)S(1)} %get-tuple-element.46), channel_id=1, source_target_pairs={{0,16},{16,0},{1,17},{17,1},{2,18},{18,2},{3,19},{19,3},{4,20},{20... | collective-permute-start | bytes 1572872 | tf_op jit(solution)/shard_map/ppermute | solution.py:108
  56.6 31.3 %collective-permute-start.12 = (bf16[1,256,1024]{2,1,0:T(8,128)(2,1)S(1)}, bf16[1,256,1024]{2,1,0:T(8,128)(2,1)S(1)}, u32[]{:S(2)}, u32[]{:S(2)}) collective-permute-start(bf16[1,256,1024]{2,1,0:T(8,128)(2,1)S(1)} %get-tuple-element.39), channel_id=1, source_target_pairs={{0,16},{16,0},{1,17},{17,1},{2,18},{18,2},{3,19},{19,3},{4,20},{20... | collective-permute-start | bytes 1572872 | tf_op jit(solution)/shard_map/ppermute | solution.py:108
  61.9 37.2 %collective-permute-start.11 = (bf16[1,256,1024]{2,1,0:T(8,128)(2,1)}, bf16[1,256,1024]{2,1,0:T(8,128)(2,1)S(1)}, u32[]{:S(2)}, u32[]{:S(2)}) collective-permute-start(bf16[1,256,1024]{2,1,0:T(8,128)(2,1)} %get-tuple-element.38), channel_id=1, source_target_pairs={{0,16},{16,0},{1,17},{17,1},{2,18},{18,2},{3,19},{19,3},{4,20},{20... | collective-permute-start | bytes 1572872 | tf_op jit(solution)/shard_map/ppermute | solution.py:108
  65.7 44.6 %collective-permute-start.10 = (bf16[1,256,1024]{2,1,0:T(8,128)(2,1)}, bf16[1,256,1024]{2,1,0:T(8,128)(2,1)S(1)}, u32[]{:S(2)}, u32[]{:S(2)}) collective-permute-start(bf16[1,256,1024]{2,1,0:T(8,128)(2,1)} %get-tuple-element.37), channel_id=1, source_target_pairs={{0,16},{16,0},{1,17},{17,1},{2,18},{18,2},{3,19},{19,3},{4,20},{20... | collective-permute-start | bytes 1572872 | tf_op jit(solution)/shard_map/ppermute | solution.py:108
  70.9 50.6 %collective-permute-start.9 = (bf16[1,256,1024]{2,1,0:T(8,128)(2,1)}, bf16[1,256,1024]{2,1,0:T(8,128)(2,1)S(1)}, u32[]{:S(2)}, u32[]{:S(2)}) collective-permute-start(bf16[1,256,1024]{2,1,0:T(8,128)(2,1)} %get-tuple-element.36), channel_id=1, source_target_pairs={{0,16},{16,0},{1,17},{17,1},{2,18},{18,2},{3,19},{19,3},{4,20},{20... | collective-permute-start | bytes 1572872 | tf_op jit(solution)/shard_map/ppermute | solution.py:108
  76.6 56.2 %collective-permute-start.8 = (bf16[1,256,1024]{2,1,0:T(8,128)(2,1)}, bf16[1,256,1024]{2,1,0:T(8,128)(2,1)S(1)}, u32[]{:S(2)}, u32[]{:S(2)}) collective-permute-start(bf16[1,256,1024]{2,1,0:T(8,128)(2,1)} %get-tuple-element.35), channel_id=1, source_target_pairs={{0,16},{16,0},{1,17},{17,1},{2,18},{18,2},{3,19},{19,3},{4,20},{20... | collective-permute-start | bytes 1572872 | tf_op jit(solution)/shard_map/ppermute | solution.py:108
  87.9 54.3 %collective-permute-start.7 = (bf16[1,256,1024]{2,1,0:T(8,128)(2,1)}, bf16[1,256,1024]{2,1,0:T(8,128)(2,1)S(1)}, u32[]{:S(2)}, u32[]{:S(2)}) collective-permute-start(bf16[1,256,1024]{2,1,0:T(8,128)(2,1)} %get-tuple-element.34), channel_id=1, source_target_pairs={{0,16},{16,0},{1,17},{17,1},{2,18},{18,2},{3,19},{19,3},{4,20},{20... | collective-permute-start | bytes 1572872 | tf_op jit(solution)/shard_map/ppermute | solution.py:108

commit v4 on v3

--- a/solution.py
+++ b/solution.py
@@ -12,21 +12,34 @@
 vmem_bytes = 48 * 1024 * 1024
 
 
-def update_kernel(groups, me_ref, mine_ref, *refs):
-    others, refs = refs[: groups - 1], refs[groups - 1 :]
-    anchor_ref, inner_ref, refs = refs[0], refs[1], refs[2:]
-    arrived, refs = refs[: groups - 1], refs[groups - 1 :]
-    momentum_ref, refs = refs[0], refs[1:]
+def share_kernel(*refs):
+    counts, shares_ref = refs[:-1], refs[-1]
+    values = [ref[0].astype(jnp.float32) for ref in counts]
+    total = values[0]
+    for value in values[1:]:
+        total = total + value
+    for g, value in enumerate(values):
+        shares_ref[g] = value / total
+
+
+def share(counts):
+    scalar = pl.BlockSpec(memory_space=pltpu.SMEM)
+    return pl.pallas_call(
+        share_kernel,
+        in_specs=[scalar] * len(counts),
+        out_specs=scalar,
+        out_shape=jax.ShapeDtypeStruct((len(counts),), jnp.float32),
+        name="share",
+    )(*counts)
+
+
+def update_kernel(groups, me_ref, shares_ref, anchor_ref, inner_ref, *refs):
+    arrived, momentum_ref = refs[: groups - 1], refs[groups - 1]
     new_ref, weights_ref, moments_ref = refs[-3:]
     base = anchor_ref[...].astype(jnp.float32)
-    mine = mine_ref[0].astype(jnp.float32)
-    total = mine
-    acc = mine * (base - inner_ref[...].astype(jnp.float32))
-    for count_ref, block_ref in zip(others, arrived):
-        count = count_ref[0].astype(jnp.float32)
-        total = total + count
-        acc = acc + count * (base - block_ref[...].astype(jnp.float32))
-    pseudo = acc / total
+    pseudo = shares_ref[0] * (base - inner_ref[...].astype(jnp.float32))
+    for g, block_ref in enumerate(arrived, 1):
+        pseudo = pseudo + shares_ref[g] * (base - block_ref[...].astype(jnp.float32))
     moment = momentum_rate * momentum_ref[...] + pseudo
     new = (base - outer_rate * (pseudo + momentum_rate * moment)).astype(jnp.bfloat16)
     moments_ref[...] = moment
@@ -34,7 +47,7 @@
     new_ref[...] = new
 
 
-def update(groups, chunk, me, counts, anchor, inner, arrived, momentum, held):
+def update(groups, chunk, me, shares, anchor, inner, arrived, momentum, held):
     lo, hi = chunk
     parts, owned, width = momentum.shape
     rows = min(owned, 128)
@@ -44,18 +57,14 @@
     spread = pl.BlockSpec(block, lambda p, r, me_ref: (lo + p, me_ref[0] * steps + r, 0))
     packed = pl.BlockSpec(block, lambda p, r, me_ref: (p, r, 0))
     kept = pl.BlockSpec(block, lambda p, r, me_ref: (lo + p, r, 0))
-    aliases = {}
-    if held:
-        first = 1 + groups + 2 + (groups - 1) + 1
-        aliases = {first: 1, first + 1: 2}
+    aliases = {groups + 4: 1, groups + 5: 2} if held else {}
     size = (hi - lo) * owned * width
     return pl.pallas_call(
         functools.partial(update_kernel, groups),
         grid_spec=pltpu.PrefetchScalarGridSpec(
             num_scalar_prefetch=1,
             grid=(hi - lo, steps),
-            in_specs=[scalar] * groups
-            + [spread, spread]
+            in_specs=[scalar, spread, spread]
             + [packed] * (groups - 1)
             + [kept]
             + [pl.BlockSpec(memory_space=pl.ANY)] * len(held),
@@ -72,7 +81,7 @@
             flops=12 * size, bytes_accessed=(14 + 2 * groups) * size, transcendentals=0
         ),
         name="update",
-    )(me, *counts, anchor, inner, *arrived, momentum, *held)
+    )(me, shares, anchor, inner, *arrived, momentum, *held)
 
 
 def place_kernel(lo, at_ref, block_ref, _, weights_ref, sem):
@@ -122,19 +131,20 @@
             sizes = (chunk[1] - chunk[0], owned, width)
             return lax.dynamic_slice(array, (chunk[0], target * owned, 0), sizes)
 
+        other_counts = [shifted(counts, s) for s in shifts]
         targets = [(me + s) % groups for s in shifts]
         first = [rows_for(inner, chunks[0], t) for t in targets]
-        first, rest = lax.optimization_barrier((first, inner))
+        first, rest, other_counts = lax.optimization_barrier((first, inner, other_counts))
+        shares = share([counts] + other_counts)
         sent = [first] + [[rows_for(rest, c, t) for t in targets] for c in chunks[1:]]
         arrived = [[shifted(v, s) for v, s in zip(values, shifts)] for values in sent]
-        all_counts = [counts] + [shifted(counts, s) for s in shifts]
 
         where = me.reshape(1).astype(jnp.int32)
         held = []
         travelled = []
         for chunk, blocks in zip(chunks, arrived):
             new, *held = update(
-                groups, chunk, where, all_counts, anchor, inner, blocks, momentum, held
+                groups, chunk, where, shares, anchor, inner, blocks, momentum, held
             )
             travelled.append([shifted(new, s) for s in shifts])
         weights, moments = held

time: 143 us -> 143 us (level)
  starting transfers between devices: 16.8 us -> 23.2 us
  waiting for transfers between devices: 96.1 us -> 90.5 us
  Pallas kernels: 25.6 us -> 22.6 us
  local copies, waits for them, and re-layouts: 2.99 us -> 4.95 us
    ppermute x13, starting transfers between devices: 16.8 us -> 23.2 us  [shifted(): return lax.ppermute(value, 'replica', pairs)]
    ppermute x13, waiting for transfers between devices: 96.1 us -> 90.5 us  [shifted(): return lax.ppermute(value, 'replica', pairs)]
    pallas_call x6, Pallas kernels: 20.8 us -> 16.7 us  [update(): pl.pallas_call(functools.partial(update_kernel, groups), grid_spec=pltpu....]
  transfers between devices with their start and end apart: 13 -> 13, of which waited for: 8 -> 13; matrix products, arithmetic and copies ran while one was open for 1% -> 3% of each run, Pallas kernels for 17% -> 15%
where the time goes in v4:
time: 143 us
  waiting for transfers between devices  90.5 us (63%)
  starting transfers between devices  23.2 us (16%)
  Pallas kernels  22.6 us (16%)
  local copies, waits for them, and re-layouts  4.95 us (3%)
    ppermute x13, waiting for transfers between devices, shifted(): return lax.ppermute(value, 'replica', pairs)  90.5 us
    ppermute x13, starting transfers between devices, shifted(): return lax.ppermute(value, 'replica', pairs)  23.2 us
    pallas_call x6, Pallas kernels, update(): pl.pallas_call(functools.partial(update_kernel, groups), grid_spec=pltpu....  16.7 us
    pallas_call x6, Pallas kernels, place(): pl.pallas_call(functools.partial(place_kernel, chunk[0]), in_specs=[pl.Bl...  4.8 us
    dynamic_slice x2, local copies, waits for them, and re-layouts, rows_for(): return lax.dynamic_slice(array, (chunk[0], target * owned, 0), sizes)  4.29 us
  transfers between devices with their start and end apart: 13, of which 13 were waited for; matrix products, arithmetic and copies ran while one was open for 3% of the time, Pallas kernels for 15%

profile of v4, /device:TPU:0, one launch (start us, length us, event | category | flops | bytes accessed | tf_op | source)
XLA Modules:
  0.0 142.6 jit_solution(15957128943573288238)
XLA Ops:
  0.6 3.0 %collective-permute-start = (s32[1]{0:T(128)}, s32[1]{0:T(128)}, u32[]{:S(2)}, u32[]{:S(2)}) collective-permute-start(s32[1]{0:T(128)} %param.4), channel_id=1, source_target_pairs={{0,16},{16,0},{1,17},{17,1},{2,18},{18,2},{3,19},{19,3},{4,20},{20... | collective-permute-start | bytes 20 | tf_op jit(solution)/shard_map/ppermute | solution.py:117
  3.6 1.1 constant_dynamic-slice_fusion.5
  5.4 2.0 %collective-permute-start.6 = (bf16[1,256,1024]{2,1,0:T(8,128)(2,1)S(1)}, bf16[1,256,1024]{2,1,0:T(8,128)(2,1)S(1)}, u32[]{:S(2)}, u32[]{:S(2)}) collective-permute-start(bf16[1,256,1024]{2,1,0:T(8,128)(2,1)S(1)} %constant_dynamic-slice_fusion.5), channel_id=1, source_target_pairs={{0,16},{16,0},{1,17},{17,1},{2,18},{18,2},{3,19},{19,3},{4,20},{20... | collective-permute-start | bytes 1572872 | tf_op jit(solution)/shard_map/ppermute | solution.py:117
  7.4 3.2 %constant_dynamic-slice_fusion = (bf16[1,256,1024]{2,1,0:T(8,128)(2,1)}, bf16[1,256,1024]{2,1,0:T(8,128)(2,1)}, bf16[1,256,1024]{2,1,0:T(8,128)(2,1)}, bf16[1,256,1024]{2,1,0:T(8,128)(2,1)}, bf16[1,256,1024]{2,1,0:T(8,128)(2,1)}) fusion(bf16[6,512,1024]{2,1,0:T(8,128)(2,1)} %bitcast.9, s32[]{:T(128)S(6)} %select_n.31), kind=kLoop, calls=%fused_computation | loop fusion | bytes 5242884 | tf_op jit(solution)/shard_map/dynamic_slice | solution.py:132
  10.6 2.0 %collective-permute-start.4 = (bf16[1,256,1024]{2,1,0:T(8,128)(2,1)}, bf16[1,256,1024]{2,1,0:T(8,128)(2,1)S(1)}, u32[]{:S(2)}, u32[]{:S(2)}) collective-permute-start(bf16[1,256,1024]{2,1,0:T(8,128)(2,1)} %get-tuple-element.45), channel_id=1, source_target_pairs={{0,16},{16,0},{1,17},{17,1},{2,18},{18,2},{3,19},{19,3},{4,20},{20... | collective-permute-start | bytes 1572872 | tf_op jit(solution)/shard_map/ppermute | solution.py:117
  12.7 2.0 %collective-permute-start.2 = (bf16[1,256,1024]{2,1,0:T(8,128)(2,1)}, bf16[1,256,1024]{2,1,0:T(8,128)(2,1)S(1)}, u32[]{:S(2)}, u32[]{:S(2)}) collective-permute-start(bf16[1,256,1024]{2,1,0:T(8,128)(2,1)} %get-tuple-element.47), channel_id=1, source_target_pairs={{0,16},{16,0},{1,17},{17,1},{2,18},{18,2},{3,19},{19,3},{4,20},{20... | collective-permute-start | bytes 1572872 | tf_op jit(solution)/shard_map/ppermute | solution.py:117
  15.3 1.1 share.1.shares_ref
  16.4 3.8 %collective-permute-done.6.refs_0_ = bf16[1,256,1024]{2,1,0:T(8,128)(2,1)S(1)} collective-permute-done((bf16[1,256,1024]{2,1,0:T(8,128)(2,1)S(1)}, bf16[1,256,1024]{2,1,0:T(8,128)(2,1)S(1)}, u32[]{:S(2)}, u32[]{:S(2)}) %collective-permute-start.6) | collective-permute-done | bytes 524320 | tf_op jit(solution)/shard_map/ppermute | solution.py:117
  20.3 2.0 %collective-permute-start.1 = (bf16[1,256,1024]{2,1,0:T(8,128)(2,1)}, bf16[1,256,1024]{2,1,0:T(8,128)(2,1)S(1)}, u32[]{:S(2)}, u32[]{:S(2)}) collective-permute-start(bf16[1,256,1024]{2,1,0:T(8,128)(2,1)} %get-tuple-element.48), channel_id=1, source_target_pairs={{0,16},{16,0},{1,17},{17,1},{2,18},{18,2},{3,19},{19,3},{4,20},{20... | collective-permute-start | bytes 1572872 | tf_op jit(solution)/shard_map/ppermute | solution.py:117
  22.9 2.6 %update.6 = (bf16[1,256,1024]{2,1,0:T(8,128)(2,1)S(1)}, bf16[6,512,1024]{2,1,0:T(8,128)(2,1)}, f32[6,256,1024]{2,1,0:T(8,128)}) custom-call(s32[1]{0:T(128)} %bitcast.1.me_ref, f32[2]{0:T(128)S(1)} %copy-done, bf16[6,512,1024]{2,1,0:T(8,128)(2,1)} %bitcast.16, bf16[6,512,1024]{2,1,0:T(8,128)(2,1)} %bitcast.10, ...), custom_call_target="tpu_custom_call" | custom-call | flops 3145728 | bytes 4718592 | tf_op jit(solution)/shard_map/update/pallas_call | solution.py:62
  25.6 5.9 %collective-permute-done.5.refs_0_ = bf16[1,256,1024]{2,1,0:T(8,128)(2,1)S(1)} collective-permute-done((bf16[1,256,1024]{2,1,0:T(8,128)(2,1)}, bf16[1,256,1024]{2,1,0:T(8,128)(2,1)S(1)}, u32[]{:S(2)}, u32[]{:S(2)}) %collective-permute-start.5) | collective-permute-done | bytes 524320 | tf_op jit(solution)/shard_map/ppermute | solution.py:117
  31.5 2.0 %collective-permute-start.12 = (bf16[1,256,1024]{2,1,0:T(8,128)(2,1)S(1)}, bf16[1,256,1024]{2,1,0:T(8,128)(2,1)S(1)}, u32[]{:S(2)}, u32[]{:S(2)}) collective-permute-start(bf16[1,256,1024]{2,1,0:T(8,128)(2,1)S(1)} %get-tuple-element.41), channel_id=1, source_target_pairs={{0,16},{16,0},{1,17},{17,1},{2,18},{18,2},{3,19},{19,3},{4,20},{20... | collective-permute-start | bytes 1572872 | tf_op jit(solution)/shard_map/ppermute | solution.py:117
  33.5 2.8 %update.7 = (bf16[1,256,1024]{2,1,0:T(8,128)(2,1)}, bf16[6,512,1024]{2,1,0:T(8,128)(2,1)}, f32[6,256,1024]{2,1,0:T(8,128)}) custom-call(s32[1]{0:T(128)} %bitcast.1.me_ref, f32[2]{0:T(128)S(1)} %copy-done, bf16[6,512,1024]{2,1,0:T(8,128)(2,1)} %bitcast.17, bf16[6,512,1024]{2,1,0:T(8,128)(2,1)} %bitcast.11, ...), custom_call_target="tpu_custom_call", output_to_operand_aliasing={{1}: (6, {}), {2}: (7, {})} | custom-call | flops 3145728 | bytes 4718592 | tf_op jit(solution)/shard_map/update/pallas_call | solution.py:62
  36.3 6.4 %collective-permute-done.4.refs_0_ = bf16[1,256,1024]{2,1,0:T(8,128)(2,1)S(1)} collective-permute-done((bf16[1,256,1024]{2,1,0:T(8,128)(2,1)}, bf16[1,256,1024]{2,1,0:T(8,128)(2,1)S(1)}, u32[]{:S(2)}, u32[]{:S(2)}) %collective-permute-start.4) | collective-permute-done | bytes 524320 | tf_op jit(solution)/shard_map/ppermute | solution.py:117
  42.7 2.0 %collective-permute-start.11 = (bf16[1,256,1024]{2,1,0:T(8,128)(2,1)}, bf16[1,256,1024]{2,1,0:T(8,128)(2,1)S(1)}, u32[]{:S(2)}, u32[]{:S(2)}) collective-permute-start(bf16[1,256,1024]{2,1,0:T(8,128)(2,1)} %get-tuple-element.40), channel_id=1, source_target_pairs={{0,16},{16,0},{1,17},{17,1},{2,18},{18,2},{3,19},{19,3},{4,20},{20... | collective-permute-start | bytes 1572872 | tf_op jit(solution)/shard_map/ppermute | solution.py:117
  44.7 2.8 %update.8 = (bf16[1,256,1024]{2,1,0:T(8,128)(2,1)}, bf16[6,512,1024]{2,1,0:T(8,128)(2,1)}, f32[6,256,1024]{2,1,0:T(8,128)}) custom-call(s32[1]{0:T(128)} %bitcast.1.me_ref, f32[2]{0:T(128)S(1)} %copy-done, bf16[6,512,1024]{2,1,0:T(8,128)(2,1)} %bitcast.18, bf16[6,512,1024]{2,1,0:T(8,128)(2,1)} %bitcast.12, ...), custom_call_target="tpu_custom_call", output_to_operand_aliasing={{1}: (6, {}), {2}: (7, {})} | custom-call | flops 3145728 | bytes 4718592 | tf_op jit(solution)/shard_map/update/pallas_call | solution.py:62
  47.6 6.4 %collective-permute-done.3.refs_0_ = bf16[1,256,1024]{2,1,0:T(8,128)(2,1)S(1)} collective-permute-done((bf16[1,256,1024]{2,1,0:T(8,128)(2,1)}, bf16[1,256,1024]{2,1,0:T(8,128)(2,1)S(1)}, u32[]{:S(2)}, u32[]{:S(2)}) %collective-permute-start.3) | collective-permute-done | bytes 524320 | tf_op jit(solution)/shard_map/ppermute | solution.py:117
  54.0 2.0 %collective-permute-start.10 = (bf16[1,256,1024]{2,1,0:T(8,128)(2,1)}, bf16[1,256,1024]{2,1,0:T(8,128)(2,1)S(1)}, u32[]{:S(2)}, u32[]{:S(2)}) collective-permute-start(bf16[1,256,1024]{2,1,0:T(8,128)(2,1)} %get-tuple-element.39), channel_id=1, source_target_pairs={{0,16},{16,0},{1,17},{17,1},{2,18},{18,2},{3,19},{19,3},{4,20},{20... | collective-permute-start | bytes 1572872 | tf_op jit(solution)/shard_map/ppermute | solution.py:117
  56.0 2.8 %update.9 = (bf16[1,256,1024]{2,1,0:T(8,128)(2,1)}, bf16[6,512,1024]{2,1,0:T(8,128)(2,1)}, f32[6,256,1024]{2,1,0:T(8,128)}) custom-call(s32[1]{0:T(128)} %bitcast.1.me_ref, f32[2]{0:T(128)S(1)} %copy-done, bf16[6,512,1024]{2,1,0:T(8,128)(2,1)} %bitcast.19, bf16[6,512,1024]{2,1,0:T(8,128)(2,1)} %bitcast.13, ...), custom_call_target="tpu_custom_call", output_to_operand_aliasing={{1}: (6, {}), {2}: (7, {})} | custom-call | flops 3145728 | bytes 4718592 | tf_op jit(solution)/shard_map/update/pallas_call | solution.py:62
  58.8 6.4 %collective-permute-done.2.refs_0_ = bf16[1,256,1024]{2,1,0:T(8,128)(2,1)S(1)} collective-permute-done((bf16[1,256,1024]{2,1,0:T(8,128)(2,1)}, bf16[1,256,1024]{2,1,0:T(8,128)(2,1)S(1)}, u32[]{:S(2)}, u32[]{:S(2)}) %collective-permute-start.2) | collective-permute-done | bytes 524320 | tf_op jit(solution)/shard_map/ppermute | solution.py:117
  65.2 2.0 %collective-permute-start.9 = (bf16[1,256,1024]{2,1,0:T(8,128)(2,1)}, bf16[1,256,1024]{2,1,0:T(8,128)(2,1)S(1)}, u32[]{:S(2)}, u32[]{:S(2)}) collective-permute-start(bf16[1,256,1024]{2,1,0:T(8,128)(2,1)} %get-tuple-element.38), channel_id=1, source_target_pairs={{0,16},{16,0},{1,17},{17,1},{2,18},{18,2},{3,19},{19,3},{4,20},{20... | collective-permute-start | bytes 1572872 | tf_op jit(solution)/shard_map/ppermute | solution.py:117
  67.2 2.8 %update.10 = (bf16[1,256,1024]{2,1,0:T(8,128)(2,1)}, bf16[6,512,1024]{2,1,0:T(8,128)(2,1)}, f32[6,256,1024]{2,1,0:T(8,128)}) custom-call(s32[1]{0:T(128)} %bitcast.1.me_ref, f32[2]{0:T(128)S(1)} %copy-done, bf16[6,512,1024]{2,1,0:T(8,128)(2,1)} %bitcast.20, bf16[6,512,1024]{2,1,0:T(8,128)(2,1)} %bitcast.14, ...), custom_call_target="tpu_custom_call", output_to_operand_aliasing={{1}: (6, {}), {2}: (7, {})} | custom-call | flops 3145728 | bytes 4718592 | tf_op jit(solution)/shard_map/update/pallas_call | solution.py:62
  70.0 6.4 %collective-permute-done.1.refs_0_ = bf16[1,256,1024]{2,1,0:T(8,128)(2,1)S(1)} collective-permute-done((bf16[1,256,1024]{2,1,0:T(8,128)(2,1)}, bf16[1,256,1024]{2,1,0:T(8,128)(2,1)S(1)}, u32[]{:S(2)}, u32[]{:S(2)}) %collective-permute-start.1) | collective-permute-done | bytes 524320 | tf_op jit(solution)/shard_map/ppermute | solution.py:117
  76.4 2.0 %collective-permute-start.8 = (bf16[1,256,1024]{2,1,0:T(8,128)(2,1)}, bf16[1,256,1024]{2,1,0:T(8,128)(2,1)S(1)}, u32[]{:S(2)}, u32[]{:S(2)}) collective-permute-start(bf16[1,256,1024]{2,1,0:T(8,128)(2,1)} %get-tuple-element.37), channel_id=1, source_target_pairs={{0,16},{16,0},{1,17},{17,1},{2,18},{18,2},{3,19},{19,3},{4,20},{20... | collective-permute-start | bytes 1572872 | tf_op jit(solution)/shard_map/ppermute | solution.py:117
  78.5 2.8 %update.11 = (bf16[1,256,1024]{2,1,0:T(8,128)(2,1)}, bf16[6,512,1024]{2,1,0:T(8,128)(2,1)}, f32[6,256,1024]{2,1,0:T(8,128)}) custom-call(s32[1]{0:T(128)} %bitcast.1.me_ref, f32[2]{0:T(128)S(1)} %copy-done, bf16[6,512,1024]{2,1,0:T(8,128)(2,1)} %bitcast.21, bf16[6,512,1024]{2,1,0:T(8,128)(2,1)} %bitcast.15, ...), custom_call_target="tpu_custom_call", output_to_operand_aliasing={{1}: (6, {}), {2}: (7, {})} | custom-call | flops 3145728 | bytes 4718592 | tf_op jit(solution)/shard_map/update/pallas_call | solution.py:62
  81.3 6.4 %collective-permute-done.12.block_ref = bf16[1,256,1024]{2,1,0:T(8,128)(2,1)S(1)} collective-permute-done((bf16[1,256,1024]{2,1,0:T(8,128)(2,1)S(1)}, bf16[1,256,1024]{2,1,0:T(8,128)(2,1)S(1)}, u32[]{:S(2)}, u32[]{:S(2)}) %collective-permute-start.12) | collective-permute-done | bytes 524320 | tf_op jit(solution)/shard_map/ppermute | solution.py:117
  87.7 2.0 %collective-permute-start.7 = (bf16[1,256,1024]{2,1,0:T(8,128)(2,1)}, bf16[1,256,1024]{2,1,0:T(8,128)(2,1)S(1)}, u32[]{:S(2)}, u32[]{:S(2)}) collective-permute-start(bf16[1,256,1024]{2,1,0:T(8,128)(2,1)} %get-tuple-element.36), channel_id=1, source_target_pairs={{0,16},{16,0},{1,17},{17,1},{2,18},{18,2},{3,19},{19,3},{4,20},{20... | collective-permute-start | bytes 1572872 | tf_op jit(solution)/shard_map/ppermute | solution.py:117
  90.5 8.4 %collective-permute-done.11.block_ref = bf16[1,256,1024]{2,1,0:T(8,128)(2,1)S(1)} collective-permute-done((bf16[1,256,1024]{2,1,0:T(8,128)(2,1)}, bf16[1,256,1024]{2,1,0:T(8,128)(2,1)S(1)}, u32[]{:S(2)}, u32[]{:S(2)}) %collective-permute-start.11) | collective-permute-done | bytes 524320 | tf_op jit(solution)/shard_map/ppermute | solution.py:117
  99.7 10.4 %collective-permute-done.10.block_ref = bf16[1,256,1024]{2,1,0:T(8,128)(2,1)S(1)} collective-permute-done((bf16[1,256,1024]{2,1,0:T(8,128)(2,1)}, bf16[1,256,1024]{2,1,0:T(8,128)(2,1)S(1)}, u32[]{:S(2)}, u32[]{:S(2)}) %collective-permute-start.10) | collective-permute-done | bytes 524320 | tf_op jit(solution)/shard_map/ppermute | solution.py:117
  110.9 10.4 %collective-permute-done.9.block_ref = bf16[1,256,1024]{2,1,0:T(8,128)(2,1)S(1)} collective-permute-done((bf16[1,256,1024]{2,1,0:T(8,128)(2,1)}, bf16[1,256,1024]{2,1,0:T(8,128)(2,1)S(1)}, u32[]{:S(2)}, u32[]{:S(2)}) %collective-permute-start.9) | collective-permute-done | bytes 524320 | tf_op jit(solution)/shard_map/ppermute | solution.py:117
  122.2 10.4 %collective-permute-done.8.block_ref = bf16[1,256,1024]{2,1,0:T(8,128)(2,1)S(1)} collective-permute-done((bf16[1,256,1024]{2,1,0:T(8,128)(2,1)}, bf16[1,256,1024]{2,1,0:T(8,128)(2,1)S(1)}, u32[]{:S(2)}, u32[]{:S(2)}) %collective-permute-start.8) | collective-permute-done | bytes 524320 | tf_op jit(solution)/shard_map/ppermute | solution.py:117
  133.4 8.3 %collective-permute-done.7.block_ref = bf16[1,256,1024]{2,1,0:T(8,128)(2,1)S(1)} collective-permute-done((bf16[1,256,1024]{2,1,0:T(8,128)(2,1)}, bf16[1,256,1024]{2,1,0:T(8,128)(2,1)S(1)}, u32[]{:S(2)}, u32[]{:S(2)}) %collective-permute-start.7) | collective-permute-done | bytes 524320 | tf_op jit(solution)/shard_map/ppermute | solution.py:117
  (11 shorter events, 6.2 us)
Async XLA Ops:
  0.6 4.8 %collective-permute-start = (s32[1]{0:T(128)}, s32[1]{0:T(128)}, u32[]{:S(2)}, u32[]{:S(2)}) collective-permute-start(s32[1]{0:T(128)} %param.4), channel_id=1, source_target_pairs={{0,16},{16,0},{1,17},{17,1},{2,18},{18,2},{3,19},{19,3},{4,20},{20... | collective-permute-start | bytes 20 | tf_op jit(solution)/shard_map/ppermute | solution.py:117
  5.4 14.9 %collective-permute-start.6 = (bf16[1,256,1024]{2,1,0:T(8,128)(2,1)S(1)}, bf16[1,256,1024]{2,1,0:T(8,128)(2,1)S(1)}, u32[]{:S(2)}, u32[]{:S(2)}) collective-permute-start(bf16[1,256,1024]{2,1,0:T(8,128)(2,1)S(1)} %constant_dynamic-slice_fusion.5), channel_id=1, source_target_pairs={{0,16},{16,0},{1,17},{17,1},{2,18},{18,2},{3,19},{19,3},{4,20},{20... | collective-permute-start | bytes 1572872 | tf_op jit(solution)/shard_map/ppermute | solution.py:117
  10.6 20.9 %collective-permute-start.5 = (bf16[1,256,1024]{2,1,0:T(8,128)(2,1)}, bf16[1,256,1024]{2,1,0:T(8,128)(2,1)S(1)}, u32[]{:S(2)}, u32[]{:S(2)}) collective-permute-start(bf16[1,256,1024]{2,1,0:T(8,128)(2,1)} %get-tuple-element.44), channel_id=1, source_target_pairs={{0,16},{16,0},{1,17},{17,1},{2,18},{18,2},{3,19},{19,3},{4,20},{20... | collective-permute-start | bytes 1572872 | tf_op jit(solution)/shard_map/ppermute | solution.py:117
  10.6 32.1 %collective-permute-start.4 = (bf16[1,256,1024]{2,1,0:T(8,128)(2,1)}, bf16[1,256,1024]{2,1,0:T(8,128)(2,1)S(1)}, u32[]{:S(2)}, u32[]{:S(2)}) collective-permute-start(bf16[1,256,1024]{2,1,0:T(8,128)(2,1)} %get-tuple-element.45), channel_id=1, source_target_pairs={{0,16},{16,0},{1,17},{17,1},{2,18},{18,2},{3,19},{19,3},{4,20},{20... | collective-permute-start | bytes 1572872 | tf_op jit(solution)/shard_map/ppermute | solution.py:117
  12.7 41.3 %collective-permute-start.3 = (bf16[1,256,1024]{2,1,0:T(8,128)(2,1)}, bf16[1,256,1024]{2,1,0:T(8,128)(2,1)S(1)}, u32[]{:S(2)}, u32[]{:S(2)}) collective-permute-start(bf16[1,256,1024]{2,1,0:T(8,128)(2,1)} %get-tuple-element.46), channel_id=1, source_target_pairs={{0,16},{16,0},{1,17},{17,1},{2,18},{18,2},{3,19},{19,3},{4,20},{20... | collective-permute-start | bytes 1572872 | tf_op jit(solution)/shard_map/ppermute | solution.py:117
  12.7 52.5 %collective-permute-start.2 = (bf16[1,256,1024]{2,1,0:T(8,128)(2,1)}, bf16[1,256,1024]{2,1,0:T(8,128)(2,1)S(1)}, u32[]{:S(2)}, u32[]{:S(2)}) collective-permute-start(bf16[1,256,1024]{2,1,0:T(8,128)(2,1)} %get-tuple-element.47), channel_id=1, source_target_pairs={{0,16},{16,0},{1,17},{17,1},{2,18},{18,2},{3,19},{19,3},{4,20},{20... | collective-permute-start | bytes 1572872 | tf_op jit(solution)/shard_map/ppermute | solution.py:117
  20.3 56.2 %collective-permute-start.1 = (bf16[1,256,1024]{2,1,0:T(8,128)(2,1)}, bf16[1,256,1024]{2,1,0:T(8,128)(2,1)S(1)}, u32[]{:S(2)}, u32[]{:S(2)}) collective-permute-start(bf16[1,256,1024]{2,1,0:T(8,128)(2,1)} %get-tuple-element.48), channel_id=1, source_target_pairs={{0,16},{16,0},{1,17},{17,1},{2,18},{18,2},{3,19},{19,3},{4,20},{20... | collective-permute-start | bytes 1572872 | tf_op jit(solution)/shard_map/ppermute | solution.py:117
  22.3 0.7 copy-start
  31.5 56.2 %collective-permute-start.12 = (bf16[1,256,1024]{2,1,0:T(8,128)(2,1)S(1)}, bf16[1,256,1024]{2,1,0:T(8,128)(2,1)S(1)}, u32[]{:S(2)}, u32[]{:S(2)}) collective-permute-start(bf16[1,256,1024]{2,1,0:T(8,128)(2,1)S(1)} %get-tuple-element.41), channel_id=1, source_target_pairs={{0,16},{16,0},{1,17},{17,1},{2,18},{18,2},{3,19},{19,3},{4,20},{20... | collective-permute-start | bytes 1572872 | tf_op jit(solution)/shard_map/ppermute | solution.py:117
  42.7 56.2 %collective-permute-start.11 = (bf16[1,256,1024]{2,1,0:T(8,128)(2,1)}, bf16[1,256,1024]{2,1,0:T(8,128)(2,1)S(1)}, u32[]{:S(2)}, u32[]{:S(2)}) collective-permute-start(bf16[1,256,1024]{2,1,0:T(8,128)(2,1)} %get-tuple-element.40), channel_id=1, source_target_pairs={{0,16},{16,0},{1,17},{17,1},{2,18},{18,2},{3,19},{19,3},{4,20},{20... | collective-permute-start | bytes 1572872 | tf_op jit(solution)/shard_map/ppermute | solution.py:117
  54.0 56.2 %collective-permute-start.10 = (bf16[1,256,1024]{2,1,0:T(8,128)(2,1)}, bf16[1,256,1024]{2,1,0:T(8,128)(2,1)S(1)}, u32[]{:S(2)}, u32[]{:S(2)}) collective-permute-start(bf16[1,256,1024]{2,1,0:T(8,128)(2,1)} %get-tuple-element.39), channel_id=1, source_target_pairs={{0,16},{16,0},{1,17},{17,1},{2,18},{18,2},{3,19},{19,3},{4,20},{20... | collective-permute-start | bytes 1572872 | tf_op jit(solution)/shard_map/ppermute | solution.py:117
  65.2 56.2 %collective-permute-start.9 = (bf16[1,256,1024]{2,1,0:T(8,128)(2,1)}, bf16[1,256,1024]{2,1,0:T(8,128)(2,1)S(1)}, u32[]{:S(2)}, u32[]{:S(2)}) collective-permute-start(bf16[1,256,1024]{2,1,0:T(8,128)(2,1)} %get-tuple-element.38), channel_id=1, source_target_pairs={{0,16},{16,0},{1,17},{17,1},{2,18},{18,2},{3,19},{19,3},{4,20},{20... | collective-permute-start | bytes 1572872 | tf_op jit(solution)/shard_map/ppermute | solution.py:117
  76.4 56.2 %collective-permute-start.8 = (bf16[1,256,1024]{2,1,0:T(8,128)(2,1)}, bf16[1,256,1024]{2,1,0:T(8,128)(2,1)S(1)}, u32[]{:S(2)}, u32[]{:S(2)}) collective-permute-start(bf16[1,256,1024]{2,1,0:T(8,128)(2,1)} %get-tuple-element.37), channel_id=1, source_target_pairs={{0,16},{16,0},{1,17},{17,1},{2,18},{18,2},{3,19},{19,3},{4,20},{20... | collective-permute-start | bytes 1572872 | tf_op jit(solution)/shard_map/ppermute | solution.py:117
  87.7 54.1 %collective-permute-start.7 = (bf16[1,256,1024]{2,1,0:T(8,128)(2,1)}, bf16[1,256,1024]{2,1,0:T(8,128)(2,1)S(1)}, u32[]{:S(2)}, u32[]{:S(2)}) collective-permute-start(bf16[1,256,1024]{2,1,0:T(8,128)(2,1)} %get-tuple-element.36), channel_id=1, source_target_pairs={{0,16},{16,0},{1,17},{17,1},{2,18},{18,2},{3,19},{19,3},{4,20},{20... | collective-permute-start | bytes 1572872 | tf_op jit(solution)/shard_map/ppermute | solution.py:117

commit v5 on v4

--- a/solution.py
+++ b/solution.py
@@ -9,12 +9,68 @@
 
 outer_rate = 0.7
 momentum_rate = 0.9
+lanes = 128
+spare = 16
 vmem_bytes = 48 * 1024 * 1024
 
 
-def share_kernel(*refs):
-    counts, shares_ref = refs[:-1], refs[-1]
-    values = [ref[0].astype(jnp.float32) for ref in counts]
+def pack_kernel(target_ref, count_ref, inner_ref, out_ref, tile_ref, sems):
+    owned = (out_ref.shape[0] - spare) // (inner_ref.shape[2] // lanes)
+    start = pl.multiple_of(target_ref[0] * owned, owned)
+    copies = [
+        pltpu.make_async_copy(
+            inner_ref.at[0, pl.ds(start, owned), pl.ds(j * lanes, lanes)],
+            out_ref.at[pl.ds(j * owned, owned), :],
+            sems.at[j],
+        )
+        for j in range(inner_ref.shape[2] // lanes)
+    ]
+    for copy in copies:
+        copy.start()
+    count = count_ref[0]
+    high = (count >> 8).astype(jnp.float32)
+    low = (count & 255).astype(jnp.float32)
+    row = lax.broadcasted_iota(jnp.int32, tile_ref.shape, 0)
+    tile_ref[...] = jnp.where(row == 0, high, low).astype(jnp.bfloat16)
+    copies.append(
+        pltpu.make_async_copy(
+            tile_ref,
+            out_ref.at[pl.ds(out_ref.shape[0] - spare, spare), :],
+            sems.at[len(copies)],
+        )
+    )
+    copies[-1].start()
+    for copy in copies:
+        copy.wait()
+
+
+def pack(target, counts, inner, owned):
+    blocks = inner.shape[2] // lanes
+    scalar = pl.BlockSpec(memory_space=pltpu.SMEM)
+    anywhere = pl.BlockSpec(memory_space=pl.ANY)
+    return pl.pallas_call(
+        pack_kernel,
+        in_specs=[scalar, scalar, anywhere],
+        out_specs=anywhere,
+        out_shape=jax.ShapeDtypeStruct((blocks * owned + spare, lanes), jnp.bfloat16),
+        scratch_shapes=[
+            pltpu.VMEM((spare, lanes), jnp.bfloat16),
+            pltpu.SemaphoreType.DMA((blocks + 1,)),
+        ],
+        compiler_params=pltpu.CompilerParams(vmem_limit_bytes=vmem_bytes),
+        cost_estimate=pl.CostEstimate(
+            flops=0, bytes_accessed=4 * blocks * owned * lanes, transcendentals=0
+        ),
+        name="pack",
+    )(target, counts, inner)
+
+
+def share_kernel(mine_ref, *refs):
+    tiles, shares_ref = refs[:-1], refs[-1]
+    values = [mine_ref[0].astype(jnp.float32)]
+    for ref in tiles:
+        tile = ref[...].astype(jnp.float32)
+        values.append(tile[0, 0] * 256.0 + tile[1, 0])
     total = values[0]
     for value in values[1:]:
         total = total + value
@@ -22,15 +78,18 @@
         shares_ref[g] = value / total
 
 
-def share(counts):
+def share(counts, arrived):
     scalar = pl.BlockSpec(memory_space=pltpu.SMEM)
+    last = arrived[0].shape[0] // spare - 1
+    tile = pl.BlockSpec((spare, lanes), lambda i: (last, 0))
     return pl.pallas_call(
         share_kernel,
-        in_specs=[scalar] * len(counts),
+        grid=(1,),
+        in_specs=[scalar] + [tile] * len(arrived),
         out_specs=scalar,
-        out_shape=jax.ShapeDtypeStruct((len(counts),), jnp.float32),
+        out_shape=jax.ShapeDtypeStruct((1 + len(arrived),), jnp.float32),
         name="share",
-    )(*counts)
+    )(counts, *arrived)
 
 
 def update_kernel(groups, me_ref, shares_ref, anchor_ref, inner_ref, *refs):
@@ -39,7 +98,8 @@
     base = anchor_ref[...].astype(jnp.float32)
     pseudo = shares_ref[0] * (base - inner_ref[...].astype(jnp.float32))
     for g, block_ref in enumerate(arrived, 1):
-        pseudo = pseudo + shares_ref[g] * (base - block_ref[...].astype(jnp.float32))
+        block = block_ref[...].astype(jnp.float32).reshape(base.shape)
+        pseudo = pseudo + shares_ref[g] * (base - block)
     moment = momentum_rate * momentum_ref[...] + pseudo
     new = (base - outer_rate * (pseudo + momentum_rate * moment)).astype(jnp.bfloat16)
     moments_ref[...] = moment
@@ -50,22 +110,32 @@
 def update(groups, chunk, me, shares, anchor, inner, arrived, momentum, held):
     lo, hi = chunk
     parts, owned, width = momentum.shape
-    rows = min(owned, 128)
-    steps = owned // rows
-    block = (1, rows, width)
+    if held:
+        rows = min(owned, 128)
+        steps = owned // rows
+        grid = (hi - lo, steps)
+        block = (1, rows, width)
+        came = pl.BlockSpec(block, lambda p, r, me_ref: (p, r, 0))
+        packed = came
+        spread = pl.BlockSpec(block, lambda p, r, me_ref: (lo + p, me_ref[0] * steps + r, 0))
+        kept = pl.BlockSpec(block, lambda p, r, me_ref: (lo + p, r, 0))
+    else:
+        grid = (1, width // lanes)
+        block = (1, owned, lanes)
+        came = pl.BlockSpec((owned, lanes), lambda p, j, me_ref: (j, 0))
+        packed = pl.BlockSpec(block, lambda p, j, me_ref: (0, 0, j))
+        spread = pl.BlockSpec(block, lambda p, j, me_ref: (lo, me_ref[0], j))
+        kept = pl.BlockSpec(block, lambda p, j, me_ref: (lo, 0, j))
     scalar = pl.BlockSpec(memory_space=pltpu.SMEM)
-    spread = pl.BlockSpec(block, lambda p, r, me_ref: (lo + p, me_ref[0] * steps + r, 0))
-    packed = pl.BlockSpec(block, lambda p, r, me_ref: (p, r, 0))
-    kept = pl.BlockSpec(block, lambda p, r, me_ref: (lo + p, r, 0))
     aliases = {groups + 4: 1, groups + 5: 2} if held else {}
     size = (hi - lo) * owned * width
     return pl.pallas_call(
         functools.partial(update_kernel, groups),
         grid_spec=pltpu.PrefetchScalarGridSpec(
             num_scalar_prefetch=1,
-            grid=(hi - lo, steps),
+            grid=grid,
             in_specs=[scalar, spread, spread]
-            + [packed] * (groups - 1)
+            + [came] * (groups - 1)
             + [kept]
             + [pl.BlockSpec(memory_space=pl.ANY)] * len(held),
             out_specs=[packed, spread, kept],
@@ -131,13 +201,12 @@
             sizes = (chunk[1] - chunk[0], owned, width)
             return lax.dynamic_slice(array, (chunk[0], target * owned, 0), sizes)
 
-        other_counts = [shifted(counts, s) for s in shifts]
         targets = [(me + s) % groups for s in shifts]
-        first = [rows_for(inner, chunks[0], t) for t in targets]
-        first, rest, other_counts = lax.optimization_barrier((first, inner, other_counts))
-        shares = share([counts] + other_counts)
+        first = [pack(t.reshape(1).astype(jnp.int32), counts, inner, owned) for t in targets]
+        first, rest = lax.optimization_barrier((first, inner))
         sent = [first] + [[rows_for(rest, c, t) for t in targets] for c in chunks[1:]]
         arrived = [[shifted(v, s) for v, s in zip(values, shifts)] for values in sent]
+        shares = share(counts, arrived[0])
 
         where = me.reshape(1).astype(jnp.int32)
         held = []

time: 143 us -> 142 us (level)
  Pallas kernels: 22.6 us -> 27.2 us
  waiting for transfers between devices: 90.5 us -> 86.9 us
  starting transfers between devices: 23.2 us -> 21.5 us
    ppermute x13 -> x12, waiting for transfers between devices: 90.5 us -> 86.9 us  [shifted(): return lax.ppermute(value, 'replica', pairs)]
    pallas_call x6, Pallas kernels: 16.7 us -> 20 us  [update(): pl.pallas_call(functools.partial(update_kernel, groups), grid_spec=pltpu....]
    ppermute x13 -> x12, starting transfers between devices: 23.2 us -> 21.5 us  [shifted(): return lax.ppermute(value, 'replica', pairs)]
    dynamic_slice x2 -> x1, local copies, waits for them, and re-layouts: 4.29 us -> 3.2 us  [rows_for(): return lax.dynamic_slice(array, (chunk[0], target * owned, 0), sizes)]
  transfers between devices with their start and end apart: 13 -> 12, of which waited for: 13 -> 12; matrix products, arithmetic and copies ran while one was open for 3% -> 2% of each run, Pallas kernels for 15% -> 18%
where the time goes in v5:
time: 142 us
  waiting for transfers between devices  86.9 us (61%)
  Pallas kernels  27.2 us (19%)
  starting transfers between devices  21.5 us (15%)
  local copies, waits for them, and re-layouts  4.9 us (3%)
    ppermute x12, waiting for transfers between devices, shifted(): return lax.ppermute(value, 'replica', pairs)  86.9 us
    ppermute x12, starting transfers between devices, shifted(): return lax.ppermute(value, 'replica', pairs)  21.5 us
    pallas_call x6, Pallas kernels, update(): pl.pallas_call(functools.partial(update_kernel, groups), grid_spec=pltpu....  20 us
    pallas_call x6, Pallas kernels, place(): pl.pallas_call(functools.partial(place_kernel, chunk[0]), in_specs=[pl.Bl...  4.8 us
    dynamic_slice x1, local copies, waits for them, and re-layouts, rows_for(): return lax.dynamic_slice(array, (chunk[0], target * owned, 0), sizes)  3.2 us
  transfers between devices with their start and end apart: 12, of which 12 were waited for; matrix products, arithmetic and copies ran while one was open for 2% of the time, Pallas kernels for 18%

profile of v5, /device:TPU:0, one launch (start us, length us, event | category | flops | bytes accessed | tf_op | source)
XLA Modules:
  0.0 141.9 jit_solution(17110293169480741559)
XLA Ops:
  1.3 1.2 pack.1
  2.5 3.0 %collective-permute-start = (bf16[2064,128]{1,0:T(8,128)(2,1)S(1)}, bf16[2064,128]{1,0:T(8,128)(2,1)S(1)}, u32[]{:S(2)}, u32[]{:S(2)}) collective-permute-start(bf16[2064,128]{1,0:T(8,128)(2,1)S(1)} %pack.1), channel_id=1, source_target_pairs={{0,16},{16,0},{1,17},{17,1},{2,18},{18,2},{3,19},{19,3},{4,20},{20... | collective-permute-start | bytes 1585160 | tf_op jit(solution)/shard_map/ppermute | solution.py:187
  5.5 3.2 %constant_dynamic-slice_fusion = (bf16[1,256,1024]{2,1,0:T(8,128)(2,1)}, bf16[1,256,1024]{2,1,0:T(8,128)(2,1)}, bf16[1,256,1024]{2,1,0:T(8,128)(2,1)}, bf16[1,256,1024]{2,1,0:T(8,128)(2,1)}, bf16[1,256,1024]{2,1,0:T(8,128)(2,1)}) fusion(bf16[6,512,1024]{2,1,0:T(8,128)(2,1)} %bitcast.10, s32[]{:T(128)S(6)} %select_n.30), kind=kLoop, calls=%fused_computation | loop fusion | bytes 5242884 | tf_op jit(solution)/shard_map/dynamic_slice | solution.py:202
  8.7 2.0 %collective-permute-start.4 = (bf16[1,256,1024]{2,1,0:T(8,128)(2,1)}, bf16[1,256,1024]{2,1,0:T(8,128)(2,1)S(1)}, u32[]{:S(2)}, u32[]{:S(2)}) collective-permute-start(bf16[1,256,1024]{2,1,0:T(8,128)(2,1)} %get-tuple-element.43), channel_id=1, source_target_pairs={{0,16},{16,0},{1,17},{17,1},{2,18},{18,2},{3,19},{19,3},{4,20},{20... | collective-permute-start | bytes 1572872 | tf_op jit(solution)/shard_map/ppermute | solution.py:187
  10.7 2.0 %collective-permute-start.2 = (bf16[1,256,1024]{2,1,0:T(8,128)(2,1)}, bf16[1,256,1024]{2,1,0:T(8,128)(2,1)S(1)}, u32[]{:S(2)}, u32[]{:S(2)}) collective-permute-start(bf16[1,256,1024]{2,1,0:T(8,128)(2,1)} %get-tuple-element.45), channel_id=1, source_target_pairs={{0,16},{16,0},{1,17},{17,1},{2,18},{18,2},{3,19},{19,3},{4,20},{20... | collective-permute-start | bytes 1572872 | tf_op jit(solution)/shard_map/ppermute | solution.py:187
  12.7 5.6 %collective-permute-done.refs_0_ = bf16[2064,128]{1,0:T(8,128)(2,1)S(1)} collective-permute-done((bf16[2064,128]{1,0:T(8,128)(2,1)S(1)}, bf16[2064,128]{1,0:T(8,128)(2,1)S(1)}, u32[]{:S(2)}, u32[]{:S(2)}) %collective-permute-start) | collective-permute-done | bytes 528416 | tf_op jit(solution)/shard_map/ppermute | solution.py:187
  18.3 2.1 %collective-permute-start.1 = (bf16[1,256,1024]{2,1,0:T(8,128)(2,1)}, bf16[1,256,1024]{2,1,0:T(8,128)(2,1)S(1)}, u32[]{:S(2)}, u32[]{:S(2)}) collective-permute-start(bf16[1,256,1024]{2,1,0:T(8,128)(2,1)} %get-tuple-element.46), channel_id=1, source_target_pairs={{0,16},{16,0},{1,17},{17,1},{2,18},{18,2},{3,19},{19,3},{4,20},{20... | collective-permute-start | bytes 1572872 | tf_op jit(solution)/shard_map/ppermute | solution.py:187
  20.4 1.3 share.1.shares_ref
  21.7 1.0 copy-done.1
  23.4 5.9 %update.6 = (bf16[1,256,1024]{2,1,0:T(8,128)(2,1)S(1)}, bf16[6,512,1024]{2,1,0:T(8,128)(2,1)}, f32[6,256,1024]{2,1,0:T(8,128)}) custom-call(s32[1]{0:T(128)} %bitcast.1.me_ref, f32[2]{0:T(128)S(1)} %copy-done.2, bf16[6,512,1024]{2,1,0:T(8,128)(2,1)} %bitcast.17, bf16[6,512,1024]{2,1,0:T(8,128)(2,1)} %bitcast.11, bf16[2064,128]{1,0:T(8,128)(2,1)S(1)} %copy-done.1, ...), custom_call_target="tpu_custom_call" | custom-call | flops 3145728 | bytes 4718592 | tf_op jit(solution)/shard_map/update/pallas_call | solution.py:132
  29.5 2.1 %collective-permute-start.11 = (bf16[1,256,1024]{2,1,0:T(8,128)(2,1)S(1)}, bf16[1,256,1024]{2,1,0:T(8,128)(2,1)S(1)}, u32[]{:S(2)}, u32[]{:S(2)}) collective-permute-start(bf16[1,256,1024]{2,1,0:T(8,128)(2,1)S(1)} %get-tuple-element.39), channel_id=1, source_target_pairs={{0,16},{16,0},{1,17},{17,1},{2,18},{18,2},{3,19},{19,3},{4,20},{20... | collective-permute-start | bytes 1572872 | tf_op jit(solution)/shard_map/ppermute | solution.py:187
  31.6 2.8 %update.7 = (bf16[1,256,1024]{2,1,0:T(8,128)(2,1)}, bf16[6,512,1024]{2,1,0:T(8,128)(2,1)}, f32[6,256,1024]{2,1,0:T(8,128)}) custom-call(s32[1]{0:T(128)} %bitcast.1.me_ref, f32[2]{0:T(128)S(1)} %copy-done.2, bf16[6,512,1024]{2,1,0:T(8,128)(2,1)} %bitcast.18, bf16[6,512,1024]{2,1,0:T(8,128)(2,1)} %bitcast.12, ...), custom_call_target="tpu_custom_call", output_to_operand_aliasing={{1}: (6, {}), {2}: (7, {})} | custom-call | flops 3145728 | bytes 4718592 | tf_op jit(solution)/shard_map/update/pallas_call | solution.py:132
  34.4 6.4 %collective-permute-done.4.refs_0_ = bf16[1,256,1024]{2,1,0:T(8,128)(2,1)S(1)} collective-permute-done((bf16[1,256,1024]{2,1,0:T(8,128)(2,1)}, bf16[1,256,1024]{2,1,0:T(8,128)(2,1)S(1)}, u32[]{:S(2)}, u32[]{:S(2)}) %collective-permute-start.4) | collective-permute-done | bytes 524320 | tf_op jit(solution)/shard_map/ppermute | solution.py:187
  40.8 2.1 %collective-permute-start.10 = (bf16[1,256,1024]{2,1,0:T(8,128)(2,1)}, bf16[1,256,1024]{2,1,0:T(8,128)(2,1)S(1)}, u32[]{:S(2)}, u32[]{:S(2)}) collective-permute-start(bf16[1,256,1024]{2,1,0:T(8,128)(2,1)} %get-tuple-element.38), channel_id=1, source_target_pairs={{0,16},{16,0},{1,17},{17,1},{2,18},{18,2},{3,19},{19,3},{4,20},{20... | collective-permute-start | bytes 1572872 | tf_op jit(solution)/shard_map/ppermute | solution.py:187
  42.8 2.8 %update.8 = (bf16[1,256,1024]{2,1,0:T(8,128)(2,1)}, bf16[6,512,1024]{2,1,0:T(8,128)(2,1)}, f32[6,256,1024]{2,1,0:T(8,128)}) custom-call(s32[1]{0:T(128)} %bitcast.1.me_ref, f32[2]{0:T(128)S(1)} %copy-done.2, bf16[6,512,1024]{2,1,0:T(8,128)(2,1)} %bitcast.19, bf16[6,512,1024]{2,1,0:T(8,128)(2,1)} %bitcast.13, ...), custom_call_target="tpu_custom_call", output_to_operand_aliasing={{1}: (6, {}), {2}: (7, {})} | custom-call | flops 3145728 | bytes 4718592 | tf_op jit(solution)/shard_map/update/pallas_call | solution.py:132
  45.6 6.4 %collective-permute-done.3.refs_0_ = bf16[1,256,1024]{2,1,0:T(8,128)(2,1)S(1)} collective-permute-done((bf16[1,256,1024]{2,1,0:T(8,128)(2,1)}, bf16[1,256,1024]{2,1,0:T(8,128)(2,1)S(1)}, u32[]{:S(2)}, u32[]{:S(2)}) %collective-permute-start.3) | collective-permute-done | bytes 524320 | tf_op jit(solution)/shard_map/ppermute | solution.py:187
  52.0 2.1 %collective-permute-start.9 = (bf16[1,256,1024]{2,1,0:T(8,128)(2,1)}, bf16[1,256,1024]{2,1,0:T(8,128)(2,1)S(1)}, u32[]{:S(2)}, u32[]{:S(2)}) collective-permute-start(bf16[1,256,1024]{2,1,0:T(8,128)(2,1)} %get-tuple-element.37), channel_id=1, source_target_pairs={{0,16},{16,0},{1,17},{17,1},{2,18},{18,2},{3,19},{19,3},{4,20},{20... | collective-permute-start | bytes 1572872 | tf_op jit(solution)/shard_map/ppermute | solution.py:187
  54.1 2.8 %update.9 = (bf16[1,256,1024]{2,1,0:T(8,128)(2,1)}, bf16[6,512,1024]{2,1,0:T(8,128)(2,1)}, f32[6,256,1024]{2,1,0:T(8,128)}) custom-call(s32[1]{0:T(128)} %bitcast.1.me_ref, f32[2]{0:T(128)S(1)} %copy-done.2, bf16[6,512,1024]{2,1,0:T(8,128)(2,1)} %bitcast.20, bf16[6,512,1024]{2,1,0:T(8,128)(2,1)} %bitcast.14, ...), custom_call_target="tpu_custom_call", output_to_operand_aliasing={{1}: (6, {}), {2}: (7, {})} | custom-call | flops 3145728 | bytes 4718592 | tf_op jit(solution)/shard_map/update/pallas_call | solution.py:132
  56.9 6.4 %collective-permute-done.2.refs_0_ = bf16[1,256,1024]{2,1,0:T(8,128)(2,1)S(1)} collective-permute-done((bf16[1,256,1024]{2,1,0:T(8,128)(2,1)}, bf16[1,256,1024]{2,1,0:T(8,128)(2,1)S(1)}, u32[]{:S(2)}, u32[]{:S(2)}) %collective-permute-start.2) | collective-permute-done | bytes 524320 | tf_op jit(solution)/shard_map/ppermute | solution.py:187
  63.2 2.1 %collective-permute-start.8 = (bf16[1,256,1024]{2,1,0:T(8,128)(2,1)}, bf16[1,256,1024]{2,1,0:T(8,128)(2,1)S(1)}, u32[]{:S(2)}, u32[]{:S(2)}) collective-permute-start(bf16[1,256,1024]{2,1,0:T(8,128)(2,1)} %get-tuple-element.36), channel_id=1, source_target_pairs={{0,16},{16,0},{1,17},{17,1},{2,18},{18,2},{3,19},{19,3},{4,20},{20... | collective-permute-start | bytes 1572872 | tf_op jit(solution)/shard_map/ppermute | solution.py:187
  65.3 2.8 %update.10 = (bf16[1,256,1024]{2,1,0:T(8,128)(2,1)}, bf16[6,512,1024]{2,1,0:T(8,128)(2,1)}, f32[6,256,1024]{2,1,0:T(8,128)}) custom-call(s32[1]{0:T(128)} %bitcast.1.me_ref, f32[2]{0:T(128)S(1)} %copy-done.2, bf16[6,512,1024]{2,1,0:T(8,128)(2,1)} %bitcast.21, bf16[6,512,1024]{2,1,0:T(8,128)(2,1)} %bitcast.15, ...), custom_call_target="tpu_custom_call", output_to_operand_aliasing={{1}: (6, {}), {2}: (7, {})} | custom-call | flops 3145728 | bytes 4718592 | tf_op jit(solution)/shard_map/update/pallas_call | solution.py:132
  68.1 6.4 %collective-permute-done.1.refs_0_ = bf16[1,256,1024]{2,1,0:T(8,128)(2,1)S(1)} collective-permute-done((bf16[1,256,1024]{2,1,0:T(8,128)(2,1)}, bf16[1,256,1024]{2,1,0:T(8,128)(2,1)S(1)}, u32[]{:S(2)}, u32[]{:S(2)}) %collective-permute-start.1) | collective-permute-done | bytes 524320 | tf_op jit(solution)/shard_map/ppermute | solution.py:187
  74.5 2.1 %collective-permute-start.7 = (bf16[1,256,1024]{2,1,0:T(8,128)(2,1)}, bf16[1,256,1024]{2,1,0:T(8,128)(2,1)S(1)}, u32[]{:S(2)}, u32[]{:S(2)}) collective-permute-start(bf16[1,256,1024]{2,1,0:T(8,128)(2,1)} %get-tuple-element.35), channel_id=1, source_target_pairs={{0,16},{16,0},{1,17},{17,1},{2,18},{18,2},{3,19},{19,3},{4,20},{20... | collective-permute-start | bytes 1572872 | tf_op jit(solution)/shard_map/ppermute | solution.py:187
  76.5 2.8 %update.11 = (bf16[1,256,1024]{2,1,0:T(8,128)(2,1)}, bf16[6,512,1024]{2,1,0:T(8,128)(2,1)}, f32[6,256,1024]{2,1,0:T(8,128)}) custom-call(s32[1]{0:T(128)} %bitcast.1.me_ref, f32[2]{0:T(128)S(1)} %copy-done.2, bf16[6,512,1024]{2,1,0:T(8,128)(2,1)} %bitcast.22, bf16[6,512,1024]{2,1,0:T(8,128)(2,1)} %bitcast.16, ...), custom_call_target="tpu_custom_call", output_to_operand_aliasing={{1}: (6, {}), {2}: (7, {})} | custom-call | flops 3145728 | bytes 4718592 | tf_op jit(solution)/shard_map/update/pallas_call | solution.py:132
  79.3 6.4 %collective-permute-done.11.block_ref = bf16[1,256,1024]{2,1,0:T(8,128)(2,1)S(1)} collective-permute-done((bf16[1,256,1024]{2,1,0:T(8,128)(2,1)S(1)}, bf16[1,256,1024]{2,1,0:T(8,128)(2,1)S(1)}, u32[]{:S(2)}, u32[]{:S(2)}) %collective-permute-start.11) | collective-permute-done | bytes 524320 | tf_op jit(solution)/shard_map/ppermute | solution.py:187
  85.7 2.1 %collective-permute-start.6 = (bf16[1,256,1024]{2,1,0:T(8,128)(2,1)}, bf16[1,256,1024]{2,1,0:T(8,128)(2,1)S(1)}, u32[]{:S(2)}, u32[]{:S(2)}) collective-permute-start(bf16[1,256,1024]{2,1,0:T(8,128)(2,1)} %get-tuple-element.34), channel_id=1, source_target_pairs={{0,16},{16,0},{1,17},{17,1},{2,18},{18,2},{3,19},{19,3},{4,20},{20... | collective-permute-start | bytes 1572872 | tf_op jit(solution)/shard_map/ppermute | solution.py:187
  88.6 8.4 %collective-permute-done.10.block_ref = bf16[1,256,1024]{2,1,0:T(8,128)(2,1)S(1)} collective-permute-done((bf16[1,256,1024]{2,1,0:T(8,128)(2,1)}, bf16[1,256,1024]{2,1,0:T(8,128)(2,1)S(1)}, u32[]{:S(2)}, u32[]{:S(2)}) %collective-permute-start.10) | collective-permute-done | bytes 524320 | tf_op jit(solution)/shard_map/ppermute | solution.py:187
  96.9 0.8 place.7._
  97.8 10.4 %collective-permute-done.9.block_ref = bf16[1,256,1024]{2,1,0:T(8,128)(2,1)S(1)} collective-permute-done((bf16[1,256,1024]{2,1,0:T(8,128)(2,1)}, bf16[1,256,1024]{2,1,0:T(8,128)(2,1)S(1)}, u32[]{:S(2)}, u32[]{:S(2)}) %collective-permute-start.9) | collective-permute-done | bytes 524320 | tf_op jit(solution)/shard_map/ppermute | solution.py:187
  109.0 10.4 %collective-permute-done.8.block_ref = bf16[1,256,1024]{2,1,0:T(8,128)(2,1)S(1)} collective-permute-done((bf16[1,256,1024]{2,1,0:T(8,128)(2,1)}, bf16[1,256,1024]{2,1,0:T(8,128)(2,1)S(1)}, u32[]{:S(2)}, u32[]{:S(2)}) %collective-permute-start.8) | collective-permute-done | bytes 524320 | tf_op jit(solution)/shard_map/ppermute | solution.py:187
  120.2 10.4 %collective-permute-done.7.block_ref = bf16[1,256,1024]{2,1,0:T(8,128)(2,1)S(1)} collective-permute-done((bf16[1,256,1024]{2,1,0:T(8,128)(2,1)}, bf16[1,256,1024]{2,1,0:T(8,128)(2,1)S(1)}, u32[]{:S(2)}, u32[]{:S(2)}) %collective-permute-start.7) | collective-permute-done | bytes 524320 | tf_op jit(solution)/shard_map/ppermute | solution.py:187
  131.5 9.6 %collective-permute-done.6.block_ref = bf16[1,256,1024]{2,1,0:T(8,128)(2,1)S(1)} collective-permute-done((bf16[1,256,1024]{2,1,0:T(8,128)(2,1)}, bf16[1,256,1024]{2,1,0:T(8,128)(2,1)S(1)}, u32[]{:S(2)}, u32[]{:S(2)}) %collective-permute-start.6) | collective-permute-done | bytes 524320 | tf_op jit(solution)/shard_map/ppermute | solution.py:187
  (13 shorter events, 5.0 us)
Async XLA Ops:
  2.5 15.8 %collective-permute-start = (bf16[2064,128]{1,0:T(8,128)(2,1)S(1)}, bf16[2064,128]{1,0:T(8,128)(2,1)S(1)}, u32[]{:S(2)}, u32[]{:S(2)}) collective-permute-start(bf16[2064,128]{1,0:T(8,128)(2,1)S(1)} %pack.1), channel_id=1, source_target_pairs={{0,16},{16,0},{1,17},{17,1},{2,18},{18,2},{3,19},{19,3},{4,20},{20... | collective-permute-start | bytes 1585160 | tf_op jit(solution)/shard_map/ppermute | solution.py:187
  8.7 20.9 %collective-permute-start.5 = (bf16[1,256,1024]{2,1,0:T(8,128)(2,1)}, bf16[1,256,1024]{2,1,0:T(8,128)(2,1)S(1)}, u32[]{:S(2)}, u32[]{:S(2)}) collective-permute-start(bf16[1,256,1024]{2,1,0:T(8,128)(2,1)} %get-tuple-element.42), channel_id=1, source_target_pairs={{0,16},{16,0},{1,17},{17,1},{2,18},{18,2},{3,19},{19,3},{4,20},{20... | collective-permute-start | bytes 1572872 | tf_op jit(solution)/shard_map/ppermute | solution.py:187
  8.7 32.1 %collective-permute-start.4 = (bf16[1,256,1024]{2,1,0:T(8,128)(2,1)}, bf16[1,256,1024]{2,1,0:T(8,128)(2,1)S(1)}, u32[]{:S(2)}, u32[]{:S(2)}) collective-permute-start(bf16[1,256,1024]{2,1,0:T(8,128)(2,1)} %get-tuple-element.43), channel_id=1, source_target_pairs={{0,16},{16,0},{1,17},{17,1},{2,18},{18,2},{3,19},{19,3},{4,20},{20... | collective-permute-start | bytes 1572872 | tf_op jit(solution)/shard_map/ppermute | solution.py:187
  10.7 41.3 %collective-permute-start.3 = (bf16[1,256,1024]{2,1,0:T(8,128)(2,1)}, bf16[1,256,1024]{2,1,0:T(8,128)(2,1)S(1)}, u32[]{:S(2)}, u32[]{:S(2)}) collective-permute-start(bf16[1,256,1024]{2,1,0:T(8,128)(2,1)} %get-tuple-element.44), channel_id=1, source_target_pairs={{0,16},{16,0},{1,17},{17,1},{2,18},{18,2},{3,19},{19,3},{4,20},{20... | collective-permute-start | bytes 1572872 | tf_op jit(solution)/shard_map/ppermute | solution.py:187
  10.7 52.5 %collective-permute-start.2 = (bf16[1,256,1024]{2,1,0:T(8,128)(2,1)}, bf16[1,256,1024]{2,1,0:T(8,128)(2,1)S(1)}, u32[]{:S(2)}, u32[]{:S(2)}) collective-permute-start(bf16[1,256,1024]{2,1,0:T(8,128)(2,1)} %get-tuple-element.45), channel_id=1, source_target_pairs={{0,16},{16,0},{1,17},{17,1},{2,18},{18,2},{3,19},{19,3},{4,20},{20... | collective-permute-start | bytes 1572872 | tf_op jit(solution)/shard_map/ppermute | solution.py:187
  18.3 2.1 %copy-start = (bf16[2064,128]{1,0:T(8,128)(2,1)}, bf16[2064,128]{1,0:T(8,128)(2,1)S(1)}, u32[]{:S(2)}) copy-start(bf16[2064,128]{1,0:T(8,128)(2,1)S(1)} %collective-permute-done.refs_0_) | copy-start | bytes 1585156
  18.3 56.2 %collective-permute-start.1 = (bf16[1,256,1024]{2,1,0:T(8,128)(2,1)}, bf16[1,256,1024]{2,1,0:T(8,128)(2,1)S(1)}, u32[]{:S(2)}, u32[]{:S(2)}) collective-permute-start(bf16[1,256,1024]{2,1,0:T(8,128)(2,1)} %get-tuple-element.46), channel_id=1, source_target_pairs={{0,16},{16,0},{1,17},{17,1},{2,18},{18,2},{3,19},{19,3},{4,20},{20... | collective-permute-start | bytes 1572872 | tf_op jit(solution)/shard_map/ppermute | solution.py:187
  21.6 1.0 copy-start.1
  22.7 0.7 copy-start.2
  29.5 56.2 %collective-permute-start.11 = (bf16[1,256,1024]{2,1,0:T(8,128)(2,1)S(1)}, bf16[1,256,1024]{2,1,0:T(8,128)(2,1)S(1)}, u32[]{:S(2)}, u32[]{:S(2)}) collective-permute-start(bf16[1,256,1024]{2,1,0:T(8,128)(2,1)S(1)} %get-tuple-element.39), channel_id=1, source_target_pairs={{0,16},{16,0},{1,17},{17,1},{2,18},{18,2},{3,19},{19,3},{4,20},{20... | collective-permute-start | bytes 1572872 | tf_op jit(solution)/shard_map/ppermute | solution.py:187
  40.8 56.2 %collective-permute-start.10 = (bf16[1,256,1024]{2,1,0:T(8,128)(2,1)}, bf16[1,256,1024]{2,1,0:T(8,128)(2,1)S(1)}, u32[]{:S(2)}, u32[]{:S(2)}) collective-permute-start(bf16[1,256,1024]{2,1,0:T(8,128)(2,1)} %get-tuple-element.38), channel_id=1, source_target_pairs={{0,16},{16,0},{1,17},{17,1},{2,18},{18,2},{3,19},{19,3},{4,20},{20... | collective-permute-start | bytes 1572872 | tf_op jit(solution)/shard_map/ppermute | solution.py:187
  52.0 56.2 %collective-permute-start.9 = (bf16[1,256,1024]{2,1,0:T(8,128)(2,1)}, bf16[1,256,1024]{2,1,0:T(8,128)(2,1)S(1)}, u32[]{:S(2)}, u32[]{:S(2)}) collective-permute-start(bf16[1,256,1024]{2,1,0:T(8,128)(2,1)} %get-tuple-element.37), channel_id=1, source_target_pairs={{0,16},{16,0},{1,17},{17,1},{2,18},{18,2},{3,19},{19,3},{4,20},{20... | collective-permute-start | bytes 1572872 | tf_op jit(solution)/shard_map/ppermute | solution.py:187
  63.2 56.2 %collective-permute-start.8 = (bf16[1,256,1024]{2,1,0:T(8,128)(2,1)}, bf16[1,256,1024]{2,1,0:T(8,128)(2,1)S(1)}, u32[]{:S(2)}, u32[]{:S(2)}) collective-permute-start(bf16[1,256,1024]{2,1,0:T(8,128)(2,1)} %get-tuple-element.36), channel_id=1, source_target_pairs={{0,16},{16,0},{1,17},{17,1},{2,18},{18,2},{3,19},{19,3},{4,20},{20... | collective-permute-start | bytes 1572872 | tf_op jit(solution)/shard_map/ppermute | solution.py:187
  74.5 56.2 %collective-permute-start.7 = (bf16[1,256,1024]{2,1,0:T(8,128)(2,1)}, bf16[1,256,1024]{2,1,0:T(8,128)(2,1)S(1)}, u32[]{:S(2)}, u32[]{:S(2)}) collective-permute-start(bf16[1,256,1024]{2,1,0:T(8,128)(2,1)} %get-tuple-element.35), channel_id=1, source_target_pairs={{0,16},{16,0},{1,17},{17,1},{2,18},{18,2},{3,19},{19,3},{4,20},{20... | collective-permute-start | bytes 1572872 | tf_op jit(solution)/shard_map/ppermute | solution.py:187
  85.7 55.3 %collective-permute-start.6 = (bf16[1,256,1024]{2,1,0:T(8,128)(2,1)}, bf16[1,256,1024]{2,1,0:T(8,128)(2,1)S(1)}, u32[]{:S(2)}, u32[]{:S(2)}) collective-permute-start(bf16[1,256,1024]{2,1,0:T(8,128)(2,1)} %get-tuple-element.34), channel_id=1, source_target_pairs={{0,16},{16,0},{1,17},{17,1},{2,18},{18,2},{3,19},{19,3},{4,20},{20... | collective-permute-start | bytes 1572872 | tf_op jit(solution)/shard_map/ppermute | solution.py:187

commit v6 on v5

--- a/solution.py
+++ b/solution.py
@@ -1,4 +1,6 @@
 import functools
+import math
+from typing import NamedTuple
 
 import jax
 import jax.numpy as jnp
@@ -14,13 +16,20 @@
 vmem_bytes = 48 * 1024 * 1024
 
 
-def pack_kernel(target_ref, count_ref, inner_ref, out_ref, tile_ref, sems):
-    owned = (out_ref.shape[0] - spare) // (inner_ref.shape[2] // lanes)
-    start = pl.multiple_of(target_ref[0] * owned, owned)
+class Chunk(NamedTuple):
+    lo: int
+    parts: int
+    row: int
+    rows: int
+
+
+def pack_kernel(owned, part, row, target_ref, count_ref, inner_ref, out_ref, tile_ref, sems):
+    rows = (out_ref.shape[0] - spare) // (inner_ref.shape[2] // lanes)
+    start = pl.multiple_of(target_ref[0] * owned + row, spare)
     copies = [
         pltpu.make_async_copy(
-            inner_ref.at[0, pl.ds(start, owned), pl.ds(j * lanes, lanes)],
-            out_ref.at[pl.ds(j * owned, owned), :],
+            inner_ref.at[part, pl.ds(start, rows), pl.ds(j * lanes, lanes)],
+            out_ref.at[pl.ds(j * rows, rows), :],
             sems.at[j],
         )
         for j in range(inner_ref.shape[2] // lanes)
@@ -44,22 +53,23 @@
         copy.wait()
 
 
-def pack(target, counts, inner, owned):
+def pack(chunk, target, counts, inner, owned):
+    part, row, rows = chunk.lo, chunk.row, chunk.rows
     blocks = inner.shape[2] // lanes
     scalar = pl.BlockSpec(memory_space=pltpu.SMEM)
     anywhere = pl.BlockSpec(memory_space=pl.ANY)
     return pl.pallas_call(
-        pack_kernel,
+        functools.partial(pack_kernel, owned, part, row),
         in_specs=[scalar, scalar, anywhere],
         out_specs=anywhere,
-        out_shape=jax.ShapeDtypeStruct((blocks * owned + spare, lanes), jnp.bfloat16),
+        out_shape=jax.ShapeDtypeStruct((blocks * rows + spare, lanes), jnp.bfloat16),
         scratch_shapes=[
             pltpu.VMEM((spare, lanes), jnp.bfloat16),
             pltpu.SemaphoreType.DMA((blocks + 1,)),
         ],
         compiler_params=pltpu.CompilerParams(vmem_limit_bytes=vmem_bytes),
         cost_estimate=pl.CostEstimate(
-            flops=0, bytes_accessed=4 * blocks * owned * lanes, transcendentals=0
+            flops=0, bytes_accessed=4 * blocks * rows * lanes, transcendentals=0
         ),
         name="pack",
     )(target, counts, inner)
@@ -108,27 +118,30 @@
 
 
 def update(groups, chunk, me, shares, anchor, inner, arrived, momentum, held):
-    lo, hi = chunk
-    parts, owned, width = momentum.shape
-    if held:
-        rows = min(owned, 128)
-        steps = owned // rows
-        grid = (hi - lo, steps)
-        block = (1, rows, width)
+    _, owned, width = momentum.shape
+    lo, row, rows = chunk.lo, chunk.row, chunk.rows
+    if arrived[0].ndim == 2:
+        grid = (1, width // lanes)
+        block = (1, rows, lanes)
+        ahead, mine = row // rows, owned // rows
+        came = pl.BlockSpec((rows, lanes), lambda p, j, me_ref: (j, 0))
+        packed = pl.BlockSpec(block, lambda p, j, me_ref: (0, 0, j))
+        spread = pl.BlockSpec(block, lambda p, j, me_ref: (lo, me_ref[0] * mine + ahead, j))
+        kept = pl.BlockSpec(block, lambda p, j, me_ref: (lo, ahead, j))
+    else:
+        tall = math.gcd(row, rows, owned, 128)
+        grid = (chunk.parts, rows // tall)
+        block = (1, tall, width)
+        ahead, mine = row // tall, owned // tall
         came = pl.BlockSpec(block, lambda p, r, me_ref: (p, r, 0))
         packed = came
-        spread = pl.BlockSpec(block, lambda p, r, me_ref: (lo + p, me_ref[0] * steps + r, 0))
-        kept = pl.BlockSpec(block, lambda p, r, me_ref: (lo + p, r, 0))
-    else:
-        grid = (1, width // lanes)
-        block = (1, owned, lanes)
-        came = pl.BlockSpec((owned, lanes), lambda p, j, me_ref: (j, 0))
-        packed = pl.BlockSpec(block, lambda p, j, me_ref: (0, 0, j))
-        spread = pl.BlockSpec(block, lambda p, j, me_ref: (lo, me_ref[0], j))
-        kept = pl.BlockSpec(block, lambda p, j, me_ref: (lo, 0, j))
+        spread = pl.BlockSpec(
+            block, lambda p, r, me_ref: (lo + p, me_ref[0] * mine + ahead + r, 0)
+        )
+        kept = pl.BlockSpec(block, lambda p, r, me_ref: (lo + p, ahead + r, 0))
     scalar = pl.BlockSpec(memory_space=pltpu.SMEM)
     aliases = {groups + 4: 1, groups + 5: 2} if held else {}
-    size = (hi - lo) * owned * width
+    size = chunk.parts * rows * width
     return pl.pallas_call(
         functools.partial(update_kernel, groups),
         grid_spec=pltpu.PrefetchScalarGridSpec(
@@ -141,7 +154,7 @@
             out_specs=[packed, spread, kept],
         ),
         out_shape=[
-            jax.ShapeDtypeStruct((hi - lo, owned, width), jnp.bfloat16),
+            jax.ShapeDtypeStruct((chunk.parts, rows, width), jnp.bfloat16),
             jax.ShapeDtypeStruct(anchor.shape, jnp.bfloat16),
             jax.ShapeDtypeStruct(momentum.shape, jnp.float32),
         ],
@@ -154,20 +167,19 @@
     )(me, shares, anchor, inner, *arrived, momentum, *held)
 
 
-def place_kernel(lo, at_ref, block_ref, _, weights_ref, sem):
-    parts, owned, _ = block_ref.shape
-    start = pl.multiple_of(at_ref[0] * owned, owned)
+def place_kernel(owned, chunk, at_ref, block_ref, _, weights_ref, sem):
+    start = pl.multiple_of(at_ref[0] * owned + chunk.row, spare)
     copy = pltpu.make_async_copy(
-        block_ref, weights_ref.at[pl.ds(lo, parts), pl.ds(start, owned), :], sem
+        block_ref, weights_ref.at[pl.ds(chunk.lo, chunk.parts), pl.ds(start, chunk.rows), :], sem
     )
     copy.start()
     copy.wait()
 
 
-def place(chunk, at, block, weights):
+def place(owned, chunk, at, block, weights):
     anywhere = pl.BlockSpec(memory_space=pl.ANY)
     return pl.pallas_call(
-        functools.partial(place_kernel, chunk[0]),
+        functools.partial(place_kernel, owned, chunk),
         in_specs=[pl.BlockSpec(memory_space=pltpu.SMEM), anywhere, anywhere],
         out_specs=anywhere,
         out_shape=jax.ShapeDtypeStruct(weights.shape, weights.dtype),
@@ -194,19 +206,30 @@
         anchor = anchor.reshape(parts, *shape[-2:])
         momentum = momentum.reshape(parts, owned, width)
         me = lax.axis_index("replica")
-        chunks = [(p, p + 1) for p in range(parts)]
+        half = owned // 2
+        last = max(16, owned // 8)
+        chunks = [Chunk(0, 1, 0, half), Chunk(0, 1, half, half)]
+        chunks += [Chunk(p, 1, 0, owned) for p in range(1, parts - 1)]
+        chunks += [
+            Chunk(parts - 1, 1, 0, owned - last),
+            Chunk(parts - 1, 1, owned - last, last),
+        ]
         shifts = range(1, groups)
 
         def rows_for(array, chunk, target):
-            sizes = (chunk[1] - chunk[0], owned, width)
-            return lax.dynamic_slice(array, (chunk[0], target * owned, 0), sizes)
+            sizes = (chunk.parts, chunk.rows, width)
+            return lax.dynamic_slice(array, (chunk.lo, target * owned + chunk.row, 0), sizes)
 
         targets = [(me + s) % groups for s in shifts]
-        first = [pack(t.reshape(1).astype(jnp.int32), counts, inner, owned) for t in targets]
-        first, rest = lax.optimization_barrier((first, inner))
-        sent = [first] + [[rows_for(rest, c, t) for t in targets] for c in chunks[1:]]
+        first = [rows_for(inner, chunks[0], t) for t in targets]
+        first, rest, later_counts = lax.optimization_barrier((first, inner, counts))
+        second = [
+            pack(chunks[1], t.reshape(1).astype(jnp.int32), later_counts, rest, owned)
+            for t in targets
+        ]
+        sent = [first, second] + [[rows_for(rest, c, t) for t in targets] for c in chunks[2:]]
         arrived = [[shifted(v, s) for v, s in zip(values, shifts)] for values in sent]
-        shares = share(counts, arrived[0])
+        shares = share(later_counts, arrived[1])
 
         where = me.reshape(1).astype(jnp.int32)
         held = []
@@ -220,7 +243,7 @@
         for chunk, blocks in zip(chunks, travelled):
             for s, block in zip(shifts, blocks):
                 source = ((me - s) % groups).reshape(1).astype(jnp.int32)
-                weights = place(chunk, source, block, weights)
+                weights = place(owned, chunk, source, block, weights)
         return weights.reshape(shape), moments.reshape(*shape[:2], owned, width)
 
     placed = (

time: 142 us -> 142 us (level)
  waiting for transfers between devices: 86.9 us -> 76.1 us
  Pallas kernels: 27.2 us -> 34.1 us
  local copies, waits for them, and re-layouts: 4.9 us -> 7.12 us
    ppermute x12 -> x16, waiting for transfers between devices: 86.9 us -> 76.1 us  [shifted(): return lax.ppermute(value, 'replica', pairs)]
    pallas_call x6 -> x8, Pallas kernels: 20 us -> 25.9 us  [update(): pl.pallas_call(functools.partial(update_kernel, groups), grid_spec=pltpu....]
    dynamic_slice x1 -> x4, local copies, waits for them, and re-layouts: 3.2 us -> 6.5 us  [rows_for(): lax.dynamic_slice(array, (chunk.lo, target * owned + chunk.row, 0), sizes)]
    pallas_call x7 -> x9, Pallas kernels: 5.96 us -> 7.02 us  [the longest x8 6.05 us: place(): pl.pallas_call(functools.partial(place_kernel, owned, chunk), in_specs=[p...]
    ppermute x12 -> x16, starting transfers between devices: 21.5 us -> 22.2 us  [shifted(): return lax.ppermute(value, 'replica', pairs)]
  transfers between devices with their start and end apart: 12 -> 16, of which waited for: 12 -> 8; matrix products, arithmetic and copies ran while one was open for 2% -> 4% of each run, Pallas kernels for 18% -> 24%
where the time goes in v6:
time: 142 us; the launch traced here: 141 us
  waiting for transfers between devices  76.1 us (54%)
  Pallas kernels  34.1 us (24%)
  starting transfers between devices  22.2 us (16%)
  local copies, waits for them, and re-layouts  7.12 us (5%)
  between operations  1.42 us (1%)
    ppermute x16, waiting for transfers between devices, shifted(): return lax.ppermute(value, 'replica', pairs)  76.1 us
    pallas_call x8, Pallas kernels, update(): pl.pallas_call(functools.partial(update_kernel, groups), grid_spec=pltpu....  25.9 us
    ppermute x16, starting transfers between devices, shifted(): return lax.ppermute(value, 'replica', pairs)  22.2 us
    dynamic_slice x4, local copies, waits for them, and re-layouts, rows_for(): lax.dynamic_slice(array, (chunk.lo, target * owned + chunk.row, 0), sizes)  6.5 us
    pallas_call x8, Pallas kernels, place(): pl.pallas_call(functools.partial(place_kernel, owned, chunk), in_specs=[p...  6.05 us
  transfers between devices with their start and end apart: 16, of which 8 were waited for; matrix products, arithmetic and copies ran while one was open for 4% of the time, Pallas kernels for 24%

profile of v6, /device:TPU:0, one launch (start us, length us, event | category | flops | bytes accessed | tf_op | source)
XLA Modules:
  0.0 141.0 jit_solution(5194068381994989774)
XLA Ops:
  0.6 1.0 constant_dynamic-slice_fusion.6
  1.6 3.0 %collective-permute-start.7 = (bf16[1,128,1024]{2,1,0:T(8,128)(2,1)S(1)}, bf16[1,128,1024]{2,1,0:T(8,128)(2,1)S(1)}, u32[]{:S(2)}, u32[]{:S(2)}) collective-permute-start(bf16[1,128,1024]{2,1,0:T(8,128)(2,1)S(1)} %constant_dynamic-slice_fusion.6), channel_id=1, source_target_pairs={{0,16},{16,0},{1,17},{17,1},{2,18},{18,2},{3,19},{19,3},{4,20},{20... | collective-permute-start | bytes 786440 | tf_op jit(solution)/shard_map/ppermute | solution.py:199
  4.6 2.9 %constant_dynamic-slice_fusion = (bf16[1,256,1024]{2,1,0:T(8,128)(2,1)}, bf16[1,256,1024]{2,1,0:T(8,128)(2,1)}, bf16[1,256,1024]{2,1,0:T(8,128)(2,1)}, bf16[1,256,1024]{2,1,0:T(8,128)(2,1)}) fusion(bf16[6,512,1024]{2,1,0:T(8,128)(2,1)} %bitcast.10, s32[]{:T(128)S(6)} %select_n.38), kind=kLoop, calls=%fused_computation | loop fusion | bytes 4194308 | tf_op jit(solution)/shard_map/dynamic_slice | solution.py:221
  8.2 1.0 pack.1
  9.1 2.1 %collective-permute-start = (bf16[1040,128]{1,0:T(8,128)(2,1)S(1)}, bf16[1040,128]{1,0:T(8,128)(2,1)S(1)}, u32[]{:S(2)}, u32[]{:S(2)}) collective-permute-start(bf16[1040,128]{1,0:T(8,128)(2,1)S(1)} %pack.1), channel_id=1, source_target_pairs={{0,16},{16,0},{1,17},{17,1},{2,18},{18,2},{3,19},{19,3},{4,20},{20... | collective-permute-start | bytes 798728 | tf_op jit(solution)/shard_map/ppermute | solution.py:199
  11.3 1.9 %collective-permute-start.4 = (bf16[1,256,1024]{2,1,0:T(8,128)(2,1)}, bf16[1,256,1024]{2,1,0:T(8,128)(2,1)S(1)}, u32[]{:S(2)}, u32[]{:S(2)}) collective-permute-start(bf16[1,256,1024]{2,1,0:T(8,128)(2,1)} %get-tuple-element.58), channel_id=1, source_target_pairs={{0,16},{16,0},{1,17},{17,1},{2,18},{18,2},{3,19},{19,3},{4,20},{20... | collective-permute-start | bytes 1572872 | tf_op jit(solution)/shard_map/ppermute | solution.py:199
  13.8 1.8 %constant_dynamic-slice_fusion.4 = bf16[1,224,1024]{2,1,0:T(8,128)(2,1)} fusion(bf16[6,512,1024]{2,1,0:T(8,128)(2,1)} %bitcast.12, s32[]{:T(128)S(6)} %select_n.38), kind=kLoop, calls=%fused_computation.4 | loop fusion | bytes 917508 | tf_op jit(solution)/shard_map/dynamic_slice | solution.py:221
  15.6 13.1 %collective-permute-done.refs_0_ = bf16[1040,128]{1,0:T(8,128)(2,1)S(1)} collective-permute-done((bf16[1040,128]{1,0:T(8,128)(2,1)S(1)}, bf16[1040,128]{1,0:T(8,128)(2,1)S(1)}, u32[]{:S(2)}, u32[]{:S(2)}) %collective-permute-start) | collective-permute-done | bytes 266272 | tf_op jit(solution)/shard_map/ppermute | solution.py:199
  28.7 2.1 %collective-permute-start.2 = (bf16[1,224,1024]{2,1,0:T(8,128)(2,1)}, bf16[1,224,1024]{2,1,0:T(8,128)(2,1)S(1)}, u32[]{:S(2)}, u32[]{:S(2)}) collective-permute-start(bf16[1,224,1024]{2,1,0:T(8,128)(2,1)} %constant_dynamic-slice_fusion.4), channel_id=1, source_target_pairs={{0,16},{16,0},{1,17},{17,1},{2,18},{18,2},{3,19},{19,3},{4,20},{20... | collective-permute-start | bytes 1376264 | tf_op jit(solution)/shard_map/ppermute | solution.py:199
  30.8 1.3 share.1.shares_ref
  32.6 2.5 %update.8 = (bf16[1,128,1024]{2,1,0:T(8,128)(2,1)}, bf16[6,512,1024]{2,1,0:T(8,128)(2,1)}, f32[6,256,1024]{2,1,0:T(8,128)}) custom-call(s32[1]{0:T(128)} %bitcast.1.me_ref, f32[2]{0:T(128)S(1)} %copy-done.2, bf16[6,512,1024]{2,1,0:T(8,128)(2,1)} %bitcast.22, bf16[6,512,1024]{2,1,0:T(8,128)(2,1)} %bitcast.13, ...), custom_call_target="tpu_custom_call" | custom-call | flops 1572864 | bytes 2359296 | tf_op jit(solution)/shard_map/update/pallas_call | solution.py:145
  35.8 5.2 %update.9 = (bf16[1,128,1024]{2,1,0:T(8,128)(2,1)}, bf16[6,512,1024]{2,1,0:T(8,128)(2,1)}, f32[6,256,1024]{2,1,0:T(8,128)}) custom-call(s32[1]{0:T(128)} %bitcast.1.me_ref, f32[2]{0:T(128)S(1)} %copy-done.2, bf16[6,512,1024]{2,1,0:T(8,128)(2,1)} %bitcast.23, bf16[6,512,1024]{2,1,0:T(8,128)(2,1)} %bitcast.14, ...), custom_call_target="tpu_custom_call", output_to_operand_aliasing={{1}: (6, {}), {2}: (7, {})} | custom-call | flops 1572864 | bytes 2359296 | tf_op jit(solution)/shard_map/update/pallas_call | solution.py:145
  41.0 1.4 collective-permute-start.14
  42.4 0.8 constant_dynamic-slice_fusion.5
  43.3 7.9 %collective-permute-done.4.refs_0_ = bf16[1,256,1024]{2,1,0:T(8,128)(2,1)S(1)} collective-permute-done((bf16[1,256,1024]{2,1,0:T(8,128)(2,1)}, bf16[1,256,1024]{2,1,0:T(8,128)(2,1)S(1)}, u32[]{:S(2)}, u32[]{:S(2)}) %collective-permute-start.4) | collective-permute-done | bytes 524320 | tf_op jit(solution)/shard_map/ppermute | solution.py:199
  51.2 2.1 %collective-permute-start.1 = (bf16[1,32,1024]{2,1,0:T(8,128)(2,1)S(1)}, bf16[1,32,1024]{2,1,0:T(8,128)(2,1)S(1)}, u32[]{:S(2)}, u32[]{:S(2)}) collective-permute-start(bf16[1,32,1024]{2,1,0:T(8,128)(2,1)S(1)} %constant_dynamic-slice_fusion.5), channel_id=1, source_target_pairs={{0,16},{16,0},{1,17},{17,1},{2,18},{18,2},{3,19},{19,3},{4,20},{20... | collective-permute-start | bytes 196616 | tf_op jit(solution)/shard_map/ppermute | solution.py:199
  53.2 2.6 %update.10 = (bf16[1,256,1024]{2,1,0:T(8,128)(2,1)S(1)}, bf16[6,512,1024]{2,1,0:T(8,128)(2,1)}, f32[6,256,1024]{2,1,0:T(8,128)}) custom-call(s32[1]{0:T(128)} %bitcast.1.me_ref, f32[2]{0:T(128)S(1)} %copy-done.3, bf16[6,512,1024]{2,1,0:T(8,128)(2,1)} %bitcast.24, bf16[6,512,1024]{2,1,0:T(8,128)(2,1)} %bitcast.16, ...), custom_call_target="tpu_custom_call", output_to_operand_aliasing={{1}: (6, {}), {2}: (7, {})} | custom-call | flops 3145728 | bytes 4718592 | tf_op jit(solution)/shard_map/update/pallas_call | solution.py:145
  55.9 6.5 %collective-permute-done.3.refs_0_ = bf16[1,256,1024]{2,1,0:T(8,128)(2,1)S(1)} collective-permute-done((bf16[1,256,1024]{2,1,0:T(8,128)(2,1)}, bf16[1,256,1024]{2,1,0:T(8,128)(2,1)S(1)}, u32[]{:S(2)}, u32[]{:S(2)}) %collective-permute-start.3) | collective-permute-done | bytes 524320 | tf_op jit(solution)/shard_map/ppermute | solution.py:199
  62.4 2.1 %collective-permute-start.13 = (bf16[1,256,1024]{2,1,0:T(8,128)(2,1)S(1)}, bf16[1,256,1024]{2,1,0:T(8,128)(2,1)S(1)}, u32[]{:S(2)}, u32[]{:S(2)}) collective-permute-start(bf16[1,256,1024]{2,1,0:T(8,128)(2,1)S(1)} %get-tuple-element.51), channel_id=1, source_target_pairs={{0,16},{16,0},{1,17},{17,1},{2,18},{18,2},{3,19},{19,3},{4,20},{20... | collective-permute-start | bytes 1572872 | tf_op jit(solution)/shard_map/ppermute | solution.py:199
  64.5 2.8 %update.11 = (bf16[1,256,1024]{2,1,0:T(8,128)(2,1)}, bf16[6,512,1024]{2,1,0:T(8,128)(2,1)}, f32[6,256,1024]{2,1,0:T(8,128)}) custom-call(s32[1]{0:T(128)} %bitcast.1.me_ref, f32[2]{0:T(128)S(1)} %copy-done.3, bf16[6,512,1024]{2,1,0:T(8,128)(2,1)} %bitcast.25, bf16[6,512,1024]{2,1,0:T(8,128)(2,1)} %bitcast.17, ...), custom_call_target="tpu_custom_call", output_to_operand_aliasing={{1}: (6, {}), {2}: (7, {})} | custom-call | flops 3145728 | bytes 4718592 | tf_op jit(solution)/shard_map/update/pallas_call | solution.py:145
  67.3 2.8 %update.12 = (bf16[1,256,1024]{2,1,0:T(8,128)(2,1)}, bf16[6,512,1024]{2,1,0:T(8,128)(2,1)}, f32[6,256,1024]{2,1,0:T(8,128)}) custom-call(s32[1]{0:T(128)} %bitcast.1.me_ref, f32[2]{0:T(128)S(1)} %copy-done.3, bf16[6,512,1024]{2,1,0:T(8,128)(2,1)} %bitcast.26, bf16[6,512,1024]{2,1,0:T(8,128)(2,1)} %bitcast.18, ...), custom_call_target="tpu_custom_call", output_to_operand_aliasing={{1}: (6, {}), {2}: (7, {})} | custom-call | flops 3145728 | bytes 4718592 | tf_op jit(solution)/shard_map/update/pallas_call | solution.py:145
  70.1 2.8 %update.13 = (bf16[1,256,1024]{2,1,0:T(8,128)(2,1)}, bf16[6,512,1024]{2,1,0:T(8,128)(2,1)}, f32[6,256,1024]{2,1,0:T(8,128)}) custom-call(s32[1]{0:T(128)} %bitcast.1.me_ref, f32[2]{0:T(128)S(1)} %copy-done.3, bf16[6,512,1024]{2,1,0:T(8,128)(2,1)} %bitcast.27, bf16[6,512,1024]{2,1,0:T(8,128)(2,1)} %bitcast.19, ...), custom_call_target="tpu_custom_call", output_to_operand_aliasing={{1}: (6, {}), {2}: (7, {})} | custom-call | flops 3145728 | bytes 4718592 | tf_op jit(solution)/shard_map/update/pallas_call | solution.py:145
  72.9 11.9 %collective-permute-done.1.refs_0_ = bf16[1,32,1024]{2,1,0:T(8,128)(2,1)S(1)} collective-permute-done((bf16[1,32,1024]{2,1,0:T(8,128)(2,1)S(1)}, bf16[1,32,1024]{2,1,0:T(8,128)(2,1)S(1)}, u32[]{:S(2)}, u32[]{:S(2)}) %collective-permute-start.1) | collective-permute-done | bytes 65568 | tf_op jit(solution)/shard_map/ppermute | solution.py:199
  84.9 2.1 %collective-permute-start.12 = (bf16[1,256,1024]{2,1,0:T(8,128)(2,1)}, bf16[1,256,1024]{2,1,0:T(8,128)(2,1)S(1)}, u32[]{:S(2)}, u32[]{:S(2)}) collective-permute-start(bf16[1,256,1024]{2,1,0:T(8,128)(2,1)} %get-tuple-element.50), channel_id=1, source_target_pairs={{0,16},{16,0},{1,17},{17,1},{2,18},{18,2},{3,19},{19,3},{4,20},{20... | collective-permute-start | bytes 1572872 | tf_op jit(solution)/shard_map/ppermute | solution.py:199
  87.0 2.0 %collective-permute-start.10 = (bf16[1,256,1024]{2,1,0:T(8,128)(2,1)}, bf16[1,256,1024]{2,1,0:T(8,128)(2,1)S(1)}, u32[]{:S(2)}, u32[]{:S(2)}) collective-permute-start(bf16[1,256,1024]{2,1,0:T(8,128)(2,1)} %get-tuple-element.48), channel_id=1, source_target_pairs={{0,16},{16,0},{1,17},{17,1},{2,18},{18,2},{3,19},{19,3},{4,20},{20... | collective-permute-start | bytes 1572872 | tf_op jit(solution)/shard_map/ppermute | solution.py:199
  89.0 5.4 %update.14 = (bf16[1,224,1024]{2,1,0:T(8,128)(2,1)}, bf16[6,512,1024]{2,1,0:T(8,128)(2,1)}, f32[6,256,1024]{2,1,0:T(8,128)}) custom-call(s32[1]{0:T(128)} %bitcast.1.me_ref, f32[2]{0:T(128)S(1)} %copy-done.3, bf16[6,512,1024]{2,1,0:T(8,128)(2,1)} %bitcast.28, bf16[6,512,1024]{2,1,0:T(8,128)(2,1)} %bitcast.20, ...), custom_call_target="tpu_custom_call", output_to_operand_aliasing={{1}: (6, {}), {2}: (7, {})} | custom-call | flops 2752512 | bytes 4128768 | tf_op jit(solution)/shard_map/update/pallas_call | solution.py:145
  94.5 1.7 %update.15 = (bf16[1,32,1024]{2,1,0:T(8,128)(2,1)S(1)}, bf16[6,512,1024]{2,1,0:T(8,128)(2,1)}, f32[6,256,1024]{2,1,0:T(8,128)}) custom-call(s32[1]{0:T(128)} %bitcast.1.me_ref, f32[2]{0:T(128)S(1)} %copy-done.3, bf16[6,512,1024]{2,1,0:T(8,128)(2,1)} %bitcast.29, bf16[6,512,1024]{2,1,0:T(8,128)(2,1)} %bitcast.21, ...), custom_call_target="tpu_custom_call", output_to_operand_aliasing={{1}: (6, {}), {2}: (7, {})} | custom-call | flops 393216 | bytes 589824 | tf_op jit(solution)/shard_map/update/pallas_call | solution.py:145
  96.2 2.0 %collective-permute-start.8 = (bf16[1,32,1024]{2,1,0:T(8,128)(2,1)S(1)}, bf16[1,32,1024]{2,1,0:T(8,128)(2,1)S(1)}, u32[]{:S(2)}, u32[]{:S(2)}) collective-permute-start(bf16[1,32,1024]{2,1,0:T(8,128)(2,1)S(1)} %get-tuple-element.46), channel_id=1, source_target_pairs={{0,16},{16,0},{1,17},{17,1},{2,18},{18,2},{3,19},{19,3},{4,20},{20... | collective-permute-start | bytes 196616 | tf_op jit(solution)/shard_map/ppermute | solution.py:199
  100.4 6.9 %collective-permute-done.12.block_ref = bf16[1,256,1024]{2,1,0:T(8,128)(2,1)S(1)} collective-permute-done((bf16[1,256,1024]{2,1,0:T(8,128)(2,1)}, bf16[1,256,1024]{2,1,0:T(8,128)(2,1)S(1)}, u32[]{:S(2)}, u32[]{:S(2)}) %collective-permute-start.12) | collective-permute-done | bytes 524320 | tf_op jit(solution)/shard_map/ppermute | solution.py:199
  108.2 10.4 %collective-permute-done.11.block_ref = bf16[1,256,1024]{2,1,0:T(8,128)(2,1)S(1)} collective-permute-done((bf16[1,256,1024]{2,1,0:T(8,128)(2,1)}, bf16[1,256,1024]{2,1,0:T(8,128)(2,1)S(1)}, u32[]{:S(2)}, u32[]{:S(2)}) %collective-permute-start.11) | collective-permute-done | bytes 524320 | tf_op jit(solution)/shard_map/ppermute | solution.py:199
  119.4 10.4 %collective-permute-done.10.block_ref = bf16[1,256,1024]{2,1,0:T(8,128)(2,1)S(1)} collective-permute-done((bf16[1,256,1024]{2,1,0:T(8,128)(2,1)}, bf16[1,256,1024]{2,1,0:T(8,128)(2,1)S(1)}, u32[]{:S(2)}, u32[]{:S(2)}) %collective-permute-start.10) | collective-permute-done | bytes 524320 | tf_op jit(solution)/shard_map/ppermute | solution.py:199
  130.6 8.9 %collective-permute-done.9.block_ref = bf16[1,224,1024]{2,1,0:T(8,128)(2,1)S(1)} collective-permute-done((bf16[1,224,1024]{2,1,0:T(8,128)(2,1)}, bf16[1,224,1024]{2,1,0:T(8,128)(2,1)S(1)}, u32[]{:S(2)}, u32[]{:S(2)}) %collective-permute-start.9) | collective-permute-done | bytes 458784 | tf_op jit(solution)/shard_map/ppermute | solution.py:199
  (30 shorter events, 8.2 us)
Async XLA Ops:
  1.6 11.6 %collective-permute-start.7 = (bf16[1,128,1024]{2,1,0:T(8,128)(2,1)S(1)}, bf16[1,128,1024]{2,1,0:T(8,128)(2,1)S(1)}, u32[]{:S(2)}, u32[]{:S(2)}) collective-permute-start(bf16[1,128,1024]{2,1,0:T(8,128)(2,1)S(1)} %constant_dynamic-slice_fusion.6), channel_id=1, source_target_pairs={{0,16},{16,0},{1,17},{17,1},{2,18},{18,2},{3,19},{19,3},{4,20},{20... | collective-permute-start | bytes 786440 | tf_op jit(solution)/shard_map/ppermute | solution.py:199
  7.5 27.6 %collective-permute-start.6 = (bf16[1,256,1024]{2,1,0:T(8,128)(2,1)}, bf16[1,256,1024]{2,1,0:T(8,128)(2,1)S(1)}, u32[]{:S(2)}, u32[]{:S(2)}) collective-permute-start(bf16[1,256,1024]{2,1,0:T(8,128)(2,1)} %get-tuple-element.56), channel_id=1, source_target_pairs={{0,16},{16,0},{1,17},{17,1},{2,18},{18,2},{3,19},{19,3},{4,20},{20... | collective-permute-start | bytes 1572872 | tf_op jit(solution)/shard_map/ppermute | solution.py:199
  9.1 19.6 %collective-permute-start = (bf16[1040,128]{1,0:T(8,128)(2,1)S(1)}, bf16[1040,128]{1,0:T(8,128)(2,1)S(1)}, u32[]{:S(2)}, u32[]{:S(2)}) collective-permute-start(bf16[1040,128]{1,0:T(8,128)(2,1)S(1)} %pack.1), channel_id=1, source_target_pairs={{0,16},{16,0},{1,17},{17,1},{2,18},{18,2},{3,19},{19,3},{4,20},{20... | collective-permute-start | bytes 798728 | tf_op jit(solution)/shard_map/ppermute | solution.py:199
  11.2 29.8 %collective-permute-start.5 = (bf16[1,256,1024]{2,1,0:T(8,128)(2,1)}, bf16[1,256,1024]{2,1,0:T(8,128)(2,1)S(1)}, u32[]{:S(2)}, u32[]{:S(2)}) collective-permute-start(bf16[1,256,1024]{2,1,0:T(8,128)(2,1)} %get-tuple-element.57), channel_id=1, source_target_pairs={{0,16},{16,0},{1,17},{17,1},{2,18},{18,2},{3,19},{19,3},{4,20},{20... | collective-permute-start | bytes 1572872 | tf_op jit(solution)/shard_map/ppermute | solution.py:199
  11.3 39.9 %collective-permute-start.4 = (bf16[1,256,1024]{2,1,0:T(8,128)(2,1)}, bf16[1,256,1024]{2,1,0:T(8,128)(2,1)S(1)}, u32[]{:S(2)}, u32[]{:S(2)}) collective-permute-start(bf16[1,256,1024]{2,1,0:T(8,128)(2,1)} %get-tuple-element.58), channel_id=1, source_target_pairs={{0,16},{16,0},{1,17},{17,1},{2,18},{18,2},{3,19},{19,3},{4,20},{20... | collective-permute-start | bytes 1572872 | tf_op jit(solution)/shard_map/ppermute | solution.py:199
  13.2 49.2 %collective-permute-start.3 = (bf16[1,256,1024]{2,1,0:T(8,128)(2,1)}, bf16[1,256,1024]{2,1,0:T(8,128)(2,1)S(1)}, u32[]{:S(2)}, u32[]{:S(2)}) collective-permute-start(bf16[1,256,1024]{2,1,0:T(8,128)(2,1)} %get-tuple-element.59), channel_id=1, source_target_pairs={{0,16},{16,0},{1,17},{17,1},{2,18},{18,2},{3,19},{19,3},{4,20},{20... | collective-permute-start | bytes 1572872 | tf_op jit(solution)/shard_map/ppermute | solution.py:199
  28.7 2.1 %copy-start = (bf16[1040,128]{1,0:T(8,128)(2,1)}, bf16[1040,128]{1,0:T(8,128)(2,1)S(1)}, u32[]{:S(2)}) copy-start(bf16[1040,128]{1,0:T(8,128)(2,1)S(1)} %collective-permute-done.refs_0_) | copy-start | bytes 798724
  28.7 58.2 %collective-permute-start.2 = (bf16[1,224,1024]{2,1,0:T(8,128)(2,1)}, bf16[1,224,1024]{2,1,0:T(8,128)(2,1)S(1)}, u32[]{:S(2)}, u32[]{:S(2)}) collective-permute-start(bf16[1,224,1024]{2,1,0:T(8,128)(2,1)} %constant_dynamic-slice_fusion.4), channel_id=1, source_target_pairs={{0,16},{16,0},{1,17},{17,1},{2,18},{18,2},{3,19},{19,3},{4,20},{20... | collective-permute-start | bytes 1376264 | tf_op jit(solution)/shard_map/ppermute | solution.py:199
  32.0 0.6 copy-start.2
  32.6 3.2 %copy-start.1 = (bf16[1040,128]{1,0:T(8,128)(2,1)S(1)}, bf16[1040,128]{1,0:T(8,128)(2,1)}, u32[]{:S(2)}) copy-start(bf16[1040,128]{1,0:T(8,128)(2,1)} %copy-done) | copy-start | bytes 798724
  35.1 51.9 %collective-permute-start.15 = (bf16[1,128,1024]{2,1,0:T(8,128)(2,1)}, bf16[1,128,1024]{2,1,0:T(8,128)(2,1)S(1)}, u32[]{:S(2)}, u32[]{:S(2)}) collective-permute-start(bf16[1,128,1024]{2,1,0:T(8,128)(2,1)} %get-tuple-element.53), channel_id=1, source_target_pairs={{0,16},{16,0},{1,17},{17,1},{2,18},{18,2},{3,19},{19,3},{4,20},{20... | collective-permute-start | bytes 786440 | tf_op jit(solution)/shard_map/ppermute | solution.py:199
  35.8 17.4 %copy-start.3 = (f32[2]{0:T(128)S(1)}, f32[2]{0:T(128)}, u32[]{:S(2)}) copy-start(f32[2]{0:T(128)} %share.1.shares_ref) | copy-start | bytes 28
  41.0 53.3 %collective-permute-start.14 = (bf16[1,128,1024]{2,1,0:T(8,128)(2,1)}, bf16[1,128,1024]{2,1,0:T(8,128)(2,1)S(1)}, u32[]{:S(2)}, u32[]{:S(2)}) collective-permute-start(bf16[1,128,1024]{2,1,0:T(8,128)(2,1)} %get-tuple-element.52), channel_id=1, source_target_pairs={{0,16},{16,0},{1,17},{17,1},{2,18},{18,2},{3,19},{19,3},{4,20},{20... | collective-permute-start | bytes 786440 | tf_op jit(solution)/shard_map/ppermute | solution.py:199
  51.2 33.7 %collective-permute-start.1 = (bf16[1,32,1024]{2,1,0:T(8,128)(2,1)S(1)}, bf16[1,32,1024]{2,1,0:T(8,128)(2,1)S(1)}, u32[]{:S(2)}, u32[]{:S(2)}) collective-permute-start(bf16[1,32,1024]{2,1,0:T(8,128)(2,1)S(1)} %constant_dynamic-slice_fusion.5), channel_id=1, source_target_pairs={{0,16},{16,0},{1,17},{17,1},{2,18},{18,2},{3,19},{19,3},{4,20},{20... | collective-permute-start | bytes 196616 | tf_op jit(solution)/shard_map/ppermute | solution.py:199
  62.4 33.8 %collective-permute-start.13 = (bf16[1,256,1024]{2,1,0:T(8,128)(2,1)S(1)}, bf16[1,256,1024]{2,1,0:T(8,128)(2,1)S(1)}, u32[]{:S(2)}, u32[]{:S(2)}) collective-permute-start(bf16[1,256,1024]{2,1,0:T(8,128)(2,1)S(1)} %get-tuple-element.51), channel_id=1, source_target_pairs={{0,16},{16,0},{1,17},{17,1},{2,18},{18,2},{3,19},{19,3},{4,20},{20... | collective-permute-start | bytes 1572872 | tf_op jit(solution)/shard_map/ppermute | solution.py:199
  84.9 22.5 %collective-permute-start.12 = (bf16[1,256,1024]{2,1,0:T(8,128)(2,1)}, bf16[1,256,1024]{2,1,0:T(8,128)(2,1)S(1)}, u32[]{:S(2)}, u32[]{:S(2)}) collective-permute-start(bf16[1,256,1024]{2,1,0:T(8,128)(2,1)} %get-tuple-element.50), channel_id=1, source_target_pairs={{0,16},{16,0},{1,17},{17,1},{2,18},{18,2},{3,19},{19,3},{4,20},{20... | collective-permute-start | bytes 1572872 | tf_op jit(solution)/shard_map/ppermute | solution.py:199
  86.9 31.6 %collective-permute-start.11 = (bf16[1,256,1024]{2,1,0:T(8,128)(2,1)}, bf16[1,256,1024]{2,1,0:T(8,128)(2,1)S(1)}, u32[]{:S(2)}, u32[]{:S(2)}) collective-permute-start(bf16[1,256,1024]{2,1,0:T(8,128)(2,1)} %get-tuple-element.49), channel_id=1, source_target_pairs={{0,16},{16,0},{1,17},{17,1},{2,18},{18,2},{3,19},{19,3},{4,20},{20... | collective-permute-start | bytes 1572872 | tf_op jit(solution)/shard_map/ppermute | solution.py:199
  87.0 42.8 %collective-permute-start.10 = (bf16[1,256,1024]{2,1,0:T(8,128)(2,1)}, bf16[1,256,1024]{2,1,0:T(8,128)(2,1)S(1)}, u32[]{:S(2)}, u32[]{:S(2)}) collective-permute-start(bf16[1,256,1024]{2,1,0:T(8,128)(2,1)} %get-tuple-element.48), channel_id=1, source_target_pairs={{0,16},{16,0},{1,17},{17,1},{2,18},{18,2},{3,19},{19,3},{4,20},{20... | collective-permute-start | bytes 1572872 | tf_op jit(solution)/shard_map/ppermute | solution.py:199
  94.4 45.2 %collective-permute-start.9 = (bf16[1,224,1024]{2,1,0:T(8,128)(2,1)}, bf16[1,224,1024]{2,1,0:T(8,128)(2,1)S(1)}, u32[]{:S(2)}, u32[]{:S(2)}) collective-permute-start(bf16[1,224,1024]{2,1,0:T(8,128)(2,1)} %get-tuple-element.47), channel_id=1, source_target_pairs={{0,16},{16,0},{1,17},{17,1},{2,18},{18,2},{3,19},{19,3},{4,20},{20... | collective-permute-start | bytes 1376264 | tf_op jit(solution)/shard_map/ppermute | solution.py:199
  96.2 44.1 %collective-permute-start.8 = (bf16[1,32,1024]{2,1,0:T(8,128)(2,1)S(1)}, bf16[1,32,1024]{2,1,0:T(8,128)(2,1)S(1)}, u32[]{:S(2)}, u32[]{:S(2)}) collective-permute-start(bf16[1,32,1024]{2,1,0:T(8,128)(2,1)S(1)} %get-tuple-element.46), channel_id=1, source_target_pairs={{0,16},{16,0},{1,17},{17,1},{2,18},{18,2},{3,19},{19,3},{4,20},{20... | collective-permute-start | bytes 196616 | tf_op jit(solution)/shard_map/ppermute | solution.py:199

commit v7 on v6

--- a/solution.py
+++ b/solution.py
@@ -21,6 +21,32 @@
     parts: int
     row: int
     rows: int
+
+
+def cut_kernel(groups, owned, chunk, shift, inner_ref, out_ref, sem):
+    target = lax.rem(lax.axis_index("replica") + shift, groups)
+    start = pl.multiple_of(target * owned + chunk.row, spare)
+    copy = pltpu.make_async_copy(
+        inner_ref.at[pl.ds(chunk.lo, chunk.parts), pl.ds(start, chunk.rows), :], out_ref, sem
+    )
+    copy.start()
+    copy.wait()
+
+
+def cut(groups, owned, chunk, shift, inner):
+    shape = (chunk.parts, chunk.rows, inner.shape[2])
+    return pl.pallas_call(
+        functools.partial(cut_kernel, groups, owned, chunk, shift),
+        in_specs=[pl.BlockSpec(memory_space=pl.ANY)],
+        out_specs=pl.BlockSpec(memory_space=pltpu.VMEM),
+        out_shape=jax.ShapeDtypeStruct(shape, inner.dtype),
+        scratch_shapes=[pltpu.SemaphoreType.DMA],
+        compiler_params=pltpu.CompilerParams(vmem_limit_bytes=vmem_bytes),
+        cost_estimate=pl.CostEstimate(
+            flops=0, bytes_accessed=4 * math.prod(shape), transcendentals=0
+        ),
+        name="cut",
+    )(inner)
 
 
 def pack_kernel(owned, part, row, target_ref, count_ref, inner_ref, out_ref, tile_ref, sems):
@@ -167,8 +193,9 @@
     )(me, shares, anchor, inner, *arrived, momentum, *held)
 
 
-def place_kernel(owned, chunk, at_ref, block_ref, _, weights_ref, sem):
-    start = pl.multiple_of(at_ref[0] * owned + chunk.row, spare)
+def place_kernel(groups, owned, chunk, shift, block_ref, _, weights_ref, sem):
+    source = lax.rem(lax.axis_index("replica") + groups - shift, groups)
+    start = pl.multiple_of(source * owned + chunk.row, spare)
     copy = pltpu.make_async_copy(
         block_ref, weights_ref.at[pl.ds(chunk.lo, chunk.parts), pl.ds(start, chunk.rows), :], sem
     )
@@ -176,19 +203,19 @@
     copy.wait()
 
 
-def place(owned, chunk, at, block, weights):
+def place(groups, owned, chunk, shift, block, weights):
     anywhere = pl.BlockSpec(memory_space=pl.ANY)
     return pl.pallas_call(
-        functools.partial(place_kernel, owned, chunk),
-        in_specs=[pl.BlockSpec(memory_space=pltpu.SMEM), anywhere, anywhere],
+        functools.partial(place_kernel, groups, owned, chunk, shift),
+        in_specs=[anywhere, anywhere],
         out_specs=anywhere,
         out_shape=jax.ShapeDtypeStruct(weights.shape, weights.dtype),
         scratch_shapes=[pltpu.SemaphoreType.DMA],
-        input_output_aliases={2: 0},
+        input_output_aliases={1: 0},
         compiler_params=pltpu.CompilerParams(vmem_limit_bytes=vmem_bytes),
         cost_estimate=pl.CostEstimate(flops=0, bytes_accessed=4 * block.size, transcendentals=0),
         name="place",
-    )(at, block, weights)
+    )(block, weights)
 
 
 def solution(mesh):
@@ -207,7 +234,7 @@
         momentum = momentum.reshape(parts, owned, width)
         me = lax.axis_index("replica")
         half = owned // 2
-        last = max(16, owned // 8)
+        last = max(16, owned // 4)
         chunks = [Chunk(0, 1, 0, half), Chunk(0, 1, half, half)]
         chunks += [Chunk(p, 1, 0, owned) for p in range(1, parts - 1)]
         chunks += [
@@ -221,7 +248,7 @@
             return lax.dynamic_slice(array, (chunk.lo, target * owned + chunk.row, 0), sizes)
 
         targets = [(me + s) % groups for s in shifts]
-        first = [rows_for(inner, chunks[0], t) for t in targets]
+        first = [cut(groups, owned, chunks[0], s, inner) for s in shifts]
         first, rest, later_counts = lax.optimization_barrier((first, inner, counts))
         second = [
             pack(chunks[1], t.reshape(1).astype(jnp.int32), later_counts, rest, owned)
@@ -242,8 +269,7 @@
         weights, moments = held
         for chunk, blocks in zip(chunks, travelled):
             for s, block in zip(shifts, blocks):
-                source = ((me - s) % groups).reshape(1).astype(jnp.int32)
-                weights = place(owned, chunk, source, block, weights)
+                weights = place(groups, owned, chunk, s, block, weights)
         return weights.reshape(shape), moments.reshape(*shape[:2], owned, width)
 
     placed = (

time: 142 us -> 142 us (level)
  waiting for transfers between devices: 76.1 us -> 78.3 us
    pallas_call x8, Pallas kernels: 25.9 us -> 23.5 us  [update(): pl.pallas_call(functools.partial(update_kernel, groups), grid_spec=pltpu....]
    ppermute x16, waiting for transfers between devices: 76.1 us -> 78.3 us  [shifted(): return lax.ppermute(value, 'replica', pairs)]
    pallas_call x8 -> x9, Pallas kernels: 6.05 us -> 7.05 us  [the longest x8 6.07 us: place(): pl.pallas_call(functools.partial(place_kernel, groups, owned, chunk, shif...]
    dynamic_slice x4 -> x3, local copies, waits for them, and re-layouts: 6.5 us -> 5.57 us  [rows_for(): lax.dynamic_slice(array, (chunk.lo, target * owned + chunk.row, 0), sizes)]
  transfers between devices with their start and end apart: 16 -> 16, of which waited for: 8 -> 10; matrix products, arithmetic and copies ran while one was open for 4% -> 4% of each run, Pallas kernels for 24% -> 22%
where the time goes in v7:
time: 142 us; the launch traced here: 141 us
  waiting for transfers between devices  78.3 us (55%)
  Pallas kernels  32.7 us (23%)
  starting transfers between devices  22.2 us (16%)
  local copies, waits for them, and re-layouts  6.18 us (4%)
    ppermute x16, waiting for transfers between devices, shifted(): return lax.ppermute(value, 'replica', pairs)  78.3 us
    pallas_call x8, Pallas kernels, update(): pl.pallas_call(functools.partial(update_kernel, groups), grid_spec=pltpu....  23.5 us
    ppermute x16, starting transfers between devices, shifted(): return lax.ppermute(value, 'replica', pairs)  22.2 us
    pallas_call x8, Pallas kernels, place(): pl.pallas_call(functools.partial(place_kernel, groups, owned, chunk, shif...  6.07 us
    dynamic_slice x3, local copies, waits for them, and re-layouts, rows_for(): lax.dynamic_slice(array, (chunk.lo, target * owned + chunk.row, 0), sizes)  5.57 us
  transfers between devices with their start and end apart: 16, of which 10 were waited for; matrix products, arithmetic and copies ran while one was open for 4% of the time, Pallas kernels for 22%

profile of v7, /device:TPU:0, one launch (start us, length us, event | category | flops | bytes accessed | tf_op | source)
XLA Modules:
  0.0 140.9 jit_solution(10566205609796771914)
XLA Ops:
  0.6 1.0 cut.1
  1.6 3.0 %collective-permute-start.7 = (bf16[1,128,1024]{2,1,0:T(8,128)(2,1)S(1)}, bf16[1,128,1024]{2,1,0:T(8,128)(2,1)S(1)}, u32[]{:S(2)}, u32[]{:S(2)}) collective-permute-start(bf16[1,128,1024]{2,1,0:T(8,128)(2,1)S(1)} %cut.1), channel_id=1, source_target_pairs={{0,16},{16,0},{1,17},{17,1},{2,18},{18,2},{3,19},{19,3},{4,20},{20... | collective-permute-start | bytes 786440 | tf_op jit(solution)/shard_map/ppermute | solution.py:226
  4.6 2.9 %constant_dynamic-slice_fusion = (bf16[1,256,1024]{2,1,0:T(8,128)(2,1)}, bf16[1,256,1024]{2,1,0:T(8,128)(2,1)}, bf16[1,256,1024]{2,1,0:T(8,128)(2,1)}, bf16[1,256,1024]{2,1,0:T(8,128)(2,1)}) fusion(bf16[6,512,1024]{2,1,0:T(8,128)(2,1)} %bitcast.9, s32[]{:T(128)S(6)} %select_n.19), kind=kLoop, calls=%fused_computation | loop fusion | bytes 4194308 | tf_op jit(solution)/shard_map/dynamic_slice | solution.py:248
  9.2 2.1 %collective-permute-start = (bf16[1040,128]{1,0:T(8,128)(2,1)S(1)}, bf16[1040,128]{1,0:T(8,128)(2,1)S(1)}, u32[]{:S(2)}, u32[]{:S(2)}) collective-permute-start(bf16[1040,128]{1,0:T(8,128)(2,1)S(1)} %pack.1), channel_id=1, source_target_pairs={{0,16},{16,0},{1,17},{17,1},{2,18},{18,2},{3,19},{19,3},{4,20},{20... | collective-permute-start | bytes 798728 | tf_op jit(solution)/shard_map/ppermute | solution.py:226
  11.3 1.9 %collective-permute-start.4 = (bf16[1,256,1024]{2,1,0:T(8,128)(2,1)}, bf16[1,256,1024]{2,1,0:T(8,128)(2,1)S(1)}, u32[]{:S(2)}, u32[]{:S(2)}) collective-permute-start(bf16[1,256,1024]{2,1,0:T(8,128)(2,1)} %get-tuple-element.58), channel_id=1, source_target_pairs={{0,16},{16,0},{1,17},{17,1},{2,18},{18,2},{3,19},{19,3},{4,20},{20... | collective-permute-start | bytes 1572872 | tf_op jit(solution)/shard_map/ppermute | solution.py:226
  13.8 1.8 %constant_dynamic-slice_fusion.4 = bf16[1,192,1024]{2,1,0:T(8,128)(2,1)} fusion(bf16[6,512,1024]{2,1,0:T(8,128)(2,1)} %bitcast.11, s32[]{:T(128)S(6)} %select_n.19), kind=kLoop, calls=%fused_computation.4 | loop fusion | bytes 786436 | tf_op jit(solution)/shard_map/dynamic_slice | solution.py:248
  15.6 13.1 %collective-permute-done.refs_0_ = bf16[1040,128]{1,0:T(8,128)(2,1)S(1)} collective-permute-done((bf16[1040,128]{1,0:T(8,128)(2,1)S(1)}, bf16[1040,128]{1,0:T(8,128)(2,1)S(1)}, u32[]{:S(2)}, u32[]{:S(2)}) %collective-permute-start) | collective-permute-done | bytes 266272 | tf_op jit(solution)/shard_map/ppermute | solution.py:226
  28.7 2.1 %collective-permute-start.2 = (bf16[1,192,1024]{2,1,0:T(8,128)(2,1)}, bf16[1,192,1024]{2,1,0:T(8,128)(2,1)S(1)}, u32[]{:S(2)}, u32[]{:S(2)}) collective-permute-start(bf16[1,192,1024]{2,1,0:T(8,128)(2,1)} %constant_dynamic-slice_fusion.4), channel_id=1, source_target_pairs={{0,16},{16,0},{1,17},{17,1},{2,18},{18,2},{3,19},{19,3},{4,20},{20... | collective-permute-start | bytes 1179656 | tf_op jit(solution)/shard_map/ppermute | solution.py:226
  30.8 1.3 share.1.shares_ref
  32.6 2.3 %update.8 = (bf16[1,128,1024]{2,1,0:T(8,128)(2,1)S(1)}, bf16[6,512,1024]{2,1,0:T(8,128)(2,1)}, f32[6,256,1024]{2,1,0:T(8,128)}) custom-call(s32[1]{0:T(128)} %bitcast.me_ref, f32[2]{0:T(128)S(1)} %copy-done.2, bf16[6,512,1024]{2,1,0:T(8,128)(2,1)} %bitcast.21, bf16[6,512,1024]{2,1,0:T(8,128)(2,1)} %bitcast.12, ...), custom_call_target="tpu_custom_call" | custom-call | flops 1572864 | bytes 2359296 | tf_op jit(solution)/shard_map/update/pallas_call | solution.py:171
  36.6 5.2 %update.9 = (bf16[1,128,1024]{2,1,0:T(8,128)(2,1)S(1)}, bf16[6,512,1024]{2,1,0:T(8,128)(2,1)}, f32[6,256,1024]{2,1,0:T(8,128)}) custom-call(s32[1]{0:T(128)} %bitcast.me_ref, f32[2]{0:T(128)S(1)} %copy-done.3, bf16[6,512,1024]{2,1,0:T(8,128)(2,1)} %bitcast.22, bf16[6,512,1024]{2,1,0:T(8,128)(2,1)} %bitcast.14, ...), custom_call_target="tpu_custom_call", output_to_operand_aliasing={{1}: (6, {}), {2}: (7, {})} | custom-call | flops 1572864 | bytes 2359296 | tf_op jit(solution)/shard_map/update/pallas_call | solution.py:171
  41.8 1.4 collective-permute-start.1
  43.2 2.6 %update.10 = (bf16[1,256,1024]{2,1,0:T(8,128)(2,1)S(1)}, bf16[6,512,1024]{2,1,0:T(8,128)(2,1)}, f32[6,256,1024]{2,1,0:T(8,128)}) custom-call(s32[1]{0:T(128)} %bitcast.me_ref, f32[2]{0:T(128)S(1)} %copy-done.3, bf16[6,512,1024]{2,1,0:T(8,128)(2,1)} %bitcast.23, bf16[6,512,1024]{2,1,0:T(8,128)(2,1)} %bitcast.15, ...), custom_call_target="tpu_custom_call", output_to_operand_aliasing={{1}: (6, {}), {2}: (7, {})} | custom-call | flops 3145728 | bytes 4718592 | tf_op jit(solution)/shard_map/update/pallas_call | solution.py:171
  45.8 5.3 %collective-permute-done.4.refs_0_ = bf16[1,256,1024]{2,1,0:T(8,128)(2,1)S(1)} collective-permute-done((bf16[1,256,1024]{2,1,0:T(8,128)(2,1)}, bf16[1,256,1024]{2,1,0:T(8,128)(2,1)S(1)}, u32[]{:S(2)}, u32[]{:S(2)}) %collective-permute-start.4) | collective-permute-done | bytes 524320 | tf_op jit(solution)/shard_map/ppermute | solution.py:226
  51.2 2.1 %collective-permute-start.14 = (bf16[1,128,1024]{2,1,0:T(8,128)(2,1)S(1)}, bf16[1,128,1024]{2,1,0:T(8,128)(2,1)S(1)}, u32[]{:S(2)}, u32[]{:S(2)}) collective-permute-start(bf16[1,128,1024]{2,1,0:T(8,128)(2,1)S(1)} %get-tuple-element.52), channel_id=1, source_target_pairs={{0,16},{16,0},{1,17},{17,1},{2,18},{18,2},{3,19},{19,3},{4,20},{20... | collective-permute-start | bytes 786440 | tf_op jit(solution)/shard_map/ppermute | solution.py:226
  53.2 9.2 %collective-permute-done.3.refs_0_ = bf16[1,256,1024]{2,1,0:T(8,128)(2,1)S(1)} collective-permute-done((bf16[1,256,1024]{2,1,0:T(8,128)(2,1)}, bf16[1,256,1024]{2,1,0:T(8,128)(2,1)S(1)}, u32[]{:S(2)}, u32[]{:S(2)}) %collective-permute-start.3) | collective-permute-done | bytes 524320 | tf_op jit(solution)/shard_map/ppermute | solution.py:226
  62.4 2.1 %collective-permute-start.13 = (bf16[1,256,1024]{2,1,0:T(8,128)(2,1)S(1)}, bf16[1,256,1024]{2,1,0:T(8,128)(2,1)S(1)}, u32[]{:S(2)}, u32[]{:S(2)}) collective-permute-start(bf16[1,256,1024]{2,1,0:T(8,128)(2,1)S(1)} %get-tuple-element.51), channel_id=1, source_target_pairs={{0,16},{16,0},{1,17},{17,1},{2,18},{18,2},{3,19},{19,3},{4,20},{20... | collective-permute-start | bytes 1572872 | tf_op jit(solution)/shard_map/ppermute | solution.py:226
  64.5 2.6 %update.11 = (bf16[1,256,1024]{2,1,0:T(8,128)(2,1)S(1)}, bf16[6,512,1024]{2,1,0:T(8,128)(2,1)}, f32[6,256,1024]{2,1,0:T(8,128)}) custom-call(s32[1]{0:T(128)} %bitcast.me_ref, f32[2]{0:T(128)S(1)} %copy-done.3, bf16[6,512,1024]{2,1,0:T(8,128)(2,1)} %bitcast.24, bf16[6,512,1024]{2,1,0:T(8,128)(2,1)} %bitcast.16, ...), custom_call_target="tpu_custom_call", output_to_operand_aliasing={{1}: (6, {}), {2}: (7, {})} | custom-call | flops 3145728 | bytes 4718592 | tf_op jit(solution)/shard_map/update/pallas_call | solution.py:171
  67.1 2.6 %update.12 = (bf16[1,256,1024]{2,1,0:T(8,128)(2,1)S(1)}, bf16[6,512,1024]{2,1,0:T(8,128)(2,1)}, f32[6,256,1024]{2,1,0:T(8,128)}) custom-call(s32[1]{0:T(128)} %bitcast.me_ref, f32[2]{0:T(128)S(1)} %copy-done.3, bf16[6,512,1024]{2,1,0:T(8,128)(2,1)} %bitcast.25, bf16[6,512,1024]{2,1,0:T(8,128)(2,1)} %bitcast.17, ...), custom_call_target="tpu_custom_call", output_to_operand_aliasing={{1}: (6, {}), {2}: (7, {})} | custom-call | flops 3145728 | bytes 4718592 | tf_op jit(solution)/shard_map/update/pallas_call | solution.py:171
  69.7 2.6 %update.13 = (bf16[1,256,1024]{2,1,0:T(8,128)(2,1)S(1)}, bf16[6,512,1024]{2,1,0:T(8,128)(2,1)}, f32[6,256,1024]{2,1,0:T(8,128)}) custom-call(s32[1]{0:T(128)} %bitcast.me_ref, f32[2]{0:T(128)S(1)} %copy-done.3, bf16[6,512,1024]{2,1,0:T(8,128)(2,1)} %bitcast.26, bf16[6,512,1024]{2,1,0:T(8,128)(2,1)} %bitcast.18, ...), custom_call_target="tpu_custom_call", output_to_operand_aliasing={{1}: (6, {}), {2}: (7, {})} | custom-call | flops 3145728 | bytes 4718592 | tf_op jit(solution)/shard_map/update/pallas_call | solution.py:171
  72.4 6.9 %collective-permute-done.1.refs_0_ = bf16[1,64,1024]{2,1,0:T(8,128)(2,1)S(1)} collective-permute-done((bf16[1,64,1024]{2,1,0:T(8,128)(2,1)S(1)}, bf16[1,64,1024]{2,1,0:T(8,128)(2,1)S(1)}, u32[]{:S(2)}, u32[]{:S(2)}) %collective-permute-start.1) | collective-permute-done | bytes 131104 | tf_op jit(solution)/shard_map/ppermute | solution.py:226
  79.2 2.1 %collective-permute-start.12 = (bf16[1,256,1024]{2,1,0:T(8,128)(2,1)S(1)}, bf16[1,256,1024]{2,1,0:T(8,128)(2,1)S(1)}, u32[]{:S(2)}, u32[]{:S(2)}) collective-permute-start(bf16[1,256,1024]{2,1,0:T(8,128)(2,1)S(1)} %get-tuple-element.50), channel_id=1, source_target_pairs={{0,16},{16,0},{1,17},{17,1},{2,18},{18,2},{3,19},{19,3},{4,20},{20... | collective-permute-start | bytes 1572872 | tf_op jit(solution)/shard_map/ppermute | solution.py:226
  81.3 2.0 %collective-permute-start.10 = (bf16[1,256,1024]{2,1,0:T(8,128)(2,1)S(1)}, bf16[1,256,1024]{2,1,0:T(8,128)(2,1)S(1)}, u32[]{:S(2)}, u32[]{:S(2)}) collective-permute-start(bf16[1,256,1024]{2,1,0:T(8,128)(2,1)S(1)} %get-tuple-element.48), channel_id=1, source_target_pairs={{0,16},{16,0},{1,17},{17,1},{2,18},{18,2},{3,19},{19,3},{4,20},{20... | collective-permute-start | bytes 1572872 | tf_op jit(solution)/shard_map/ppermute | solution.py:226
  83.3 3.4 %update.14 = (bf16[1,192,1024]{2,1,0:T(8,128)(2,1)S(1)}, bf16[6,512,1024]{2,1,0:T(8,128)(2,1)}, f32[6,256,1024]{2,1,0:T(8,128)}) custom-call(s32[1]{0:T(128)} %bitcast.me_ref, f32[2]{0:T(128)S(1)} %copy-done.3, bf16[6,512,1024]{2,1,0:T(8,128)(2,1)} %bitcast.27, bf16[6,512,1024]{2,1,0:T(8,128)(2,1)} %bitcast.19, ...), custom_call_target="tpu_custom_call", output_to_operand_aliasing={{1}: (6, {}), {2}: (7, {})} | custom-call | flops 2359296 | bytes 3538944 | tf_op jit(solution)/shard_map/update/pallas_call | solution.py:171
  86.9 1.9 %update.15 = (bf16[1,64,1024]{2,1,0:T(8,128)(2,1)S(1)}, bf16[6,512,1024]{2,1,0:T(8,128)(2,1)}, f32[6,256,1024]{2,1,0:T(8,128)}) custom-call(s32[1]{0:T(128)} %bitcast.me_ref, f32[2]{0:T(128)S(1)} %copy-done.3, bf16[6,512,1024]{2,1,0:T(8,128)(2,1)} %bitcast.28, bf16[6,512,1024]{2,1,0:T(8,128)(2,1)} %bitcast.20, ...), custom_call_target="tpu_custom_call", output_to_operand_aliasing={{1}: (6, {}), {2}: (7, {})} | custom-call | flops 786432 | bytes 1179648 | tf_op jit(solution)/shard_map/update/pallas_call | solution.py:171
  88.9 7.2 %collective-permute-done.13.block_ref = bf16[1,256,1024]{2,1,0:T(8,128)(2,1)S(1)} collective-permute-done((bf16[1,256,1024]{2,1,0:T(8,128)(2,1)S(1)}, bf16[1,256,1024]{2,1,0:T(8,128)(2,1)S(1)}, u32[]{:S(2)}, u32[]{:S(2)}) %collective-permute-start.13) | collective-permute-done | bytes 524320 | tf_op jit(solution)/shard_map/ppermute | solution.py:226
  96.1 2.1 %collective-permute-start.8 = (bf16[1,64,1024]{2,1,0:T(8,128)(2,1)S(1)}, bf16[1,64,1024]{2,1,0:T(8,128)(2,1)S(1)}, u32[]{:S(2)}, u32[]{:S(2)}) collective-permute-start(bf16[1,64,1024]{2,1,0:T(8,128)(2,1)S(1)} %get-tuple-element.46), channel_id=1, source_target_pairs={{0,16},{16,0},{1,17},{17,1},{2,18},{18,2},{3,19},{19,3},{4,20},{20... | collective-permute-start | bytes 393224 | tf_op jit(solution)/shard_map/ppermute | solution.py:226
  100.4 6.9 %collective-permute-done.12.block_ref = bf16[1,256,1024]{2,1,0:T(8,128)(2,1)S(1)} collective-permute-done((bf16[1,256,1024]{2,1,0:T(8,128)(2,1)S(1)}, bf16[1,256,1024]{2,1,0:T(8,128)(2,1)S(1)}, u32[]{:S(2)}, u32[]{:S(2)}) %collective-permute-start.12) | collective-permute-done | bytes 524320 | tf_op jit(solution)/shard_map/ppermute | solution.py:226
  108.1 10.4 %collective-permute-done.11.block_ref = bf16[1,256,1024]{2,1,0:T(8,128)(2,1)S(1)} collective-permute-done((bf16[1,256,1024]{2,1,0:T(8,128)(2,1)S(1)}, bf16[1,256,1024]{2,1,0:T(8,128)(2,1)S(1)}, u32[]{:S(2)}, u32[]{:S(2)}) %collective-permute-start.11) | collective-permute-done | bytes 524320 | tf_op jit(solution)/shard_map/ppermute | solution.py:226
  119.4 10.4 %collective-permute-done.10.block_ref = bf16[1,256,1024]{2,1,0:T(8,128)(2,1)S(1)} collective-permute-done((bf16[1,256,1024]{2,1,0:T(8,128)(2,1)S(1)}, bf16[1,256,1024]{2,1,0:T(8,128)(2,1)S(1)}, u32[]{:S(2)}, u32[]{:S(2)}) %collective-permute-start.10) | collective-permute-done | bytes 524320 | tf_op jit(solution)/shard_map/ppermute | solution.py:226
  130.6 7.6 %collective-permute-done.9.block_ref = bf16[1,192,1024]{2,1,0:T(8,128)(2,1)S(1)} collective-permute-done((bf16[1,192,1024]{2,1,0:T(8,128)(2,1)S(1)}, bf16[1,192,1024]{2,1,0:T(8,128)(2,1)S(1)}, u32[]{:S(2)}, u32[]{:S(2)}) %collective-permute-start.9) | collective-permute-done | bytes 393248 | tf_op jit(solution)/shard_map/ppermute | solution.py:226
  139.0 1.2 collective-permute-done.8.block_ref
  (30 shorter events, 10.1 us)
Async XLA Ops:
  1.6 11.6 %collective-permute-start.7 = (bf16[1,128,1024]{2,1,0:T(8,128)(2,1)S(1)}, bf16[1,128,1024]{2,1,0:T(8,128)(2,1)S(1)}, u32[]{:S(2)}, u32[]{:S(2)}) collective-permute-start(bf16[1,128,1024]{2,1,0:T(8,128)(2,1)S(1)} %cut.1), channel_id=1, source_target_pairs={{0,16},{16,0},{1,17},{17,1},{2,18},{18,2},{3,19},{19,3},{4,20},{20... | collective-permute-start | bytes 786440 | tf_op jit(solution)/shard_map/ppermute | solution.py:226
  7.5 27.4 %collective-permute-start.6 = (bf16[1,256,1024]{2,1,0:T(8,128)(2,1)}, bf16[1,256,1024]{2,1,0:T(8,128)(2,1)S(1)}, u32[]{:S(2)}, u32[]{:S(2)}) collective-permute-start(bf16[1,256,1024]{2,1,0:T(8,128)(2,1)} %get-tuple-element.56), channel_id=1, source_target_pairs={{0,16},{16,0},{1,17},{17,1},{2,18},{18,2},{3,19},{19,3},{4,20},{20... | collective-permute-start | bytes 1572872 | tf_op jit(solution)/shard_map/ppermute | solution.py:226
  9.2 19.5 %collective-permute-start = (bf16[1040,128]{1,0:T(8,128)(2,1)S(1)}, bf16[1040,128]{1,0:T(8,128)(2,1)S(1)}, u32[]{:S(2)}, u32[]{:S(2)}) collective-permute-start(bf16[1040,128]{1,0:T(8,128)(2,1)S(1)} %pack.1), channel_id=1, source_target_pairs={{0,16},{16,0},{1,17},{17,1},{2,18},{18,2},{3,19},{19,3},{4,20},{20... | collective-permute-start | bytes 798728 | tf_op jit(solution)/shard_map/ppermute | solution.py:226
  11.2 30.6 %collective-permute-start.5 = (bf16[1,256,1024]{2,1,0:T(8,128)(2,1)}, bf16[1,256,1024]{2,1,0:T(8,128)(2,1)S(1)}, u32[]{:S(2)}, u32[]{:S(2)}) collective-permute-start(bf16[1,256,1024]{2,1,0:T(8,128)(2,1)} %get-tuple-element.57), channel_id=1, source_target_pairs={{0,16},{16,0},{1,17},{17,1},{2,18},{18,2},{3,19},{19,3},{4,20},{20... | collective-permute-start | bytes 1572872 | tf_op jit(solution)/shard_map/ppermute | solution.py:226
  11.3 39.9 %collective-permute-start.4 = (bf16[1,256,1024]{2,1,0:T(8,128)(2,1)}, bf16[1,256,1024]{2,1,0:T(8,128)(2,1)S(1)}, u32[]{:S(2)}, u32[]{:S(2)}) collective-permute-start(bf16[1,256,1024]{2,1,0:T(8,128)(2,1)} %get-tuple-element.58), channel_id=1, source_target_pairs={{0,16},{16,0},{1,17},{17,1},{2,18},{18,2},{3,19},{19,3},{4,20},{20... | collective-permute-start | bytes 1572872 | tf_op jit(solution)/shard_map/ppermute | solution.py:226
  13.3 49.1 %collective-permute-start.3 = (bf16[1,256,1024]{2,1,0:T(8,128)(2,1)}, bf16[1,256,1024]{2,1,0:T(8,128)(2,1)S(1)}, u32[]{:S(2)}, u32[]{:S(2)}) collective-permute-start(bf16[1,256,1024]{2,1,0:T(8,128)(2,1)} %get-tuple-element.59), channel_id=1, source_target_pairs={{0,16},{16,0},{1,17},{17,1},{2,18},{18,2},{3,19},{19,3},{4,20},{20... | collective-permute-start | bytes 1572872 | tf_op jit(solution)/shard_map/ppermute | solution.py:226
  28.7 2.1 %copy-start = (bf16[1040,128]{1,0:T(8,128)(2,1)}, bf16[1040,128]{1,0:T(8,128)(2,1)S(1)}, u32[]{:S(2)}) copy-start(bf16[1040,128]{1,0:T(8,128)(2,1)S(1)} %collective-permute-done.refs_0_) | copy-start | bytes 798724
  28.7 52.6 %collective-permute-start.2 = (bf16[1,192,1024]{2,1,0:T(8,128)(2,1)}, bf16[1,192,1024]{2,1,0:T(8,128)(2,1)S(1)}, u32[]{:S(2)}, u32[]{:S(2)}) collective-permute-start(bf16[1,192,1024]{2,1,0:T(8,128)(2,1)} %constant_dynamic-slice_fusion.4), channel_id=1, source_target_pairs={{0,16},{16,0},{1,17},{17,1},{2,18},{18,2},{3,19},{19,3},{4,20},{20... | collective-permute-start | bytes 1179656 | tf_op jit(solution)/shard_map/ppermute | solution.py:226
  32.0 0.6 copy-start.2
  32.6 4.0 %copy-start.1 = (bf16[1040,128]{1,0:T(8,128)(2,1)S(1)}, bf16[1040,128]{1,0:T(8,128)(2,1)}, u32[]{:S(2)}) copy-start(bf16[1040,128]{1,0:T(8,128)(2,1)} %copy-done) | copy-start | bytes 798724
  32.6 4.0 %copy-start.3 = (f32[2]{0:T(128)S(1)}, f32[2]{0:T(128)}, u32[]{:S(2)}) copy-start(f32[2]{0:T(128)} %share.1.shares_ref) | copy-start | bytes 28
  35.0 46.4 %collective-permute-start.15 = (bf16[1,128,1024]{2,1,0:T(8,128)(2,1)S(1)}, bf16[1,128,1024]{2,1,0:T(8,128)(2,1)S(1)}, u32[]{:S(2)}, u32[]{:S(2)}) collective-permute-start(bf16[1,128,1024]{2,1,0:T(8,128)(2,1)S(1)} %get-tuple-element.53), channel_id=1, source_target_pairs={{0,16},{16,0},{1,17},{17,1},{2,18},{18,2},{3,19},{19,3},{4,20},{20... | collective-permute-start | bytes 786440 | tf_op jit(solution)/shard_map/ppermute | solution.py:226
  41.8 37.4 %collective-permute-start.1 = (bf16[1,64,1024]{2,1,0:T(8,128)(2,1)S(1)}, bf16[1,64,1024]{2,1,0:T(8,128)(2,1)S(1)}, u32[]{:S(2)}, u32[]{:S(2)}) collective-permute-start(bf16[1,64,1024]{2,1,0:T(8,128)(2,1)S(1)} %constant_dynamic-slice_fusion.5), channel_id=1, source_target_pairs={{0,16},{16,0},{1,17},{17,1},{2,18},{18,2},{3,19},{19,3},{4,20},{20... | collective-permute-start | bytes 393224 | tf_op jit(solution)/shard_map/ppermute | solution.py:226
  51.2 35.6 %collective-permute-start.14 = (bf16[1,128,1024]{2,1,0:T(8,128)(2,1)S(1)}, bf16[1,128,1024]{2,1,0:T(8,128)(2,1)S(1)}, u32[]{:S(2)}, u32[]{:S(2)}) collective-permute-start(bf16[1,128,1024]{2,1,0:T(8,128)(2,1)S(1)} %get-tuple-element.52), channel_id=1, source_target_pairs={{0,16},{16,0},{1,17},{17,1},{2,18},{18,2},{3,19},{19,3},{4,20},{20... | collective-permute-start | bytes 786440 | tf_op jit(solution)/shard_map/ppermute | solution.py:226
  62.4 33.7 %collective-permute-start.13 = (bf16[1,256,1024]{2,1,0:T(8,128)(2,1)S(1)}, bf16[1,256,1024]{2,1,0:T(8,128)(2,1)S(1)}, u32[]{:S(2)}, u32[]{:S(2)}) collective-permute-start(bf16[1,256,1024]{2,1,0:T(8,128)(2,1)S(1)} %get-tuple-element.51), channel_id=1, source_target_pairs={{0,16},{16,0},{1,17},{17,1},{2,18},{18,2},{3,19},{19,3},{4,20},{20... | collective-permute-start | bytes 1572872 | tf_op jit(solution)/shard_map/ppermute | solution.py:226
  79.2 28.1 %collective-permute-start.12 = (bf16[1,256,1024]{2,1,0:T(8,128)(2,1)S(1)}, bf16[1,256,1024]{2,1,0:T(8,128)(2,1)S(1)}, u32[]{:S(2)}, u32[]{:S(2)}) collective-permute-start(bf16[1,256,1024]{2,1,0:T(8,128)(2,1)S(1)} %get-tuple-element.50), channel_id=1, source_target_pairs={{0,16},{16,0},{1,17},{17,1},{2,18},{18,2},{3,19},{19,3},{4,20},{20... | collective-permute-start | bytes 1572872 | tf_op jit(solution)/shard_map/ppermute | solution.py:226
  81.3 37.3 %collective-permute-start.11 = (bf16[1,256,1024]{2,1,0:T(8,128)(2,1)S(1)}, bf16[1,256,1024]{2,1,0:T(8,128)(2,1)S(1)}, u32[]{:S(2)}, u32[]{:S(2)}) collective-permute-start(bf16[1,256,1024]{2,1,0:T(8,128)(2,1)S(1)} %get-tuple-element.49), channel_id=1, source_target_pairs={{0,16},{16,0},{1,17},{17,1},{2,18},{18,2},{3,19},{19,3},{4,20},{20... | collective-permute-start | bytes 1572872 | tf_op jit(solution)/shard_map/ppermute | solution.py:226
  81.3 48.5 %collective-permute-start.10 = (bf16[1,256,1024]{2,1,0:T(8,128)(2,1)S(1)}, bf16[1,256,1024]{2,1,0:T(8,128)(2,1)S(1)}, u32[]{:S(2)}, u32[]{:S(2)}) collective-permute-start(bf16[1,256,1024]{2,1,0:T(8,128)(2,1)S(1)} %get-tuple-element.48), channel_id=1, source_target_pairs={{0,16},{16,0},{1,17},{17,1},{2,18},{18,2},{3,19},{19,3},{4,20},{20... | collective-permute-start | bytes 1572872 | tf_op jit(solution)/shard_map/ppermute | solution.py:226
  86.8 51.5 %collective-permute-start.9 = (bf16[1,192,1024]{2,1,0:T(8,128)(2,1)S(1)}, bf16[1,192,1024]{2,1,0:T(8,128)(2,1)S(1)}, u32[]{:S(2)}, u32[]{:S(2)}) collective-permute-start(bf16[1,192,1024]{2,1,0:T(8,128)(2,1)S(1)} %get-tuple-element.47), channel_id=1, source_target_pairs={{0,16},{16,0},{1,17},{17,1},{2,18},{18,2},{3,19},{19,3},{4,20},{20... | collective-permute-start | bytes 1179656 | tf_op jit(solution)/shard_map/ppermute | solution.py:226
  96.1 44.1 %collective-permute-start.8 = (bf16[1,64,1024]{2,1,0:T(8,128)(2,1)S(1)}, bf16[1,64,1024]{2,1,0:T(8,128)(2,1)S(1)}, u32[]{:S(2)}, u32[]{:S(2)}) collective-permute-start(bf16[1,64,1024]{2,1,0:T(8,128)(2,1)S(1)} %get-tuple-element.46), channel_id=1, source_target_pairs={{0,16},{16,0},{1,17},{17,1},{2,18},{18,2},{3,19},{19,3},{4,20},{20... | collective-permute-start | bytes 393224 | tf_op jit(solution)/shard_map/ppermute | solution.py:226

commit v8 on v7

--- a/solution.py
+++ b/solution.py
@@ -233,13 +233,12 @@
         anchor = anchor.reshape(parts, *shape[-2:])
         momentum = momentum.reshape(parts, owned, width)
         me = lax.axis_index("replica")
-        half = owned // 2
-        last = max(16, owned // 4)
-        chunks = [Chunk(0, 1, 0, half), Chunk(0, 1, half, half)]
-        chunks += [Chunk(p, 1, 0, owned) for p in range(1, parts - 1)]
-        chunks += [
-            Chunk(parts - 1, 1, 0, owned - last),
-            Chunk(parts - 1, 1, owned - last, last),
+        middle = (parts - 2) // 2
+        chunks = [
+            Chunk(1, middle, 0, owned),
+            Chunk(1 + middle, parts - 2 - middle, 0, owned),
+            Chunk(0, 1, 0, owned),
+            Chunk(parts - 1, 1, 0, owned),
         ]
         shifts = range(1, groups)
 
@@ -250,13 +249,13 @@
         targets = [(me + s) % groups for s in shifts]
         first = [cut(groups, owned, chunks[0], s, inner) for s in shifts]
         first, rest, later_counts = lax.optimization_barrier((first, inner, counts))
-        second = [
-            pack(chunks[1], t.reshape(1).astype(jnp.int32), later_counts, rest, owned)
+        sent = [first] + [[rows_for(rest, c, t) for t in targets] for c in chunks[1:]]
+        sent[2] = [
+            pack(chunks[2], t.reshape(1).astype(jnp.int32), later_counts, rest, owned)
             for t in targets
         ]
-        sent = [first, second] + [[rows_for(rest, c, t) for t in targets] for c in chunks[2:]]
         arrived = [[shifted(v, s) for v, s in zip(values, shifts)] for values in sent]
-        shares = share(later_counts, arrived[1])
+        shares = share(later_counts, arrived[2])
 
         where = me.reshape(1).astype(jnp.int32)
         held = []

time: 142 us -> 142 us (level)
  waiting for transfers between devices: 78.3 us -> 99.6 us
  starting transfers between devices: 22.2 us -> 9.25 us
  Pallas kernels: 32.7 us -> 25.5 us
    ppermute x16 -> x8, waiting for transfers between devices: 78.3 us -> 99.6 us  [shifted(): return lax.ppermute(value, 'replica', pairs)]
    ppermute x16 -> x8, starting transfers between devices: 22.2 us -> 9.25 us  [shifted(): return lax.ppermute(value, 'replica', pairs)]
    pallas_call x8 -> x4, Pallas kernels: 23.5 us -> 18.3 us  [update(): pl.pallas_call(functools.partial(update_kernel, groups), grid_spec=pltpu....]
    pallas_call x8 -> x4, Pallas kernels: 6.07 us -> 3.56 us  [place(): pl.pallas_call(functools.partial(place_kernel, groups, owned, chunk, shif...]
    dynamic_slice x3 -> x2, local copies, waits for them, and re-layouts: 5.57 us -> 4.16 us  [rows_for(): lax.dynamic_slice(array, (chunk.lo, target * owned + chunk.row, 0), sizes)]
  transfers between devices with their start and end apart: 16 -> 8, of which waited for: 10 -> 5; matrix products, arithmetic and copies ran while one was open for 4% -> 3% of each run, Pallas kernels for 22% -> 17%
where the time goes in v8:
time: 142 us; the launch traced here: 141 us
  waiting for transfers between devices  99.6 us (70%)
  Pallas kernels  25.5 us (18%)
  starting transfers between devices  9.25 us (7%)
  local copies, waits for them, and re-layouts  5.63 us (4%)
    ppermute x8, waiting for transfers between devices, shifted(): return lax.ppermute(value, 'replica', pairs)  99.6 us
    pallas_call x4, Pallas kernels, update(): pl.pallas_call(functools.partial(update_kernel, groups), grid_spec=pltpu....  18.3 us
    ppermute x8, starting transfers between devices, shifted(): return lax.ppermute(value, 'replica', pairs)  9.25 us
    dynamic_slice x2, local copies, waits for them, and re-layouts, rows_for(): lax.dynamic_slice(array, (chunk.lo, target * owned + chunk.row, 0), sizes)  4.16 us
    pallas_call x4, Pallas kernels, place(): pl.pallas_call(functools.partial(place_kernel, groups, owned, chunk, shif...  3.56 us
  transfers between devices with their start and end apart: 8, of which 5 were waited for; matrix products, arithmetic and copies ran while one was open for 3% of the time, Pallas kernels for 17%

profile of v8, /device:TPU:0, one launch (start us, length us, event | category | flops | bytes accessed | tf_op | source)
XLA Modules:
  0.0 141.3 jit_solution(9658464408836381439)
XLA Ops:
  0.6 1.2 cut.1
  1.9 3.0 %collective-permute-start.3 = (bf16[2,256,1024]{2,1,0:T(8,128)(2,1)S(1)}, bf16[2,256,1024]{2,1,0:T(8,128)(2,1)S(1)}, u32[]{:S(2)}, u32[]{:S(2)}) collective-permute-start(bf16[2,256,1024]{2,1,0:T(8,128)(2,1)S(1)} %cut.1), channel_id=1, source_target_pairs={{0,16},{16,0},{1,17},{17,1},{2,18},{18,2},{3,19},{19,3},{4,20},{20... | collective-permute-start | bytes 3145736 | tf_op jit(solution)/shard_map/ppermute | solution.py:226
  4.9 2.3 %constant_dynamic-slice_fusion = bf16[2,256,1024]{2,1,0:T(8,128)(2,1)} fusion(bf16[6,512,1024]{2,1,0:T(8,128)(2,1)} %bitcast.9, s32[]{:T(128)S(6)} %select_n.12), kind=kLoop, calls=%fused_computation | loop fusion | bytes 2097156 | tf_op jit(solution)/shard_map/dynamic_slice | solution.py:247
  7.2 0.0 collective-permute-start.2
  7.9 1.2 pack.1
  9.0 2.1 %collective-permute-start = (bf16[2064,128]{1,0:T(8,128)(2,1)S(1)}, bf16[2064,128]{1,0:T(8,128)(2,1)S(1)}, u32[]{:S(2)}, u32[]{:S(2)}) collective-permute-start(bf16[2064,128]{1,0:T(8,128)(2,1)S(1)} %pack.1), channel_id=1, source_target_pairs={{0,16},{16,0},{1,17},{17,1},{2,18},{18,2},{3,19},{19,3},{4,20},{20... | collective-permute-start | bytes 1585160 | tf_op jit(solution)/shard_map/ppermute | solution.py:226
  11.1 1.9 %constant_dynamic-slice_fusion.1 = bf16[1,256,1024]{2,1,0:T(8,128)(2,1)} fusion(bf16[6,512,1024]{2,1,0:T(8,128)(2,1)} %bitcast.11, s32[]{:T(128)S(6)} %select_n.12), kind=kLoop, calls=%fused_computation.1 | loop fusion | bytes 1048580 | tf_op jit(solution)/shard_map/dynamic_slice | solution.py:247
  13.0 0.0 collective-permute-start.1
  13.0 49.7 %collective-permute-done.refs_0_ = bf16[2064,128]{1,0:T(8,128)(2,1)S(1)} collective-permute-done((bf16[2064,128]{1,0:T(8,128)(2,1)S(1)}, bf16[2064,128]{1,0:T(8,128)(2,1)S(1)}, u32[]{:S(2)}, u32[]{:S(2)}) %collective-permute-start) | collective-permute-done | bytes 528416 | tf_op jit(solution)/shard_map/ppermute | solution.py:226
  62.7 0.8 copy-done
  63.5 1.3 share.1.shares_ref
  64.8 0.0 collective-permute-done.3.refs_0_
  64.8 0.0 copy-start.2
  64.8 0.6 copy-done.2
  65.4 4.7 %update.4 = (bf16[2,256,1024]{2,1,0:T(8,128)(2,1)S(1)}, bf16[6,512,1024]{2,1,0:T(8,128)(2,1)}, f32[6,256,1024]{2,1,0:T(8,128)}) custom-call(s32[1]{0:T(128)} %bitcast.me_ref, f32[2]{0:T(128)S(1)} %copy-done.2, bf16[6,512,1024]{2,1,0:T(8,128)(2,1)} %bitcast.16, bf16[6,512,1024]{2,1,0:T(8,128)(2,1)} %bitcast.12, ...), custom_call_target="tpu_custom_call" | custom-call | flops 6291456 | bytes 9437184 | tf_op jit(solution)/shard_map/update/pallas_call | solution.py:171
  70.1 2.1 %collective-permute-start.7 = (bf16[2,256,1024]{2,1,0:T(8,128)(2,1)S(1)}, bf16[2,256,1024]{2,1,0:T(8,128)(2,1)S(1)}, u32[]{:S(2)}, u32[]{:S(2)}) collective-permute-start(bf16[2,256,1024]{2,1,0:T(8,128)(2,1)S(1)} %get-tuple-element.29), channel_id=1, source_target_pairs={{0,16},{16,0},{1,17},{17,1},{2,18},{18,2},{3,19},{19,3},{4,20},{20... | collective-permute-start | bytes 3145736 | tf_op jit(solution)/shard_map/ppermute | solution.py:226
  72.2 0.0 collective-permute-done.2.refs_0_
  72.2 5.0 %update.5 = (bf16[2,256,1024]{2,1,0:T(8,128)(2,1)S(1)}, bf16[6,512,1024]{2,1,0:T(8,128)(2,1)}, f32[6,256,1024]{2,1,0:T(8,128)}) custom-call(s32[1]{0:T(128)} %bitcast.me_ref, f32[2]{0:T(128)S(1)} %copy-done.2, bf16[6,512,1024]{2,1,0:T(8,128)(2,1)} %bitcast.17, bf16[6,512,1024]{2,1,0:T(8,128)(2,1)} %bitcast.13, ...), custom_call_target="tpu_custom_call", output_to_operand_aliasing={{1}: (6, {}), {2}: (7, {})} | custom-call | flops 6291456 | bytes 9437184 | tf_op jit(solution)/shard_map/update/pallas_call | solution.py:171
  77.2 0.0 collective-permute-start.6
  77.2 5.9 %update.6 = (bf16[1,256,1024]{2,1,0:T(8,128)(2,1)S(1)}, bf16[6,512,1024]{2,1,0:T(8,128)(2,1)}, f32[6,256,1024]{2,1,0:T(8,128)}) custom-call(s32[1]{0:T(128)} %bitcast.me_ref, f32[2]{0:T(128)S(1)} %copy-done.2, bf16[6,512,1024]{2,1,0:T(8,128)(2,1)} %bitcast.18, bf16[6,512,1024]{2,1,0:T(8,128)(2,1)} %bitcast.14, ...), custom_call_target="tpu_custom_call", output_to_operand_aliasing={{1}: (6, {}), {2}: (7, {})} | custom-call | flops 3145728 | bytes 4718592 | tf_op jit(solution)/shard_map/update/pallas_call | solution.py:171
  83.1 2.0 %collective-permute-start.5 = (bf16[1,256,1024]{2,1,0:T(8,128)(2,1)S(1)}, bf16[1,256,1024]{2,1,0:T(8,128)(2,1)S(1)}, u32[]{:S(2)}, u32[]{:S(2)}) collective-permute-start(bf16[1,256,1024]{2,1,0:T(8,128)(2,1)S(1)} %get-tuple-element.27), channel_id=1, source_target_pairs={{0,16},{16,0},{1,17},{17,1},{2,18},{18,2},{3,19},{19,3},{4,20},{20... | collective-permute-start | bytes 1572872 | tf_op jit(solution)/shard_map/ppermute | solution.py:226
  85.1 0.0 collective-permute-done.1.refs_0_
  85.1 2.6 %update.7 = (bf16[1,256,1024]{2,1,0:T(8,128)(2,1)S(1)}, bf16[6,512,1024]{2,1,0:T(8,128)(2,1)}, f32[6,256,1024]{2,1,0:T(8,128)}) custom-call(s32[1]{0:T(128)} %bitcast.me_ref, f32[2]{0:T(128)S(1)} %copy-done.2, bf16[6,512,1024]{2,1,0:T(8,128)(2,1)} %bitcast.19, bf16[6,512,1024]{2,1,0:T(8,128)(2,1)} %bitcast.15, ...), custom_call_target="tpu_custom_call", output_to_operand_aliasing={{1}: (6, {}), {2}: (7, {})} | custom-call | flops 3145728 | bytes 4718592 | tf_op jit(solution)/shard_map/update/pallas_call | solution.py:171
  87.8 0.0 collective-permute-start.4
  87.8 8.6 %collective-permute-done.7.block_ref = bf16[2,256,1024]{2,1,0:T(8,128)(2,1)S(1)} collective-permute-done((bf16[2,256,1024]{2,1,0:T(8,128)(2,1)S(1)}, bf16[2,256,1024]{2,1,0:T(8,128)(2,1)S(1)}, u32[]{:S(2)}, u32[]{:S(2)}) %collective-permute-start.7) | collective-permute-done | bytes 1048608 | tf_op jit(solution)/shard_map/ppermute | solution.py:226
  96.4 1.0 place.4._
  97.4 21.5 %collective-permute-done.6.block_ref = bf16[2,256,1024]{2,1,0:T(8,128)(2,1)S(1)} collective-permute-done((bf16[2,256,1024]{2,1,0:T(8,128)(2,1)S(1)}, bf16[2,256,1024]{2,1,0:T(8,128)(2,1)S(1)}, u32[]{:S(2)}, u32[]{:S(2)}) %collective-permute-start.6) | collective-permute-done | bytes 1048608 | tf_op jit(solution)/shard_map/ppermute | solution.py:226
  118.8 1.0 place.5._
  119.8 10.2 %collective-permute-done.5.block_ref = bf16[1,256,1024]{2,1,0:T(8,128)(2,1)S(1)} collective-permute-done((bf16[1,256,1024]{2,1,0:T(8,128)(2,1)S(1)}, bf16[1,256,1024]{2,1,0:T(8,128)(2,1)S(1)}, u32[]{:S(2)}, u32[]{:S(2)}) %collective-permute-start.5) | collective-permute-done | bytes 524320 | tf_op jit(solution)/shard_map/ppermute | solution.py:226
  130.1 0.8 place.6._
  130.9 9.6 %collective-permute-done.4.block_ref = bf16[1,256,1024]{2,1,0:T(8,128)(2,1)S(1)} collective-permute-done((bf16[1,256,1024]{2,1,0:T(8,128)(2,1)S(1)}, bf16[1,256,1024]{2,1,0:T(8,128)(2,1)S(1)}, u32[]{:S(2)}, u32[]{:S(2)}) %collective-permute-start.4) | collective-permute-done | bytes 524320 | tf_op jit(solution)/shard_map/ppermute | solution.py:226
  140.5 0.8 place.7
  (3 shorter events, 0.0 us)
Async XLA Ops:
  1.9 62.9 %collective-permute-start.3 = (bf16[2,256,1024]{2,1,0:T(8,128)(2,1)S(1)}, bf16[2,256,1024]{2,1,0:T(8,128)(2,1)S(1)}, u32[]{:S(2)}, u32[]{:S(2)}) collective-permute-start(bf16[2,256,1024]{2,1,0:T(8,128)(2,1)S(1)} %cut.1), channel_id=1, source_target_pairs={{0,16},{16,0},{1,17},{17,1},{2,18},{18,2},{3,19},{19,3},{4,20},{20... | collective-permute-start | bytes 3145736 | tf_op jit(solution)/shard_map/ppermute | solution.py:226
  7.2 65.0 %collective-permute-start.2 = (bf16[2,256,1024]{2,1,0:T(8,128)(2,1)}, bf16[2,256,1024]{2,1,0:T(8,128)(2,1)}, u32[]{:S(2)}, u32[]{:S(2)}) collective-permute-start(bf16[2,256,1024]{2,1,0:T(8,128)(2,1)} %constant_dynamic-slice_fusion), channel_id=1, source_target_pairs={{0,16},{16,0},{1,17},{17,1},{2,18},{18,2},{3,19},{19,3},{4,20},{20... | collective-permute-start | bytes 3145736 | tf_op jit(solution)/shard_map/ppermute | solution.py:226
  9.0 53.6 %collective-permute-start = (bf16[2064,128]{1,0:T(8,128)(2,1)S(1)}, bf16[2064,128]{1,0:T(8,128)(2,1)S(1)}, u32[]{:S(2)}, u32[]{:S(2)}) collective-permute-start(bf16[2064,128]{1,0:T(8,128)(2,1)S(1)} %pack.1), channel_id=1, source_target_pairs={{0,16},{16,0},{1,17},{17,1},{2,18},{18,2},{3,19},{19,3},{4,20},{20... | collective-permute-start | bytes 1585160 | tf_op jit(solution)/shard_map/ppermute | solution.py:226
  13.0 72.2 %collective-permute-start.1 = (bf16[1,256,1024]{2,1,0:T(8,128)(2,1)}, bf16[1,256,1024]{2,1,0:T(8,128)(2,1)S(1)}, u32[]{:S(2)}, u32[]{:S(2)}) collective-permute-start(bf16[1,256,1024]{2,1,0:T(8,128)(2,1)} %constant_dynamic-slice_fusion.1), channel_id=1, source_target_pairs={{0,16},{16,0},{1,17},{17,1},{2,18},{18,2},{3,19},{19,3},{4,20},{20... | collective-permute-start | bytes 1572872 | tf_op jit(solution)/shard_map/ppermute | solution.py:226
  62.7 0.8 copy-start
  64.8 0.7 copy-start.2
  70.1 26.3 %collective-permute-start.7 = (bf16[2,256,1024]{2,1,0:T(8,128)(2,1)S(1)}, bf16[2,256,1024]{2,1,0:T(8,128)(2,1)S(1)}, u32[]{:S(2)}, u32[]{:S(2)}) collective-permute-start(bf16[2,256,1024]{2,1,0:T(8,128)(2,1)S(1)} %get-tuple-element.29), channel_id=1, source_target_pairs={{0,16},{16,0},{1,17},{17,1},{2,18},{18,2},{3,19},{19,3},{4,20},{20... | collective-permute-start | bytes 3145736 | tf_op jit(solution)/shard_map/ppermute | solution.py:226
  72.2 5.0 %copy-start.1 = (bf16[2064,128]{1,0:T(8,128)(2,1)S(1)}, bf16[2064,128]{1,0:T(8,128)(2,1)}, u32[]{:S(2)}) copy-start(bf16[2064,128]{1,0:T(8,128)(2,1)} %copy-done) | copy-start | bytes 1585156
  77.2 41.7 %collective-permute-start.6 = (bf16[2,256,1024]{2,1,0:T(8,128)(2,1)S(1)}, bf16[2,256,1024]{2,1,0:T(8,128)(2,1)S(1)}, u32[]{:S(2)}, u32[]{:S(2)}) collective-permute-start(bf16[2,256,1024]{2,1,0:T(8,128)(2,1)S(1)} %get-tuple-element.28), channel_id=1, source_target_pairs={{0,16},{16,0},{1,17},{17,1},{2,18},{18,2},{3,19},{19,3},{4,20},{20... | collective-permute-start | bytes 3145736 | tf_op jit(solution)/shard_map/ppermute | solution.py:226
  83.1 46.9 %collective-permute-start.5 = (bf16[1,256,1024]{2,1,0:T(8,128)(2,1)S(1)}, bf16[1,256,1024]{2,1,0:T(8,128)(2,1)S(1)}, u32[]{:S(2)}, u32[]{:S(2)}) collective-permute-start(bf16[1,256,1024]{2,1,0:T(8,128)(2,1)S(1)} %get-tuple-element.27), channel_id=1, source_target_pairs={{0,16},{16,0},{1,17},{17,1},{2,18},{18,2},{3,19},{19,3},{4,20},{20... | collective-permute-start | bytes 1572872 | tf_op jit(solution)/shard_map/ppermute | solution.py:226
  87.8 52.7 %collective-permute-start.4 = (bf16[1,256,1024]{2,1,0:T(8,128)(2,1)S(1)}, bf16[1,256,1024]{2,1,0:T(8,128)(2,1)S(1)}, u32[]{:S(2)}, u32[]{:S(2)}) collective-permute-start(bf16[1,256,1024]{2,1,0:T(8,128)(2,1)S(1)} %get-tuple-element.26), channel_id=1, source_target_pairs={{0,16},{16,0},{1,17},{17,1},{2,18},{18,2},{3,19},{19,3},{4,20},{20... | collective-permute-start | bytes 1572872 | tf_op jit(solution)/shard_map/ppermute | solution.py:226

commit v9 on v7

--- a/solution.py
+++ b/solution.py
@@ -193,31 +193,6 @@
     )(me, shares, anchor, inner, *arrived, momentum, *held)
 
 
-def place_kernel(groups, owned, chunk, shift, block_ref, _, weights_ref, sem):
-    source = lax.rem(lax.axis_index("replica") + groups - shift, groups)
-    start = pl.multiple_of(source * owned + chunk.row, spare)
-    copy = pltpu.make_async_copy(
-        block_ref, weights_ref.at[pl.ds(chunk.lo, chunk.parts), pl.ds(start, chunk.rows), :], sem
-    )
-    copy.start()
-    copy.wait()
-
-
-def place(groups, owned, chunk, shift, block, weights):
-    anywhere = pl.BlockSpec(memory_space=pl.ANY)
-    return pl.pallas_call(
-        functools.partial(place_kernel, groups, owned, chunk, shift),
-        in_specs=[anywhere, anywhere],
-        out_specs=anywhere,
-        out_shape=jax.ShapeDtypeStruct(weights.shape, weights.dtype),
-        scratch_shapes=[pltpu.SemaphoreType.DMA],
-        input_output_aliases={1: 0},
-        compiler_params=pltpu.CompilerParams(vmem_limit_bytes=vmem_bytes),
-        cost_estimate=pl.CostEstimate(flops=0, bytes_accessed=4 * block.size, transcendentals=0),
-        name="place",
-    )(block, weights)
-
-
 def solution(mesh):
     groups = mesh.shape["replica"]
 
@@ -269,7 +244,10 @@
         weights, moments = held
         for chunk, blocks in zip(chunks, travelled):
             for s, block in zip(shifts, blocks):
-                weights = place(groups, owned, chunk, s, block, weights)
+                source = (me - s) % groups
+                weights = lax.dynamic_update_slice(
+                    weights, block, (chunk.lo, source * owned + chunk.row, 0)
+                )
         return weights.reshape(shape), moments.reshape(*shape[:2], owned, width)
 
     placed = (

time: 142 us -> 147 us (1.035)
  local copies, waits for them, and re-layouts: 6.18 us -> 16.5 us
  Pallas kernels: 32.7 us -> 26.8 us
  waiting for transfers between devices: 78.3 us -> 80.3 us
    dynamic_update_slice x0 -> x8, local copies, waits for them, and re-layouts: none -> 10.3 us  [on_device(): lax.dynamic_update_slice(weights, block, (chunk.lo, source * owned + chun...]
    pallas_call x8 -> x0, Pallas kernels: 6.07 us -> none  [place(): pl.pallas_call(functools.partial(place_kernel, groups, owned, chunk, shif...]
    ppermute x16, waiting for transfers between devices: 78.3 us -> 80.3 us  [shifted(): return lax.ppermute(value, 'replica', pairs)]
  transfers between devices with their start and end apart: 16 -> 16, of which waited for: 10 -> 9; matrix products, arithmetic and copies ran while one was open for 4% -> 8% of each run, Pallas kernels for 22% -> 18%
where the time goes in v9:
time: 147 us; the launch traced here: 146 us
  waiting for transfers between devices  80.3 us (55%)
  Pallas kernels  26.8 us (18%)
  starting transfers between devices  21 us (14%)
  local copies, waits for them, and re-layouts  16.5 us (11%)
    ppermute x16, waiting for transfers between devices, shifted(): return lax.ppermute(value, 'replica', pairs)  80.3 us
    pallas_call x8, Pallas kernels, update(): pl.pallas_call(functools.partial(update_kernel, groups), grid_spec=pltpu....  23.6 us
    ppermute x16, starting transfers between devices, shifted(): return lax.ppermute(value, 'replica', pairs)  21 us
    dynamic_update_slice x8, local copies, waits for them, and re-layouts, on_device(): lax.dynamic_update_slice(weights, block, (chunk.lo, source * owned + chun...  10.3 us
    dynamic_slice x3, local copies, waits for them, and re-layouts, rows_for(): lax.dynamic_slice(array, (chunk.lo, target * owned + chunk.row, 0), sizes)  5.57 us
  transfers between devices with their start and end apart: 16, of which 9 were waited for; matrix products, arithmetic and copies ran while one was open for 8% of the time, Pallas kernels for 18%

profile of v9, /device:TPU:0, one launch (start us, length us, event | category | flops | bytes accessed | tf_op | source)
XLA Modules:
  0.0 146.0 jit_solution(12668814300583594436)
XLA Ops:
  1.6 2.9 %constant_dynamic-slice_fusion = (bf16[1,256,1024]{2,1,0:T(8,128)(2,1)}, bf16[1,256,1024]{2,1,0:T(8,128)(2,1)}, bf16[1,256,1024]{2,1,0:T(8,128)(2,1)}, bf16[1,256,1024]{2,1,0:T(8,128)(2,1)}) fusion(bf16[6,512,1024]{2,1,0:T(8,128)(2,1)} %bitcast.8, s32[]{:T(128)S(6)} %select_n.51), kind=kLoop, calls=%fused_computation.8 | loop fusion | bytes 4194308 | tf_op jit(solution)/shard_map/dynamic_slice | solution.py:223
  4.5 2.9 %collective-permute-start.6 = (bf16[1,256,1024]{2,1,0:T(8,128)(2,1)}, bf16[1,256,1024]{2,1,0:T(8,128)(2,1)S(1)}, u32[]{:S(2)}, u32[]{:S(2)}) collective-permute-start(bf16[1,256,1024]{2,1,0:T(8,128)(2,1)} %get-tuple-element.56), channel_id=1, source_target_pairs={{0,16},{16,0},{1,17},{17,1},{2,18},{18,2},{3,19},{19,3},{4,20},{20... | collective-permute-start | bytes 1572872 | tf_op jit(solution)/shard_map/ppermute | solution.py:201
  9.1 2.1 %collective-permute-start = (bf16[1040,128]{1,0:T(8,128)(2,1)S(1)}, bf16[1040,128]{1,0:T(8,128)(2,1)S(1)}, u32[]{:S(2)}, u32[]{:S(2)}) collective-permute-start(bf16[1040,128]{1,0:T(8,128)(2,1)S(1)} %pack.1), channel_id=1, source_target_pairs={{0,16},{16,0},{1,17},{17,1},{2,18},{18,2},{3,19},{19,3},{4,20},{20... | collective-permute-start | bytes 798728 | tf_op jit(solution)/shard_map/ppermute | solution.py:201
  11.3 1.9 %collective-permute-start.4 = (bf16[1,256,1024]{2,1,0:T(8,128)(2,1)}, bf16[1,256,1024]{2,1,0:T(8,128)(2,1)S(1)}, u32[]{:S(2)}, u32[]{:S(2)}) collective-permute-start(bf16[1,256,1024]{2,1,0:T(8,128)(2,1)} %get-tuple-element.58), channel_id=1, source_target_pairs={{0,16},{16,0},{1,17},{17,1},{2,18},{18,2},{3,19},{19,3},{4,20},{20... | collective-permute-start | bytes 1572872 | tf_op jit(solution)/shard_map/ppermute | solution.py:201
  13.2 12.8 %collective-permute-done.7.refs_0_ = bf16[1,128,1024]{2,1,0:T(8,128)(2,1)S(1)} collective-permute-done((bf16[1,128,1024]{2,1,0:T(8,128)(2,1)S(1)}, bf16[1,128,1024]{2,1,0:T(8,128)(2,1)S(1)}, u32[]{:S(2)}, u32[]{:S(2)}) %collective-permute-start.7) | collective-permute-done | bytes 262176 | tf_op jit(solution)/shard_map/ppermute | solution.py:201
  26.0 2.1 %collective-permute-start.3 = (bf16[1,256,1024]{2,1,0:T(8,128)(2,1)}, bf16[1,256,1024]{2,1,0:T(8,128)(2,1)S(1)}, u32[]{:S(2)}, u32[]{:S(2)}) collective-permute-start(bf16[1,256,1024]{2,1,0:T(8,128)(2,1)} %get-tuple-element.59), channel_id=1, source_target_pairs={{0,16},{16,0},{1,17},{17,1},{2,18},{18,2},{3,19},{19,3},{4,20},{20... | collective-permute-start | bytes 1572872 | tf_op jit(solution)/shard_map/ppermute | solution.py:201
  28.1 1.8 %constant_dynamic-slice_fusion.4 = bf16[1,192,1024]{2,1,0:T(8,128)(2,1)} fusion(bf16[6,512,1024]{2,1,0:T(8,128)(2,1)} %bitcast.10, s32[]{:T(128)S(6)} %select_n.51), kind=kLoop, calls=%fused_computation.12 | loop fusion | bytes 786436 | tf_op jit(solution)/shard_map/dynamic_slice | solution.py:223
  29.9 1.9 %collective-permute-done.refs_0_ = bf16[1040,128]{1,0:T(8,128)(2,1)S(1)} collective-permute-done((bf16[1040,128]{1,0:T(8,128)(2,1)S(1)}, bf16[1040,128]{1,0:T(8,128)(2,1)S(1)}, u32[]{:S(2)}, u32[]{:S(2)}) %collective-permute-start) | collective-permute-done | bytes 266272 | tf_op jit(solution)/shard_map/ppermute | solution.py:201
  31.7 2.1 %collective-permute-start.2 = (bf16[1,192,1024]{2,1,0:T(8,128)(2,1)}, bf16[1,192,1024]{2,1,0:T(8,128)(2,1)S(1)}, u32[]{:S(2)}, u32[]{:S(2)}) collective-permute-start(bf16[1,192,1024]{2,1,0:T(8,128)(2,1)} %constant_dynamic-slice_fusion.4), channel_id=1, source_target_pairs={{0,16},{16,0},{1,17},{17,1},{2,18},{18,2},{3,19},{19,3},{4,20},{20... | collective-permute-start | bytes 1179656 | tf_op jit(solution)/shard_map/ppermute | solution.py:201
  36.9 2.3 %update.8 = (bf16[1,128,1024]{2,1,0:T(8,128)(2,1)S(1)}, bf16[6,512,1024]{2,1,0:T(8,128)(2,1)}, f32[6,256,1024]{2,1,0:T(8,128)}) custom-call(s32[1]{0:T(128)} %bitcast.me_ref, f32[2]{0:T(128)S(1)} %copy-done.2, bf16[6,512,1024]{2,1,0:T(8,128)(2,1)} %bitcast.20, bf16[6,512,1024]{2,1,0:T(8,128)(2,1)} %bitcast.12, ...), custom_call_target="tpu_custom_call" | custom-call | flops 1572864 | bytes 2359296 | tf_op jit(solution)/shard_map/update/pallas_call | solution.py:171
  39.2 5.2 %update.9 = (bf16[1,128,1024]{2,1,0:T(8,128)(2,1)S(1)}, bf16[6,512,1024]{2,1,0:T(8,128)(2,1)}, f32[6,256,1024]{2,1,0:T(8,128)}) custom-call(s32[1]{0:T(128)} %bitcast.me_ref, f32[2]{0:T(128)S(1)} %copy-done.2, bf16[6,512,1024]{2,1,0:T(8,128)(2,1)} %bitcast.21, bf16[6,512,1024]{2,1,0:T(8,128)(2,1)} %bitcast.13, ...), custom_call_target="tpu_custom_call", output_to_operand_aliasing={{1}: (6, {}), {2}: (7, {})} | custom-call | flops 1572864 | bytes 2359296 | tf_op jit(solution)/shard_map/update/pallas_call | solution.py:171
  44.4 2.8 %update.10 = (bf16[1,256,1024]{2,1,0:T(8,128)(2,1)}, bf16[6,512,1024]{2,1,0:T(8,128)(2,1)}, f32[6,256,1024]{2,1,0:T(8,128)}) custom-call(s32[1]{0:T(128)} %bitcast.me_ref, f32[2]{0:T(128)S(1)} %copy-done.2, bf16[6,512,1024]{2,1,0:T(8,128)(2,1)} %bitcast.22, bf16[6,512,1024]{2,1,0:T(8,128)(2,1)} %bitcast.14, ...), custom_call_target="tpu_custom_call", output_to_operand_aliasing={{1}: (6, {}), {2}: (7, {})} | custom-call | flops 3145728 | bytes 4718592 | tf_op jit(solution)/shard_map/update/pallas_call | solution.py:171
  47.2 28.7 %collective-permute-done.1.refs_0_ = bf16[1,64,1024]{2,1,0:T(8,128)(2,1)S(1)} collective-permute-done((bf16[1,64,1024]{2,1,0:T(8,128)(2,1)S(1)}, bf16[1,64,1024]{2,1,0:T(8,128)(2,1)S(1)}, u32[]{:S(2)}, u32[]{:S(2)}) %collective-permute-start.1) | collective-permute-done | bytes 131104 | tf_op jit(solution)/shard_map/ppermute | solution.py:201
  75.9 1.7 %collective-permute-start.10 = (bf16[1,256,1024]{2,1,0:T(8,128)(2,1)}, bf16[1,256,1024]{2,1,0:T(8,128)(2,1)}, u32[]{:S(2)}, u32[]{:S(2)}) collective-permute-start(bf16[1,256,1024]{2,1,0:T(8,128)(2,1)} %get-tuple-element.49), channel_id=1, source_target_pairs={{0,16},{16,0},{1,17},{17,1},{2,18},{18,2},{3,19},{19,3},{4,20},{20... | collective-permute-start | bytes 1572872 | tf_op jit(solution)/shard_map/ppermute | solution.py:201
  77.9 2.6 %update.11 = (bf16[1,256,1024]{2,1,0:T(8,128)(2,1)S(1)}, bf16[6,512,1024]{2,1,0:T(8,128)(2,1)}, f32[6,256,1024]{2,1,0:T(8,128)}) custom-call(s32[1]{0:T(128)} %bitcast.me_ref, f32[2]{0:T(128)S(1)} %copy-done.2, bf16[6,512,1024]{2,1,0:T(8,128)(2,1)} %bitcast.23, bf16[6,512,1024]{2,1,0:T(8,128)(2,1)} %bitcast.15, ...), custom_call_target="tpu_custom_call", output_to_operand_aliasing={{1}: (6, {}), {2}: (7, {})} | custom-call | flops 3145728 | bytes 4718592 | tf_op jit(solution)/shard_map/update/pallas_call | solution.py:171
  80.5 1.8 %collective-permute-start.11 = (bf16[1,256,1024]{2,1,0:T(8,128)(2,1)S(1)}, bf16[1,256,1024]{2,1,0:T(8,128)(2,1)}, u32[]{:S(2)}, u32[]{:S(2)}) collective-permute-start(bf16[1,256,1024]{2,1,0:T(8,128)(2,1)S(1)} %get-tuple-element.50), channel_id=1, source_target_pairs={{0,16},{16,0},{1,17},{17,1},{2,18},{18,2},{3,19},{19,3},{4,20},{20... | collective-permute-start | bytes 1572872 | tf_op jit(solution)/shard_map/ppermute | solution.py:201
  82.6 2.6 %update.12 = (bf16[1,256,1024]{2,1,0:T(8,128)(2,1)S(1)}, bf16[6,512,1024]{2,1,0:T(8,128)(2,1)}, f32[6,256,1024]{2,1,0:T(8,128)}) custom-call(s32[1]{0:T(128)} %bitcast.me_ref, f32[2]{0:T(128)S(1)} %copy-done.2, bf16[6,512,1024]{2,1,0:T(8,128)(2,1)} %bitcast.24, bf16[6,512,1024]{2,1,0:T(8,128)(2,1)} %bitcast.16, ...), custom_call_target="tpu_custom_call", output_to_operand_aliasing={{1}: (6, {}), {2}: (7, {})} | custom-call | flops 3145728 | bytes 4718592 | tf_op jit(solution)/shard_map/update/pallas_call | solution.py:171
  85.3 1.8 %collective-permute-start.12 = (bf16[1,256,1024]{2,1,0:T(8,128)(2,1)S(1)}, bf16[1,256,1024]{2,1,0:T(8,128)(2,1)}, u32[]{:S(2)}, u32[]{:S(2)}) collective-permute-start(bf16[1,256,1024]{2,1,0:T(8,128)(2,1)S(1)} %get-tuple-element.51), channel_id=1, source_target_pairs={{0,16},{16,0},{1,17},{17,1},{2,18},{18,2},{3,19},{19,3},{4,20},{20... | collective-permute-start | bytes 1572872 | tf_op jit(solution)/shard_map/ppermute | solution.py:201
  87.1 2.6 %update.13 = (bf16[1,256,1024]{2,1,0:T(8,128)(2,1)S(1)}, bf16[6,512,1024]{2,1,0:T(8,128)(2,1)}, f32[6,256,1024]{2,1,0:T(8,128)}) custom-call(s32[1]{0:T(128)} %bitcast.me_ref, f32[2]{0:T(128)S(1)} %copy-done.3, bf16[6,512,1024]{2,1,0:T(8,128)(2,1)} %bitcast.25, bf16[6,512,1024]{2,1,0:T(8,128)(2,1)} %bitcast.17, ...), custom_call_target="tpu_custom_call", output_to_operand_aliasing={{1}: (6, {}), {2}: (7, {})} | custom-call | flops 3145728 | bytes 4718592 | tf_op jit(solution)/shard_map/update/pallas_call | solution.py:171
  89.7 3.5 %update.14 = (bf16[1,192,1024]{2,1,0:T(8,128)(2,1)S(1)}, bf16[6,512,1024]{2,1,0:T(8,128)(2,1)}, f32[6,256,1024]{2,1,0:T(8,128)}) custom-call(s32[1]{0:T(128)} %bitcast.me_ref, f32[2]{0:T(128)S(1)} %copy-done.3, bf16[6,512,1024]{2,1,0:T(8,128)(2,1)} %bitcast.26, bf16[6,512,1024]{2,1,0:T(8,128)(2,1)} %bitcast.18, ...), custom_call_target="tpu_custom_call", output_to_operand_aliasing={{1}: (6, {}), {2}: (7, {})} | custom-call | flops 2359296 | bytes 3538944 | tf_op jit(solution)/shard_map/update/pallas_call | solution.py:171
  93.2 1.9 %update.15 = (bf16[1,64,1024]{2,1,0:T(8,128)(2,1)S(1)}, bf16[6,512,1024]{2,1,0:T(8,128)(2,1)}, f32[6,256,1024]{2,1,0:T(8,128)}) custom-call(s32[1]{0:T(128)} %bitcast.me_ref, f32[2]{0:T(128)S(1)} %copy-done.3, bf16[6,512,1024]{2,1,0:T(8,128)(2,1)} %bitcast.27, bf16[6,512,1024]{2,1,0:T(8,128)(2,1)} %bitcast.19, ...), custom_call_target="tpu_custom_call", output_to_operand_aliasing={{1}: (6, {}), {2}: (7, {})} | custom-call | flops 786432 | bytes 1179648 | tf_op jit(solution)/shard_map/update/pallas_call | solution.py:171
  95.1 1.4 collective-permute-done.8
  96.5 1.7 %collective-permute-start.13 = (bf16[1,256,1024]{2,1,0:T(8,128)(2,1)S(1)}, bf16[1,256,1024]{2,1,0:T(8,128)(2,1)S(1)}, u32[]{:S(2)}, u32[]{:S(2)}) collective-permute-start(bf16[1,256,1024]{2,1,0:T(8,128)(2,1)S(1)} %get-tuple-element.52), channel_id=1, source_target_pairs={{0,16},{16,0},{1,17},{17,1},{2,18},{18,2},{3,19},{19,3},{4,20},{20... | collective-permute-start | bytes 1572872 | tf_op jit(solution)/shard_map/ppermute | solution.py:201
  99.0 14.5 %collective-permute-done.9 = bf16[1,128,1024]{2,1,0:T(8,128)(2,1)} collective-permute-done((bf16[1,128,1024]{2,1,0:T(8,128)(2,1)S(1)}, bf16[1,128,1024]{2,1,0:T(8,128)(2,1)}, u32[]{:S(2)}, u32[]{:S(2)}) %collective-permute-start.9) | collective-permute-done | bytes 262176 | tf_op jit(solution)/shard_map/ppermute | solution.py:201
  113.5 1.7 %collective-permute-start.14 = (bf16[1,192,1024]{2,1,0:T(8,128)(2,1)S(1)}, bf16[1,192,1024]{2,1,0:T(8,128)(2,1)S(1)}, u32[]{:S(2)}, u32[]{:S(2)}) collective-permute-start(bf16[1,192,1024]{2,1,0:T(8,128)(2,1)S(1)} %get-tuple-element.53), channel_id=1, source_target_pairs={{0,16},{16,0},{1,17},{17,1},{2,18},{18,2},{3,19},{19,3},{4,20},{20... | collective-permute-start | bytes 1179656 | tf_op jit(solution)/shard_map/ppermute | solution.py:201
  115.2 1.7 %constant_dynamic-update-slice_fusion.6 = bf16[6,512,1024]{2,1,0:T(8,128)(2,1)} fusion(bf16[6,512,1024]{2,1,0:T(8,128)(2,1)} %constant_dynamic-update-slice_fusion.7, bf16[1,128,1024]{2,1,0:T(8,128)(2,1)} %collective-permute-done.9, s32[]{:T(128)S(6)} %select_n.54), kind=kLoop, calls=%fused_computation.6 | loop fusion | bytes 524292 | tf_op jit(solution)/shard_map/dynamic_update_slice | solution.py:248
  117.2 1.9 %constant_dynamic-update-slice_fusion.5 = bf16[6,512,1024]{2,1,0:T(8,128)(2,1)} fusion(bf16[6,512,1024]{2,1,0:T(8,128)(2,1)} %constant_dynamic-update-slice_fusion.6, bf16[1,256,1024]{2,1,0:T(8,128)(2,1)} %collective-permute-done.10, s32[]{:T(128)S(6)} %select_n.53), kind=kLoop, calls=%fused_computation.5 | loop fusion | bytes 1048580 | tf_op jit(solution)/shard_map/dynamic_update_slice | solution.py:248
  119.1 1.9 %constant_dynamic-update-slice_fusion.4 = bf16[6,512,1024]{2,1,0:T(8,128)(2,1)} fusion(bf16[6,512,1024]{2,1,0:T(8,128)(2,1)} %constant_dynamic-update-slice_fusion.5, bf16[1,256,1024]{2,1,0:T(8,128)(2,1)} %collective-permute-done.11, s32[]{:T(128)S(6)} %select_n.53), kind=kLoop, calls=%fused_computation.4 | loop fusion | bytes 1048580 | tf_op jit(solution)/shard_map/dynamic_update_slice | solution.py:248
  120.9 3.8 %collective-permute-done.12 = bf16[1,256,1024]{2,1,0:T(8,128)(2,1)} collective-permute-done((bf16[1,256,1024]{2,1,0:T(8,128)(2,1)S(1)}, bf16[1,256,1024]{2,1,0:T(8,128)(2,1)}, u32[]{:S(2)}, u32[]{:S(2)}) %collective-permute-start.12) | collective-permute-done | bytes 524320 | tf_op jit(solution)/shard_map/ppermute | solution.py:201
  124.7 1.9 %constant_dynamic-update-slice_fusion.3 = bf16[6,512,1024]{2,1,0:T(8,128)(2,1)} fusion(bf16[6,512,1024]{2,1,0:T(8,128)(2,1)} %constant_dynamic-update-slice_fusion.4, bf16[1,256,1024]{2,1,0:T(8,128)(2,1)} %collective-permute-done.12, s32[]{:T(128)S(6)} %select_n.53), kind=kLoop, calls=%fused_computation.3 | loop fusion | bytes 1048580 | tf_op jit(solution)/shard_map/dynamic_update_slice | solution.py:248
  126.6 9.3 %collective-permute-done.13 = bf16[1,256,1024]{2,1,0:T(8,128)(2,1)S(1)} collective-permute-done((bf16[1,256,1024]{2,1,0:T(8,128)(2,1)S(1)}, bf16[1,256,1024]{2,1,0:T(8,128)(2,1)S(1)}, u32[]{:S(2)}, u32[]{:S(2)}) %collective-permute-start.13) | collective-permute-done | bytes 524320 | tf_op jit(solution)/shard_map/ppermute | solution.py:201
  136.7 7.3 %collective-permute-done.14 = bf16[1,192,1024]{2,1,0:T(8,128)(2,1)S(1)} collective-permute-done((bf16[1,192,1024]{2,1,0:T(8,128)(2,1)S(1)}, bf16[1,192,1024]{2,1,0:T(8,128)(2,1)S(1)}, u32[]{:S(2)}, u32[]{:S(2)}) %collective-permute-start.14) | collective-permute-done | bytes 393248 | tf_op jit(solution)/shard_map/ppermute | solution.py:201
  (30 shorter events, 9.5 us)
Async XLA Ops:
  4.5 30.2 %collective-permute-start.6 = (bf16[1,256,1024]{2,1,0:T(8,128)(2,1)}, bf16[1,256,1024]{2,1,0:T(8,128)(2,1)S(1)}, u32[]{:S(2)}, u32[]{:S(2)}) collective-permute-start(bf16[1,256,1024]{2,1,0:T(8,128)(2,1)} %get-tuple-element.56), channel_id=1, source_target_pairs={{0,16},{16,0},{1,17},{17,1},{2,18},{18,2},{3,19},{19,3},{4,20},{20... | collective-permute-start | bytes 1572872 | tf_op jit(solution)/shard_map/ppermute | solution.py:201
  7.5 18.6 %collective-permute-start.7 = (bf16[1,128,1024]{2,1,0:T(8,128)(2,1)S(1)}, bf16[1,128,1024]{2,1,0:T(8,128)(2,1)S(1)}, u32[]{:S(2)}, u32[]{:S(2)}) collective-permute-start(bf16[1,128,1024]{2,1,0:T(8,128)(2,1)S(1)} %cut.1), channel_id=1, source_target_pairs={{0,16},{16,0},{1,17},{17,1},{2,18},{18,2},{3,19},{19,3},{4,20},{20... | collective-permute-start | bytes 786440 | tf_op jit(solution)/shard_map/ppermute | solution.py:201
  9.1 22.6 %collective-permute-start = (bf16[1040,128]{1,0:T(8,128)(2,1)S(1)}, bf16[1040,128]{1,0:T(8,128)(2,1)S(1)}, u32[]{:S(2)}, u32[]{:S(2)}) collective-permute-start(bf16[1040,128]{1,0:T(8,128)(2,1)S(1)} %pack.1), channel_id=1, source_target_pairs={{0,16},{16,0},{1,17},{17,1},{2,18},{18,2},{3,19},{19,3},{4,20},{20... | collective-permute-start | bytes 798728 | tf_op jit(solution)/shard_map/ppermute | solution.py:201
  11.2 66.4 %collective-permute-start.5 = (bf16[1,256,1024]{2,1,0:T(8,128)(2,1)}, bf16[1,256,1024]{2,1,0:T(8,128)(2,1)S(1)}, u32[]{:S(2)}, u32[]{:S(2)}) collective-permute-start(bf16[1,256,1024]{2,1,0:T(8,128)(2,1)} %get-tuple-element.57), channel_id=1, source_target_pairs={{0,16},{16,0},{1,17},{17,1},{2,18},{18,2},{3,19},{19,3},{4,20},{20... | collective-permute-start | bytes 1572872 | tf_op jit(solution)/shard_map/ppermute | solution.py:201
  11.3 71.1 %collective-permute-start.4 = (bf16[1,256,1024]{2,1,0:T(8,128)(2,1)}, bf16[1,256,1024]{2,1,0:T(8,128)(2,1)S(1)}, u32[]{:S(2)}, u32[]{:S(2)}) collective-permute-start(bf16[1,256,1024]{2,1,0:T(8,128)(2,1)} %get-tuple-element.58), channel_id=1, source_target_pairs={{0,16},{16,0},{1,17},{17,1},{2,18},{18,2},{3,19},{19,3},{4,20},{20... | collective-permute-start | bytes 1572872 | tf_op jit(solution)/shard_map/ppermute | solution.py:201
  26.0 59.2 %collective-permute-start.3 = (bf16[1,256,1024]{2,1,0:T(8,128)(2,1)}, bf16[1,256,1024]{2,1,0:T(8,128)(2,1)S(1)}, u32[]{:S(2)}, u32[]{:S(2)}) collective-permute-start(bf16[1,256,1024]{2,1,0:T(8,128)(2,1)} %get-tuple-element.59), channel_id=1, source_target_pairs={{0,16},{16,0},{1,17},{17,1},{2,18},{18,2},{3,19},{19,3},{4,20},{20... | collective-permute-start | bytes 1572872 | tf_op jit(solution)/shard_map/ppermute | solution.py:201
  31.7 3.2 %copy-start = (bf16[1040,128]{1,0:T(8,128)(2,1)}, bf16[1040,128]{1,0:T(8,128)(2,1)S(1)}, u32[]{:S(2)}) copy-start(bf16[1040,128]{1,0:T(8,128)(2,1)S(1)} %collective-permute-done.refs_0_) | copy-start | bytes 798724
  31.7 48.8 %collective-permute-start.2 = (bf16[1,192,1024]{2,1,0:T(8,128)(2,1)}, bf16[1,192,1024]{2,1,0:T(8,128)(2,1)S(1)}, u32[]{:S(2)}, u32[]{:S(2)}) collective-permute-start(bf16[1,192,1024]{2,1,0:T(8,128)(2,1)} %constant_dynamic-slice_fusion.4), channel_id=1, source_target_pairs={{0,16},{16,0},{1,17},{17,1},{2,18},{18,2},{3,19},{19,3},{4,20},{20... | collective-permute-start | bytes 1179656 | tf_op jit(solution)/shard_map/ppermute | solution.py:201
  34.7 41.1 %collective-permute-start.1 = (bf16[1,64,1024]{2,1,0:T(8,128)(2,1)S(1)}, bf16[1,64,1024]{2,1,0:T(8,128)(2,1)S(1)}, u32[]{:S(2)}, u32[]{:S(2)}) collective-permute-start(bf16[1,64,1024]{2,1,0:T(8,128)(2,1)S(1)} %constant_dynamic-slice_fusion.5), channel_id=1, source_target_pairs={{0,16},{16,0},{1,17},{17,1},{2,18},{18,2},{3,19},{19,3},{4,20},{20... | collective-permute-start | bytes 393224 | tf_op jit(solution)/shard_map/ppermute | solution.py:201
  36.2 0.7 copy-start.2
  36.8 2.3 %copy-start.1 = (bf16[1040,128]{1,0:T(8,128)(2,1)S(1)}, bf16[1040,128]{1,0:T(8,128)(2,1)}, u32[]{:S(2)}) copy-start(bf16[1040,128]{1,0:T(8,128)(2,1)} %copy-done) | copy-start | bytes 798724
  75.9 41.1 %collective-permute-start.10 = (bf16[1,256,1024]{2,1,0:T(8,128)(2,1)}, bf16[1,256,1024]{2,1,0:T(8,128)(2,1)}, u32[]{:S(2)}, u32[]{:S(2)}) collective-permute-start(bf16[1,256,1024]{2,1,0:T(8,128)(2,1)} %get-tuple-element.49), channel_id=1, source_target_pairs={{0,16},{16,0},{1,17},{17,1},{2,18},{18,2},{3,19},{19,3},{4,20},{20... | collective-permute-start | bytes 1572872 | tf_op jit(solution)/shard_map/ppermute | solution.py:201
  77.6 18.9 %collective-permute-start.8 = (bf16[1,128,1024]{2,1,0:T(8,128)(2,1)S(1)}, bf16[1,128,1024]{2,1,0:T(8,128)(2,1)S(1)}, u32[]{:S(2)}, u32[]{:S(2)}) collective-permute-start(bf16[1,128,1024]{2,1,0:T(8,128)(2,1)S(1)} %get-tuple-element.47), channel_id=1, source_target_pairs={{0,16},{16,0},{1,17},{17,1},{2,18},{18,2},{3,19},{19,3},{4,20},{20... | collective-permute-start | bytes 786440 | tf_op jit(solution)/shard_map/ppermute | solution.py:201
  80.5 38.5 %collective-permute-start.11 = (bf16[1,256,1024]{2,1,0:T(8,128)(2,1)S(1)}, bf16[1,256,1024]{2,1,0:T(8,128)(2,1)}, u32[]{:S(2)}, u32[]{:S(2)}) collective-permute-start(bf16[1,256,1024]{2,1,0:T(8,128)(2,1)S(1)} %get-tuple-element.50), channel_id=1, source_target_pairs={{0,16},{16,0},{1,17},{17,1},{2,18},{18,2},{3,19},{19,3},{4,20},{20... | collective-permute-start | bytes 1572872 | tf_op jit(solution)/shard_map/ppermute | solution.py:201
  82.3 31.2 %collective-permute-start.9 = (bf16[1,128,1024]{2,1,0:T(8,128)(2,1)S(1)}, bf16[1,128,1024]{2,1,0:T(8,128)(2,1)}, u32[]{:S(2)}, u32[]{:S(2)}) collective-permute-start(bf16[1,128,1024]{2,1,0:T(8,128)(2,1)S(1)} %get-tuple-element.48), channel_id=1, source_target_pairs={{0,16},{16,0},{1,17},{17,1},{2,18},{18,2},{3,19},{19,3},{4,20},{20... | collective-permute-start | bytes 786440 | tf_op jit(solution)/shard_map/ppermute | solution.py:201
  82.6 4.4 %copy-start.3 = (f32[2]{0:T(128)S(1)}, f32[2]{0:T(128)}, u32[]{:S(2)}) copy-start(f32[2]{0:T(128)} %share.1.shares_ref) | copy-start | bytes 28
  85.3 39.5 %collective-permute-start.12 = (bf16[1,256,1024]{2,1,0:T(8,128)(2,1)S(1)}, bf16[1,256,1024]{2,1,0:T(8,128)(2,1)}, u32[]{:S(2)}, u32[]{:S(2)}) collective-permute-start(bf16[1,256,1024]{2,1,0:T(8,128)(2,1)S(1)} %get-tuple-element.51), channel_id=1, source_target_pairs={{0,16},{16,0},{1,17},{17,1},{2,18},{18,2},{3,19},{19,3},{4,20},{20... | collective-permute-start | bytes 1572872 | tf_op jit(solution)/shard_map/ppermute | solution.py:201
  96.5 39.3 %collective-permute-start.13 = (bf16[1,256,1024]{2,1,0:T(8,128)(2,1)S(1)}, bf16[1,256,1024]{2,1,0:T(8,128)(2,1)S(1)}, u32[]{:S(2)}, u32[]{:S(2)}) collective-permute-start(bf16[1,256,1024]{2,1,0:T(8,128)(2,1)S(1)} %get-tuple-element.52), channel_id=1, source_target_pairs={{0,16},{16,0},{1,17},{17,1},{2,18},{18,2},{3,19},{19,3},{4,20},{20... | collective-permute-start | bytes 1572872 | tf_op jit(solution)/shard_map/ppermute | solution.py:201
  113.5 30.4 %collective-permute-start.14 = (bf16[1,192,1024]{2,1,0:T(8,128)(2,1)S(1)}, bf16[1,192,1024]{2,1,0:T(8,128)(2,1)S(1)}, u32[]{:S(2)}, u32[]{:S(2)}) collective-permute-start(bf16[1,192,1024]{2,1,0:T(8,128)(2,1)S(1)} %get-tuple-element.53), channel_id=1, source_target_pairs={{0,16},{16,0},{1,17},{17,1},{2,18},{18,2},{3,19},{19,3},{4,20},{20... | collective-permute-start | bytes 1179656 | tf_op jit(solution)/shard_map/ppermute | solution.py:201
  116.9 28.4 %collective-permute-start.15 = (bf16[1,64,1024]{2,1,0:T(8,128)(2,1)S(1)}, bf16[1,64,1024]{2,1,0:T(8,128)(2,1)S(1)}, u32[]{:S(2)}, u32[]{:S(2)}) collective-permute-start(bf16[1,64,1024]{2,1,0:T(8,128)(2,1)S(1)} %get-tuple-element.54), channel_id=1, source_target_pairs={{0,16},{16,0},{1,17},{17,1},{2,18},{18,2},{3,19},{19,3},{4,20},{20... | collective-permute-start | bytes 393224 | tf_op jit(solution)/shard_map/ppermute | solution.py:201

commit v10 on v4

--- a/solution.py
+++ b/solution.py
@@ -1,4 +1,6 @@
 import functools
+import math
+from typing import NamedTuple
 
 import jax
 import jax.numpy as jnp
@@ -9,7 +11,41 @@
 
 outer_rate = 0.7
 momentum_rate = 0.9
+spare = 16
 vmem_bytes = 48 * 1024 * 1024
+
+
+class Chunk(NamedTuple):
+    lo: int
+    parts: int
+    row: int
+    rows: int
+
+
+def cut_kernel(groups, owned, chunk, shift, inner_ref, out_ref, sem):
+    target = lax.rem(lax.axis_index("replica") + shift, groups)
+    start = pl.multiple_of(target * owned + chunk.row, spare)
+    copy = pltpu.make_async_copy(
+        inner_ref.at[pl.ds(chunk.lo, chunk.parts), pl.ds(start, chunk.rows), :], out_ref, sem
+    )
+    copy.start()
+    copy.wait()
+
+
+def cut(groups, owned, chunk, shift, inner):
+    shape = (chunk.parts, chunk.rows, inner.shape[2])
+    return pl.pallas_call(
+        functools.partial(cut_kernel, groups, owned, chunk, shift),
+        in_specs=[pl.BlockSpec(memory_space=pl.ANY)],
+        out_specs=pl.BlockSpec(memory_space=pltpu.VMEM),
+        out_shape=jax.ShapeDtypeStruct(shape, inner.dtype),
+        scratch_shapes=[pltpu.SemaphoreType.DMA],
+        compiler_params=pltpu.CompilerParams(vmem_limit_bytes=vmem_bytes),
+        cost_estimate=pl.CostEstimate(
+            flops=0, bytes_accessed=4 * math.prod(shape), transcendentals=0
+        ),
+        name="cut",
+    )(inner)
 
 
 def share_kernel(*refs):
@@ -48,30 +84,34 @@
 
 
 def update(groups, chunk, me, shares, anchor, inner, arrived, momentum, held):
-    lo, hi = chunk
-    parts, owned, width = momentum.shape
-    rows = min(owned, 128)
-    steps = owned // rows
-    block = (1, rows, width)
+    _, owned, width = momentum.shape
+    lo, row, rows = chunk.lo, chunk.row, chunk.rows
+    tall = math.gcd(row, rows, owned, 128)
+    grid = (chunk.parts, rows // tall)
+    block = (1, tall, width)
+    ahead, mine = row // tall, owned // tall
+    came = pl.BlockSpec(block, lambda p, r, me_ref: (p, r, 0))
+    packed = came
+    spread = pl.BlockSpec(
+        block, lambda p, r, me_ref: (lo + p, me_ref[0] * mine + ahead + r, 0)
+    )
+    kept = pl.BlockSpec(block, lambda p, r, me_ref: (lo + p, ahead + r, 0))
     scalar = pl.BlockSpec(memory_space=pltpu.SMEM)
-    spread = pl.BlockSpec(block, lambda p, r, me_ref: (lo + p, me_ref[0] * steps + r, 0))
-    packed = pl.BlockSpec(block, lambda p, r, me_ref: (p, r, 0))
-    kept = pl.BlockSpec(block, lambda p, r, me_ref: (lo + p, r, 0))
     aliases = {groups + 4: 1, groups + 5: 2} if held else {}
-    size = (hi - lo) * owned * width
+    size = chunk.parts * rows * width
     return pl.pallas_call(
         functools.partial(update_kernel, groups),
         grid_spec=pltpu.PrefetchScalarGridSpec(
             num_scalar_prefetch=1,
-            grid=(hi - lo, steps),
+            grid=grid,
             in_specs=[scalar, spread, spread]
-            + [packed] * (groups - 1)
+            + [came] * (groups - 1)
             + [kept]
             + [pl.BlockSpec(memory_space=pl.ANY)] * len(held),
             out_specs=[packed, spread, kept],
         ),
         out_shape=[
-            jax.ShapeDtypeStruct((hi - lo, owned, width), jnp.bfloat16),
+            jax.ShapeDtypeStruct((chunk.parts, rows, width), jnp.bfloat16),
             jax.ShapeDtypeStruct(anchor.shape, jnp.bfloat16),
             jax.ShapeDtypeStruct(momentum.shape, jnp.float32),
         ],
@@ -84,29 +124,29 @@
     )(me, shares, anchor, inner, *arrived, momentum, *held)
 
 
-def place_kernel(lo, at_ref, block_ref, _, weights_ref, sem):
-    parts, owned, _ = block_ref.shape
-    start = pl.multiple_of(at_ref[0] * owned, owned)
+def place_kernel(groups, owned, chunk, shift, block_ref, _, weights_ref, sem):
+    source = lax.rem(lax.axis_index("replica") + groups - shift, groups)
+    start = pl.multiple_of(source * owned + chunk.row, spare)
     copy = pltpu.make_async_copy(
-        block_ref, weights_ref.at[pl.ds(lo, parts), pl.ds(start, owned), :], sem
+        block_ref, weights_ref.at[pl.ds(chunk.lo, chunk.parts), pl.ds(start, chunk.rows), :], sem
     )
     copy.start()
     copy.wait()
 
 
-def place(chunk, at, block, weights):
+def place(groups, owned, chunk, shift, block, weights):
     anywhere = pl.BlockSpec(memory_space=pl.ANY)
     return pl.pallas_call(
-        functools.partial(place_kernel, chunk[0]),
-        in_specs=[pl.BlockSpec(memory_space=pltpu.SMEM), anywhere, anywhere],
+        functools.partial(place_kernel, groups, owned, chunk, shift),
+        in_specs=[anywhere, anywhere],
         out_specs=anywhere,
         out_shape=jax.ShapeDtypeStruct(weights.shape, weights.dtype),
         scratch_shapes=[pltpu.SemaphoreType.DMA],
-        input_output_aliases={2: 0},
+        input_output_aliases={1: 0},
         compiler_params=pltpu.CompilerParams(vmem_limit_bytes=vmem_bytes),
         cost_estimate=pl.CostEstimate(flops=0, bytes_accessed=4 * block.size, transcendentals=0),
         name="place",
-    )(at, block, weights)
+    )(block, weights)
 
 
 def solution(mesh):
@@ -124,20 +164,25 @@
         anchor = anchor.reshape(parts, *shape[-2:])
         momentum = momentum.reshape(parts, owned, width)
         me = lax.axis_index("replica")
-        chunks = [(p, p + 1) for p in range(parts)]
+        middle = (parts - 2) // 2
+        chunks = [
+            Chunk(1, middle, 0, owned),
+            Chunk(1 + middle, parts - 2 - middle, 0, owned),
+            Chunk(0, 1, 0, owned),
+            Chunk(parts - 1, 1, 0, owned),
+        ]
         shifts = range(1, groups)
 
         def rows_for(array, chunk, target):
-            sizes = (chunk[1] - chunk[0], owned, width)
-            return lax.dynamic_slice(array, (chunk[0], target * owned, 0), sizes)
-
-        other_counts = [shifted(counts, s) for s in shifts]
+            sizes = (chunk.parts, chunk.rows, width)
+            return lax.dynamic_slice(array, (chunk.lo, target * owned + chunk.row, 0), sizes)
+
         targets = [(me + s) % groups for s in shifts]
-        first = [rows_for(inner, chunks[0], t) for t in targets]
-        first, rest, other_counts = lax.optimization_barrier((first, inner, other_counts))
-        shares = share([counts] + other_counts)
+        first = [cut(groups, owned, chunks[0], s, inner) for s in shifts]
+        first, rest, later_counts = lax.optimization_barrier((first, inner, counts))
         sent = [first] + [[rows_for(rest, c, t) for t in targets] for c in chunks[1:]]
         arrived = [[shifted(v, s) for v, s in zip(values, shifts)] for values in sent]
+        shares = share([counts] + [shifted(later_counts, s) for s in shifts])
 
         where = me.reshape(1).astype(jnp.int32)
         held = []
@@ -150,8 +195,7 @@
         weights, moments = held
         for chunk, blocks in zip(chunks, travelled):
             for s, block in zip(shifts, blocks):
-                source = ((me - s) % groups).reshape(1).astype(jnp.int32)
-                weights = place(chunk, source, block, weights)
+                weights = place(groups, owned, chunk, s, block, weights)
         return weights.reshape(shape), moments.reshape(*shape[:2], owned, width)
 
     placed = (

time: 143 us -> 142 us (level)
  waiting for transfers between devices: 90.5 us -> 101 us
  starting transfers between devices: 23.2 us -> 13.2 us
  Pallas kernels: 22.6 us -> 20.9 us
    ppermute x13 -> x9, waiting for transfers between devices: 90.5 us -> 101 us  [shifted(): return lax.ppermute(value, 'replica', pairs)]
    ppermute x13 -> x9, starting transfers between devices: 23.2 us -> 13.2 us  [shifted(): return lax.ppermute(value, 'replica', pairs)]
    pallas_call x6 -> x4, Pallas kernels: 16.7 us -> 15 us  [update(): pl.pallas_call(functools.partial(update_kernel, groups), grid_spec=pltpu....]
    pallas_call x6 -> x5, Pallas kernels: 4.8 us -> 4.8 us  [the longest x4 3.56 us: place(): pl.pallas_call(functools.partial(place_kernel, groups, owned, chunk, shif...]
  transfers between devices with their start and end apart: 13 -> 9, of which waited for: 13 -> 6; matrix products, arithmetic and copies ran while one was open for 3% -> 3% of each run, Pallas kernels for 15% -> 13%
where the time goes in v10:
time: 142 us; the launch traced here: 141 us
  waiting for transfers between devices  101 us (71%)
  Pallas kernels  20.9 us (15%)
  starting transfers between devices  13.2 us (9%)
  local copies, waits for them, and re-layouts  5.19 us (4%)
    ppermute x9, waiting for transfers between devices, shifted(): return lax.ppermute(value, 'replica', pairs)  101 us
    pallas_call x4, Pallas kernels, update(): pl.pallas_call(functools.partial(update_kernel, groups), grid_spec=pltpu....  15 us
    ppermute x9, starting transfers between devices, shifted(): return lax.ppermute(value, 'replica', pairs)  13.2 us
    dynamic_slice x2, local copies, waits for them, and re-layouts, rows_for(): lax.dynamic_slice(array, (chunk.lo, target * owned + chunk.row, 0), sizes)  4.54 us
    pallas_call x4, Pallas kernels, place(): pl.pallas_call(functools.partial(place_kernel, groups, owned, chunk, shif...  3.56 us
  transfers between devices with their start and end apart: 9, of which 6 were waited for; matrix products, arithmetic and copies ran while one was open for 3% of the time, Pallas kernels for 13%

profile of v10, /device:TPU:0, one launch (start us, length us, event | category | flops | bytes accessed | tf_op | source)
XLA Modules:
  0.0 141.2 jit_solution(15011345642422770618)
XLA Ops:
  0.6 1.2 cut.1
  1.9 3.0 %collective-permute-start.4 = (bf16[2,256,1024]{2,1,0:T(8,128)(2,1)S(1)}, bf16[2,256,1024]{2,1,0:T(8,128)(2,1)S(1)}, u32[]{:S(2)}, u32[]{:S(2)}) collective-permute-start(bf16[2,256,1024]{2,1,0:T(8,128)(2,1)S(1)} %cut.1), channel_id=1, source_target_pairs={{0,16},{16,0},{1,17},{17,1},{2,18},{18,2},{3,19},{19,3},{4,20},{20... | collective-permute-start | bytes 3145736 | tf_op jit(solution)/shard_map/ppermute | solution.py:157
  4.9 2.3 %constant_dynamic-slice_fusion = bf16[2,256,1024]{2,1,0:T(8,128)(2,1)} fusion(bf16[6,512,1024]{2,1,0:T(8,128)(2,1)} %bitcast.8, s32[]{:T(128)S(6)} %select_n.13), kind=kLoop, calls=%fused_computation | loop fusion | bytes 2097156 | tf_op jit(solution)/shard_map/dynamic_slice | solution.py:178
  7.2 0.0 collective-permute-start.3
  7.2 2.0 %collective-permute-start = (s32[1]{0:T(128)}, s32[1]{0:T(128)}, u32[]{:S(2)}, u32[]{:S(2)}) collective-permute-start(s32[1]{0:T(128)} %param.4), channel_id=1, source_target_pairs={{0,16},{16,0},{1,17},{17,1},{2,18},{18,2},{3,19},{19,3},{4,20},{20... | collective-permute-start | bytes 20 | tf_op jit(solution)/shard_map/ppermute | solution.py:157
  9.2 2.3 %constant_dynamic-slice_fusion.1 = (bf16[1,256,1024]{2,1,0:T(8,128)(2,1)}, bf16[1,256,1024]{2,1,0:T(8,128)(2,1)}) fusion(bf16[6,512,1024]{2,1,0:T(8,128)(2,1)} %bitcast.9, s32[]{:T(128)S(6)} %select_n.13), kind=kLoop, calls=%fused_computation.1 | loop fusion | bytes 2097156 | tf_op jit(solution)/shard_map/dynamic_slice | solution.py:178
  11.5 0.0 collective-permute-start.2
  11.5 2.0 %collective-permute-start.1 = (bf16[1,256,1024]{2,1,0:T(8,128)(2,1)}, bf16[1,256,1024]{2,1,0:T(8,128)(2,1)}, u32[]{:S(2)}, u32[]{:S(2)}) collective-permute-start(bf16[1,256,1024]{2,1,0:T(8,128)(2,1)} %get-tuple-element.33), channel_id=1, source_target_pairs={{0,16},{16,0},{1,17},{17,1},{2,18},{18,2},{3,19},{19,3},{4,20},{20... | collective-permute-start | bytes 1572872 | tf_op jit(solution)/shard_map/ppermute | solution.py:157
  14.1 37.3 %collective-permute-done.refs_1_ = s32[1]{0:T(128)} collective-permute-done((s32[1]{0:T(128)}, s32[1]{0:T(128)}, u32[]{:S(2)}, u32[]{:S(2)}) %collective-permute-start) | collective-permute-done | bytes 36 | tf_op jit(solution)/shard_map/ppermute | solution.py:157
  51.4 1.1 share.1.shares_ref
  52.6 0.0 collective-permute-done.4.refs_0_
  52.6 0.0 copy-start
  52.6 0.6 copy-done
  53.2 4.7 %update.4 = (bf16[2,256,1024]{2,1,0:T(8,128)(2,1)S(1)}, bf16[6,512,1024]{2,1,0:T(8,128)(2,1)}, f32[6,256,1024]{2,1,0:T(8,128)}) custom-call(s32[1]{0:T(128)} %bitcast.me_ref, f32[2]{0:T(128)S(1)} %copy-done, bf16[6,512,1024]{2,1,0:T(8,128)(2,1)} %bitcast.14, bf16[6,512,1024]{2,1,0:T(8,128)(2,1)} %bitcast.10, ...), custom_call_target="tpu_custom_call" | custom-call | flops 6291456 | bytes 9437184 | tf_op jit(solution)/shard_map/update/pallas_call | solution.py:102
  57.9 2.1 %collective-permute-start.8 = (bf16[2,256,1024]{2,1,0:T(8,128)(2,1)S(1)}, bf16[2,256,1024]{2,1,0:T(8,128)(2,1)S(1)}, u32[]{:S(2)}, u32[]{:S(2)}) collective-permute-start(bf16[2,256,1024]{2,1,0:T(8,128)(2,1)S(1)} %get-tuple-element.29), channel_id=1, source_target_pairs={{0,16},{16,0},{1,17},{17,1},{2,18},{18,2},{3,19},{19,3},{4,20},{20... | collective-permute-start | bytes 3145736 | tf_op jit(solution)/shard_map/ppermute | solution.py:157
  60.0 0.0 collective-permute-done.3.refs_0_
  60.0 4.7 %update.5 = (bf16[2,256,1024]{2,1,0:T(8,128)(2,1)S(1)}, bf16[6,512,1024]{2,1,0:T(8,128)(2,1)}, f32[6,256,1024]{2,1,0:T(8,128)}) custom-call(s32[1]{0:T(128)} %bitcast.me_ref, f32[2]{0:T(128)S(1)} %copy-done, bf16[6,512,1024]{2,1,0:T(8,128)(2,1)} %bitcast.15, bf16[6,512,1024]{2,1,0:T(8,128)(2,1)} %bitcast.11, ...), custom_call_target="tpu_custom_call", output_to_operand_aliasing={{1}: (6, {}), {2}: (7, {})} | custom-call | flops 6291456 | bytes 9437184 | tf_op jit(solution)/shard_map/update/pallas_call | solution.py:102
  64.7 0.0 collective-permute-start.7
  64.7 0.0 collective-permute-done.2.refs_0_
  64.7 2.8 %update.6 = (bf16[1,256,1024]{2,1,0:T(8,128)(2,1)S(1)}, bf16[6,512,1024]{2,1,0:T(8,128)(2,1)}, f32[6,256,1024]{2,1,0:T(8,128)}) custom-call(s32[1]{0:T(128)} %bitcast.me_ref, f32[2]{0:T(128)S(1)} %copy-done, bf16[6,512,1024]{2,1,0:T(8,128)(2,1)} %bitcast.16, bf16[6,512,1024]{2,1,0:T(8,128)(2,1)} %bitcast.12, ...), custom_call_target="tpu_custom_call", output_to_operand_aliasing={{1}: (6, {}), {2}: (7, {})} | custom-call | flops 3145728 | bytes 4718592 | tf_op jit(solution)/shard_map/update/pallas_call | solution.py:102
  67.5 2.0 %collective-permute-start.6 = (bf16[1,256,1024]{2,1,0:T(8,128)(2,1)S(1)}, bf16[1,256,1024]{2,1,0:T(8,128)(2,1)S(1)}, u32[]{:S(2)}, u32[]{:S(2)}) collective-permute-start(bf16[1,256,1024]{2,1,0:T(8,128)(2,1)S(1)} %get-tuple-element.27), channel_id=1, source_target_pairs={{0,16},{16,0},{1,17},{17,1},{2,18},{18,2},{3,19},{19,3},{4,20},{20... | collective-permute-start | bytes 1572872 | tf_op jit(solution)/shard_map/ppermute | solution.py:157
  69.5 4.4 %collective-permute-done.1.refs_0_ = bf16[1,256,1024]{2,1,0:T(8,128)(2,1)} collective-permute-done((bf16[1,256,1024]{2,1,0:T(8,128)(2,1)}, bf16[1,256,1024]{2,1,0:T(8,128)(2,1)}, u32[]{:S(2)}, u32[]{:S(2)}) %collective-permute-start.1) | collective-permute-done | bytes 524320 | tf_op jit(solution)/shard_map/ppermute | solution.py:157
  73.9 2.8 %update.7 = (bf16[1,256,1024]{2,1,0:T(8,128)(2,1)S(1)}, bf16[6,512,1024]{2,1,0:T(8,128)(2,1)}, f32[6,256,1024]{2,1,0:T(8,128)}) custom-call(s32[1]{0:T(128)} %bitcast.me_ref, f32[2]{0:T(128)S(1)} %copy-done, bf16[6,512,1024]{2,1,0:T(8,128)(2,1)} %bitcast.17, bf16[6,512,1024]{2,1,0:T(8,128)(2,1)} %bitcast.13, ...), custom_call_target="tpu_custom_call", output_to_operand_aliasing={{1}: (6, {}), {2}: (7, {})} | custom-call | flops 3145728 | bytes 4718592 | tf_op jit(solution)/shard_map/update/pallas_call | solution.py:102
  76.7 2.1 %collective-permute-start.5 = (bf16[1,256,1024]{2,1,0:T(8,128)(2,1)S(1)}, bf16[1,256,1024]{2,1,0:T(8,128)(2,1)S(1)}, u32[]{:S(2)}, u32[]{:S(2)}) collective-permute-start(bf16[1,256,1024]{2,1,0:T(8,128)(2,1)S(1)} %get-tuple-element.26), channel_id=1, source_target_pairs={{0,16},{16,0},{1,17},{17,1},{2,18},{18,2},{3,19},{19,3},{4,20},{20... | collective-permute-start | bytes 1572872 | tf_op jit(solution)/shard_map/ppermute | solution.py:157
  78.8 17.5 %collective-permute-done.8.block_ref = bf16[2,256,1024]{2,1,0:T(8,128)(2,1)S(1)} collective-permute-done((bf16[2,256,1024]{2,1,0:T(8,128)(2,1)S(1)}, bf16[2,256,1024]{2,1,0:T(8,128)(2,1)S(1)}, u32[]{:S(2)}, u32[]{:S(2)}) %collective-permute-start.8) | collective-permute-done | bytes 1048608 | tf_op jit(solution)/shard_map/ppermute | solution.py:157
  96.3 1.0 place.4._
  97.3 21.5 %collective-permute-done.7.block_ref = bf16[2,256,1024]{2,1,0:T(8,128)(2,1)S(1)} collective-permute-done((bf16[2,256,1024]{2,1,0:T(8,128)(2,1)S(1)}, bf16[2,256,1024]{2,1,0:T(8,128)(2,1)S(1)}, u32[]{:S(2)}, u32[]{:S(2)}) %collective-permute-start.7) | collective-permute-done | bytes 1048608 | tf_op jit(solution)/shard_map/ppermute | solution.py:157
  118.8 1.0 place.5._
  119.8 10.2 %collective-permute-done.6.block_ref = bf16[1,256,1024]{2,1,0:T(8,128)(2,1)S(1)} collective-permute-done((bf16[1,256,1024]{2,1,0:T(8,128)(2,1)S(1)}, bf16[1,256,1024]{2,1,0:T(8,128)(2,1)S(1)}, u32[]{:S(2)}, u32[]{:S(2)}) %collective-permute-start.6) | collective-permute-done | bytes 524320 | tf_op jit(solution)/shard_map/ppermute | solution.py:157
  130.0 0.8 place.6._
  130.8 9.6 %collective-permute-done.5.block_ref = bf16[1,256,1024]{2,1,0:T(8,128)(2,1)S(1)} collective-permute-done((bf16[1,256,1024]{2,1,0:T(8,128)(2,1)S(1)}, bf16[1,256,1024]{2,1,0:T(8,128)(2,1)S(1)}, u32[]{:S(2)}, u32[]{:S(2)}) %collective-permute-start.5) | collective-permute-done | bytes 524320 | tf_op jit(solution)/shard_map/ppermute | solution.py:157
  140.4 0.8 place.7
Async XLA Ops:
  1.9 50.7 %collective-permute-start.4 = (bf16[2,256,1024]{2,1,0:T(8,128)(2,1)S(1)}, bf16[2,256,1024]{2,1,0:T(8,128)(2,1)S(1)}, u32[]{:S(2)}, u32[]{:S(2)}) collective-permute-start(bf16[2,256,1024]{2,1,0:T(8,128)(2,1)S(1)} %cut.1), channel_id=1, source_target_pairs={{0,16},{16,0},{1,17},{17,1},{2,18},{18,2},{3,19},{19,3},{4,20},{20... | collective-permute-start | bytes 3145736 | tf_op jit(solution)/shard_map/ppermute | solution.py:157
  7.2 52.8 %collective-permute-start.3 = (bf16[2,256,1024]{2,1,0:T(8,128)(2,1)}, bf16[2,256,1024]{2,1,0:T(8,128)(2,1)S(1)}, u32[]{:S(2)}, u32[]{:S(2)}) collective-permute-start(bf16[2,256,1024]{2,1,0:T(8,128)(2,1)} %constant_dynamic-slice_fusion), channel_id=1, source_target_pairs={{0,16},{16,0},{1,17},{17,1},{2,18},{18,2},{3,19},{19,3},{4,20},{20... | collective-permute-start | bytes 3145736 | tf_op jit(solution)/shard_map/ppermute | solution.py:157
  7.2 44.2 %collective-permute-start = (s32[1]{0:T(128)}, s32[1]{0:T(128)}, u32[]{:S(2)}, u32[]{:S(2)}) collective-permute-start(s32[1]{0:T(128)} %param.4), channel_id=1, source_target_pairs={{0,16},{16,0},{1,17},{17,1},{2,18},{18,2},{3,19},{19,3},{4,20},{20... | collective-permute-start | bytes 20 | tf_op jit(solution)/shard_map/ppermute | solution.py:157
  11.5 53.2 %collective-permute-start.2 = (bf16[1,256,1024]{2,1,0:T(8,128)(2,1)}, bf16[1,256,1024]{2,1,0:T(8,128)(2,1)}, u32[]{:S(2)}, u32[]{:S(2)}) collective-permute-start(bf16[1,256,1024]{2,1,0:T(8,128)(2,1)} %get-tuple-element.32), channel_id=1, source_target_pairs={{0,16},{16,0},{1,17},{17,1},{2,18},{18,2},{3,19},{19,3},{4,20},{20... | collective-permute-start | bytes 1572872 | tf_op jit(solution)/shard_map/ppermute | solution.py:157
  11.5 62.4 %collective-permute-start.1 = (bf16[1,256,1024]{2,1,0:T(8,128)(2,1)}, bf16[1,256,1024]{2,1,0:T(8,128)(2,1)}, u32[]{:S(2)}, u32[]{:S(2)}) collective-permute-start(bf16[1,256,1024]{2,1,0:T(8,128)(2,1)} %get-tuple-element.33), channel_id=1, source_target_pairs={{0,16},{16,0},{1,17},{17,1},{2,18},{18,2},{3,19},{19,3},{4,20},{20... | collective-permute-start | bytes 1572872 | tf_op jit(solution)/shard_map/ppermute | solution.py:157
  52.6 0.7 copy-start
  57.9 38.4 %collective-permute-start.8 = (bf16[2,256,1024]{2,1,0:T(8,128)(2,1)S(1)}, bf16[2,256,1024]{2,1,0:T(8,128)(2,1)S(1)}, u32[]{:S(2)}, u32[]{:S(2)}) collective-permute-start(bf16[2,256,1024]{2,1,0:T(8,128)(2,1)S(1)} %get-tuple-element.29), channel_id=1, source_target_pairs={{0,16},{16,0},{1,17},{17,1},{2,18},{18,2},{3,19},{19,3},{4,20},{20... | collective-permute-start | bytes 3145736 | tf_op jit(solution)/shard_map/ppermute | solution.py:157
  64.7 54.1 %collective-permute-start.7 = (bf16[2,256,1024]{2,1,0:T(8,128)(2,1)S(1)}, bf16[2,256,1024]{2,1,0:T(8,128)(2,1)S(1)}, u32[]{:S(2)}, u32[]{:S(2)}) collective-permute-start(bf16[2,256,1024]{2,1,0:T(8,128)(2,1)S(1)} %get-tuple-element.28), channel_id=1, source_target_pairs={{0,16},{16,0},{1,17},{17,1},{2,18},{18,2},{3,19},{19,3},{4,20},{20... | collective-permute-start | bytes 3145736 | tf_op jit(solution)/shard_map/ppermute | solution.py:157
  67.5 62.5 %collective-permute-start.6 = (bf16[1,256,1024]{2,1,0:T(8,128)(2,1)S(1)}, bf16[1,256,1024]{2,1,0:T(8,128)(2,1)S(1)}, u32[]{:S(2)}, u32[]{:S(2)}) collective-permute-start(bf16[1,256,1024]{2,1,0:T(8,128)(2,1)S(1)} %get-tuple-element.27), channel_id=1, source_target_pairs={{0,16},{16,0},{1,17},{17,1},{2,18},{18,2},{3,19},{19,3},{4,20},{20... | collective-permute-start | bytes 1572872 | tf_op jit(solution)/shard_map/ppermute | solution.py:157
  76.7 63.7 %collective-permute-start.5 = (bf16[1,256,1024]{2,1,0:T(8,128)(2,1)S(1)}, bf16[1,256,1024]{2,1,0:T(8,128)(2,1)S(1)}, u32[]{:S(2)}, u32[]{:S(2)}) collective-permute-start(bf16[1,256,1024]{2,1,0:T(8,128)(2,1)S(1)} %get-tuple-element.26), channel_id=1, source_target_pairs={{0,16},{16,0},{1,17},{17,1},{2,18},{18,2},{3,19},{19,3},{4,20},{20... | collective-permute-start | bytes 1572872 | tf_op jit(solution)/shard_map/ppermute | solution.py:157

commit v11 on v10

--- a/solution.py
+++ b/solution.py
@@ -164,13 +164,11 @@
         anchor = anchor.reshape(parts, *shape[-2:])
         momentum = momentum.reshape(parts, owned, width)
         me = lax.axis_index("replica")
-        middle = (parts - 2) // 2
-        chunks = [
-            Chunk(1, middle, 0, owned),
-            Chunk(1 + middle, parts - 2 - middle, 0, owned),
-            Chunk(0, 1, 0, owned),
-            Chunk(parts - 1, 1, 0, owned),
-        ]
+        last = max(16, owned // 4)
+        top = owned - last
+        chunks = [Chunk(0, parts - 1, top, last)]
+        chunks += [Chunk(p, 1, 0, top) for p in range(parts)]
+        chunks += [Chunk(parts - 1, 1, top, last)]
         shifts = range(1, groups)
 
         def rows_for(array, chunk, target):

time: 142 us -> 142 us (level)
  waiting for transfers between devices: 101 us -> 78.9 us
  Pallas kernels: 20.9 us -> 36.4 us
  starting transfers between devices: 13.2 us -> 19.6 us
    ppermute x9 -> x17, waiting for transfers between devices: 101 us -> 78.9 us  [shifted(): return lax.ppermute(value, 'replica', pairs)]
    pallas_call x4 -> x8, Pallas kernels: 15 us -> 28.1 us  [update(): pl.pallas_call(functools.partial(update_kernel, groups), grid_spec=pltpu....]
    ppermute x9 -> x17, starting transfers between devices: 13.2 us -> 19.6 us  [shifted(): return lax.ppermute(value, 'replica', pairs)]
    pallas_call x4 -> x8, Pallas kernels: 3.56 us -> 6.08 us  [place(): pl.pallas_call(functools.partial(place_kernel, groups, owned, chunk, shif...]
  transfers between devices with their start and end apart: 9 -> 17, of which waited for: 6 -> 7; matrix products, arithmetic and copies ran while one was open for 3% -> 3% of each run, Pallas kernels for 13% -> 25%
where the time goes in v11:
time: 142 us; the launch traced here: 141 us
  waiting for transfers between devices  78.9 us (56%)
  Pallas kernels  36.4 us (26%)
  starting transfers between devices  19.6 us (14%)
  local copies, waits for them, and re-layouts  4.52 us (3%)
    ppermute x17, waiting for transfers between devices, shifted(): return lax.ppermute(value, 'replica', pairs)  78.9 us
    pallas_call x8, Pallas kernels, update(): pl.pallas_call(functools.partial(update_kernel, groups), grid_spec=pltpu....  28.1 us
    ppermute x17, starting transfers between devices, shifted(): return lax.ppermute(value, 'replica', pairs)  19.6 us
    pallas_call x8, Pallas kernels, place(): pl.pallas_call(functools.partial(place_kernel, groups, owned, chunk, shif...  6.08 us
    dynamic_slice x2, local copies, waits for them, and re-layouts, rows_for(): lax.dynamic_slice(array, (chunk.lo, target * owned + chunk.row, 0), sizes)  3.85 us
  transfers between devices with their start and end apart: 17, of which 7 were waited for; matrix products, arithmetic and copies ran while one was open for 3% of the time, Pallas kernels for 25%

profile of v11, /device:TPU:0, one launch (start us, length us, event | category | flops | bytes accessed | tf_op | source)
XLA Modules:
  0.0 140.9 jit_solution(2642651572301042917)
XLA Ops:
  0.6 1.1 cut.1
  1.7 3.0 %collective-permute-start.8 = (bf16[5,64,1024]{2,1,0:T(8,128)(2,1)S(1)}, bf16[5,64,1024]{2,1,0:T(8,128)(2,1)S(1)}, u32[]{:S(2)}, u32[]{:S(2)}) collective-permute-start(bf16[5,64,1024]{2,1,0:T(8,128)(2,1)S(1)} %cut.1), channel_id=1, source_target_pairs={{0,16},{16,0},{1,17},{17,1},{2,18},{18,2},{3,19},{19,3},{4,20},{20... | collective-permute-start | bytes 1966088 | tf_op jit(solution)/shard_map/ppermute | solution.py:157
  4.8 2.9 %constant_dynamic-slice_fusion = (bf16[1,192,1024]{2,1,0:T(8,128)(2,1)S(1)}, bf16[1,192,1024]{2,1,0:T(8,128)(2,1)}, bf16[1,192,1024]{2,1,0:T(8,128)(2,1)}, bf16[...) fusion(bf16[6,512,1024]{2,1,0:T(8,128)(2,1)} %bitcast.8, s32[]{:T(128)S(6)} %select_n.20), kind=kLoop, calls=%fused_computation | loop fusion | bytes 4718596 | tf_op jit(solution)/shard_map/dynamic_slice | solution.py:176
  7.7 2.0 %collective-permute-start.6 = (bf16[1,192,1024]{2,1,0:T(8,128)(2,1)}, bf16[1,192,1024]{2,1,0:T(8,128)(2,1)S(1)}, u32[]{:S(2)}, u32[]{:S(2)}) collective-permute-start(bf16[1,192,1024]{2,1,0:T(8,128)(2,1)} %get-tuple-element.57), channel_id=1, source_target_pairs={{0,16},{16,0},{1,17},{17,1},{2,18},{18,2},{3,19},{19,3},{4,20},{20... | collective-permute-start | bytes 1179656 | tf_op jit(solution)/shard_map/ppermute | solution.py:157
  9.8 2.0 %collective-permute-start.5 = (bf16[1,192,1024]{2,1,0:T(8,128)(2,1)}, bf16[1,192,1024]{2,1,0:T(8,128)(2,1)S(1)}, u32[]{:S(2)}, u32[]{:S(2)}) collective-permute-start(bf16[1,192,1024]{2,1,0:T(8,128)(2,1)} %get-tuple-element.58), channel_id=1, source_target_pairs={{0,16},{16,0},{1,17},{17,1},{2,18},{18,2},{3,19},{19,3},{4,20},{20... | collective-permute-start | bytes 1179656 | tf_op jit(solution)/shard_map/ppermute | solution.py:157
  11.7 25.5 %collective-permute-done.refs_1_ = s32[1]{0:T(128)} collective-permute-done((s32[1]{0:T(128)}, s32[1]{0:T(128)}, u32[]{:S(2)}, u32[]{:S(2)}) %collective-permute-start) | collective-permute-done | bytes 36 | tf_op jit(solution)/shard_map/ppermute | solution.py:157
  37.3 2.1 %collective-permute-start.4 = (bf16[1,192,1024]{2,1,0:T(8,128)(2,1)}, bf16[1,192,1024]{2,1,0:T(8,128)(2,1)S(1)}, u32[]{:S(2)}, u32[]{:S(2)}) collective-permute-start(bf16[1,192,1024]{2,1,0:T(8,128)(2,1)} %get-tuple-element.59), channel_id=1, source_target_pairs={{0,16},{16,0},{1,17},{17,1},{2,18},{18,2},{3,19},{19,3},{4,20},{20... | collective-permute-start | bytes 1179656 | tf_op jit(solution)/shard_map/ppermute | solution.py:157
  40.0 1.1 share.1.shares_ref
  41.8 5.1 %update.8 = (bf16[5,64,1024]{2,1,0:T(8,128)(2,1)}, bf16[6,512,1024]{2,1,0:T(8,128)(2,1)}, f32[6,256,1024]{2,1,0:T(8,128)}) custom-call(s32[1]{0:T(128)} %bitcast.me_ref, f32[2]{0:T(128)S(1)} %copy-done, bf16[6,512,1024]{2,1,0:T(8,128)(2,1)} %bitcast.18, bf16[6,512,1024]{2,1,0:T(8,128)(2,1)} %bitcast.9, ...), custom_call_target="tpu_custom_call" | custom-call | flops 3932160 | bytes 5898240 | tf_op jit(solution)/shard_map/update/pallas_call | solution.py:102
  46.9 2.0 %collective-permute-start.2 = (bf16[1,192,1024]{2,1,0:T(8,128)(2,1)}, bf16[1,192,1024]{2,1,0:T(8,128)(2,1)S(1)}, u32[]{:S(2)}, u32[]{:S(2)}) collective-permute-start(bf16[1,192,1024]{2,1,0:T(8,128)(2,1)} %get-tuple-element.61), channel_id=1, source_target_pairs={{0,16},{16,0},{1,17},{17,1},{2,18},{18,2},{3,19},{19,3},{4,20},{20... | collective-permute-start | bytes 1179656 | tf_op jit(solution)/shard_map/ppermute | solution.py:157
  48.9 3.6 %update.9 = (bf16[1,192,1024]{2,1,0:T(8,128)(2,1)}, bf16[6,512,1024]{2,1,0:T(8,128)(2,1)}, f32[6,256,1024]{2,1,0:T(8,128)}) custom-call(s32[1]{0:T(128)} %bitcast.me_ref, f32[2]{0:T(128)S(1)} %copy-done, bf16[6,512,1024]{2,1,0:T(8,128)(2,1)} %bitcast.19, bf16[6,512,1024]{2,1,0:T(8,128)(2,1)} %bitcast.10, ...), custom_call_target="tpu_custom_call", output_to_operand_aliasing={{1}: (6, {}), {2}: (7, {})} | custom-call | flops 2359296 | bytes 3538944 | tf_op jit(solution)/shard_map/update/pallas_call | solution.py:102
  52.7 3.7 %update.10 = (bf16[1,192,1024]{2,1,0:T(8,128)(2,1)}, bf16[6,512,1024]{2,1,0:T(8,128)(2,1)}, f32[6,256,1024]{2,1,0:T(8,128)}) custom-call(s32[1]{0:T(128)} %bitcast.me_ref, f32[2]{0:T(128)S(1)} %copy-done, bf16[6,512,1024]{2,1,0:T(8,128)(2,1)} %bitcast.20, bf16[6,512,1024]{2,1,0:T(8,128)(2,1)} %bitcast.11, ...), custom_call_target="tpu_custom_call", output_to_operand_aliasing={{1}: (6, {}), {2}: (7, {})} | custom-call | flops 2359296 | bytes 3538944 | tf_op jit(solution)/shard_map/update/pallas_call | solution.py:102
  56.3 2.0 %collective-permute-start.14 = (bf16[1,192,1024]{2,1,0:T(8,128)(2,1)}, bf16[1,192,1024]{2,1,0:T(8,128)(2,1)S(1)}, u32[]{:S(2)}, u32[]{:S(2)}) collective-permute-start(bf16[1,192,1024]{2,1,0:T(8,128)(2,1)} %get-tuple-element.51), channel_id=1, source_target_pairs={{0,16},{16,0},{1,17},{17,1},{2,18},{18,2},{3,19},{19,3},{4,20},{20... | collective-permute-start | bytes 1179656 | tf_op jit(solution)/shard_map/ppermute | solution.py:157
  58.4 0.9 constant_dynamic-slice_fusion.6
  59.3 3.1 %collective-permute-done.3.refs_0_ = bf16[1,192,1024]{2,1,0:T(8,128)(2,1)S(1)} collective-permute-done((bf16[1,192,1024]{2,1,0:T(8,128)(2,1)}, bf16[1,192,1024]{2,1,0:T(8,128)(2,1)S(1)}, u32[]{:S(2)}, u32[]{:S(2)}) %collective-permute-start.3) | collective-permute-done | bytes 393248 | tf_op jit(solution)/shard_map/ppermute | solution.py:157
  62.5 2.1 %collective-permute-start.1 = (bf16[1,64,1024]{2,1,0:T(8,128)(2,1)S(1)}, bf16[1,64,1024]{2,1,0:T(8,128)(2,1)S(1)}, u32[]{:S(2)}, u32[]{:S(2)}) collective-permute-start(bf16[1,64,1024]{2,1,0:T(8,128)(2,1)S(1)} %constant_dynamic-slice_fusion.6), channel_id=1, source_target_pairs={{0,16},{16,0},{1,17},{17,1},{2,18},{18,2},{3,19},{19,3},{4,20},{20... | collective-permute-start | bytes 393224 | tf_op jit(solution)/shard_map/ppermute | solution.py:157
  64.5 3.4 %update.11 = (bf16[1,192,1024]{2,1,0:T(8,128)(2,1)S(1)}, bf16[6,512,1024]{2,1,0:T(8,128)(2,1)}, f32[6,256,1024]{2,1,0:T(8,128)}) custom-call(s32[1]{0:T(128)} %bitcast.me_ref, f32[2]{0:T(128)S(1)} %copy-done.1, bf16[6,512,1024]{2,1,0:T(8,128)(2,1)} %bitcast.21, bf16[6,512,1024]{2,1,0:T(8,128)(2,1)} %bitcast.13, ...), custom_call_target="tpu_custom_call", output_to_operand_aliasing={{1}: (6, {}), {2}: (7, {})} | custom-call | flops 2359296 | bytes 3538944 | tf_op jit(solution)/shard_map/update/pallas_call | solution.py:102
  68.0 3.5 %update.12 = (bf16[1,192,1024]{2,1,0:T(8,128)(2,1)S(1)}, bf16[6,512,1024]{2,1,0:T(8,128)(2,1)}, f32[6,256,1024]{2,1,0:T(8,128)}) custom-call(s32[1]{0:T(128)} %bitcast.me_ref, f32[2]{0:T(128)S(1)} %copy-done.1, bf16[6,512,1024]{2,1,0:T(8,128)(2,1)} %bitcast.22, bf16[6,512,1024]{2,1,0:T(8,128)(2,1)} %bitcast.14, ...), custom_call_target="tpu_custom_call", output_to_operand_aliasing={{1}: (6, {}), {2}: (7, {})} | custom-call | flops 2359296 | bytes 3538944 | tf_op jit(solution)/shard_map/update/pallas_call | solution.py:102
  71.4 3.5 %update.13 = (bf16[1,192,1024]{2,1,0:T(8,128)(2,1)S(1)}, bf16[6,512,1024]{2,1,0:T(8,128)(2,1)}, f32[6,256,1024]{2,1,0:T(8,128)}) custom-call(s32[1]{0:T(128)} %bitcast.me_ref, f32[2]{0:T(128)S(1)} %copy-done.1, bf16[6,512,1024]{2,1,0:T(8,128)(2,1)} %bitcast.23, bf16[6,512,1024]{2,1,0:T(8,128)(2,1)} %bitcast.15, ...), custom_call_target="tpu_custom_call", output_to_operand_aliasing={{1}: (6, {}), {2}: (7, {})} | custom-call | flops 2359296 | bytes 3538944 | tf_op jit(solution)/shard_map/update/pallas_call | solution.py:102
  74.9 3.5 %update.14 = (bf16[1,192,1024]{2,1,0:T(8,128)(2,1)S(1)}, bf16[6,512,1024]{2,1,0:T(8,128)(2,1)}, f32[6,256,1024]{2,1,0:T(8,128)}) custom-call(s32[1]{0:T(128)} %bitcast.me_ref, f32[2]{0:T(128)S(1)} %copy-done.1, bf16[6,512,1024]{2,1,0:T(8,128)(2,1)} %bitcast.24, bf16[6,512,1024]{2,1,0:T(8,128)(2,1)} %bitcast.16, ...), custom_call_target="tpu_custom_call", output_to_operand_aliasing={{1}: (6, {}), {2}: (7, {})} | custom-call | flops 2359296 | bytes 3538944 | tf_op jit(solution)/shard_map/update/pallas_call | solution.py:102
  78.4 26.2 %collective-permute-done.1.refs_0_ = bf16[1,64,1024]{2,1,0:T(8,128)(2,1)S(1)} collective-permute-done((bf16[1,64,1024]{2,1,0:T(8,128)(2,1)S(1)}, bf16[1,64,1024]{2,1,0:T(8,128)(2,1)S(1)}, u32[]{:S(2)}, u32[]{:S(2)}) %collective-permute-start.1) | collective-permute-done | bytes 131104 | tf_op jit(solution)/shard_map/ppermute | solution.py:157
  104.6 2.1 %collective-permute-start.12 = (bf16[1,192,1024]{2,1,0:T(8,128)(2,1)S(1)}, bf16[1,192,1024]{2,1,0:T(8,128)(2,1)S(1)}, u32[]{:S(2)}, u32[]{:S(2)}) collective-permute-start(bf16[1,192,1024]{2,1,0:T(8,128)(2,1)S(1)} %get-tuple-element.49), channel_id=1, source_target_pairs={{0,16},{16,0},{1,17},{17,1},{2,18},{18,2},{3,19},{19,3},{4,20},{20... | collective-permute-start | bytes 1179656 | tf_op jit(solution)/shard_map/ppermute | solution.py:157
  106.7 2.0 %collective-permute-start.10 = (bf16[1,192,1024]{2,1,0:T(8,128)(2,1)S(1)}, bf16[1,192,1024]{2,1,0:T(8,128)(2,1)S(1)}, u32[]{:S(2)}, u32[]{:S(2)}) collective-permute-start(bf16[1,192,1024]{2,1,0:T(8,128)(2,1)S(1)} %get-tuple-element.47), channel_id=1, source_target_pairs={{0,16},{16,0},{1,17},{17,1},{2,18},{18,2},{3,19},{19,3},{4,20},{20... | collective-permute-start | bytes 1179656 | tf_op jit(solution)/shard_map/ppermute | solution.py:157
  108.7 1.9 %update.15 = (bf16[1,64,1024]{2,1,0:T(8,128)(2,1)S(1)}, bf16[6,512,1024]{2,1,0:T(8,128)(2,1)}, f32[6,256,1024]{2,1,0:T(8,128)}) custom-call(s32[1]{0:T(128)} %bitcast.me_ref, f32[2]{0:T(128)S(1)} %copy-done.1, bf16[6,512,1024]{2,1,0:T(8,128)(2,1)} %bitcast.25, bf16[6,512,1024]{2,1,0:T(8,128)(2,1)} %bitcast.17, ...), custom_call_target="tpu_custom_call", output_to_operand_aliasing={{1}: (6, {}), {2}: (7, {})} | custom-call | flops 786432 | bytes 1179648 | tf_op jit(solution)/shard_map/update/pallas_call | solution.py:102
  110.7 0.8 place.8._
  111.5 0.8 place.9._
  112.3 0.8 place.10._
  113.1 0.8 place.11._
  113.9 7.5 %collective-permute-done.12.block_ref = bf16[1,192,1024]{2,1,0:T(8,128)(2,1)S(1)} collective-permute-done((bf16[1,192,1024]{2,1,0:T(8,128)(2,1)S(1)}, bf16[1,192,1024]{2,1,0:T(8,128)(2,1)S(1)}, u32[]{:S(2)}, u32[]{:S(2)}) %collective-permute-start.12) | collective-permute-done | bytes 393248 | tf_op jit(solution)/shard_map/ppermute | solution.py:157
  122.2 7.7 %collective-permute-done.11.block_ref = bf16[1,192,1024]{2,1,0:T(8,128)(2,1)S(1)} collective-permute-done((bf16[1,192,1024]{2,1,0:T(8,128)(2,1)S(1)}, bf16[1,192,1024]{2,1,0:T(8,128)(2,1)S(1)}, u32[]{:S(2)}, u32[]{:S(2)}) %collective-permute-start.11) | collective-permute-done | bytes 393248 | tf_op jit(solution)/shard_map/ppermute | solution.py:157
  130.6 7.7 %collective-permute-done.10.block_ref = bf16[1,192,1024]{2,1,0:T(8,128)(2,1)S(1)} collective-permute-done((bf16[1,192,1024]{2,1,0:T(8,128)(2,1)S(1)}, bf16[1,192,1024]{2,1,0:T(8,128)(2,1)S(1)}, u32[]{:S(2)}, u32[]{:S(2)}) %collective-permute-start.10) | collective-permute-done | bytes 393248 | tf_op jit(solution)/shard_map/ppermute | solution.py:157
  139.1 1.2 collective-permute-done.9.block_ref
  (26 shorter events, 4.1 us)
Async XLA Ops:
  1.7 37.6 %collective-permute-start.8 = (bf16[5,64,1024]{2,1,0:T(8,128)(2,1)S(1)}, bf16[5,64,1024]{2,1,0:T(8,128)(2,1)S(1)}, u32[]{:S(2)}, u32[]{:S(2)}) collective-permute-start(bf16[5,64,1024]{2,1,0:T(8,128)(2,1)S(1)} %cut.1), channel_id=1, source_target_pairs={{0,16},{16,0},{1,17},{17,1},{2,18},{18,2},{3,19},{19,3},{4,20},{20... | collective-permute-start | bytes 1966088 | tf_op jit(solution)/shard_map/ppermute | solution.py:157
  7.7 39.2 %collective-permute-start.7 = (bf16[1,192,1024]{2,1,0:T(8,128)(2,1)S(1)}, bf16[1,192,1024]{2,1,0:T(8,128)(2,1)S(1)}, u32[]{:S(2)}, u32[]{:S(2)}) collective-permute-start(bf16[1,192,1024]{2,1,0:T(8,128)(2,1)S(1)} %get-tuple-element.56), channel_id=1, source_target_pairs={{0,16},{16,0},{1,17},{17,1},{2,18},{18,2},{3,19},{19,3},{4,20},{20... | collective-permute-start | bytes 1179656 | tf_op jit(solution)/shard_map/ppermute | solution.py:157
  7.7 44.8 %collective-permute-start.6 = (bf16[1,192,1024]{2,1,0:T(8,128)(2,1)}, bf16[1,192,1024]{2,1,0:T(8,128)(2,1)S(1)}, u32[]{:S(2)}, u32[]{:S(2)}) collective-permute-start(bf16[1,192,1024]{2,1,0:T(8,128)(2,1)} %get-tuple-element.57), channel_id=1, source_target_pairs={{0,16},{16,0},{1,17},{17,1},{2,18},{18,2},{3,19},{19,3},{4,20},{20... | collective-permute-start | bytes 1179656 | tf_op jit(solution)/shard_map/ppermute | solution.py:157
  9.7 27.5 %collective-permute-start = (s32[1]{0:T(128)}, s32[1]{0:T(128)}, u32[]{:S(2)}, u32[]{:S(2)}) collective-permute-start(s32[1]{0:T(128)} %param.4), channel_id=1, source_target_pairs={{0,16},{16,0},{1,17},{17,1},{2,18},{18,2},{3,19},{19,3},{4,20},{20... | collective-permute-start | bytes 20 | tf_op jit(solution)/shard_map/ppermute | solution.py:157
  9.8 46.6 %collective-permute-start.5 = (bf16[1,192,1024]{2,1,0:T(8,128)(2,1)}, bf16[1,192,1024]{2,1,0:T(8,128)(2,1)S(1)}, u32[]{:S(2)}, u32[]{:S(2)}) collective-permute-start(bf16[1,192,1024]{2,1,0:T(8,128)(2,1)} %get-tuple-element.58), channel_id=1, source_target_pairs={{0,16},{16,0},{1,17},{17,1},{2,18},{18,2},{3,19},{19,3},{4,20},{20... | collective-permute-start | bytes 1179656 | tf_op jit(solution)/shard_map/ppermute | solution.py:157
  37.3 21.1 %collective-permute-start.4 = (bf16[1,192,1024]{2,1,0:T(8,128)(2,1)}, bf16[1,192,1024]{2,1,0:T(8,128)(2,1)S(1)}, u32[]{:S(2)}, u32[]{:S(2)}) collective-permute-start(bf16[1,192,1024]{2,1,0:T(8,128)(2,1)} %get-tuple-element.59), channel_id=1, source_target_pairs={{0,16},{16,0},{1,17},{17,1},{2,18},{18,2},{3,19},{19,3},{4,20},{20... | collective-permute-start | bytes 1179656 | tf_op jit(solution)/shard_map/ppermute | solution.py:157
  39.3 23.1 %collective-permute-start.3 = (bf16[1,192,1024]{2,1,0:T(8,128)(2,1)}, bf16[1,192,1024]{2,1,0:T(8,128)(2,1)S(1)}, u32[]{:S(2)}, u32[]{:S(2)}) collective-permute-start(bf16[1,192,1024]{2,1,0:T(8,128)(2,1)} %get-tuple-element.60), channel_id=1, source_target_pairs={{0,16},{16,0},{1,17},{17,1},{2,18},{18,2},{3,19},{19,3},{4,20},{20... | collective-permute-start | bytes 1179656 | tf_op jit(solution)/shard_map/ppermute | solution.py:157
  41.1 0.7 copy-start
  46.9 28.0 %collective-permute-start.2 = (bf16[1,192,1024]{2,1,0:T(8,128)(2,1)}, bf16[1,192,1024]{2,1,0:T(8,128)(2,1)S(1)}, u32[]{:S(2)}, u32[]{:S(2)}) collective-permute-start(bf16[1,192,1024]{2,1,0:T(8,128)(2,1)} %get-tuple-element.61), channel_id=1, source_target_pairs={{0,16},{16,0},{1,17},{17,1},{2,18},{18,2},{3,19},{19,3},{4,20},{20... | collective-permute-start | bytes 1179656 | tf_op jit(solution)/shard_map/ppermute | solution.py:157
  52.6 54.1 %collective-permute-start.15 = (bf16[1,192,1024]{2,1,0:T(8,128)(2,1)}, bf16[1,192,1024]{2,1,0:T(8,128)(2,1)S(1)}, u32[]{:S(2)}, u32[]{:S(2)}) collective-permute-start(bf16[1,192,1024]{2,1,0:T(8,128)(2,1)} %get-tuple-element.52), channel_id=1, source_target_pairs={{0,16},{16,0},{1,17},{17,1},{2,18},{18,2},{3,19},{19,3},{4,20},{20... | collective-permute-start | bytes 1179656 | tf_op jit(solution)/shard_map/ppermute | solution.py:157
  52.6 11.9 %copy-start.1 = (f32[2]{0:T(128)S(1)}, f32[2]{0:T(128)}, u32[]{:S(2)}) copy-start(f32[2]{0:T(128)} %share.1.shares_ref) | copy-start | bytes 28
  56.3 50.4 %collective-permute-start.14 = (bf16[1,192,1024]{2,1,0:T(8,128)(2,1)}, bf16[1,192,1024]{2,1,0:T(8,128)(2,1)S(1)}, u32[]{:S(2)}, u32[]{:S(2)}) collective-permute-start(bf16[1,192,1024]{2,1,0:T(8,128)(2,1)} %get-tuple-element.51), channel_id=1, source_target_pairs={{0,16},{16,0},{1,17},{17,1},{2,18},{18,2},{3,19},{19,3},{4,20},{20... | collective-permute-start | bytes 1179656 | tf_op jit(solution)/shard_map/ppermute | solution.py:157
  58.3 52.3 %collective-permute-start.16 = (bf16[5,64,1024]{2,1,0:T(8,128)(2,1)}, bf16[5,64,1024]{2,1,0:T(8,128)(2,1)S(1)}, u32[]{:S(2)}, u32[]{:S(2)}) collective-permute-start(bf16[5,64,1024]{2,1,0:T(8,128)(2,1)} %get-tuple-element.53), channel_id=1, source_target_pairs={{0,16},{16,0},{1,17},{17,1},{2,18},{18,2},{3,19},{19,3},{4,20},{20... | collective-permute-start | bytes 1966088 | tf_op jit(solution)/shard_map/ppermute | solution.py:157
  62.5 42.1 %collective-permute-start.1 = (bf16[1,64,1024]{2,1,0:T(8,128)(2,1)S(1)}, bf16[1,64,1024]{2,1,0:T(8,128)(2,1)S(1)}, u32[]{:S(2)}, u32[]{:S(2)}) collective-permute-start(bf16[1,64,1024]{2,1,0:T(8,128)(2,1)S(1)} %constant_dynamic-slice_fusion.6), channel_id=1, source_target_pairs={{0,16},{16,0},{1,17},{17,1},{2,18},{18,2},{3,19},{19,3},{4,20},{20... | collective-permute-start | bytes 393224 | tf_op jit(solution)/shard_map/ppermute | solution.py:157
  74.9 38.2 %collective-permute-start.13 = (bf16[1,192,1024]{2,1,0:T(8,128)(2,1)S(1)}, bf16[1,192,1024]{2,1,0:T(8,128)(2,1)S(1)}, u32[]{:S(2)}, u32[]{:S(2)}) collective-permute-start(bf16[1,192,1024]{2,1,0:T(8,128)(2,1)S(1)} %get-tuple-element.50), channel_id=1, source_target_pairs={{0,16},{16,0},{1,17},{17,1},{2,18},{18,2},{3,19},{19,3},{4,20},{20... | collective-permute-start | bytes 1179656 | tf_op jit(solution)/shard_map/ppermute | solution.py:157
  104.6 16.9 %collective-permute-start.12 = (bf16[1,192,1024]{2,1,0:T(8,128)(2,1)S(1)}, bf16[1,192,1024]{2,1,0:T(8,128)(2,1)S(1)}, u32[]{:S(2)}, u32[]{:S(2)}) collective-permute-start(bf16[1,192,1024]{2,1,0:T(8,128)(2,1)S(1)} %get-tuple-element.49), channel_id=1, source_target_pairs={{0,16},{16,0},{1,17},{17,1},{2,18},{18,2},{3,19},{19,3},{4,20},{20... | collective-permute-start | bytes 1179656 | tf_op jit(solution)/shard_map/ppermute | solution.py:157
  106.6 23.2 %collective-permute-start.11 = (bf16[1,192,1024]{2,1,0:T(8,128)(2,1)S(1)}, bf16[1,192,1024]{2,1,0:T(8,128)(2,1)S(1)}, u32[]{:S(2)}, u32[]{:S(2)}) collective-permute-start(bf16[1,192,1024]{2,1,0:T(8,128)(2,1)S(1)} %get-tuple-element.48), channel_id=1, source_target_pairs={{0,16},{16,0},{1,17},{17,1},{2,18},{18,2},{3,19},{19,3},{4,20},{20... | collective-permute-start | bytes 1179656 | tf_op jit(solution)/shard_map/ppermute | solution.py:157
  106.7 31.6 %collective-permute-start.10 = (bf16[1,192,1024]{2,1,0:T(8,128)(2,1)S(1)}, bf16[1,192,1024]{2,1,0:T(8,128)(2,1)S(1)}, u32[]{:S(2)}, u32[]{:S(2)}) collective-permute-start(bf16[1,192,1024]{2,1,0:T(8,128)(2,1)S(1)} %get-tuple-element.47), channel_id=1, source_target_pairs={{0,16},{16,0},{1,17},{17,1},{2,18},{18,2},{3,19},{19,3},{4,20},{20... | collective-permute-start | bytes 1179656 | tf_op jit(solution)/shard_map/ppermute | solution.py:157
  110.6 29.6 %collective-permute-start.9 = (bf16[1,64,1024]{2,1,0:T(8,128)(2,1)S(1)}, bf16[1,64,1024]{2,1,0:T(8,128)(2,1)S(1)}, u32[]{:S(2)}, u32[]{:S(2)}) collective-permute-start(bf16[1,64,1024]{2,1,0:T(8,128)(2,1)S(1)} %get-tuple-element.46), channel_id=1, source_target_pairs={{0,16},{16,0},{1,17},{17,1},{2,18},{18,2},{3,19},{19,3},{4,20},{20... | collective-permute-start | bytes 393224 | tf_op jit(solution)/shard_map/ppermute | solution.py:157

commit v12 on v11

--- a/solution.py
+++ b/solution.py
@@ -22,14 +22,19 @@
     rows: int
 
 
-def cut_kernel(groups, owned, chunk, shift, inner_ref, out_ref, sem):
+def cut_kernel(groups, owned, chunk, shift, inner_ref, out_ref, sems):
     target = lax.rem(lax.axis_index("replica") + shift, groups)
     start = pl.multiple_of(target * owned + chunk.row, spare)
-    copy = pltpu.make_async_copy(
-        inner_ref.at[pl.ds(chunk.lo, chunk.parts), pl.ds(start, chunk.rows), :], out_ref, sem
-    )
-    copy.start()
-    copy.wait()
+    copies = [
+        pltpu.make_async_copy(
+            inner_ref.at[chunk.lo + p, pl.ds(start, chunk.rows), :], out_ref.at[p], sems.at[p]
+        )
+        for p in range(chunk.parts)
+    ]
+    for copy in copies:
+        copy.start()
+    for copy in copies:
+        copy.wait()
 
 
 def cut(groups, owned, chunk, shift, inner):
@@ -39,7 +44,7 @@
         in_specs=[pl.BlockSpec(memory_space=pl.ANY)],
         out_specs=pl.BlockSpec(memory_space=pltpu.VMEM),
         out_shape=jax.ShapeDtypeStruct(shape, inner.dtype),
-        scratch_shapes=[pltpu.SemaphoreType.DMA],
+        scratch_shapes=[pltpu.SemaphoreType.DMA((chunk.parts,))],
         compiler_params=pltpu.CompilerParams(vmem_limit_bytes=vmem_bytes),
         cost_estimate=pl.CostEstimate(
             flops=0, bytes_accessed=4 * math.prod(shape), transcendentals=0
@@ -166,9 +171,10 @@
         me = lax.axis_index("replica")
         last = max(16, owned // 4)
         top = owned - last
-        chunks = [Chunk(0, parts - 1, top, last)]
+        early = 2 * parts // 3
+        chunks = [Chunk(0, early, top, last)]
         chunks += [Chunk(p, 1, 0, top) for p in range(parts)]
-        chunks += [Chunk(parts - 1, 1, top, last)]
+        chunks += [Chunk(early, parts - early, top, last)]
         shifts = range(1, groups)
 
         def rows_for(array, chunk, target):

time: 142 us -> 142 us (level)
  transfers between devices with their start and end apart: 17 -> 17, of which waited for: 7 -> 7; matrix products, arithmetic and copies ran while one was open for 3% -> 3% of each run, Pallas kernels for 25% -> 24%
where the time goes in v12:
time: 142 us; the launch traced here: 141 us
  waiting for transfers between devices  79.8 us (56%)
  Pallas kernels  35.6 us (25%)
  starting transfers between devices  19.7 us (14%)
  local copies, waits for them, and re-layouts  4.48 us (3%)
    ppermute x17, waiting for transfers between devices, shifted(): return lax.ppermute(value, 'replica', pairs)  79.8 us
    pallas_call x8, Pallas kernels, update(): pl.pallas_call(functools.partial(update_kernel, groups), grid_spec=pltpu....  27.1 us
    ppermute x17, starting transfers between devices, shifted(): return lax.ppermute(value, 'replica', pairs)  19.7 us
    pallas_call x8, Pallas kernels, place(): pl.pallas_call(functools.partial(place_kernel, groups, owned, chunk, shif...  6.08 us
    dynamic_slice x2, local copies, waits for them, and re-layouts, rows_for(): lax.dynamic_slice(array, (chunk.lo, target * owned + chunk.row, 0), sizes)  3.88 us
  transfers between devices with their start and end apart: 17, of which 7 were waited for; matrix products, arithmetic and copies ran while one was open for 3% of the time, Pallas kernels for 24%

profile of v12, /device:TPU:0, one launch (start us, length us, event | category | flops | bytes accessed | tf_op | source)
XLA Modules:
  0.0 141.0 jit_solution(15162310877446714172)
XLA Ops:
  0.6 1.1 cut.1
  1.8 3.0 %collective-permute-start.8 = (bf16[4,64,1024]{2,1,0:T(8,128)(2,1)S(1)}, bf16[4,64,1024]{2,1,0:T(8,128)(2,1)S(1)}, u32[]{:S(2)}, u32[]{:S(2)}) collective-permute-start(bf16[4,64,1024]{2,1,0:T(8,128)(2,1)S(1)} %cut.1), channel_id=1, source_target_pairs={{0,16},{16,0},{1,17},{17,1},{2,18},{18,2},{3,19},{19,3},{4,20},{20... | collective-permute-start | bytes 1572872 | tf_op jit(solution)/shard_map/ppermute | solution.py:162
  4.8 2.9 %constant_dynamic-slice_fusion = (bf16[1,192,1024]{2,1,0:T(8,128)(2,1)S(1)}, bf16[1,192,1024]{2,1,0:T(8,128)(2,1)}, bf16[1,192,1024]{2,1,0:T(8,128)(2,1)}, bf16[...) fusion(bf16[6,512,1024]{2,1,0:T(8,128)(2,1)} %bitcast.8, s32[]{:T(128)S(6)} %select_n.20), kind=kLoop, calls=%fused_computation | loop fusion | bytes 4718596 | tf_op jit(solution)/shard_map/dynamic_slice | solution.py:182
  7.7 2.0 %collective-permute-start.6 = (bf16[1,192,1024]{2,1,0:T(8,128)(2,1)}, bf16[1,192,1024]{2,1,0:T(8,128)(2,1)S(1)}, u32[]{:S(2)}, u32[]{:S(2)}) collective-permute-start(bf16[1,192,1024]{2,1,0:T(8,128)(2,1)} %get-tuple-element.57), channel_id=1, source_target_pairs={{0,16},{16,0},{1,17},{17,1},{2,18},{18,2},{3,19},{19,3},{4,20},{20... | collective-permute-start | bytes 1179656 | tf_op jit(solution)/shard_map/ppermute | solution.py:162
  9.8 2.0 %collective-permute-start.5 = (bf16[1,192,1024]{2,1,0:T(8,128)(2,1)}, bf16[1,192,1024]{2,1,0:T(8,128)(2,1)S(1)}, u32[]{:S(2)}, u32[]{:S(2)}) collective-permute-start(bf16[1,192,1024]{2,1,0:T(8,128)(2,1)} %get-tuple-element.58), channel_id=1, source_target_pairs={{0,16},{16,0},{1,17},{17,1},{2,18},{18,2},{3,19},{19,3},{4,20},{20... | collective-permute-start | bytes 1179656 | tf_op jit(solution)/shard_map/ppermute | solution.py:162
  11.8 22.7 %collective-permute-done.refs_1_ = s32[1]{0:T(128)} collective-permute-done((s32[1]{0:T(128)}, s32[1]{0:T(128)}, u32[]{:S(2)}, u32[]{:S(2)}) %collective-permute-start) | collective-permute-done | bytes 36 | tf_op jit(solution)/shard_map/ppermute | solution.py:162
  34.4 2.1 %collective-permute-start.4 = (bf16[1,192,1024]{2,1,0:T(8,128)(2,1)}, bf16[1,192,1024]{2,1,0:T(8,128)(2,1)S(1)}, u32[]{:S(2)}, u32[]{:S(2)}) collective-permute-start(bf16[1,192,1024]{2,1,0:T(8,128)(2,1)} %get-tuple-element.59), channel_id=1, source_target_pairs={{0,16},{16,0},{1,17},{17,1},{2,18},{18,2},{3,19},{19,3},{4,20},{20... | collective-permute-start | bytes 1179656 | tf_op jit(solution)/shard_map/ppermute | solution.py:162
  37.2 1.2 share.1.shares_ref
  39.0 3.9 %update.8 = (bf16[4,64,1024]{2,1,0:T(8,128)(2,1)S(1)}, bf16[6,512,1024]{2,1,0:T(8,128)(2,1)}, f32[6,256,1024]{2,1,0:T(8,128)}) custom-call(s32[1]{0:T(128)} %bitcast.me_ref, f32[2]{0:T(128)S(1)} %copy-done, bf16[6,512,1024]{2,1,0:T(8,128)(2,1)} %bitcast.18, bf16[6,512,1024]{2,1,0:T(8,128)(2,1)} %bitcast.9, ...), custom_call_target="tpu_custom_call" | custom-call | flops 3145728 | bytes 4718592 | tf_op jit(solution)/shard_map/update/pallas_call | solution.py:107
  42.9 2.1 %collective-permute-start.2 = (bf16[1,192,1024]{2,1,0:T(8,128)(2,1)}, bf16[1,192,1024]{2,1,0:T(8,128)(2,1)S(1)}, u32[]{:S(2)}, u32[]{:S(2)}) collective-permute-start(bf16[1,192,1024]{2,1,0:T(8,128)(2,1)} %get-tuple-element.61), channel_id=1, source_target_pairs={{0,16},{16,0},{1,17},{17,1},{2,18},{18,2},{3,19},{19,3},{4,20},{20... | collective-permute-start | bytes 1179656 | tf_op jit(solution)/shard_map/ppermute | solution.py:162
  44.9 3.6 %update.9 = (bf16[1,192,1024]{2,1,0:T(8,128)(2,1)}, bf16[6,512,1024]{2,1,0:T(8,128)(2,1)}, f32[6,256,1024]{2,1,0:T(8,128)}) custom-call(s32[1]{0:T(128)} %bitcast.me_ref, f32[2]{0:T(128)S(1)} %copy-done, bf16[6,512,1024]{2,1,0:T(8,128)(2,1)} %bitcast.19, bf16[6,512,1024]{2,1,0:T(8,128)(2,1)} %bitcast.10, ...), custom_call_target="tpu_custom_call", output_to_operand_aliasing={{1}: (6, {}), {2}: (7, {})} | custom-call | flops 2359296 | bytes 3538944 | tf_op jit(solution)/shard_map/update/pallas_call | solution.py:107
  48.7 3.7 %update.10 = (bf16[1,192,1024]{2,1,0:T(8,128)(2,1)}, bf16[6,512,1024]{2,1,0:T(8,128)(2,1)}, f32[6,256,1024]{2,1,0:T(8,128)}) custom-call(s32[1]{0:T(128)} %bitcast.me_ref, f32[2]{0:T(128)S(1)} %copy-done, bf16[6,512,1024]{2,1,0:T(8,128)(2,1)} %bitcast.20, bf16[6,512,1024]{2,1,0:T(8,128)(2,1)} %bitcast.11, ...), custom_call_target="tpu_custom_call", output_to_operand_aliasing={{1}: (6, {}), {2}: (7, {})} | custom-call | flops 2359296 | bytes 3538944 | tf_op jit(solution)/shard_map/update/pallas_call | solution.py:107
  52.3 2.0 %collective-permute-start.14 = (bf16[1,192,1024]{2,1,0:T(8,128)(2,1)}, bf16[1,192,1024]{2,1,0:T(8,128)(2,1)S(1)}, u32[]{:S(2)}, u32[]{:S(2)}) collective-permute-start(bf16[1,192,1024]{2,1,0:T(8,128)(2,1)} %get-tuple-element.51), channel_id=1, source_target_pairs={{0,16},{16,0},{1,17},{17,1},{2,18},{18,2},{3,19},{19,3},{4,20},{20... | collective-permute-start | bytes 1179656 | tf_op jit(solution)/shard_map/ppermute | solution.py:162
  54.4 1.0 constant_dynamic-slice_fusion.6
  55.4 4.3 %collective-permute-done.3.refs_0_ = bf16[1,192,1024]{2,1,0:T(8,128)(2,1)S(1)} collective-permute-done((bf16[1,192,1024]{2,1,0:T(8,128)(2,1)}, bf16[1,192,1024]{2,1,0:T(8,128)(2,1)S(1)}, u32[]{:S(2)}, u32[]{:S(2)}) %collective-permute-start.3) | collective-permute-done | bytes 393248 | tf_op jit(solution)/shard_map/ppermute | solution.py:162
  59.7 2.1 %collective-permute-start.1 = (bf16[2,64,1024]{2,1,0:T(8,128)(2,1)S(1)}, bf16[2,64,1024]{2,1,0:T(8,128)(2,1)S(1)}, u32[]{:S(2)}, u32[]{:S(2)}) collective-permute-start(bf16[2,64,1024]{2,1,0:T(8,128)(2,1)S(1)} %constant_dynamic-slice_fusion.6), channel_id=1, source_target_pairs={{0,16},{16,0},{1,17},{17,1},{2,18},{18,2},{3,19},{19,3},{4,20},{20... | collective-permute-start | bytes 786440 | tf_op jit(solution)/shard_map/ppermute | solution.py:162
  61.7 3.4 %update.11 = (bf16[1,192,1024]{2,1,0:T(8,128)(2,1)S(1)}, bf16[6,512,1024]{2,1,0:T(8,128)(2,1)}, f32[6,256,1024]{2,1,0:T(8,128)}) custom-call(s32[1]{0:T(128)} %bitcast.me_ref, f32[2]{0:T(128)S(1)} %copy-done.1, bf16[6,512,1024]{2,1,0:T(8,128)(2,1)} %bitcast.21, bf16[6,512,1024]{2,1,0:T(8,128)(2,1)} %bitcast.13, ...), custom_call_target="tpu_custom_call", output_to_operand_aliasing={{1}: (6, {}), {2}: (7, {})} | custom-call | flops 2359296 | bytes 3538944 | tf_op jit(solution)/shard_map/update/pallas_call | solution.py:107
  65.2 3.5 %update.12 = (bf16[1,192,1024]{2,1,0:T(8,128)(2,1)S(1)}, bf16[6,512,1024]{2,1,0:T(8,128)(2,1)}, f32[6,256,1024]{2,1,0:T(8,128)}) custom-call(s32[1]{0:T(128)} %bitcast.me_ref, f32[2]{0:T(128)S(1)} %copy-done.1, bf16[6,512,1024]{2,1,0:T(8,128)(2,1)} %bitcast.22, bf16[6,512,1024]{2,1,0:T(8,128)(2,1)} %bitcast.14, ...), custom_call_target="tpu_custom_call", output_to_operand_aliasing={{1}: (6, {}), {2}: (7, {})} | custom-call | flops 2359296 | bytes 3538944 | tf_op jit(solution)/shard_map/update/pallas_call | solution.py:107
  68.6 3.5 %update.13 = (bf16[1,192,1024]{2,1,0:T(8,128)(2,1)S(1)}, bf16[6,512,1024]{2,1,0:T(8,128)(2,1)}, f32[6,256,1024]{2,1,0:T(8,128)}) custom-call(s32[1]{0:T(128)} %bitcast.me_ref, f32[2]{0:T(128)S(1)} %copy-done.1, bf16[6,512,1024]{2,1,0:T(8,128)(2,1)} %bitcast.23, bf16[6,512,1024]{2,1,0:T(8,128)(2,1)} %bitcast.15, ...), custom_call_target="tpu_custom_call", output_to_operand_aliasing={{1}: (6, {}), {2}: (7, {})} | custom-call | flops 2359296 | bytes 3538944 | tf_op jit(solution)/shard_map/update/pallas_call | solution.py:107
  72.2 3.5 %update.14 = (bf16[1,192,1024]{2,1,0:T(8,128)(2,1)S(1)}, bf16[6,512,1024]{2,1,0:T(8,128)(2,1)}, f32[6,256,1024]{2,1,0:T(8,128)}) custom-call(s32[1]{0:T(128)} %bitcast.me_ref, f32[2]{0:T(128)S(1)} %copy-done.1, bf16[6,512,1024]{2,1,0:T(8,128)(2,1)} %bitcast.24, bf16[6,512,1024]{2,1,0:T(8,128)(2,1)} %bitcast.16, ...), custom_call_target="tpu_custom_call", output_to_operand_aliasing={{1}: (6, {}), {2}: (7, {})} | custom-call | flops 2359296 | bytes 3538944 | tf_op jit(solution)/shard_map/update/pallas_call | solution.py:107
  75.6 26.2 %collective-permute-done.1.refs_0_ = bf16[2,64,1024]{2,1,0:T(8,128)(2,1)S(1)} collective-permute-done((bf16[2,64,1024]{2,1,0:T(8,128)(2,1)S(1)}, bf16[2,64,1024]{2,1,0:T(8,128)(2,1)S(1)}, u32[]{:S(2)}, u32[]{:S(2)}) %collective-permute-start.1) | collective-permute-done | bytes 262176 | tf_op jit(solution)/shard_map/ppermute | solution.py:162
  101.8 2.1 %collective-permute-start.12 = (bf16[1,192,1024]{2,1,0:T(8,128)(2,1)S(1)}, bf16[1,192,1024]{2,1,0:T(8,128)(2,1)S(1)}, u32[]{:S(2)}, u32[]{:S(2)}) collective-permute-start(bf16[1,192,1024]{2,1,0:T(8,128)(2,1)S(1)} %get-tuple-element.49), channel_id=1, source_target_pairs={{0,16},{16,0},{1,17},{17,1},{2,18},{18,2},{3,19},{19,3},{4,20},{20... | collective-permute-start | bytes 1179656 | tf_op jit(solution)/shard_map/ppermute | solution.py:162
  103.9 2.0 %collective-permute-start.10 = (bf16[1,192,1024]{2,1,0:T(8,128)(2,1)S(1)}, bf16[1,192,1024]{2,1,0:T(8,128)(2,1)S(1)}, u32[]{:S(2)}, u32[]{:S(2)}) collective-permute-start(bf16[1,192,1024]{2,1,0:T(8,128)(2,1)S(1)} %get-tuple-element.47), channel_id=1, source_target_pairs={{0,16},{16,0},{1,17},{17,1},{2,18},{18,2},{3,19},{19,3},{4,20},{20... | collective-permute-start | bytes 1179656 | tf_op jit(solution)/shard_map/ppermute | solution.py:162
  105.9 2.2 %update.15 = (bf16[2,64,1024]{2,1,0:T(8,128)(2,1)S(1)}, bf16[6,512,1024]{2,1,0:T(8,128)(2,1)}, f32[6,256,1024]{2,1,0:T(8,128)}) custom-call(s32[1]{0:T(128)} %bitcast.me_ref, f32[2]{0:T(128)S(1)} %copy-done.1, bf16[6,512,1024]{2,1,0:T(8,128)(2,1)} %bitcast.25, bf16[6,512,1024]{2,1,0:T(8,128)(2,1)} %bitcast.17, ...), custom_call_target="tpu_custom_call", output_to_operand_aliasing={{1}: (6, {}), {2}: (7, {})} | custom-call | flops 1572864 | bytes 2359296 | tf_op jit(solution)/shard_map/update/pallas_call | solution.py:107
  108.2 0.8 place.8._
  109.0 0.8 place.9._
  109.8 0.8 place.10._
  110.6 0.8 place.11._
  111.4 7.3 %collective-permute-done.12.block_ref = bf16[1,192,1024]{2,1,0:T(8,128)(2,1)S(1)} collective-permute-done((bf16[1,192,1024]{2,1,0:T(8,128)(2,1)S(1)}, bf16[1,192,1024]{2,1,0:T(8,128)(2,1)S(1)}, u32[]{:S(2)}, u32[]{:S(2)}) %collective-permute-start.12) | collective-permute-done | bytes 393248 | tf_op jit(solution)/shard_map/ppermute | solution.py:162
  119.4 7.7 %collective-permute-done.11.block_ref = bf16[1,192,1024]{2,1,0:T(8,128)(2,1)S(1)} collective-permute-done((bf16[1,192,1024]{2,1,0:T(8,128)(2,1)S(1)}, bf16[1,192,1024]{2,1,0:T(8,128)(2,1)S(1)}, u32[]{:S(2)}, u32[]{:S(2)}) %collective-permute-start.11) | collective-permute-done | bytes 393248 | tf_op jit(solution)/shard_map/ppermute | solution.py:162
  127.9 7.7 %collective-permute-done.10.block_ref = bf16[1,192,1024]{2,1,0:T(8,128)(2,1)S(1)} collective-permute-done((bf16[1,192,1024]{2,1,0:T(8,128)(2,1)S(1)}, bf16[1,192,1024]{2,1,0:T(8,128)(2,1)S(1)}, u32[]{:S(2)}, u32[]{:S(2)}) %collective-permute-start.10) | collective-permute-done | bytes 393248 | tf_op jit(solution)/shard_map/ppermute | solution.py:162
  136.3 4.0 %collective-permute-done.9.block_ref = bf16[2,64,1024]{2,1,0:T(8,128)(2,1)S(1)} collective-permute-done((bf16[2,64,1024]{2,1,0:T(8,128)(2,1)S(1)}, bf16[2,64,1024]{2,1,0:T(8,128)(2,1)S(1)}, u32[]{:S(2)}, u32[]{:S(2)}) %collective-permute-start.9) | collective-permute-done | bytes 262176 | tf_op jit(solution)/shard_map/ppermute | solution.py:162
  (26 shorter events, 4.1 us)
Async XLA Ops:
  1.8 34.7 %collective-permute-start.8 = (bf16[4,64,1024]{2,1,0:T(8,128)(2,1)S(1)}, bf16[4,64,1024]{2,1,0:T(8,128)(2,1)S(1)}, u32[]{:S(2)}, u32[]{:S(2)}) collective-permute-start(bf16[4,64,1024]{2,1,0:T(8,128)(2,1)S(1)} %cut.1), channel_id=1, source_target_pairs={{0,16},{16,0},{1,17},{17,1},{2,18},{18,2},{3,19},{19,3},{4,20},{20... | collective-permute-start | bytes 1572872 | tf_op jit(solution)/shard_map/ppermute | solution.py:162
  7.7 35.2 %collective-permute-start.7 = (bf16[1,192,1024]{2,1,0:T(8,128)(2,1)S(1)}, bf16[1,192,1024]{2,1,0:T(8,128)(2,1)S(1)}, u32[]{:S(2)}, u32[]{:S(2)}) collective-permute-start(bf16[1,192,1024]{2,1,0:T(8,128)(2,1)S(1)} %get-tuple-element.56), channel_id=1, source_target_pairs={{0,16},{16,0},{1,17},{17,1},{2,18},{18,2},{3,19},{19,3},{4,20},{20... | collective-permute-start | bytes 1179656 | tf_op jit(solution)/shard_map/ppermute | solution.py:162
  7.7 40.8 %collective-permute-start.6 = (bf16[1,192,1024]{2,1,0:T(8,128)(2,1)}, bf16[1,192,1024]{2,1,0:T(8,128)(2,1)S(1)}, u32[]{:S(2)}, u32[]{:S(2)}) collective-permute-start(bf16[1,192,1024]{2,1,0:T(8,128)(2,1)} %get-tuple-element.57), channel_id=1, source_target_pairs={{0,16},{16,0},{1,17},{17,1},{2,18},{18,2},{3,19},{19,3},{4,20},{20... | collective-permute-start | bytes 1179656 | tf_op jit(solution)/shard_map/ppermute | solution.py:162
  9.7 24.7 %collective-permute-start = (s32[1]{0:T(128)}, s32[1]{0:T(128)}, u32[]{:S(2)}, u32[]{:S(2)}) collective-permute-start(s32[1]{0:T(128)} %param.4), channel_id=1, source_target_pairs={{0,16},{16,0},{1,17},{17,1},{2,18},{18,2},{3,19},{19,3},{4,20},{20... | collective-permute-start | bytes 20 | tf_op jit(solution)/shard_map/ppermute | solution.py:162
  9.8 42.6 %collective-permute-start.5 = (bf16[1,192,1024]{2,1,0:T(8,128)(2,1)}, bf16[1,192,1024]{2,1,0:T(8,128)(2,1)S(1)}, u32[]{:S(2)}, u32[]{:S(2)}) collective-permute-start(bf16[1,192,1024]{2,1,0:T(8,128)(2,1)} %get-tuple-element.58), channel_id=1, source_target_pairs={{0,16},{16,0},{1,17},{17,1},{2,18},{18,2},{3,19},{19,3},{4,20},{20... | collective-permute-start | bytes 1179656 | tf_op jit(solution)/shard_map/ppermute | solution.py:162
  34.4 19.9 %collective-permute-start.4 = (bf16[1,192,1024]{2,1,0:T(8,128)(2,1)}, bf16[1,192,1024]{2,1,0:T(8,128)(2,1)S(1)}, u32[]{:S(2)}, u32[]{:S(2)}) collective-permute-start(bf16[1,192,1024]{2,1,0:T(8,128)(2,1)} %get-tuple-element.59), channel_id=1, source_target_pairs={{0,16},{16,0},{1,17},{17,1},{2,18},{18,2},{3,19},{19,3},{4,20},{20... | collective-permute-start | bytes 1179656 | tf_op jit(solution)/shard_map/ppermute | solution.py:162
  36.5 23.2 %collective-permute-start.3 = (bf16[1,192,1024]{2,1,0:T(8,128)(2,1)}, bf16[1,192,1024]{2,1,0:T(8,128)(2,1)S(1)}, u32[]{:S(2)}, u32[]{:S(2)}) collective-permute-start(bf16[1,192,1024]{2,1,0:T(8,128)(2,1)} %get-tuple-element.60), channel_id=1, source_target_pairs={{0,16},{16,0},{1,17},{17,1},{2,18},{18,2},{3,19},{19,3},{4,20},{20... | collective-permute-start | bytes 1179656 | tf_op jit(solution)/shard_map/ppermute | solution.py:162
  38.4 0.6 copy-start
  42.9 29.2 %collective-permute-start.2 = (bf16[1,192,1024]{2,1,0:T(8,128)(2,1)}, bf16[1,192,1024]{2,1,0:T(8,128)(2,1)S(1)}, u32[]{:S(2)}, u32[]{:S(2)}) collective-permute-start(bf16[1,192,1024]{2,1,0:T(8,128)(2,1)} %get-tuple-element.61), channel_id=1, source_target_pairs={{0,16},{16,0},{1,17},{17,1},{2,18},{18,2},{3,19},{19,3},{4,20},{20... | collective-permute-start | bytes 1179656 | tf_op jit(solution)/shard_map/ppermute | solution.py:162
  48.6 55.3 %collective-permute-start.15 = (bf16[1,192,1024]{2,1,0:T(8,128)(2,1)}, bf16[1,192,1024]{2,1,0:T(8,128)(2,1)S(1)}, u32[]{:S(2)}, u32[]{:S(2)}) collective-permute-start(bf16[1,192,1024]{2,1,0:T(8,128)(2,1)} %get-tuple-element.52), channel_id=1, source_target_pairs={{0,16},{16,0},{1,17},{17,1},{2,18},{18,2},{3,19},{19,3},{4,20},{20... | collective-permute-start | bytes 1179656 | tf_op jit(solution)/shard_map/ppermute | solution.py:162
  48.7 13.1 %copy-start.1 = (f32[2]{0:T(128)S(1)}, f32[2]{0:T(128)}, u32[]{:S(2)}) copy-start(f32[2]{0:T(128)} %share.1.shares_ref) | copy-start | bytes 28
  52.3 51.6 %collective-permute-start.14 = (bf16[1,192,1024]{2,1,0:T(8,128)(2,1)}, bf16[1,192,1024]{2,1,0:T(8,128)(2,1)S(1)}, u32[]{:S(2)}, u32[]{:S(2)}) collective-permute-start(bf16[1,192,1024]{2,1,0:T(8,128)(2,1)} %get-tuple-element.51), channel_id=1, source_target_pairs={{0,16},{16,0},{1,17},{17,1},{2,18},{18,2},{3,19},{19,3},{4,20},{20... | collective-permute-start | bytes 1179656 | tf_op jit(solution)/shard_map/ppermute | solution.py:162
  54.3 53.7 %collective-permute-start.16 = (bf16[4,64,1024]{2,1,0:T(8,128)(2,1)S(1)}, bf16[4,64,1024]{2,1,0:T(8,128)(2,1)S(1)}, u32[]{:S(2)}, u32[]{:S(2)}) collective-permute-start(bf16[4,64,1024]{2,1,0:T(8,128)(2,1)S(1)} %get-tuple-element.53), channel_id=1, source_target_pairs={{0,16},{16,0},{1,17},{17,1},{2,18},{18,2},{3,19},{19,3},{4,20},{20... | collective-permute-start | bytes 1572872 | tf_op jit(solution)/shard_map/ppermute | solution.py:162
  59.7 42.1 %collective-permute-start.1 = (bf16[2,64,1024]{2,1,0:T(8,128)(2,1)S(1)}, bf16[2,64,1024]{2,1,0:T(8,128)(2,1)S(1)}, u32[]{:S(2)}, u32[]{:S(2)}) collective-permute-start(bf16[2,64,1024]{2,1,0:T(8,128)(2,1)S(1)} %constant_dynamic-slice_fusion.6), channel_id=1, source_target_pairs={{0,16},{16,0},{1,17},{17,1},{2,18},{18,2},{3,19},{19,3},{4,20},{20... | collective-permute-start | bytes 786440 | tf_op jit(solution)/shard_map/ppermute | solution.py:162
  72.1 38.5 %collective-permute-start.13 = (bf16[1,192,1024]{2,1,0:T(8,128)(2,1)S(1)}, bf16[1,192,1024]{2,1,0:T(8,128)(2,1)S(1)}, u32[]{:S(2)}, u32[]{:S(2)}) collective-permute-start(bf16[1,192,1024]{2,1,0:T(8,128)(2,1)S(1)} %get-tuple-element.50), channel_id=1, source_target_pairs={{0,16},{16,0},{1,17},{17,1},{2,18},{18,2},{3,19},{19,3},{4,20},{20... | collective-permute-start | bytes 1179656 | tf_op jit(solution)/shard_map/ppermute | solution.py:162
  101.8 16.9 %collective-permute-start.12 = (bf16[1,192,1024]{2,1,0:T(8,128)(2,1)S(1)}, bf16[1,192,1024]{2,1,0:T(8,128)(2,1)S(1)}, u32[]{:S(2)}, u32[]{:S(2)}) collective-permute-start(bf16[1,192,1024]{2,1,0:T(8,128)(2,1)S(1)} %get-tuple-element.49), channel_id=1, source_target_pairs={{0,16},{16,0},{1,17},{17,1},{2,18},{18,2},{3,19},{19,3},{4,20},{20... | collective-permute-start | bytes 1179656 | tf_op jit(solution)/shard_map/ppermute | solution.py:162
  103.9 23.2 %collective-permute-start.11 = (bf16[1,192,1024]{2,1,0:T(8,128)(2,1)S(1)}, bf16[1,192,1024]{2,1,0:T(8,128)(2,1)S(1)}, u32[]{:S(2)}, u32[]{:S(2)}) collective-permute-start(bf16[1,192,1024]{2,1,0:T(8,128)(2,1)S(1)} %get-tuple-element.48), channel_id=1, source_target_pairs={{0,16},{16,0},{1,17},{17,1},{2,18},{18,2},{3,19},{19,3},{4,20},{20... | collective-permute-start | bytes 1179656 | tf_op jit(solution)/shard_map/ppermute | solution.py:162
  103.9 31.6 %collective-permute-start.10 = (bf16[1,192,1024]{2,1,0:T(8,128)(2,1)S(1)}, bf16[1,192,1024]{2,1,0:T(8,128)(2,1)S(1)}, u32[]{:S(2)}, u32[]{:S(2)}) collective-permute-start(bf16[1,192,1024]{2,1,0:T(8,128)(2,1)S(1)} %get-tuple-element.47), channel_id=1, source_target_pairs={{0,16},{16,0},{1,17},{17,1},{2,18},{18,2},{3,19},{19,3},{4,20},{20... | collective-permute-start | bytes 1179656 | tf_op jit(solution)/shard_map/ppermute | solution.py:162
  108.1 32.2 %collective-permute-start.9 = (bf16[2,64,1024]{2,1,0:T(8,128)(2,1)S(1)}, bf16[2,64,1024]{2,1,0:T(8,128)(2,1)S(1)}, u32[]{:S(2)}, u32[]{:S(2)}) collective-permute-start(bf16[2,64,1024]{2,1,0:T(8,128)(2,1)S(1)} %get-tuple-element.46), channel_id=1, source_target_pairs={{0,16},{16,0},{1,17},{17,1},{2,18},{18,2},{3,19},{19,3},{4,20},{20... | collective-permute-start | bytes 786440 | tf_op jit(solution)/shard_map/ppermute | solution.py:162

commit v13 on v7

--- a/solution.py
+++ b/solution.py
@@ -234,13 +234,8 @@
         momentum = momentum.reshape(parts, owned, width)
         me = lax.axis_index("replica")
         half = owned // 2
-        last = max(16, owned // 4)
         chunks = [Chunk(0, 1, 0, half), Chunk(0, 1, half, half)]
-        chunks += [Chunk(p, 1, 0, owned) for p in range(1, parts - 1)]
-        chunks += [
-            Chunk(parts - 1, 1, 0, owned - last),
-            Chunk(parts - 1, 1, owned - last, last),
-        ]
+        chunks += [Chunk(p, 1, 0, owned) for p in range(1, parts)]
         shifts = range(1, groups)
 
         def rows_for(array, chunk, target):

time: 142 us -> 142 us (level)
  waiting for transfers between devices: 78.3 us -> 82.9 us
  Pallas kernels: 32.7 us -> 29.4 us
  local copies, waits for them, and re-layouts: 6.18 us -> 3.89 us
    ppermute x16 -> x14, waiting for transfers between devices: 78.3 us -> 82.9 us  [shifted(): return lax.ppermute(value, 'replica', pairs)]
    pallas_call x8 -> x7, Pallas kernels: 23.5 us -> 20.7 us  [update(): pl.pallas_call(functools.partial(update_kernel, groups), grid_spec=pltpu....]
    dynamic_slice x3 -> x1, local copies, waits for them, and re-layouts: 5.57 us -> 3.23 us  [rows_for(): lax.dynamic_slice(array, (chunk.lo, target * owned + chunk.row, 0), sizes)]
    ppermute x16 -> x14, starting transfers between devices: 22.2 us -> 23.5 us  [shifted(): return lax.ppermute(value, 'replica', pairs)]
    pallas_call x8 -> x7, Pallas kernels: 6.07 us -> 5.48 us  [place(): pl.pallas_call(functools.partial(place_kernel, groups, owned, chunk, shif...]
  transfers between devices with their start and end apart: 16 -> 14, of which waited for: 10 -> 10; matrix products, arithmetic and copies ran while one was open for 4% -> 2% of each run, Pallas kernels for 22% -> 20%
where the time goes in v13:
time: 142 us; the launch traced here: 141 us
  waiting for transfers between devices  82.9 us (58%)
  Pallas kernels  29.4 us (21%)
  starting transfers between devices  23.5 us (17%)
  local copies, waits for them, and re-layouts  3.89 us (3%)
    ppermute x14, waiting for transfers between devices, shifted(): return lax.ppermute(value, 'replica', pairs)  82.9 us
    ppermute x14, starting transfers between devices, shifted(): return lax.ppermute(value, 'replica', pairs)  23.5 us
    pallas_call x7, Pallas kernels, update(): pl.pallas_call(functools.partial(update_kernel, groups), grid_spec=pltpu....  20.7 us
    pallas_call x7, Pallas kernels, place(): pl.pallas_call(functools.partial(place_kernel, groups, owned, chunk, shif...  5.48 us
    dynamic_slice x1, local copies, waits for them, and re-layouts, rows_for(): lax.dynamic_slice(array, (chunk.lo, target * owned + chunk.row, 0), sizes)  3.23 us
  transfers between devices with their start and end apart: 14, of which 10 were waited for; matrix products, arithmetic and copies ran while one was open for 2% of the time, Pallas kernels for 20%

profile of v13, /device:TPU:0, one launch (start us, length us, event | category | flops | bytes accessed | tf_op | source)
XLA Modules:
  0.0 141.0 jit_solution(9165307868335511275)
XLA Ops:
  0.6 1.0 cut.1
  1.6 3.0 %collective-permute-start.6 = (bf16[1,128,1024]{2,1,0:T(8,128)(2,1)S(1)}, bf16[1,128,1024]{2,1,0:T(8,128)(2,1)S(1)}, u32[]{:S(2)}, u32[]{:S(2)}) collective-permute-start(bf16[1,128,1024]{2,1,0:T(8,128)(2,1)S(1)} %cut.1), channel_id=1, source_target_pairs={{0,16},{16,0},{1,17},{17,1},{2,18},{18,2},{3,19},{19,3},{4,20},{20... | collective-permute-start | bytes 786440 | tf_op jit(solution)/shard_map/ppermute | solution.py:226
  5.3 1.0 pack.1
  6.3 3.2 %constant_dynamic-slice_fusion = (bf16[1,256,1024]{2,1,0:T(8,128)(2,1)}, bf16[1,256,1024]{2,1,0:T(8,128)(2,1)}, bf16[1,256,1024]{2,1,0:T(8,128)(2,1)}, bf16[1,256,1024]{2,1,0:T(8,128)(2,1)}, bf16[1,256,1024]{2,1,0:T(8,128)(2,1)}) fusion(bf16[6,512,1024]{2,1,0:T(8,128)(2,1)} %bitcast.10, s32[]{:T(128)S(6)} %select_n.15), kind=kLoop, calls=%fused_computation | loop fusion | bytes 5242884 | tf_op jit(solution)/shard_map/dynamic_slice | solution.py:243
  9.6 2.0 %collective-permute-start.5 = (bf16[1,256,1024]{2,1,0:T(8,128)(2,1)}, bf16[1,256,1024]{2,1,0:T(8,128)(2,1)S(1)}, u32[]{:S(2)}, u32[]{:S(2)}) collective-permute-start(bf16[1,256,1024]{2,1,0:T(8,128)(2,1)} %get-tuple-element.50), channel_id=1, source_target_pairs={{0,16},{16,0},{1,17},{17,1},{2,18},{18,2},{3,19},{19,3},{4,20},{20... | collective-permute-start | bytes 1572872 | tf_op jit(solution)/shard_map/ppermute | solution.py:226
  11.6 2.0 %collective-permute-start.3 = (bf16[1,256,1024]{2,1,0:T(8,128)(2,1)}, bf16[1,256,1024]{2,1,0:T(8,128)(2,1)S(1)}, u32[]{:S(2)}, u32[]{:S(2)}) collective-permute-start(bf16[1,256,1024]{2,1,0:T(8,128)(2,1)} %get-tuple-element.52), channel_id=1, source_target_pairs={{0,16},{16,0},{1,17},{17,1},{2,18},{18,2},{3,19},{19,3},{4,20},{20... | collective-permute-start | bytes 1572872 | tf_op jit(solution)/shard_map/ppermute | solution.py:226
  13.8 3.6 %collective-permute-done.refs_0_ = bf16[1040,128]{1,0:T(8,128)(2,1)S(1)} collective-permute-done((bf16[1040,128]{1,0:T(8,128)(2,1)S(1)}, bf16[1040,128]{1,0:T(8,128)(2,1)S(1)}, u32[]{:S(2)}, u32[]{:S(2)}) %collective-permute-start) | collective-permute-done | bytes 266272 | tf_op jit(solution)/shard_map/ppermute | solution.py:226
  17.5 2.1 %collective-permute-start.1 = (bf16[1,256,1024]{2,1,0:T(8,128)(2,1)}, bf16[1,256,1024]{2,1,0:T(8,128)(2,1)S(1)}, u32[]{:S(2)}, u32[]{:S(2)}) collective-permute-start(bf16[1,256,1024]{2,1,0:T(8,128)(2,1)} %get-tuple-element.54), channel_id=1, source_target_pairs={{0,16},{16,0},{1,17},{17,1},{2,18},{18,2},{3,19},{19,3},{4,20},{20... | collective-permute-start | bytes 1572872 | tf_op jit(solution)/shard_map/ppermute | solution.py:226
  19.5 1.3 share.1.shares_ref
  21.4 2.3 %update.7 = (bf16[1,128,1024]{2,1,0:T(8,128)(2,1)S(1)}, bf16[6,512,1024]{2,1,0:T(8,128)(2,1)}, f32[6,256,1024]{2,1,0:T(8,128)}) custom-call(s32[1]{0:T(128)} %bitcast.me_ref, f32[2]{0:T(128)S(1)} %copy-done.2, bf16[6,512,1024]{2,1,0:T(8,128)(2,1)} %bitcast.18, bf16[6,512,1024]{2,1,0:T(8,128)(2,1)} %bitcast.11, ...), custom_call_target="tpu_custom_call" | custom-call | flops 1572864 | bytes 2359296 | tf_op jit(solution)/shard_map/update/pallas_call | solution.py:171
  23.8 5.2 %update.8 = (bf16[1,128,1024]{2,1,0:T(8,128)(2,1)S(1)}, bf16[6,512,1024]{2,1,0:T(8,128)(2,1)}, f32[6,256,1024]{2,1,0:T(8,128)}) custom-call(s32[1]{0:T(128)} %bitcast.me_ref, f32[2]{0:T(128)S(1)} %copy-done.2, bf16[6,512,1024]{2,1,0:T(8,128)(2,1)} %bitcast.19, bf16[6,512,1024]{2,1,0:T(8,128)(2,1)} %bitcast.12, ...), custom_call_target="tpu_custom_call", output_to_operand_aliasing={{1}: (6, {}), {2}: (7, {})} | custom-call | flops 1572864 | bytes 2359296 | tf_op jit(solution)/shard_map/update/pallas_call | solution.py:171
  29.0 1.8 %collective-permute-start.12 = (bf16[1,128,1024]{2,1,0:T(8,128)(2,1)S(1)}, bf16[1,128,1024]{2,1,0:T(8,128)(2,1)S(1)}, u32[]{:S(2)}, u32[]{:S(2)}) collective-permute-start(bf16[1,128,1024]{2,1,0:T(8,128)(2,1)S(1)} %get-tuple-element.46), channel_id=1, source_target_pairs={{0,16},{16,0},{1,17},{17,1},{2,18},{18,2},{3,19},{19,3},{4,20},{20... | collective-permute-start | bytes 786440 | tf_op jit(solution)/shard_map/ppermute | solution.py:226
  30.7 9.2 %collective-permute-done.4.refs_0_ = bf16[1,256,1024]{2,1,0:T(8,128)(2,1)S(1)} collective-permute-done((bf16[1,256,1024]{2,1,0:T(8,128)(2,1)}, bf16[1,256,1024]{2,1,0:T(8,128)(2,1)S(1)}, u32[]{:S(2)}, u32[]{:S(2)}) %collective-permute-start.4) | collective-permute-done | bytes 524320 | tf_op jit(solution)/shard_map/ppermute | solution.py:226
  39.9 2.1 %collective-permute-start.13 = (bf16[1,128,1024]{2,1,0:T(8,128)(2,1)S(1)}, bf16[1,128,1024]{2,1,0:T(8,128)(2,1)S(1)}, u32[]{:S(2)}, u32[]{:S(2)}) collective-permute-start(bf16[1,128,1024]{2,1,0:T(8,128)(2,1)S(1)} %get-tuple-element.47), channel_id=1, source_target_pairs={{0,16},{16,0},{1,17},{17,1},{2,18},{18,2},{3,19},{19,3},{4,20},{20... | collective-permute-start | bytes 786440 | tf_op jit(solution)/shard_map/ppermute | solution.py:226
  42.0 2.6 %update.9 = (bf16[1,256,1024]{2,1,0:T(8,128)(2,1)S(1)}, bf16[6,512,1024]{2,1,0:T(8,128)(2,1)}, f32[6,256,1024]{2,1,0:T(8,128)}) custom-call(s32[1]{0:T(128)} %bitcast.me_ref, f32[2]{0:T(128)S(1)} %copy-done.2, bf16[6,512,1024]{2,1,0:T(8,128)(2,1)} %bitcast.20, bf16[6,512,1024]{2,1,0:T(8,128)(2,1)} %bitcast.13, ...), custom_call_target="tpu_custom_call", output_to_operand_aliasing={{1}: (6, {}), {2}: (7, {})} | custom-call | flops 3145728 | bytes 4718592 | tf_op jit(solution)/shard_map/update/pallas_call | solution.py:171
  44.6 2.6 %update.10 = (bf16[1,256,1024]{2,1,0:T(8,128)(2,1)S(1)}, bf16[6,512,1024]{2,1,0:T(8,128)(2,1)}, f32[6,256,1024]{2,1,0:T(8,128)}) custom-call(s32[1]{0:T(128)} %bitcast.me_ref, f32[2]{0:T(128)S(1)} %copy-done.2, bf16[6,512,1024]{2,1,0:T(8,128)(2,1)} %bitcast.21, bf16[6,512,1024]{2,1,0:T(8,128)(2,1)} %bitcast.14, ...), custom_call_target="tpu_custom_call", output_to_operand_aliasing={{1}: (6, {}), {2}: (7, {})} | custom-call | flops 3145728 | bytes 4718592 | tf_op jit(solution)/shard_map/update/pallas_call | solution.py:171
  47.3 3.9 %collective-permute-done.3.refs_0_ = bf16[1,256,1024]{2,1,0:T(8,128)(2,1)S(1)} collective-permute-done((bf16[1,256,1024]{2,1,0:T(8,128)(2,1)}, bf16[1,256,1024]{2,1,0:T(8,128)(2,1)S(1)}, u32[]{:S(2)}, u32[]{:S(2)}) %collective-permute-start.3) | collective-permute-done | bytes 524320 | tf_op jit(solution)/shard_map/ppermute | solution.py:226
  51.2 2.6 %update.11 = (bf16[1,256,1024]{2,1,0:T(8,128)(2,1)S(1)}, bf16[6,512,1024]{2,1,0:T(8,128)(2,1)}, f32[6,256,1024]{2,1,0:T(8,128)}) custom-call(s32[1]{0:T(128)} %bitcast.me_ref, f32[2]{0:T(128)S(1)} %copy-done.2, bf16[6,512,1024]{2,1,0:T(8,128)(2,1)} %bitcast.22, bf16[6,512,1024]{2,1,0:T(8,128)(2,1)} %bitcast.15, ...), custom_call_target="tpu_custom_call", output_to_operand_aliasing={{1}: (6, {}), {2}: (7, {})} | custom-call | flops 3145728 | bytes 4718592 | tf_op jit(solution)/shard_map/update/pallas_call | solution.py:171
  53.8 2.1 %collective-permute-start.9 = (bf16[1,256,1024]{2,1,0:T(8,128)(2,1)S(1)}, bf16[1,256,1024]{2,1,0:T(8,128)(2,1)S(1)}, u32[]{:S(2)}, u32[]{:S(2)}) collective-permute-start(bf16[1,256,1024]{2,1,0:T(8,128)(2,1)S(1)} %get-tuple-element.43), channel_id=1, source_target_pairs={{0,16},{16,0},{1,17},{17,1},{2,18},{18,2},{3,19},{19,3},{4,20},{20... | collective-permute-start | bytes 1572872 | tf_op jit(solution)/shard_map/ppermute | solution.py:226
  55.8 6.5 %collective-permute-done.2.refs_0_ = bf16[1,256,1024]{2,1,0:T(8,128)(2,1)S(1)} collective-permute-done((bf16[1,256,1024]{2,1,0:T(8,128)(2,1)}, bf16[1,256,1024]{2,1,0:T(8,128)(2,1)S(1)}, u32[]{:S(2)}, u32[]{:S(2)}) %collective-permute-start.2) | collective-permute-done | bytes 524320 | tf_op jit(solution)/shard_map/ppermute | solution.py:226
  62.4 2.1 %collective-permute-start.10 = (bf16[1,256,1024]{2,1,0:T(8,128)(2,1)S(1)}, bf16[1,256,1024]{2,1,0:T(8,128)(2,1)S(1)}, u32[]{:S(2)}, u32[]{:S(2)}) collective-permute-start(bf16[1,256,1024]{2,1,0:T(8,128)(2,1)S(1)} %get-tuple-element.44), channel_id=1, source_target_pairs={{0,16},{16,0},{1,17},{17,1},{2,18},{18,2},{3,19},{19,3},{4,20},{20... | collective-permute-start | bytes 1572872 | tf_op jit(solution)/shard_map/ppermute | solution.py:226
  64.5 2.6 %update.12 = (bf16[1,256,1024]{2,1,0:T(8,128)(2,1)S(1)}, bf16[6,512,1024]{2,1,0:T(8,128)(2,1)}, f32[6,256,1024]{2,1,0:T(8,128)}) custom-call(s32[1]{0:T(128)} %bitcast.me_ref, f32[2]{0:T(128)S(1)} %copy-done.2, bf16[6,512,1024]{2,1,0:T(8,128)(2,1)} %bitcast.23, bf16[6,512,1024]{2,1,0:T(8,128)(2,1)} %bitcast.16, ...), custom_call_target="tpu_custom_call", output_to_operand_aliasing={{1}: (6, {}), {2}: (7, {})} | custom-call | flops 3145728 | bytes 4718592 | tf_op jit(solution)/shard_map/update/pallas_call | solution.py:171
  67.1 6.5 %collective-permute-done.1.refs_0_ = bf16[1,256,1024]{2,1,0:T(8,128)(2,1)S(1)} collective-permute-done((bf16[1,256,1024]{2,1,0:T(8,128)(2,1)}, bf16[1,256,1024]{2,1,0:T(8,128)(2,1)S(1)}, u32[]{:S(2)}, u32[]{:S(2)}) %collective-permute-start.1) | collective-permute-done | bytes 524320 | tf_op jit(solution)/shard_map/ppermute | solution.py:226
  73.6 2.1 %collective-permute-start.11 = (bf16[1,256,1024]{2,1,0:T(8,128)(2,1)S(1)}, bf16[1,256,1024]{2,1,0:T(8,128)(2,1)S(1)}, u32[]{:S(2)}, u32[]{:S(2)}) collective-permute-start(bf16[1,256,1024]{2,1,0:T(8,128)(2,1)S(1)} %get-tuple-element.45), channel_id=1, source_target_pairs={{0,16},{16,0},{1,17},{17,1},{2,18},{18,2},{3,19},{19,3},{4,20},{20... | collective-permute-start | bytes 1572872 | tf_op jit(solution)/shard_map/ppermute | solution.py:226
  75.7 2.6 %update.13 = (bf16[1,256,1024]{2,1,0:T(8,128)(2,1)S(1)}, bf16[6,512,1024]{2,1,0:T(8,128)(2,1)}, f32[6,256,1024]{2,1,0:T(8,128)}) custom-call(s32[1]{0:T(128)} %bitcast.me_ref, f32[2]{0:T(128)S(1)} %copy-done.2, bf16[6,512,1024]{2,1,0:T(8,128)(2,1)} %bitcast.24, bf16[6,512,1024]{2,1,0:T(8,128)(2,1)} %bitcast.17, ...), custom_call_target="tpu_custom_call", output_to_operand_aliasing={{1}: (6, {}), {2}: (7, {})} | custom-call | flops 3145728 | bytes 4718592 | tf_op jit(solution)/shard_map/update/pallas_call | solution.py:171
  78.3 0.9 collective-permute-done.12.block_ref
  79.2 2.1 %collective-permute-start.8 = (bf16[1,256,1024]{2,1,0:T(8,128)(2,1)S(1)}, bf16[1,256,1024]{2,1,0:T(8,128)(2,1)S(1)}, u32[]{:S(2)}, u32[]{:S(2)}) collective-permute-start(bf16[1,256,1024]{2,1,0:T(8,128)(2,1)S(1)} %get-tuple-element.42), channel_id=1, source_target_pairs={{0,16},{16,0},{1,17},{17,1},{2,18},{18,2},{3,19},{19,3},{4,20},{20... | collective-permute-start | bytes 1572872 | tf_op jit(solution)/shard_map/ppermute | solution.py:226
  81.3 3.6 %collective-permute-done.13.block_ref = bf16[1,128,1024]{2,1,0:T(8,128)(2,1)S(1)} collective-permute-done((bf16[1,128,1024]{2,1,0:T(8,128)(2,1)S(1)}, bf16[1,128,1024]{2,1,0:T(8,128)(2,1)S(1)}, u32[]{:S(2)}, u32[]{:S(2)}) %collective-permute-start.13) | collective-permute-done | bytes 262176 | tf_op jit(solution)/shard_map/ppermute | solution.py:226
  84.9 2.1 %collective-permute-start.7 = (bf16[1,256,1024]{2,1,0:T(8,128)(2,1)S(1)}, bf16[1,256,1024]{2,1,0:T(8,128)(2,1)S(1)}, u32[]{:S(2)}, u32[]{:S(2)}) collective-permute-start(bf16[1,256,1024]{2,1,0:T(8,128)(2,1)S(1)} %get-tuple-element.41), channel_id=1, source_target_pairs={{0,16},{16,0},{1,17},{17,1},{2,18},{18,2},{3,19},{19,3},{4,20},{20... | collective-permute-start | bytes 1572872 | tf_op jit(solution)/shard_map/ppermute | solution.py:226
  88.4 30.2 %collective-permute-done.11.block_ref = bf16[1,256,1024]{2,1,0:T(8,128)(2,1)S(1)} collective-permute-done((bf16[1,256,1024]{2,1,0:T(8,128)(2,1)S(1)}, bf16[1,256,1024]{2,1,0:T(8,128)(2,1)S(1)}, u32[]{:S(2)}, u32[]{:S(2)}) %collective-permute-start.11) | collective-permute-done | bytes 524320 | tf_op jit(solution)/shard_map/ppermute | solution.py:226
  121.1 8.8 %collective-permute-done.8.block_ref = bf16[1,256,1024]{2,1,0:T(8,128)(2,1)S(1)} collective-permute-done((bf16[1,256,1024]{2,1,0:T(8,128)(2,1)S(1)}, bf16[1,256,1024]{2,1,0:T(8,128)(2,1)S(1)}, u32[]{:S(2)}, u32[]{:S(2)}) %collective-permute-start.8) | collective-permute-done | bytes 524320 | tf_op jit(solution)/shard_map/ppermute | solution.py:226
  130.6 9.6 %collective-permute-done.7.block_ref = bf16[1,256,1024]{2,1,0:T(8,128)(2,1)S(1)} collective-permute-done((bf16[1,256,1024]{2,1,0:T(8,128)(2,1)S(1)}, bf16[1,256,1024]{2,1,0:T(8,128)(2,1)S(1)}, u32[]{:S(2)}, u32[]{:S(2)}) %collective-permute-start.7) | collective-permute-done | bytes 524320 | tf_op jit(solution)/shard_map/ppermute | solution.py:226
  (20 shorter events, 6.5 us)
Async XLA Ops:
  1.6 12.0 %collective-permute-start.6 = (bf16[1,128,1024]{2,1,0:T(8,128)(2,1)S(1)}, bf16[1,128,1024]{2,1,0:T(8,128)(2,1)S(1)}, u32[]{:S(2)}, u32[]{:S(2)}) collective-permute-start(bf16[1,128,1024]{2,1,0:T(8,128)(2,1)S(1)} %cut.1), channel_id=1, source_target_pairs={{0,16},{16,0},{1,17},{17,1},{2,18},{18,2},{3,19},{19,3},{4,20},{20... | collective-permute-start | bytes 786440 | tf_op jit(solution)/shard_map/ppermute | solution.py:226
  6.2 11.2 %collective-permute-start = (bf16[1040,128]{1,0:T(8,128)(2,1)S(1)}, bf16[1040,128]{1,0:T(8,128)(2,1)S(1)}, u32[]{:S(2)}, u32[]{:S(2)}) collective-permute-start(bf16[1040,128]{1,0:T(8,128)(2,1)S(1)} %pack.1), channel_id=1, source_target_pairs={{0,16},{16,0},{1,17},{17,1},{2,18},{18,2},{3,19},{19,3},{4,20},{20... | collective-permute-start | bytes 798728 | tf_op jit(solution)/shard_map/ppermute | solution.py:226
  9.6 19.4 %collective-permute-start.5 = (bf16[1,256,1024]{2,1,0:T(8,128)(2,1)}, bf16[1,256,1024]{2,1,0:T(8,128)(2,1)S(1)}, u32[]{:S(2)}, u32[]{:S(2)}) collective-permute-start(bf16[1,256,1024]{2,1,0:T(8,128)(2,1)} %get-tuple-element.50), channel_id=1, source_target_pairs={{0,16},{16,0},{1,17},{17,1},{2,18},{18,2},{3,19},{19,3},{4,20},{20... | collective-permute-start | bytes 1572872 | tf_op jit(solution)/shard_map/ppermute | solution.py:226
  11.6 28.4 %collective-permute-start.4 = (bf16[1,256,1024]{2,1,0:T(8,128)(2,1)}, bf16[1,256,1024]{2,1,0:T(8,128)(2,1)S(1)}, u32[]{:S(2)}, u32[]{:S(2)}) collective-permute-start(bf16[1,256,1024]{2,1,0:T(8,128)(2,1)} %get-tuple-element.51), channel_id=1, source_target_pairs={{0,16},{16,0},{1,17},{17,1},{2,18},{18,2},{3,19},{19,3},{4,20},{20... | collective-permute-start | bytes 1572872 | tf_op jit(solution)/shard_map/ppermute | solution.py:226
  11.6 39.6 %collective-permute-start.3 = (bf16[1,256,1024]{2,1,0:T(8,128)(2,1)}, bf16[1,256,1024]{2,1,0:T(8,128)(2,1)S(1)}, u32[]{:S(2)}, u32[]{:S(2)}) collective-permute-start(bf16[1,256,1024]{2,1,0:T(8,128)(2,1)} %get-tuple-element.52), channel_id=1, source_target_pairs={{0,16},{16,0},{1,17},{17,1},{2,18},{18,2},{3,19},{19,3},{4,20},{20... | collective-permute-start | bytes 1572872 | tf_op jit(solution)/shard_map/ppermute | solution.py:226
  13.6 48.8 %collective-permute-start.2 = (bf16[1,256,1024]{2,1,0:T(8,128)(2,1)}, bf16[1,256,1024]{2,1,0:T(8,128)(2,1)S(1)}, u32[]{:S(2)}, u32[]{:S(2)}) collective-permute-start(bf16[1,256,1024]{2,1,0:T(8,128)(2,1)} %get-tuple-element.53), channel_id=1, source_target_pairs={{0,16},{16,0},{1,17},{17,1},{2,18},{18,2},{3,19},{19,3},{4,20},{20... | collective-permute-start | bytes 1572872 | tf_op jit(solution)/shard_map/ppermute | solution.py:226
  17.5 2.1 %copy-start = (bf16[1040,128]{1,0:T(8,128)(2,1)}, bf16[1040,128]{1,0:T(8,128)(2,1)S(1)}, u32[]{:S(2)}) copy-start(bf16[1040,128]{1,0:T(8,128)(2,1)S(1)} %collective-permute-done.refs_0_) | copy-start | bytes 798724
  17.5 56.2 %collective-permute-start.1 = (bf16[1,256,1024]{2,1,0:T(8,128)(2,1)}, bf16[1,256,1024]{2,1,0:T(8,128)(2,1)S(1)}, u32[]{:S(2)}, u32[]{:S(2)}) collective-permute-start(bf16[1,256,1024]{2,1,0:T(8,128)(2,1)} %get-tuple-element.54), channel_id=1, source_target_pairs={{0,16},{16,0},{1,17},{17,1},{2,18},{18,2},{3,19},{19,3},{4,20},{20... | collective-permute-start | bytes 1572872 | tf_op jit(solution)/shard_map/ppermute | solution.py:226
  20.8 0.7 copy-start.2
  21.4 2.3 %copy-start.1 = (bf16[1040,128]{1,0:T(8,128)(2,1)S(1)}, bf16[1040,128]{1,0:T(8,128)(2,1)}, u32[]{:S(2)}) copy-start(bf16[1040,128]{1,0:T(8,128)(2,1)} %copy-done) | copy-start | bytes 798724
  29.0 50.3 %collective-permute-start.12 = (bf16[1,128,1024]{2,1,0:T(8,128)(2,1)S(1)}, bf16[1,128,1024]{2,1,0:T(8,128)(2,1)S(1)}, u32[]{:S(2)}, u32[]{:S(2)}) collective-permute-start(bf16[1,128,1024]{2,1,0:T(8,128)(2,1)S(1)} %get-tuple-element.46), channel_id=1, source_target_pairs={{0,16},{16,0},{1,17},{17,1},{2,18},{18,2},{3,19},{19,3},{4,20},{20... | collective-permute-start | bytes 786440 | tf_op jit(solution)/shard_map/ppermute | solution.py:226
  39.9 44.9 %collective-permute-start.13 = (bf16[1,128,1024]{2,1,0:T(8,128)(2,1)S(1)}, bf16[1,128,1024]{2,1,0:T(8,128)(2,1)S(1)}, u32[]{:S(2)}, u32[]{:S(2)}) collective-permute-start(bf16[1,128,1024]{2,1,0:T(8,128)(2,1)S(1)} %get-tuple-element.47), channel_id=1, source_target_pairs={{0,16},{16,0},{1,17},{17,1},{2,18},{18,2},{3,19},{19,3},{4,20},{20... | collective-permute-start | bytes 786440 | tf_op jit(solution)/shard_map/ppermute | solution.py:226
  53.8 66.4 %collective-permute-start.9 = (bf16[1,256,1024]{2,1,0:T(8,128)(2,1)S(1)}, bf16[1,256,1024]{2,1,0:T(8,128)(2,1)S(1)}, u32[]{:S(2)}, u32[]{:S(2)}) collective-permute-start(bf16[1,256,1024]{2,1,0:T(8,128)(2,1)S(1)} %get-tuple-element.43), channel_id=1, source_target_pairs={{0,16},{16,0},{1,17},{17,1},{2,18},{18,2},{3,19},{19,3},{4,20},{20... | collective-permute-start | bytes 1572872 | tf_op jit(solution)/shard_map/ppermute | solution.py:226
  62.4 57.0 %collective-permute-start.10 = (bf16[1,256,1024]{2,1,0:T(8,128)(2,1)S(1)}, bf16[1,256,1024]{2,1,0:T(8,128)(2,1)S(1)}, u32[]{:S(2)}, u32[]{:S(2)}) collective-permute-start(bf16[1,256,1024]{2,1,0:T(8,128)(2,1)S(1)} %get-tuple-element.44), channel_id=1, source_target_pairs={{0,16},{16,0},{1,17},{17,1},{2,18},{18,2},{3,19},{19,3},{4,20},{20... | collective-permute-start | bytes 1572872 | tf_op jit(solution)/shard_map/ppermute | solution.py:226
  73.6 44.9 %collective-permute-start.11 = (bf16[1,256,1024]{2,1,0:T(8,128)(2,1)S(1)}, bf16[1,256,1024]{2,1,0:T(8,128)(2,1)S(1)}, u32[]{:S(2)}, u32[]{:S(2)}) collective-permute-start(bf16[1,256,1024]{2,1,0:T(8,128)(2,1)S(1)} %get-tuple-element.45), channel_id=1, source_target_pairs={{0,16},{16,0},{1,17},{17,1},{2,18},{18,2},{3,19},{19,3},{4,20},{20... | collective-permute-start | bytes 1572872 | tf_op jit(solution)/shard_map/ppermute | solution.py:226
  79.2 50.6 %collective-permute-start.8 = (bf16[1,256,1024]{2,1,0:T(8,128)(2,1)S(1)}, bf16[1,256,1024]{2,1,0:T(8,128)(2,1)S(1)}, u32[]{:S(2)}, u32[]{:S(2)}) collective-permute-start(bf16[1,256,1024]{2,1,0:T(8,128)(2,1)S(1)} %get-tuple-element.42), channel_id=1, source_target_pairs={{0,16},{16,0},{1,17},{17,1},{2,18},{18,2},{3,19},{19,3},{4,20},{20... | collective-permute-start | bytes 1572872 | tf_op jit(solution)/shard_map/ppermute | solution.py:226
  84.9 55.3 %collective-permute-start.7 = (bf16[1,256,1024]{2,1,0:T(8,128)(2,1)S(1)}, bf16[1,256,1024]{2,1,0:T(8,128)(2,1)S(1)}, u32[]{:S(2)}, u32[]{:S(2)}) collective-permute-start(bf16[1,256,1024]{2,1,0:T(8,128)(2,1)S(1)} %get-tuple-element.41), channel_id=1, source_target_pairs={{0,16},{16,0},{1,17},{17,1},{2,18},{18,2},{3,19},{19,3},{4,20},{20... | collective-permute-start | bytes 1572872 | tf_op jit(solution)/shard_map/ppermute | solution.py:226
